TPU v7x, 256 devices: a whole 4x4x8 slice. The times are simulated.
256 devices in a mesh: grp: 8 (over x, core), dev: 32 (over y, z).
Axes of the slice: x: 4, y: 4, z: 8, core: 2. Of those that a mesh axis runs over, the one named last changes fastest.
Arguments:
- features: bfloat16 [512, 128, 512], P(('grp', 'dev')), may hold values from -6 to 6
- grad_out: bfloat16 [512, 128, 512], P(('grp', 'dev')), may hold values from -6 to 6
- conv_weight: bfloat16 [27, 128, 128], replicated, may hold values from -0.109375 to 0.109375
- coarse_up: bfloat16 [128, 256], replicated, may hold values from -0.5 to 0.5
- coarse_down: bfloat16 [256, 128], replicated, may hold values from -0.375 to 0.375
- counts: int32 [256], P(('grp', 'dev')), may hold values from 1 to 2, as said below
- neighbour_owner: int32 [512, 26], P(('grp', 'dev')), may hold values from -1 to 31, as said below
- neighbour_slot: int32 [512, 26], P(('grp', 'dev')), may hold values from -1 to 1, as said below
- parent: int32 [512], P(('grp', 'dev')), may hold values from -1 to 3, as said below
- child_slot: int32 [512], P(('grp', 'dev')), may hold values from -1 to 63, as said below
Outputs:
- output: bfloat16 [512, 128, 512], P(('grp', 'dev'))
- grad_features: bfloat16 [512, 128, 512], P(('grp', 'dev'))
- grad_conv: float32 [27, 128, 128], replicated
- grad_up: float32 [128, 256], replicated
- grad_down: float32 [256, 128], replicated
Inputs may be any that keep to these rules, and one draw needn't show every extreme that they name: counts: each region has a device with exactly 2 live bricks. neighbour_owner: -1 for no neighbour and on every slot that is not live; otherwise a device of the same region. The bricks of one device name at most one distinct brick of any other device, and some device names one. neighbour_slot: -1 exactly where neighbour_owner is -1; otherwise a live slot of that owner. parent: -1 on slots that are not live; live slots of one region have distinct (parent, child_slot) pairs. child_slot: -1 on slots that are not live.
All inputs are finite; a program needn't handle non-finite values.
Results may differ from a plain program's by a relative error of at most 0.0067.
Values may be sent and summed in bfloat16 or wider, within the bound.
No kernel may reach another device: no remote copies, remote signals or barrier semaphores. Data moves between devices by JAX's collectives and lax.ppermute only.
A program may use at most 192 MiB of HBM per device.

v0:
```python
import jax
import jax.numpy as jnp
from jax import lax
from jax.sharding import PartitionSpec as P

OFFSETS = [
    (a, b, c) for a in (-1, 0, 1) for b in (-1, 0, 1) for c in (-1, 0, 1) if (a, b, c) != (0, 0, 0)
]


def source_cut(step):
    if step < 0:
        return slice(7, 8)
    if step == 0:
        return slice(0, 8)
    return slice(0, 1)


def padded_span(step):
    if step < 0:
        return slice(0, 1)
    if step == 0:
        return slice(1, 9)
    return slice(9, 10)


def assemble(center, source, lookup):
    rows = source.shape[0]
    pieces = {(0, 0, 0): center}
    for n, (a, b, c) in enumerate(OFFSETS):
        faces = source[:, :, source_cut(a), source_cut(b), source_cut(c)]
        wanted = lookup[:, n]
        taken = jnp.take(faces, jnp.clip(wanted, 0, rows - 1), axis=0)
        pieces[a, b, c] = jnp.where(
            (wanted >= 0)[:, None, None, None, None], taken, jnp.zeros_like(taken)
        )
    planes = []
    for a in (-1, 0, 1):
        lines = [jnp.concatenate([pieces[a, b, c] for c in (-1, 0, 1)], axis=4) for b in (-1, 0, 1)]
        planes.append(jnp.concatenate(lines, axis=3))
    return jnp.concatenate(planes, axis=2)


def columns(padded):
    rows, width = (padded.shape[0], padded.shape[1])
    return jnp.stack(
        [
            padded[:, :, a : a + 8, b : b + 8, c : c + 8].reshape(rows, width, 512)
            for a in range(3)
            for b in range(3)
            for c in range(3)
        ],
        axis=1,
    )


def spread(grad_cols):
    rows, width = (grad_cols.shape[0], grad_cols.shape[2])
    total = jnp.zeros((rows, width, 10, 10, 10), jnp.float32)
    k = 0
    for a in range(3):
        for b in range(3):
            for c in range(3):
                block = grad_cols[:, k].reshape(rows, width, 8, 8, 8)
                total = total + jnp.pad(block, ((0, 0), (0, 0), (a, 2 - a), (b, 2 - b), (c, 2 - c)))
                k += 1
    return total


def scatter_pieces(total, grad_pad, lookup):
    rows = total.shape[0]
    for n, (a, b, c) in enumerate(OFFSETS):
        target = jnp.where(lookup[:, n] >= 0, lookup[:, n], rows)
        total = total.at[target, :, source_cut(a), source_cut(b), source_cut(c)].add(
            grad_pad[:, :, padded_span(a), padded_span(b), padded_span(c)], mode="drop"
        )
    return total


def pool_blocks(values):
    rows, width = (values.shape[0], values.shape[1])
    return values.reshape(rows, width, 2, 4, 2, 4, 2, 4).sum(axis=(3, 5, 7)).reshape(rows, width, 8)


def expand(values):
    rows, width = (values.shape[0], values.shape[1])
    shaped = values.reshape(rows, width, 2, 1, 2, 1, 2, 1)
    return jnp.broadcast_to(shaped, (rows, width, 2, 4, 2, 4, 2, 4)).reshape(rows, width, 512)


def silu_slope(value):
    gate = jax.nn.sigmoid(value)
    return gate * (1.0 + value * (1.0 - gate))


def on_device(
    features,
    grad_out,
    conv_weight,
    coarse_up,
    coarse_down,
    counts,
    neighbour_owner,
    neighbour_slot,
    parent,
    child_slot,
):
    bricks, width = (features.shape[0], features.shape[1])
    owners = lax.axis_size("dev")
    own_rank = lax.axis_index("dev")
    kc_count = owners * bricks // 16
    slot_ids = jnp.arange(bricks, dtype=jnp.int32)
    live_rows = slot_ids < counts[0]
    live_in = jnp.where(live_rows[:, None, None], features, jnp.zeros_like(features))
    live_grad = jnp.where(live_rows[:, None, None], grad_out.astype(jnp.float32), jnp.float32(0.0))
    remote = (neighbour_owner >= 0) & (neighbour_owner != own_rank)
    ask_owner = (
        (neighbour_owner[:, :, None] == jnp.arange(owners)[None, None, :]) & remote[:, :, None]
    ).astype(jnp.float32)
    ask_slot = (neighbour_slot[:, :, None] == slot_ids[None, None, :]).astype(jnp.float32)
    needed = jnp.einsum("sdp,sdj->pj", ask_owner, ask_slot) > 0.5
    wanted = jnp.sum(jnp.where(needed, slot_ids[None, :] + 1, 0), axis=1) - 1
    asked = lax.all_to_all(wanted[:, None], "dev", split_axis=0, concat_axis=0, tiled=True)[:, 0]
    outgoing = jnp.take(live_in, jnp.clip(asked, 0, bricks - 1), axis=0)
    outgoing = jnp.where((asked >= 0)[:, None, None], outgoing, jnp.zeros_like(outgoing))
    incoming = lax.all_to_all(outgoing, "dev", split_axis=0, concat_axis=0, tiled=True)
    available = jnp.concatenate([live_in, incoming], axis=0).reshape(
        bricks + owners, width, 8, 8, 8
    )
    lookup = jnp.where(
        neighbour_owner < 0,
        -1,
        jnp.where(neighbour_owner == own_rank, neighbour_slot, bricks + neighbour_owner),
    )
    padded = assemble(live_in.reshape(bricks, width, 8, 8, 8), available, lookup)
    blocked = padded.reshape(bricks // 2, 2, width, 10, 10, 10)

    def conv_block(block):
        return jnp.einsum(
            "mkiv,kio->mov", columns(block), conv_weight, preferred_element_type=jnp.float32
        )

    pre_conv = lax.map(conv_block, blocked).reshape(bricks, width, 512)
    active = jax.nn.silu(pre_conv)
    pooled = (pool_blocks(active) / 64.0).astype(jnp.bfloat16)
    grad_pool = pool_blocks(live_grad).astype(jnp.bfloat16)
    position = jnp.where(live_rows & (parent >= 0), parent * 64 + child_slot, -1)
    onehot = (
        (position[:, None] == jnp.arange(kc_count * 64)[None, :])
        .astype(jnp.bfloat16)
        .reshape(bricks, kc_count, 64)
    )
    every_hot, every_pool, every_grad = (
        lax.all_gather(onehot.reshape(bricks, kc_count * 64), "dev", axis=0, tiled=True),
        lax.all_gather(pooled.reshape(bricks, width * 8), "dev", axis=0, tiled=True),
        lax.all_gather(grad_pool.reshape(bricks, width * 8), "dev", axis=0, tiled=True),
    )
    members = every_hot.shape[0]
    hot_table = every_hot.reshape(members, kc_count, 64)
    coarse_in = (
        jnp.einsum(
            "bkq,bcs->kcqs",
            hot_table,
            every_pool.reshape(members, width, 8),
            preferred_element_type=jnp.float32,
        )
        .reshape(kc_count, width, 512)
        .astype(jnp.bfloat16)
    )
    coarse_pre = jnp.einsum("kcv,ce->kev", coarse_in, coarse_up, preferred_element_type=jnp.float32)
    coarse_mid = jax.nn.silu(coarse_pre).astype(jnp.bfloat16)
    coarse_out = jnp.einsum(
        "kev,ec->kcv", coarse_mid, coarse_down, preferred_element_type=jnp.float32
    ).astype(jnp.bfloat16)
    coarse_out, kept_state = (coarse_out, (coarse_in, coarse_pre, coarse_mid))
    grad_coarse = (
        jnp.einsum(
            "bkq,bcs->kcqs",
            hot_table,
            every_grad.reshape(members, width, 8),
            preferred_element_type=jnp.float32,
        )
        .reshape(kc_count, width, 512)
        .astype(jnp.bfloat16)
    )
    coarse_in, coarse_pre, coarse_mid = kept_state
    grad_mid = jnp.einsum(
        "kcv,ec->kev", grad_coarse, coarse_down, preferred_element_type=jnp.float32
    )
    grad_pre = (grad_mid * silu_slope(coarse_pre)).astype(jnp.bfloat16)
    grad_down = jnp.einsum(
        "kev,kcv->ec", coarse_mid, grad_coarse, preferred_element_type=jnp.float32
    )
    grad_up = jnp.einsum("kcv,kev->ce", coarse_in, grad_pre, preferred_element_type=jnp.float32)
    grad_cin = jnp.einsum(
        "kev,ce->kcv", grad_pre, coarse_up, preferred_element_type=jnp.float32
    ).astype(jnp.bfloat16)
    grad_cin, (grad_up, grad_down) = (grad_cin, (grad_up, grad_down))
    lifted = jnp.einsum(
        "bkq,kcqs->bcs",
        onehot,
        coarse_out.reshape(kc_count, width, 64, 8),
        preferred_element_type=jnp.float32,
    )
    output = (live_in.astype(jnp.float32) + active + expand(lifted)).astype(jnp.bfloat16)
    weighting = (own_rank == 0).astype(jnp.float32)
    grad_back = jnp.einsum(
        "bkq,kcqs->bcs",
        onehot,
        grad_cin.reshape(kc_count, width, 64, 8),
        preferred_element_type=jnp.float32,
    )
    grad_conv_in = ((live_grad + expand(grad_back) / 64.0) * silu_slope(pre_conv)).astype(
        jnp.bfloat16
    )

    def back_block(pair):
        block, grad_block = pair
        grad_cols = jnp.einsum(
            "mov,kio->mkiv", grad_block, conv_weight, preferred_element_type=jnp.float32
        )
        weight_piece = jnp.einsum(
            "mkiv,mov->kio", columns(block), grad_block, preferred_element_type=jnp.float32
        )
        return (spread(grad_cols), weight_piece)

    grad_pad, weight_pieces = lax.map(
        back_block, (blocked, grad_conv_in.reshape(bricks // 2, 2, width, 512))
    )
    grad_pad = grad_pad.reshape(bricks, width, 10, 10, 10)
    weight_part = jnp.sum(weight_pieces, axis=0)
    grad_avail = scatter_pieces(
        jnp.zeros((bricks + owners, width, 8, 8, 8), jnp.float32), grad_pad, lookup
    )
    grad_total = (
        live_grad.reshape(bricks, width, 8, 8, 8)
        + grad_pad[:, :, 1:9, 1:9, 1:9]
        + grad_avail[:bricks]
    )
    sending = grad_avail[bricks:].reshape(owners, width, 512)
    returned = lax.all_to_all(
        sending.astype(jnp.bfloat16), "dev", split_axis=0, concat_axis=0, tiled=True
    ).astype(sending.dtype)
    target = jnp.where(asked >= 0, asked, bricks)
    grad_total = grad_total.reshape(bricks, width, 512).at[target].add(returned, mode="drop")
    grad_conv, grad_up, grad_down = lax.psum(
        (weight_part, grad_up * weighting, grad_down * weighting), ("grp", "dev")
    )
    return (output, grad_total.astype(jnp.bfloat16), grad_conv, grad_up, grad_down)


def solution(mesh):
    return jax.shard_map(
        on_device,
        mesh=mesh,
        in_specs=(
            P(("grp", "dev"), None, None),
            P(("grp", "dev"), None, None),
            P(),
            P(),
            P(),
            P(("grp", "dev")),
            P(("grp", "dev"), None),
            P(("grp", "dev"), None),
            P(("grp", "dev")),
            P(("grp", "dev")),
        ),
        out_specs=(P(("grp", "dev"), None, None), P(("grp", "dev"), None, None), P(), P(), P()),
        check_vma=False,
    )
```

profile of v0, /device:TPU:1, one launch (start us, length us, event | category | flops | bytes accessed | tf_op | source)
XLA Modules:
  0.0 1210.3 jit_solution(263330243556792993)
XLA Ops:
  9.6 12.0 all-to-all-start
  53.9 119.7 %all-gather.1 = bf16[32,2,256]{2,1,0:T(2,128)(2,1)S(1)} all-gather(bf16[1,2,256]{2,1,0:T(2,128)(2,1)S(1)} %fusion.79), channel_id=1, replica_groups=mesh['grp'=8,'dev'=32] {'dev'}, dimensions={0}, use_global_device_ids=true | all-gather | bytes 33792 | tf_op jit(solution)/shard_map/all_gather | solution.py:154
  174.5 32.3 %all-gather.2 = bf16[32,2,1024]{2,1,0:T(2,128)(2,1)S(1)} all-gather(bf16[1,2,1024]{2,1,0:T(2,128)(2,1)S(1)} %reshape.2154), channel_id=1, replica_groups=mesh['grp'=8,'dev'=32] {'dev'}, dimensions={0}, use_global_device_ids=true | all-gather | bytes 135168 | tf_op jit(solution)/shard_map/all_gather | solution.py:156
  322.2 31.4 %all-gather = bf16[32,2,1024]{2,1,0:T(2,128)(2,1)S(1)} all-gather(bf16[1,2,1024]{2,1,0:T(2,128)(2,1)S(1)} %reshape.2150), channel_id=1, replica_groups=mesh['grp'=8,'dev'=32] {'dev'}, dimensions={0}, use_global_device_ids=true | all-gather | bytes 135168 | tf_op jit(solution)/shard_map/all_gather | solution.py:155
  380.4 23.9 %while.35 = (s32[]{:T(128)}, f32[34,128,8,8,8]{1,4,3,2,0:T(8,128)}, s32[2,4]{1,0:T(2,128)S(1)}, f32[2,128,1,1,1]{1,4,3,2,0:T(1,128)S(1)}, s32[]{:T(128)}, /*index=5*/s32[5]{0:T(128)S(1)}, s32[1]{0:T(128)}, s32[]{:T(128)}) while((s32[]{:T(128)}, f32[34,128,8,8,8]{1,4,3,2,0:T(8,128)}, s32[2,4]{1,0:T(2,128)S(1)}, f32[2,128,1,1,1]{1,4,3,2,0:T(1,128)S(1)}, ...), condition=%wide.while_cond, body=%wide.while_body.sunk | while | flops 277 | bytes 2819 | solution.py:74
  404.3 14.1 %while.36 = (s32[]{:T(128)}, f32[34,128,8,8,8]{1,4,3,2,0:T(8,128)}, s32[2,3]{1,0:T(2,128)S(1)}, f32[2,128,1,1,8]{1,4,3,2,0:T(8,128)S(1)}, s32[]{:T(128)}, /*index=5*/s32[5]{0:T(128)S(1)}, s32[1]{0:T(128)}) while((s32[]{:T(128)}, f32[34,128,8,8,8]{1,4,3,2,0:T(8,128)}, s32[2,3]{1,0:T(2,128)S(1)}, f32[2,128,1,1,8]{1,4,3,2,0:T(8,128)S(1)}, s32[]{:T(128)}, ...), condition=%wide.while_cond.1, body=%wide.while_body.1.sunk | while | flops 2069 | bytes 15058 | solution.py:74
  418.4 23.6 %while.37 = (s32[]{:T(128)}, f32[34,128,8,8,8]{1,4,3,2,0:T(8,128)}, s32[2,4]{1,0:T(2,128)S(1)}, f32[2,128,1,1,1]{1,4,3,2,0:T(1,128)S(1)}, s32[]{:T(128)}, /*index=5*/s32[5]{0:T(128)S(1)}, s32[1]{0:T(128)}, s32[]{:T(128)}) while((s32[]{:T(128)}, f32[34,128,8,8,8]{1,4,3,2,0:T(8,128)}, s32[2,4]{1,0:T(2,128)S(1)}, f32[2,128,1,1,1]{1,4,3,2,0:T(1,128)S(1)}, ...), condition=%wide.while_cond.2, body=%wide.while_body.2.sunk | while | flops 277 | bytes 2819 | solution.py:74
  442.0 20.1 %while.38 = (s32[]{:T(128)}, f32[34,128,8,8,8]{1,4,3,2,0:T(8,128)}, s32[2,3]{1,0:T(2,128)S(1)}, f32[2,128,1,8,1]{1,4,3,2,0:T(1,128)S(1)}, s32[]{:T(128)}, /*index=5*/s32[5]{0:T(128)S(1)}, s32[1]{0:T(128)}, s32[]{:T(128)}) while((s32[]{:T(128)}, f32[34,128,8,8,8]{1,4,3,2,0:T(8,128)}, s32[2,3]{1,0:T(2,128)S(1)}, f32[2,128,1,8,1]{1,4,3,2,0:T(1,128)S(1)}, ...), condition=%wide.while_cond.3, body=%wide.while_body.3.sunk | while | flops 2069 | bytes 20719 | solution.py:74
  462.1 11.9 while.39
  473.9 19.9 %while.40 = (s32[]{:T(128)}, f32[34,128,8,8,8]{1,4,3,2,0:T(8,128)}, s32[2,3]{1,0:T(2,128)S(1)}, f32[2,128,1,8,1]{1,4,3,2,0:T(1,128)S(1)}, s32[]{:T(128)}, /*index=5*/s32[5]{0:T(128)S(1)}, s32[1]{0:T(128)}, s32[]{:T(128)}) while((s32[]{:T(128)}, f32[34,128,8,8,8]{1,4,3,2,0:T(8,128)}, s32[2,3]{1,0:T(2,128)S(1)}, f32[2,128,1,8,1]{1,4,3,2,0:T(1,128)S(1)}, ...), condition=%wide.while_cond.5, body=%wide.while_body.5.sunk | while | flops 2069 | bytes 20719 | solution.py:74
  493.8 23.2 %while.41 = (s32[]{:T(128)}, f32[34,128,8,8,8]{1,4,3,2,0:T(8,128)}, s32[2,4]{1,0:T(2,128)S(1)}, f32[2,128,1,1,1]{1,4,3,2,0:T(1,128)S(1)}, s32[]{:T(128)}, /*index=5*/s32[5]{0:T(128)S(1)}, s32[1]{0:T(128)}, s32[]{:T(128)}) while((s32[]{:T(128)}, f32[34,128,8,8,8]{1,4,3,2,0:T(8,128)}, s32[2,4]{1,0:T(2,128)S(1)}, f32[2,128,1,1,1]{1,4,3,2,0:T(1,128)S(1)}, ...), condition=%wide.while_cond.6, body=%wide.while_body.6.sunk | while | flops 277 | bytes 2819 | solution.py:74
  517.1 14.5 %while.42 = (s32[]{:T(128)}, f32[34,128,8,8,8]{1,4,3,2,0:T(8,128)}, s32[2,3]{1,0:T(2,128)S(1)}, f32[2,128,1,1,8]{1,4,3,2,0:T(8,128)S(1)}, s32[]{:T(128)}, /*index=5*/s32[5]{0:T(128)S(1)}, s32[1]{0:T(128)}) while((s32[]{:T(128)}, f32[34,128,8,8,8]{1,4,3,2,0:T(8,128)}, s32[2,3]{1,0:T(2,128)S(1)}, f32[2,128,1,1,8]{1,4,3,2,0:T(8,128)S(1)}, s32[]{:T(128)}, ...), condition=%wide.while_cond.7, body=%wide.while_body.7.sunk | while | flops 2069 | bytes 15058 | solution.py:74
  531.6 23.1 %while.43 = (s32[]{:T(128)}, f32[34,128,8,8,8]{1,4,3,2,0:T(8,128)}, s32[2,4]{1,0:T(2,128)S(1)}, f32[2,128,1,1,1]{1,4,3,2,0:T(1,128)S(1)}, s32[]{:T(128)}, /*index=5*/s32[5]{0:T(128)S(1)}, s32[1]{0:T(128)}, s32[]{:T(128)}) while((s32[]{:T(128)}, f32[34,128,8,8,8]{1,4,3,2,0:T(8,128)}, s32[2,4]{1,0:T(2,128)S(1)}, f32[2,128,1,1,1]{1,4,3,2,0:T(1,128)S(1)}, ...), condition=%wide.while_cond.8, body=%wide.while_body.8.sunk | while | flops 277 | bytes 2819 | solution.py:74
  554.7 19.9 %while.44 = (s32[]{:T(128)}, f32[34,128,8,8,8]{1,4,3,2,0:T(8,128)}, s32[2,3]{1,0:T(2,128)S(1)}, f32[2,128,8,1,1]{1,4,3,2,0:T(1,128)S(1)}, s32[]{:T(128)}, /*index=5*/s32[5]{0:T(128)S(1)}, s32[1]{0:T(128)}, s32[]{:T(128)}) while((s32[]{:T(128)}, f32[34,128,8,8,8]{1,4,3,2,0:T(8,128)}, s32[2,3]{1,0:T(2,128)S(1)}, f32[2,128,8,1,1]{1,4,3,2,0:T(1,128)S(1)}, ...), condition=%wide.while_cond.9, body=%wide.while_body.9.sunk | while | flops 2069 | bytes 20719 | solution.py:74
  574.7 11.9 while.45
  586.5 19.9 %while.46 = (s32[]{:T(128)}, f32[34,128,8,8,8]{1,4,3,2,0:T(8,128)}, s32[2,3]{1,0:T(2,128)S(1)}, f32[2,128,8,1,1]{1,4,3,2,0:T(1,128)S(1)}, s32[]{:T(128)}, /*index=5*/s32[5]{0:T(128)S(1)}, s32[1]{0:T(128)}, s32[]{:T(128)}) while((s32[]{:T(128)}, f32[34,128,8,8,8]{1,4,3,2,0:T(8,128)}, s32[2,3]{1,0:T(2,128)S(1)}, f32[2,128,8,1,1]{1,4,3,2,0:T(1,128)S(1)}, ...), condition=%wide.while_cond.11, body=%wide.while_body.11.sunk | while | flops 2069 | bytes 20719 | solution.py:74
  606.4 17.2 %while.47 = (s32[]{:T(128)}, f32[34,128,8,8,8]{1,4,3,2,0:T(8,128)}, s32[2,2]{1,0:T(2,128)S(1)}, f32[2,128,8,8,1]{1,4,3,2,0:T(1,128)S(1)}, s32[]{:T(128)}, /*index=5*/s32[5]{0:T(128)S(1)}, s32[1]{0:T(128)}, s32[]{:T(128)}) while((s32[]{:T(128)}, f32[34,128,8,8,8]{1,4,3,2,0:T(8,128)}, s32[2,2]{1,0:T(2,128)S(1)}, f32[2,128,8,8,1]{1,4,3,2,0:T(1,128)S(1)}, ...), condition=%wide.while_cond.12, body=%wide.while_body.12.sunk | while | flops 16405 | bytes 164059 | solution.py:74
  623.6 17.2 %while.48 = (s32[]{:T(128)}, f32[34,128,8,8,8]{1,4,3,2,0:T(8,128)}, s32[2,2]{1,0:T(2,128)S(1)}, f32[2,128,8,8,1]{1,4,3,2,0:T(1,128)S(1)}, s32[]{:T(128)}, /*index=5*/s32[5]{0:T(128)S(1)}, s32[1]{0:T(128)}, s32[]{:T(128)}) while((s32[]{:T(128)}, f32[34,128,8,8,8]{1,4,3,2,0:T(8,128)}, s32[2,2]{1,0:T(2,128)S(1)}, f32[2,128,8,8,1]{1,4,3,2,0:T(1,128)S(1)}, ...), condition=%wide.while_cond.13, body=%wide.while_body.13.sunk | while | flops 16405 | bytes 164059 | solution.py:74
  640.8 19.7 %while.49 = (s32[]{:T(128)}, f32[34,128,8,8,8]{1,4,3,2,0:T(8,128)}, s32[2,3]{1,0:T(2,128)S(1)}, f32[2,128,8,1,1]{1,4,3,2,0:T(1,128)S(1)}, s32[]{:T(128)}, /*index=5*/s32[5]{0:T(128)S(1)}, s32[1]{0:T(128)}, s32[]{:T(128)}) while((s32[]{:T(128)}, f32[34,128,8,8,8]{1,4,3,2,0:T(8,128)}, s32[2,3]{1,0:T(2,128)S(1)}, f32[2,128,8,1,1]{1,4,3,2,0:T(1,128)S(1)}, ...), condition=%wide.while_cond.14, body=%wide.while_body.14.sunk | while | flops 2069 | bytes 20719 | solution.py:74
  660.5 11.9 while.50
  672.3 19.9 %while.51 = (s32[]{:T(128)}, f32[34,128,8,8,8]{1,4,3,2,0:T(8,128)}, s32[2,3]{1,0:T(2,128)S(1)}, f32[2,128,8,1,1]{1,4,3,2,0:T(1,128)S(1)}, s32[]{:T(128)}, /*index=5*/s32[5]{0:T(128)S(1)}, s32[1]{0:T(128)}, s32[]{:T(128)}) while((s32[]{:T(128)}, f32[34,128,8,8,8]{1,4,3,2,0:T(8,128)}, s32[2,3]{1,0:T(2,128)S(1)}, f32[2,128,8,1,1]{1,4,3,2,0:T(1,128)S(1)}, ...), condition=%wide.while_cond.16, body=%wide.while_body.16.sunk | while | flops 2069 | bytes 20719 | solution.py:74
  692.2 23.5 %while.52 = (s32[]{:T(128)}, f32[34,128,8,8,8]{1,4,3,2,0:T(8,128)}, s32[2,4]{1,0:T(2,128)S(1)}, f32[2,128,1,1,1]{1,4,3,2,0:T(1,128)S(1)}, s32[]{:T(128)}, /*index=5*/s32[5]{0:T(128)S(1)}, s32[1]{0:T(128)}, s32[]{:T(128)}) while((s32[]{:T(128)}, f32[34,128,8,8,8]{1,4,3,2,0:T(8,128)}, s32[2,4]{1,0:T(2,128)S(1)}, f32[2,128,1,1,1]{1,4,3,2,0:T(1,128)S(1)}, ...), condition=%wide.while_cond.17, body=%wide.while_body.17.sunk | while | flops 277 | bytes 2819 | solution.py:74
  715.8 14.2 %while.53 = (s32[]{:T(128)}, f32[34,128,8,8,8]{1,4,3,2,0:T(8,128)}, s32[2,3]{1,0:T(2,128)S(1)}, f32[2,128,1,1,8]{1,4,3,2,0:T(8,128)S(1)}, s32[]{:T(128)}, /*index=5*/s32[5]{0:T(128)S(1)}, s32[1]{0:T(128)}) while((s32[]{:T(128)}, f32[34,128,8,8,8]{1,4,3,2,0:T(8,128)}, s32[2,3]{1,0:T(2,128)S(1)}, f32[2,128,1,1,8]{1,4,3,2,0:T(8,128)S(1)}, s32[]{:T(128)}, ...), condition=%wide.while_cond.18, body=%wide.while_body.18.sunk | while | flops 2069 | bytes 15058 | solution.py:74
  730.0 23.6 %while.54 = (s32[]{:T(128)}, f32[34,128,8,8,8]{1,4,3,2,0:T(8,128)}, s32[2,4]{1,0:T(2,128)S(1)}, f32[2,128,1,1,1]{1,4,3,2,0:T(1,128)S(1)}, s32[]{:T(128)}, /*index=5*/s32[5]{0:T(128)S(1)}, s32[1]{0:T(128)}, s32[]{:T(128)}) while((s32[]{:T(128)}, f32[34,128,8,8,8]{1,4,3,2,0:T(8,128)}, s32[2,4]{1,0:T(2,128)S(1)}, f32[2,128,1,1,1]{1,4,3,2,0:T(1,128)S(1)}, ...), condition=%wide.while_cond.19, body=%wide.while_body.19.sunk | while | flops 277 | bytes 2819 | solution.py:74
  753.6 19.9 %while.55 = (s32[]{:T(128)}, f32[34,128,8,8,8]{1,4,3,2,0:T(8,128)}, s32[2,3]{1,0:T(2,128)S(1)}, f32[2,128,1,8,1]{1,4,3,2,0:T(1,128)S(1)}, s32[]{:T(128)}, /*index=5*/s32[5]{0:T(128)S(1)}, s32[1]{0:T(128)}, s32[]{:T(128)}) while((s32[]{:T(128)}, f32[34,128,8,8,8]{1,4,3,2,0:T(8,128)}, s32[2,3]{1,0:T(2,128)S(1)}, f32[2,128,1,8,1]{1,4,3,2,0:T(1,128)S(1)}, ...), condition=%wide.while_cond.20, body=%wide.while_body.20.sunk | while | flops 2069 | bytes 20719 | solution.py:74
  773.5 11.8 while.56
  785.4 20.0 %while.57 = (s32[]{:T(128)}, f32[34,128,8,8,8]{1,4,3,2,0:T(8,128)}, s32[2,3]{1,0:T(2,128)S(1)}, f32[2,128,1,8,1]{1,4,3,2,0:T(1,128)S(1)}, s32[]{:T(128)}, /*index=5*/s32[5]{0:T(128)S(1)}, s32[1]{0:T(128)}, s32[]{:T(128)}) while((s32[]{:T(128)}, f32[34,128,8,8,8]{1,4,3,2,0:T(8,128)}, s32[2,3]{1,0:T(2,128)S(1)}, f32[2,128,1,8,1]{1,4,3,2,0:T(1,128)S(1)}, ...), condition=%wide.while_cond.22, body=%wide.while_body.22.sunk | while | flops 2069 | bytes 20719 | solution.py:74
  805.3 23.6 %while.58 = (s32[]{:T(128)}, f32[34,128,8,8,8]{1,4,3,2,0:T(8,128)}, s32[2,4]{1,0:T(2,128)S(1)}, f32[2,128,1,1,1]{1,4,3,2,0:T(1,128)S(1)}, s32[]{:T(128)}, /*index=5*/s32[5]{0:T(128)S(1)}, s32[1]{0:T(128)}, s32[]{:T(128)}) while((s32[]{:T(128)}, f32[34,128,8,8,8]{1,4,3,2,0:T(8,128)}, s32[2,4]{1,0:T(2,128)S(1)}, f32[2,128,1,1,1]{1,4,3,2,0:T(1,128)S(1)}, ...), condition=%wide.while_cond.23, body=%wide.while_body.23.sunk | while | flops 277 | bytes 2819 | solution.py:74
  828.9 14.2 %while.59 = (s32[]{:T(128)}, f32[34,128,8,8,8]{1,4,3,2,0:T(8,128)}, s32[2,3]{1,0:T(2,128)S(1)}, f32[2,128,1,1,8]{1,4,3,2,0:T(8,128)S(1)}, s32[]{:T(128)}, /*index=5*/s32[5]{0:T(128)S(1)}, s32[1]{0:T(128)}) while((s32[]{:T(128)}, f32[34,128,8,8,8]{1,4,3,2,0:T(8,128)}, s32[2,3]{1,0:T(2,128)S(1)}, f32[2,128,1,1,8]{1,4,3,2,0:T(8,128)S(1)}, s32[]{:T(128)}, ...), condition=%wide.while_cond.24, body=%wide.while_body.24.sunk | while | flops 2069 | bytes 15058 | solution.py:74
  843.1 23.3 %while.60 = (s32[]{:T(128)}, f32[34,128,8,8,8]{1,4,3,2,0:T(8,128)}, s32[2,4]{1,0:T(2,128)S(1)}, f32[2,128,1,1,1]{1,4,3,2,0:T(1,128)S(1)}, s32[]{:T(128)}, /*index=5*/s32[5]{0:T(128)S(1)}, s32[1]{0:T(128)}, s32[]{:T(128)}) while((s32[]{:T(128)}, f32[34,128,8,8,8]{1,4,3,2,0:T(8,128)}, s32[2,4]{1,0:T(2,128)S(1)}, f32[2,128,1,1,1]{1,4,3,2,0:T(1,128)S(1)}, ...), condition=%wide.while_cond.25, body=%wide.while_body.25.sunk | while | flops 277 | bytes 2819 | solution.py:74
  894.1 49.3 %all-to-all-done.2 = bf16[32,128,512]{1,2,0:T(8,128)(2,1)} async-done(((bf16[32,128,512]{1,2,0:T(8,128)(2,1)}), bf16[32,128,512]{1,2,0:T(8,128)(2,1)}, u32[]{:S(2)}, u32[]{:S(2)}) %all-to-all-start.2) | async-done | bytes 4194336 | tf_op jit(solution)/shard_map/all_to_all | solution.py:241
  962.8 234.4 %all-reduce.42.cloned.1.call-done = (f32[27,128,128]{2,1,0:T(8,128)}, f32[128,256]{1,0:T(8,128)}, f32[256,128]{1,0:T(8,128)}) async-done(((f32[27,128,128]{2,1,0:T(8,128)}, f32[128,256]{1,0:T(8,128)}, f32[256,128]{1,0:T(8,128)}), (f32[27,128,128]{2,1,0:T(8,128)}, f32[128,256]{1,0:T(8,128)}, f32[256,128]{1,0:T(8,128)})) %all-reduce.42.cloned.1.call-update) | async-done | bytes 2031632 | tf_op jit(solution)/shard_map/psum | solution.py:246
  (828 shorter events, 713.7 us)
Async XLA Ops:
  7.2 311.4 %copy-start = (bf16[27,128,128]{2,1,0:T(8,128)(2,1)S(1)}, bf16[27,128,128]{2,1,0:T(8,128)(2,1)}, u32[]{:S(2)}) copy-start(bf16[27,128,128]{2,1,0:T(8,128)(2,1)} %param.26) | copy-start | bytes 2654212
  9.6 24.5 %all-to-all-start = ((s32[32,1,1]{2,1,0:T(1,128)}), s32[32,1,1]{2,1,0:T(1,128)S(1)}, u32[]{:S(2)}, u32[]{:S(2)}) async-start(s32[32,1,1]{2,1,0:T(1,128)} %copy.170), calls=%async_computation | async-start | bytes 32768 | tf_op jit(solution)/shard_map/all_to_all | solution.py:123
  44.5 172.7 %copy-start.90 = (s32[2]{0:T(128)S(1)}, s32[2]{0:T(128)}, u32[]{:S(2)}) copy-start(s32[2]{0:T(128)} %get-tuple-element.765) | copy-start | bytes 28
  44.5 173.3 %copy-start.88 = (s32[2]{0:T(128)S(1)}, s32[2]{0:T(128)}, u32[]{:S(2)}) copy-start(s32[2]{0:T(128)} %get-tuple-element.763) | copy-start | bytes 28
  44.5 173.3 %copy-start.89 = (s32[2]{0:T(128)S(1)}, s32[2]{0:T(128)}, u32[]{:S(2)}) copy-start(s32[2]{0:T(128)} %get-tuple-element.764) | copy-start | bytes 28
  44.5 173.9 %copy-start.86 = (s32[2]{0:T(128)S(1)}, s32[2]{0:T(128)}, u32[]{:S(2)}) copy-start(s32[2]{0:T(128)} %get-tuple-element.767) | copy-start | bytes 28
  44.5 173.9 %copy-start.87 = (s32[2]{0:T(128)S(1)}, s32[2]{0:T(128)}, u32[]{:S(2)}) copy-start(s32[2]{0:T(128)} %get-tuple-element.768) | copy-start | bytes 28
  44.5 174.5 %copy-start.75 = (s32[2]{0:T(128)S(1)}, s32[2]{0:T(128)}, u32[]{:S(2)}) copy-start(s32[2]{0:T(128)} %get-tuple-element.290) | copy-start | bytes 28
  44.5 194.7 %all-to-all-start.1 = ((bf16[32,128,512]{1,2,0:T(8,128)(2,1)}), bf16[32,128,512]{1,2,0:T(8,128)(2,1)}, u32[]{:S(2)}, u32[]{:S(2)}) async-start(bf16[32,128,512]{1,2,0:T(8,128)(2,1)} %select_select_fusion), calls=%async_computation.1 | async-start | bytes 8388608 | tf_op jit(solution)/shard_map/all_to_all | solution.py:126
  375.3 179.4 %copy-start.109 = (s32[2,3]{1,0:T(2,128)S(1)}, s32[2,3]{1,0:T(2,128)}, u32[]{:S(2)}) copy-start(s32[2,3]{1,0:T(2,128)} %concatenate.184) | copy-start | bytes 76
  375.3 199.4 %copy-start.108 = (s32[2,2]{1,0:T(2,128)S(1)}, s32[2,2]{1,0:T(2,128)}, u32[]{:S(2)}) copy-start(s32[2,2]{1,0:T(2,128)} %concatenate.185) | copy-start | bytes 52
  375.3 179.4 %copy-start.123 = (s32[5]{0:T(128)S(1)}, s32[5]{0:T(128)}, u32[]{:S(2)}) copy-start(s32[5]{0:T(128)} %constant.1491) | copy-start | bytes 64
  375.3 199.3 %copy-start.124 = (s32[5]{0:T(128)S(1)}, s32[5]{0:T(128)}, u32[]{:S(2)}) copy-start(s32[5]{0:T(128)} %constant.1505) | copy-start | bytes 64
  375.5 211.0 %copy-start.95 = (s32[2,3]{1,0:T(2,128)S(1)}, s32[2,3]{1,0:T(2,128)}, u32[]{:S(2)}) copy-start(s32[2,3]{1,0:T(2,128)} %get-tuple-element.1911) | copy-start | bytes 76
  375.6 230.8 %copy-start.107 = (s32[2,2]{1,0:T(2,128)S(1)}, s32[2,2]{1,0:T(2,128)}, u32[]{:S(2)}) copy-start(s32[2,2]{1,0:T(2,128)} %concatenate.187) | copy-start | bytes 52
  375.6 230.8 %copy-start.125 = (s32[5]{0:T(128)S(1)}, s32[5]{0:T(128)}, u32[]{:S(2)}) copy-start(s32[5]{0:T(128)} %constant.1531) | copy-start | bytes 64
  375.6 248.0 %copy-start.106 = (s32[2,2]{1,0:T(2,128)S(1)}, s32[2,2]{1,0:T(2,128)}, u32[]{:S(2)}) copy-start(s32[2,2]{1,0:T(2,128)} %concatenate.188) | copy-start | bytes 52
  375.6 265.2 %copy-start.94 = (s32[2,3]{1,0:T(2,128)S(1)}, s32[2,3]{1,0:T(2,128)}, u32[]{:S(2)}) copy-start(s32[2,3]{1,0:T(2,128)} %get-tuple-element.1983) | copy-start | bytes 76
  375.6 284.8 %copy-start.105 = (s32[2,2]{1,0:T(2,128)S(1)}, s32[2,2]{1,0:T(2,128)}, u32[]{:S(2)}) copy-start(s32[2,2]{1,0:T(2,128)} %concatenate.190) | copy-start | bytes 52
  375.7 296.7 %copy-start.104 = (s32[2,3]{1,0:T(2,128)S(1)}, s32[2,3]{1,0:T(2,128)}, u32[]{:S(2)}) copy-start(s32[2,3]{1,0:T(2,128)} %concatenate.191) | copy-start | bytes 76
  375.7 316.6 %copy-start.98 = (s32[2,4]{1,0:T(2,128)S(1)}, s32[2,4]{1,0:T(2,128)}, u32[]{:S(2)}) copy-start(s32[2,4]{1,0:T(2,128)} %get-tuple-element.2052) | copy-start | bytes 100
  375.7 340.1 %copy-start.93 = (s32[2,3]{1,0:T(2,128)S(1)}, s32[2,3]{1,0:T(2,128)}, u32[]{:S(2)}) copy-start(s32[2,3]{1,0:T(2,128)} %get-tuple-element.2076) | copy-start | bytes 76
  380.3 349.7 %copy-start.115 = (s32[2,4]{1,0:T(2,128)S(1)}, s32[2,4]{1,0:T(2,128)}, u32[]{:S(2)}) copy-start(s32[2,4]{1,0:T(2,128)} %get-tuple-element.2097) | copy-start | bytes 100
  380.3 373.3 %copy-start.92 = (s32[2,3]{1,0:T(2,128)S(1)}, s32[2,3]{1,0:T(2,128)}, u32[]{:S(2)}) copy-start(s32[2,3]{1,0:T(2,128)} %get-tuple-element.2121) | copy-start | bytes 76
  380.3 393.2 %copy-start.103 = (s32[2,2]{1,0:T(2,128)S(1)}, s32[2,2]{1,0:T(2,128)}, u32[]{:S(2)}) copy-start(s32[2,2]{1,0:T(2,128)} %concatenate.196) | copy-start | bytes 52
  380.3 405.1 %copy-start.102 = (s32[2,3]{1,0:T(2,128)S(1)}, s32[2,3]{1,0:T(2,128)}, u32[]{:S(2)}) copy-start(s32[2,3]{1,0:T(2,128)} %concatenate.197) | copy-start | bytes 76
  380.3 425.0 %copy-start.114 = (s32[2,4]{1,0:T(2,128)S(1)}, s32[2,4]{1,0:T(2,128)}, u32[]{:S(2)}) copy-start(s32[2,4]{1,0:T(2,128)} %get-tuple-element.2190) | copy-start | bytes 100
  380.3 448.6 %copy-start.101 = (s32[2,3]{1,0:T(2,128)S(1)}, s32[2,3]{1,0:T(2,128)}, u32[]{:S(2)}) copy-start(s32[2,3]{1,0:T(2,128)} %concatenate.199) | copy-start | bytes 76
  380.4 462.8 %copy-start.113 = (s32[2,4]{1,0:T(2,128)S(1)}, s32[2,4]{1,0:T(2,128)}, u32[]{:S(2)}) copy-start(s32[2,4]{1,0:T(2,128)} %get-tuple-element.2235) | copy-start | bytes 100
  873.1 70.3 %all-to-all-start.2 = ((bf16[32,128,512]{1,2,0:T(8,128)(2,1)}), bf16[32,128,512]{1,2,0:T(8,128)(2,1)}, u32[]{:S(2)}, u32[]{:S(2)}) async-start(bf16[32,128,512]{1,2,0:T(8,128)(2,1)} %bitcast.870), calls=%async_computation.2 | async-start | bytes 8388608 | tf_op jit(solution)/shard_map/all_to_all | solution.py:241
  880.5 316.7 %all-reduce.42.cloned.1.call-start = ((), (), s32[]{:S(2)}) async-start(), calls=%async_computation.3 | async-start | bytes 4063232 | tf_op jit(solution)/shard_map/psum | solution.py:246
  950.5 252.7 %copy-start.1 = (bf16[27,128,128]{2,1,0:T(8,128)(2,1)S(1)}, bf16[27,128,128]{2,1,0:T(8,128)(2,1)}, u32[]{:S(2)}) copy-start(bf16[27,128,128]{2,1,0:T(8,128)(2,1)} %param.26) | copy-start | bytes 2654212
  (98 other events, 2336.2 us)
Sparse Core Ops, SparseCore 0:
  892.0 305.1 all-reduce.41
where the time goes:
time: 1230 us; the launch traced here: 1210 us
  local copies, waits for them, and re-layouts  376 us (31%)
  other arithmetic  299 us (24%)
  waiting for transfers between devices  284 us (23%)
  blocking collectives  183 us (15%)
  starting transfers between devices  28.9 us (2%)
  matrix products  21.7 us (2%)
  between operations  17 us (1%)
    scatter-add x192, local copies, waits for them, and re-layouts  266 us
    psum x1, waiting for transfers between devices, on_device(): lax.psum((weight_part, grad_up * weighting, grad_down * weighting), ('grp...  234 us
    scatter-add x104, other arithmetic  219 us
    all_gather x1, blocking collectives, on_device(): lax.all_gather(onehot.reshape(bricks, kc_count * 64), 'dev', axis=0, tile...  120 us
    all_to_all x1, waiting for transfers between devices, on_device(): lax.all_to_all(sending.astype(jnp.bfloat16), 'dev', split_axis=0, concat_...  49.3 us
    all_gather x1, blocking collectives, on_device(): lax.all_gather(grad_pool.reshape(bricks, width * 8), 'dev', axis=0, tiled...  32.3 us
    all_gather x1, blocking collectives, on_device(): lax.all_gather(pooled.reshape(bricks, width * 8), 'dev', axis=0, tiled=True)  31.4 us
    gather x26, local copies, waits for them, and re-layouts, assemble(): taken = jnp.take(faces, jnp.clip(wanted, 0, rows - 1), axis=0)  30.7 us
  transfers between devices with their start and end apart: 4, of which 2 were waited for; matrix products, arithmetic and copies ran while one was open for 6% of the time, Pallas kernels for 0%

commit v1 on v0

v1 whole, which is shorter than its diff:
```python
import jax
import jax.numpy as jnp
import numpy as np
from jax import lax
from jax.experimental import pallas as pl
from jax.experimental.pallas import tpu as pltpu
from jax.sharding import PartitionSpec as P

BF = jnp.bfloat16
F32 = jnp.float32

OFFSETS = [
    (a, b, c) for a in (-1, 0, 1) for b in (-1, 0, 1) for c in (-1, 0, 1) if (a, b, c) != (0, 0, 0)
]
FACES = [d for d in OFFSETS if sum(map(abs, d)) == 1]
EDGES = [d for d in OFFSETS if sum(map(abs, d)) == 2]
CORNERS = [d for d in OFFSETS if sum(map(abs, d)) == 3]
PIECE = {d: 64 * n for n, d in enumerate(FACES)}
PIECE.update({d: 384 + 8 * n for n, d in enumerate(EDGES)})
PIECE.update({d: 480 + n for n, d in enumerate(CORNERS)})


def piece_row(i, q):
    if q < 12:
        face = q // 2
        return 64 * face + 2 * i + q % 2, OFFSETS.index(FACES[face])
    if q < 15:
        flat = 32 * (q - 12) + i
        return 384 + flat, OFFSETS.index(EDGES[flat // 8])
    return 480 + i // 4, OFFSETS.index(CORNERS[i // 4])


def cut(step):
    return [7] if step < 0 else ([0] if step > 0 else list(range(8)))


def tables():
    voxel = np.full(512, -1)
    for (a, b, c), base in PIECE.items():
        cells = [x * 64 + y * 8 + z for x in cut(a) for y in cut(b) for z in cut(c)]
        voxel[base : base + len(cells)] = cells
    take = np.zeros((512, 512), np.float32)
    pack = np.zeros((512, 512), np.float32)
    unpack = np.zeros((512, 512), np.float32)
    give = np.zeros((512, 512), np.float32)
    ask = np.zeros((512, 128), np.float32)
    for i in range(32):
        for q in range(16):
            row, direction = piece_row(i, q)
            at = 16 * i + q
            take[at, voxel[row]] = 1
            pack[at, row] = 1
            ask[at, direction] = 1
            if q < 15 or i % 4 == 0:
                unpack[row, at] = 1
                give[voxel[row], at] = 1
    pool = np.zeros((16, 512), np.float32)
    for v in range(512):
        a, b, c = v // 64, v // 8 % 8, v % 8
        pool[(a // 4) * 4 + (b // 4) * 2 + c // 4, v] = 1
    return take, pack, unpack, give, ask, pool


TAKE, PACK, UNPACK, GIVE, ASK, POOL = tables()


def nn(x, y):
    return lax.dot_general(x, y, (((1,), (0,)), ((), ())), preferred_element_type=F32)


def nt(x, y):
    return lax.dot_general(x, y, (((1,), (1,)), ((), ())), preferred_element_type=F32)


def identity():
    rows = lax.broadcasted_iota(jnp.int32, (128, 128), 0)
    lanes = lax.broadcasted_iota(jnp.int32, (128, 128), 1)
    return (rows == lanes).astype(F32).astype(BF)


def ask_kernel(counts, feat, bricks, take, ask, msg):
    rows = nt(ask[...], bricks[...]).astype(BF)
    msg[:, 32:48, :] = rows.reshape(32, 16, 128)
    for s in range(2):
        live = (counts[0] > s).astype(F32)
        held = nt(take[...], feat[s]) * live
        msg[:, 16 * s : 16 * s + 16, :] = held.astype(BF).reshape(32, 16, 128)


def route_kernel(got, out):
    lanes = lax.broadcasted_iota(jnp.int32, (128, 1024), 1)
    part = lax.broadcasted_iota(jnp.int32, (128, 1), 0) & 15
    data = got[:, 0:32, :].reshape(1024, 128)
    for s in range(2):

        def step(n, _):
            rows = pl.multiple_of(n * 8, 8)
            table = got[pl.ds(rows, 8), 32:48, :].reshape(128, 128).astype(F32)
            target = table[:, s : s + 1].astype(jnp.int32) * 16 + part
            hot = (lanes == target).astype(F32).astype(BF)
            picked = nn(hot, data).astype(BF)
            out[pl.ds(rows, 8), 16 * s : 16 * s + 16, :] = picked.reshape(8, 16, 128)
            return 0

        lax.fori_loop(0, 4, step, 0)


def forward_kernel(
    counts, parent, child, core, feat, got, gout, weight, up, down, unpack, pool,
    out, grad, wsum,
    pc, s0, s1, s2, cols, grad_t, up_acc, down_acc,
):
    eye = identity()

    def brick(s, _):
        live = (counts[0] > s).astype(F32)
        place = parent[s] * 64 + child[s]
        held = (counts[0] > s) & (parent[s] >= 0) & (place >= 0)
        valid = held.astype(F32)
        live_in = feat[s].astype(F32) * live
        mine = live_in.T
        rows = got[:, pl.ds(pl.multiple_of(s * 16, 16), 16), :].reshape(512, 128)
        pc[...] = nn(unpack[...], rows)
        for a in range(8):
            s1[pl.ds(8 + ((a + 1) * 10 + 1) * 8, 64), :] = mine[a * 64 : a * 64 + 64]
            for d, b in (((0, -1, 0), 0), ((0, 1, 0), 9)):
                s1[pl.ds(8 + ((a + 1) * 10 + b) * 8, 8), :] = pc[pl.ds(PIECE[d] + 8 * a, 8), :]
        for a, x in ((-1, 0), (1, 9)):
            s1[pl.ds(8 + (x * 10 + 1) * 8, 64), :] = pc[pl.ds(PIECE[a, 0, 0], 64), :]
            for b, y in ((-1, 0), (1, 9)):
                s1[pl.ds(8 + (x * 10 + y) * 8, 8), :] = pc[pl.ds(PIECE[a, b, 0], 8), :]
        s0[...] = s1[pl.ds(7, 800), :]
        s2[...] = s1[pl.ds(9, 800), :]
        for c, ref, lane in ((-1, s0, 0), (1, s2, 7)):
            for a in range(8):
                ref[pl.ds(((a + 1) * 10 + 1) * 8 + lane, 8, stride=8), :] = pc[
                    pl.ds(PIECE[0, 0, c] + 8 * a, 8), :
                ]
            for a, x in ((-1, 0), (1, 9)):
                ref[pl.ds((x * 10 + 1) * 8 + lane, 8, stride=8), :] = pc[
                    pl.ds(PIECE[a, 0, c], 8), :
                ]
                ref[pl.ds((10 + x) * 8 + lane, 8, stride=80), :] = pc[pl.ds(PIECE[0, a, c], 8), :]
                for b, y in ((-1, 0), (1, 9)):
                    ref[pl.ds((x * 10 + y) * 8 + lane, 1), :] = pc[pl.ds(PIECE[a, b, c], 1), :]

        def plane(a, _):
            for b in range(3):
                for c, ref in enumerate((s0, s1, s2)):
                    start = pl.multiple_of((a * 10 + b) * 8 + (8 if c == 1 else 0), 8)
                    cols[s, pl.ds(pl.multiple_of(a * 64, 64), 64), pl.ds((3 * b + c) * 128, 128)] = ref[
                        pl.ds(start, 64), :
                    ].astype(BF)
            return 0

        lax.fori_loop(0, 10, plane, 0)
        pre = nn(cols[s, 0:512, :], weight[0])
        pre = pre + nn(cols[s, 64:576, :], weight[1])
        pre = pre + nn(cols[s, 128:640, :], weight[2])
        pre = pre.T
        gate = 1.0 / (1.0 + jnp.exp(-pre))
        active = pre * gate
        slope = gate * (1.0 + pre * (1.0 - gate))
        grad_in = gout[s].astype(F32) * live
        high = active.astype(BF)
        low = (active - high.astype(F32)).astype(BF)
        pooled = (nt(pool[...], high) + nt(pool[...], low)) * (1.0 / 64.0)
        coarse_in = (pooled * valid).astype(BF)
        coarse_pre = nn(coarse_in, up[...])
        coarse_gate = 1.0 / (1.0 + jnp.exp(-coarse_pre))
        coarse_mid = (coarse_pre * coarse_gate).astype(BF)
        coarse_out = nn(coarse_mid, down[...]).astype(BF)
        grad_coarse = (nt(pool[...], grad_in.astype(BF)) * valid).astype(BF)
        grad_mid = nt(grad_coarse, down[...])
        grad_pre = (
            grad_mid * (coarse_gate * (1.0 + coarse_pre * (1.0 - coarse_gate)))
        ).astype(BF)
        grad_cin = nt(grad_pre, up[...]).astype(BF)
        lifted = nn(nt(eye, coarse_out).astype(BF), pool[...])
        out[s] = (live_in + active + lifted).astype(BF)
        back = nn(nt(eye, grad_cin).astype(BF), pool[...])
        grad_pre_conv = (grad_in + back * (1.0 / 64.0)) * slope
        grad_t[s] = grad_pre_conv.astype(BF)
        grad[s] = grad_pre_conv.T.astype(BF)
        up_acc[s] = nn(nt(eye, coarse_in).astype(BF), grad_pre)
        for h in range(2):
            down_acc[s, h * 128 : h * 128 + 128, :] = nn(
                nt(eye, coarse_mid[:, h * 128 : h * 128 + 128]).astype(BF), grad_coarse
            )
        return 0

    lax.fori_loop(0, 2, brick, 0)
    mine = core[0]

    def put(block, value):
        half, at = divmod(block, 16)
        wsum[half ^ mine, pl.ds(at * 128, 128), :] = value.astype(BF)

    for a in range(3):
        total = nn(grad_t[0], cols[0, a * 64 : a * 64 + 512, :])
        total = total + nn(grad_t[1], cols[1, a * 64 : a * 64 + 512, :])
        total = total.astype(BF)
        for n in range(9):
            put(9 * a + n, nt(eye, total[:, n * 128 : n * 128 + 128]))
    up_all = up_acc[0] + up_acc[1]
    down_all = down_acc[0] + down_acc[1]
    for h in range(2):
        put(27 + h, up_all[:, h * 128 : h * 128 + 128])
        put(29 + h, down_all[h * 128 : h * 128 + 128, :])
    put(31, jnp.zeros((128, 128), F32))


def backward_kernel(grad, weight, pack, own, msg, planes, acc, pc):
    planes[0:128, :] = jnp.zeros((128, 128), BF)
    planes[640:768, :] = jnp.zeros((128, 128), BF)
    pc[488:512, :] = jnp.zeros((24, 128), F32)
    low = (lax.broadcasted_iota(jnp.int32, (64, 1), 0) & 7) != 0
    high = (lax.broadcasted_iota(jnp.int32, (64, 1), 0) & 7) != 7

    def brick(s, _):
        planes[128:640, :] = grad[s]
        acc[...] = jnp.zeros_like(acc)

        def tap(n, _):
            c = lax.rem(n, 3)
            b = lax.div(n, 3)
            part = nt(planes[128:768, :], weight[n])
            part = part + nt(planes[64:704, :], weight[n + 9])
            part = part + nt(planes[0:640, :], weight[n + 18])
            for a in range(10):
                at = pl.ds(pl.multiple_of(8 + (a * 10 + b) * 8, 8), 64)
                acc[c, at, :] = acc[c, at, :] + part[a * 64 : a * 64 + 64]
            return 0

        lax.fori_loop(0, 9, tap, 0)

        def middle(row, size):
            at = 8 + row
            total = acc[1, pl.ds(at, size), :]
            total = total + jnp.where(high[:size], acc[0, pl.ds(at + 1, size), :], 0.0)
            return total + jnp.where(low[:size], acc[2, pl.ds(at - 1, size), :], 0.0)

        for a in range(8):
            own[s, pl.ds(a * 64, 64), :] = middle(((a + 1) * 10 + 1) * 8, 64)
            for d, b in (((0, -1, 0), 0), ((0, 1, 0), 9)):
                pc[pl.ds(PIECE[d] + 8 * a, 8), :] = middle(((a + 1) * 10 + b) * 8, 8)
        for a, x in ((-1, 0), (1, 9)):
            pc[pl.ds(PIECE[a, 0, 0], 64), :] = middle((x * 10 + 1) * 8, 64)
            for b, y in ((-1, 0), (1, 9)):
                pc[pl.ds(PIECE[a, b, 0], 8), :] = middle((x * 10 + y) * 8, 8)
        for c, ref, lane in ((-1, acc.at[0], 8), (1, acc.at[2], 15)):
            for a in range(8):
                pc[pl.ds(PIECE[0, 0, c] + 8 * a, 8), :] = ref[
                    pl.ds(((a + 1) * 10 + 1) * 8 + lane, 8, stride=8), :
                ]
            for a, x in ((-1, 0), (1, 9)):
                pc[pl.ds(PIECE[a, 0, c], 8), :] = ref[
                    pl.ds((x * 10 + 1) * 8 + lane, 8, stride=8), :
                ]
                pc[pl.ds(PIECE[0, a, c], 8), :] = ref[pl.ds((10 + x) * 8 + lane, 8, stride=80), :]
                for b, y in ((-1, 0), (1, 9)):
                    pc[pl.ds(PIECE[a, b, c], 1), :] = ref[pl.ds((x * 10 + y) * 8 + lane, 1), :]
        sent = nn(pack[...], pc[...].astype(BF)).astype(BF)
        msg[:, pl.ds(pl.multiple_of(s * 16, 16), 16), :] = sent.reshape(32, 16, 128)
        return 0

    lax.fori_loop(0, 2, brick, 0)


def merge_kernel(got, table, out):
    part = lax.broadcasted_iota(jnp.int32, (1, 1024), 1) & 15
    target = table[0:1, :].astype(jnp.int32) * 16 + part
    rows = lax.broadcasted_iota(jnp.int32, (128, 1024), 0)
    data = got[:, 0:32, :].reshape(1024, 128)
    share = jnp.sum(got[:, 32:48, :].astype(F32), axis=0).astype(BF)

    def step(n, _):
        hot = (rows + n * 128 == target).astype(F32).astype(BF)
        total = nn(hot, data).astype(BF).reshape(4, 32, 128)
        at = pl.ds(pl.multiple_of(n * 4, 4), 4)
        out[at, 0:32, :] = total
        out[at, 32:48, :] = jnp.broadcast_to(share[None], (4, 16, 128))
        return 0

    lax.fori_loop(0, 8, step, 0)


def finish_kernel(counts, got, own, gout, give, out):
    for s in range(2):
        live = (counts[0] > s).astype(F32)
        rows = got[:, 16 * s : 16 * s + 16, :].reshape(512, 128)
        total = own[s] + nn(give[...], rows)
        out[s] = (total.T + gout[s].astype(F32) * live).astype(BF)


VM = pl.BlockSpec(memory_space=pltpu.VMEM)
SM = pl.BlockSpec(memory_space=pltpu.SMEM)


def call(kernel, shapes, scalars, arrays, scratch=(), flops=1e6, name=None):
    moved = sum(x.size * x.dtype.itemsize for x in arrays)
    moved += sum(int(np.prod(s.shape)) * s.dtype.itemsize for s in shapes)
    outs = pl.pallas_call(
        kernel,
        out_shape=shapes,
        in_specs=[SM] * len(scalars) + [VM] * len(arrays),
        out_specs=[VM] * len(shapes),
        scratch_shapes=list(scratch),
        compiler_params=pltpu.CompilerParams(vmem_limit_bytes=40 * 2**20),
        cost_estimate=pl.CostEstimate(
            flops=int(flops), bytes_accessed=int(moved), transcendentals=0
        ),
        name=name,
    )(*scalars, *arrays)
    return outs


def shape(dims, dtype):
    return jax.ShapeDtypeStruct(dims, dtype)


def on_device(
    features,
    grad_out,
    conv_weight,
    coarse_up,
    coarse_down,
    counts,
    neighbour_owner,
    neighbour_slot,
    parent,
    child_slot,
):
    grp = lax.axis_index("grp").astype(jnp.int32)
    core = lax.rem(grp, 2)
    line = lax.div(grp, 2)
    bricks = jnp.where(neighbour_owner >= 0, neighbour_owner * 2 + neighbour_slot, -1)
    bricks = jnp.pad(bricks.astype(BF), ((0, 126), (0, 102)))
    (msg,) = call(
        ask_kernel,
        [shape((32, 48, 128), BF)],
        [counts],
        [features, bricks, jnp.asarray(TAKE, BF), jnp.asarray(ASK, BF)],
        flops=2e8,
        name="ask",
    )
    first = lax.all_to_all(msg, "dev", split_axis=0, concat_axis=0, tiled=True)
    (answer,) = call(route_kernel, [shape((32, 32, 128), BF)], [], [first], flops=3e8, name="route")
    halo = lax.all_to_all(answer, "dev", split_axis=0, concat_axis=0, tiled=True)
    table = first[:, 32:48, 0:2].transpose(0, 2, 1).reshape(1, 1024).astype(F32)
    table = jnp.broadcast_to(table, (8, 1024))
    output, grad_pre, wsum = call(
        forward_kernel,
        [shape((2, 128, 512), BF), shape((2, 512, 128), BF), shape((2, 2048, 128), BF)],
        [counts, parent, child_slot, core.reshape(1)],
        [
            features,
            halo,
            grad_out,
            conv_weight.reshape(3, 1152, 128),
            coarse_up,
            coarse_down,
            jnp.asarray(UNPACK, BF),
            jnp.asarray(POOL, BF),
        ],
        [
            pltpu.VMEM((512, 128), F32),
            pltpu.VMEM((800, 128), F32),
            pltpu.VMEM((816, 128), F32),
            pltpu.VMEM((800, 128), F32),
            pltpu.VMEM((2, 640, 1152), BF),
            pltpu.VMEM((2, 128, 512), BF),
            pltpu.VMEM((2, 128, 256), F32),
            pltpu.VMEM((2, 256, 128), F32),
        ],
        flops=2e9,
        name="forward",
    )
    other = lax.ppermute(wsum[1], "grp", [(i, i ^ 1) for i in range(8)])
    pair = (wsum[0].astype(F32) + other.astype(F32)).reshape(4, 512, 128)
    chunk = lax.dynamic_index_in_dim(pair, line, 0, keepdims=False)
    pair = pair.astype(BF)
    for step in (1, 2, 3):
        away = lax.dynamic_index_in_dim(pair, lax.rem(line + step, 4), 0, keepdims=False)
        away = lax.ppermute(away, "grp", [(i, (i + 2 * step) % 8) for i in range(8)])
        chunk = chunk + away.astype(F32)
    own, terms = call(
        backward_kernel,
        [shape((2, 512, 128), F32), shape((32, 32, 128), BF)],
        [],
        [grad_pre, conv_weight, jnp.asarray(PACK, BF)],
        [
            pltpu.VMEM((768, 128), BF),
            pltpu.VMEM((3, 816, 128), F32),
            pltpu.VMEM((512, 128), F32),
        ],
        flops=4e9,
        name="backward",
    )
    terms = jnp.concatenate([terms, chunk.astype(BF).reshape(32, 16, 128)], axis=1)
    terms = lax.all_to_all(terms, "dev", split_axis=0, concat_axis=0, tiled=True)
    (sums,) = call(
        merge_kernel, [shape((32, 48, 128), BF)], [], [terms, table], flops=3e8, name="merge"
    )
    back = lax.all_to_all(sums, "dev", split_axis=0, concat_axis=0, tiled=True)
    chunk = back[:, 32:48, :].reshape(512, 128)
    parts = [chunk]
    for step in (1, 2, 3):
        parts.append(lax.ppermute(chunk, "grp", [(i, (i - 2 * step) % 8) for i in range(8)]))
    (grad_features,) = call(
        finish_kernel,
        [shape((2, 128, 512), BF)],
        [counts],
        [back, own, grad_out, jnp.asarray(GIVE, BF)],
        flops=3e8,
        name="finish",
    )
    half = jnp.stack(parts)
    half = jnp.take(half, lax.rem(jnp.arange(4) - line + 4, 4), axis=0).reshape(2048, 128)
    other = lax.ppermute(half, "grp", [(i, i ^ 1) for i in range(8)])
    first_half = jnp.where(core == 0, half, other)
    second_half = jnp.where(core == 0, other, half)
    weights = jnp.concatenate([first_half, second_half]).astype(F32).reshape(32, 128, 128)
    grad_conv = weights[:27]
    grad_up = jnp.concatenate([weights[27], weights[28]], axis=1)
    grad_down = jnp.concatenate([weights[29], weights[30]], axis=0)
    return (output, grad_features, grad_conv, grad_up, grad_down)


def solution(mesh):
    return jax.shard_map(
        on_device,
        mesh=mesh,
        in_specs=(
            P(("grp", "dev"), None, None),
            P(("grp", "dev"), None, None),
            P(),
            P(),
            P(),
            P(("grp", "dev")),
            P(("grp", "dev"), None),
            P(("grp", "dev"), None),
            P(("grp", "dev")),
            P(("grp", "dev")),
        ),
        out_specs=(P(("grp", "dev"), None, None), P(("grp", "dev"), None, None), P(), P(), P()),
        check_vma=False,
    )
```

time: 1230 us -> 133 us (0.11); the launches traced: 1210 us -> 133 us
  local copies, waits for them, and re-layouts: 376 us -> 6.48 us
  other arithmetic: 299 us -> 5.19 us
  waiting for transfers between devices: 284 us -> 35.6 us
  blocking collectives: 183 us -> 23.5 us
  Pallas kernels: 0 us -> 22.7 us
  matrix products: 21.7 us -> 0 us
  between operations: 17 us -> 1.59 us
    scatter-add x192 -> x0, local copies, waits for them, and re-layouts: 266 us -> none
    psum x1 -> x0, waiting for transfers between devices: 234 us -> none  [on_device(): lax.psum((weight_part, grad_up * weighting, grad_down * weighting), ('grp...]
    scatter-add x105 -> x0, other arithmetic: 231 us -> none
    all_gather x3 -> x0, blocking collectives: 183 us -> none  [the longest x1 120 us: on_device(): lax.all_gather(onehot.reshape(bricks, kc_count * 64), 'dev', axis=0, tile...]
    gather x27 -> x1, local copies, waits for them, and re-layouts: 33.8 us -> 0.65 us  [on_device(): jnp.take(half, lax.rem(jnp.arange(4) - line + 4, 4), axis=0)]
    select_n x60 -> x3, other arithmetic: 24.8 us -> 0.84 us  [the longest x1 0.49 us: on_device(): first_half = jnp.where(core == 0, half, other)]
    all_to_all x0 -> x1, blocking collectives: none -> 23.5 us  [on_device(): first = lax.all_to_all(msg, 'dev', split_axis=0, concat_axis=0, tiled=True)]
    pallas_call x0 -> x6, Pallas kernels: none -> 22.7 us  [call(): pl.pallas_call(kernel, out_shape=shapes, in_specs=[SM] * len(scalars) + [...]
  transfers between devices with their start and end apart: 4 -> 11, of which waited for: 2 -> 7; matrix products, arithmetic and copies ran while one was open for 6% -> 0% of each run, Pallas kernels for 0% -> 6%
where the time goes in v1:
time: 133 us
  starting transfers between devices  37.7 us (28%)
  waiting for transfers between devices  35.6 us (27%)
  blocking collectives  23.5 us (18%)
  Pallas kernels  22.7 us (17%)
  local copies, waits for them, and re-layouts  6.48 us (5%)
  other arithmetic  5.19 us (4%)
  between operations  1.59 us (1%)
    all_to_all x1, blocking collectives, on_device(): first = lax.all_to_all(msg, 'dev', split_axis=0, concat_axis=0, tiled=True)  23.5 us
    pallas_call x6, Pallas kernels, call(): pl.pallas_call(kernel, out_shape=shapes, in_specs=[SM] * len(scalars) + [...  22.7 us
    all_to_all x1, waiting for transfers between devices, on_device(): lax.all_to_all(terms, 'dev', split_axis=0, concat_axis=0, tiled=True)  10.3 us
    all_to_all x1, waiting for transfers between devices, on_device(): back = lax.all_to_all(sums, 'dev', split_axis=0, concat_axis=0, tiled=True)  10.2 us
    all_to_all x1, waiting for transfers between devices, on_device(): lax.all_to_all(answer, 'dev', split_axis=0, concat_axis=0, tiled=True)  9.65 us
    all_to_all x1, starting transfers between devices, on_device(): back = lax.all_to_all(sums, 'dev', split_axis=0, concat_axis=0, tiled=True)  7.6 us
    all_to_all x1, starting transfers between devices, on_device(): lax.all_to_all(answer, 'dev', split_axis=0, concat_axis=0, tiled=True)  7.45 us
    ppermute x1, starting transfers between devices, on_device(): other = lax.ppermute(half, 'grp', [(i, i ^ 1) for i in range(8)])  6.77 us
  transfers between devices with their start and end apart: 11, of which 7 were waited for; matrix products, arithmetic and copies ran while one was open for 0% of the time, Pallas kernels for 6%

profile of v1, /device:TPU:1, one launch (start us, length us, event | category | flops | bytes accessed | tf_op | source)
XLA Modules:
  0.0 132.8 jit_solution(5839807194722957450)
XLA Ops:
  1.3 0.7 fusion.3
  2.1 1.0 copy-done.1
  3.1 0.9 copy-done.2
  4.0 0.9 copy-done.5
  5.4 23.5 %all_to_all.20.got = bf16[32,48,128]{2,1,0:T(8,128)(2,1)S(1)} all-to-all(bf16[32,48,128]{2,1,0:T(8,128)(2,1)S(1)} %ask.2), channel_id=1, replica_groups=mesh['grp'=8,'dev'=32] {'dev'}, dimensions={0} | all-to-all | bytes 786432 | tf_op jit(solution)/shard_map/all_to_all | solution.py:347
  28.9 3.2 %route.1 = bf16[32,32,128]{2,1,0:T(8,128)(2,1)} custom-call(bf16[32,48,128]{2,1,0:T(8,128)(2,1)S(1)} %all_to_all.20.got), custom_call_target="tpu_custom_call" | custom-call | flops 300000000 | bytes 655360 | tf_op jit(solution)/shard_map/route/pallas_call | solution.py:303
  32.1 7.4 %all-to-all-start.1 = ((bf16[32,32,128]{2,1,0:T(8,128)(2,1)}), bf16[32,32,128]{2,1,0:T(8,128)(2,1)S(1)}, u32[]{:S(2)}, u32[]{:S(2)}) async-start(bf16[32,32,128]{2,1,0:T(8,128)(2,1)} %route.1), calls=%async_computation.1 | async-start | bytes 524288 | tf_op jit(solution)/shard_map/all_to_all | solution.py:349
  39.6 9.6 %all-to-all-done.1.got = bf16[32,32,128]{2,1,0:T(8,128)(2,1)S(1)} async-done(((bf16[32,32,128]{2,1,0:T(8,128)(2,1)}), bf16[32,32,128]{2,1,0:T(8,128)(2,1)S(1)}, u32[]{:S(2)}, u32[]{:S(2)}) %all-to-all-start.1) | async-done | bytes 262176 | tf_op jit(solution)/shard_map/all_to_all | solution.py:349
  49.3 1.0 copy-done.12
  50.3 9.1 %forward.1 = (bf16[2,128,512]{2,1,0:T(8,128)(2,1)}, bf16[2,512,128]{2,1,0:T(8,128)(2,1)S(1)}, bf16[2,2048,128]{2,1,0:T(8,128)(2,1)S(1)}) custom-call(s32[1]{0:T(128)S(6)} %copy.23.counts, s32[2]{0:T(128)S(1)} %copy-done.9, s32[2]{0:T(128)S(1)} %copy-done.10, s32[1]{0:T(128)} %bitcast.core, bf16[2,128,512]{2,1,0:T(8,128)(2,1)S(1)} %copy-done.3, ...), custom_call_target="tpu_custom_call" | custom-call | flops 2000000000 | bytes 3915776 | tf_op jit(solution)/shard_map/forward/pallas_call | solution.py:303
  59.5 3.7 %collective-permute-start = (bf16[2048,128]{1,0:T(8,128)(2,1)S(1)}, bf16[2048,128]{1,0:T(8,128)(2,1)}, u32[]{:S(2)}, u32[]{:S(2)}) collective-permute-start(bf16[2048,128]{1,0:T(8,128)(2,1)S(1)} %slice_bitcast_fusion), channel_id=1, source_target_pairs={{0,32},{32,0},{64,96},{96,64},{128,160},{160,128},{192,224},{224,1... | collective-permute-start | bytes 1572872 | tf_op jit(solution)/shard_map/ppermute | solution.py:379
  63.2 1.7 %collective-permute-done = bf16[2048,128]{1,0:T(8,128)(2,1)} collective-permute-done((bf16[2048,128]{1,0:T(8,128)(2,1)S(1)}, bf16[2048,128]{1,0:T(8,128)(2,1)}, u32[]{:S(2)}, u32[]{:S(2)}) %collective-permute-start) | collective-permute-done | bytes 524320 | tf_op jit(solution)/shard_map/ppermute | solution.py:379
  64.9 1.1 convert_add_fusion
  66.2 1.3 collective-permute-start.1
  67.5 1.5 %collective-permute-start.3 = (bf16[512,128]{1,0:T(8,128)(2,1)S(1)}, bf16[512,128]{1,0:T(8,128)(2,1)S(1)}, u32[]{:S(2)}, u32[]{:S(2)}) collective-permute-start(bf16[512,128]{1,0:T(8,128)(2,1)S(1)} %get-tuple-element.20), channel_id=1, source_target_pairs={{0,192},{32,224},{64,0},{96,32},{128,64},{160,96},{192,128},{224,1... | collective-permute-start | bytes 393224 | tf_op jit(solution)/shard_map/ppermute | solution.py:385
  68.9 1.5 %collective-permute-start.2 = (bf16[512,128]{1,0:T(8,128)(2,1)S(1)}, bf16[512,128]{1,0:T(8,128)(2,1)S(1)}, u32[]{:S(2)}, u32[]{:S(2)}) collective-permute-start(bf16[512,128]{1,0:T(8,128)(2,1)S(1)} %get-tuple-element.21), channel_id=1, source_target_pairs={{0,128},{32,160},{64,192},{96,224},{128,0},{160,32},{192,64},{224,... | collective-permute-start | bytes 393224 | tf_op jit(solution)/shard_map/ppermute | solution.py:385
  70.5 6.1 %backward.1 = (f32[2,512,128]{2,1,0:T(8,128)S(1)}, bf16[32,32,128]{2,1,0:T(8,128)(2,1)S(1)}) custom-call(bf16[2,512,128]{2,1,0:T(8,128)(2,1)S(1)} %get-tuple-element.11.grad, bf16[27,128,128]{2,1,0:T(8,128)(2,1)S(1)} %copy-done.6, bf16[512,512]{1,0:T(8,128)(2,1)S(1)} %copy-done.11), custom_call_target="tpu_custom_call" | custom-call | flops 4000000000 | bytes 2457600 | tf_op jit(solution)/shard_map/backward/pallas_call | solution.py:303
  76.7 0.8 pad_maximum_fusion.1
  77.5 4.3 %all-to-all-start.2 = ((bf16[32,48,128]{2,1,0:T(8,128)(2,1)}), bf16[32,48,128]{2,1,0:T(8,128)(2,1)S(1)}, u32[]{:S(2)}, u32[]{:S(2)}) async-start(bf16[32,48,128]{2,1,0:T(8,128)(2,1)} %pad_maximum_fusion.1), calls=%async_computation.2 | async-start | bytes 786432 | tf_op jit(solution)/shard_map/all_to_all | solution.py:401
  82.2 10.3 %all-to-all-done.2.got = bf16[32,48,128]{2,1,0:T(8,128)(2,1)S(1)} async-done(((bf16[32,48,128]{2,1,0:T(8,128)(2,1)}), bf16[32,48,128]{2,1,0:T(8,128)(2,1)S(1)}, u32[]{:S(2)}, u32[]{:S(2)}) %all-to-all-start.2) | async-done | bytes 393248 | tf_op jit(solution)/shard_map/all_to_all | solution.py:401
  92.5 2.6 %merge.1 = bf16[32,48,128]{2,1,0:T(8,128)(2,1)} custom-call(bf16[32,48,128]{2,1,0:T(8,128)(2,1)S(1)} %all-to-all-done.2.got, f32[8,1024]{1,0:T(8,128)S(1)} %broadcast_in_dim.24.table), custom_call_target="tpu_custom_call" | custom-call | flops 300000000 | bytes 819200 | tf_op jit(solution)/shard_map/merge/pallas_call | solution.py:303
  95.1 7.6 %all-to-all-start.3 = ((bf16[32,48,128]{2,1,0:T(8,128)(2,1)}), bf16[32,48,128]{2,1,0:T(8,128)(2,1)S(1)}, u32[]{:S(2)}, u32[]{:S(2)}) async-start(bf16[32,48,128]{2,1,0:T(8,128)(2,1)} %merge.1), calls=%async_computation.3 | async-start | bytes 786432 | tf_op jit(solution)/shard_map/all_to_all | solution.py:405
  102.8 10.2 %all-to-all-done.3.got = bf16[32,48,128]{2,1,0:T(8,128)(2,1)S(1)} async-done(((bf16[32,48,128]{2,1,0:T(8,128)(2,1)}), bf16[32,48,128]{2,1,0:T(8,128)(2,1)S(1)}, u32[]{:S(2)}, u32[]{:S(2)}) %all-to-all-start.3) | async-done | bytes 393248 | tf_op jit(solution)/shard_map/all_to_all | solution.py:405
  113.3 1.4 %collective-permute-start.5 = (bf16[512,128]{1,0:T(8,128)(2,1)S(1)}, bf16[512,128]{1,0:T(8,128)(2,1)S(1)}, u32[]{:S(2)}, u32[]{:S(2)}) collective-permute-start(bf16[512,128]{1,0:T(8,128)(2,1)S(1)} %bitcast.46), channel_id=1, source_target_pairs={{0,128},{32,160},{64,192},{96,224},{128,0},{160,32},{192,64},{224,... | collective-permute-start | bytes 393224 | tf_op jit(solution)/shard_map/ppermute | solution.py:409
  114.7 1.8 %collective-permute-start.4 = (bf16[512,128]{1,0:T(8,128)(2,1)S(1)}, bf16[512,128]{1,0:T(8,128)(2,1)S(1)}, u32[]{:S(2)}, u32[]{:S(2)}) collective-permute-start(bf16[512,128]{1,0:T(8,128)(2,1)S(1)} %bitcast.47), channel_id=1, source_target_pairs={{0,192},{32,224},{64,0},{96,32},{128,64},{160,96},{192,128},{224,1... | collective-permute-start | bytes 393224 | tf_op jit(solution)/shard_map/ppermute | solution.py:409
  116.6 2.9 %collective-permute-done.6 = bf16[512,128]{1,0:T(8,128)(2,1)S(1)} collective-permute-done((bf16[512,128]{1,0:T(8,128)(2,1)S(1)}, bf16[512,128]{1,0:T(8,128)(2,1)S(1)}, u32[]{:S(2)}, u32[]{:S(2)}) %collective-permute-start.6) | collective-permute-done | bytes 131104 | tf_op jit(solution)/shard_map/ppermute | solution.py:409
  120.1 0.6 gather_fusion
  121.1 6.8 %collective-permute-start.7 = (bf16[2048,128]{1,0:T(8,128)(2,1)S(1)}, bf16[2048,128]{1,0:T(8,128)(2,1)S(1)}, u32[]{:S(2)}, u32[]{:S(2)}) collective-permute-start(bf16[2048,128]{1,0:T(8,128)(2,1)S(1)} %bitcast_select_fusion), channel_id=1, source_target_pairs={{0,32},{32,0},{64,96},{96,64},{128,160},{160,128},{192,224},{224,1... | collective-permute-start | bytes 1572872 | tf_op jit(solution)/shard_map/ppermute | solution.py:420
  127.9 1.2 finish.1
  129.9 0.7 maximum_convert_fusion.1
  130.8 1.3 slice.43
  132.1 0.7 pad_maximum_fusion.2
  (52 shorter events, 3.6 us)
Async XLA Ops:
  0.6 48.6 %copy-start.13 = (bf16[16,512]{1,0:T(8,128)(2,1)S(1)}, bf16[16,512]{1,0:T(8,128)(2,1)}, u32[]{:S(2)}) copy-start(bf16[16,512]{1,0:T(8,128)(2,1)} %constant.75.clone.pool) | copy-start | bytes 49156
  0.6 48.6 %copy-start.10 = (s32[2]{0:T(128)S(1)}, s32[2]{0:T(128)}, u32[]{:S(2)}) copy-start(s32[2]{0:T(128)} %child.1) | copy-start | bytes 28
  0.7 48.6 %copy-start.9 = (s32[2]{0:T(128)S(1)}, s32[2]{0:T(128)}, u32[]{:S(2)}) copy-start(s32[2]{0:T(128)} %parent.1) | copy-start | bytes 28
  2.0 1.0 copy-start.1
  3.1 0.9 copy-start.2
  4.0 0.9 copy-start.5
  5.0 44.3 %copy-start.3 = (bf16[2,128,512]{2,1,0:T(8,128)(2,1)S(1)}, bf16[2,128,512]{2,1,0:T(8,128)(2,1)}, u32[]{:S(2)}) copy-start(bf16[2,128,512]{2,1,0:T(8,128)(2,1)} %feat.3) | copy-start | bytes 786436
  5.0 44.3 %copy-start.4 = (bf16[2,128,512]{2,1,0:T(8,128)(2,1)S(1)}, bf16[2,128,512]{2,1,0:T(8,128)(2,1)}, u32[]{:S(2)}) copy-start(bf16[2,128,512]{2,1,0:T(8,128)(2,1)} %gout.3) | copy-start | bytes 786436
  5.0 44.3 %copy-start.6 = (bf16[27,128,128]{2,1,0:T(8,128)(2,1)S(1)}, bf16[27,128,128]{2,1,0:T(8,128)(2,1)}, u32[]{:S(2)}) copy-start(bf16[27,128,128]{2,1,0:T(8,128)(2,1)} %weight.1) | copy-start | bytes 2654212
  5.0 44.3 %copy-start.7 = (bf16[128,256]{1,0:T(8,128)(2,1)S(1)}, bf16[128,256]{1,0:T(8,128)(2,1)}, u32[]{:S(2)}) copy-start(bf16[128,256]{1,0:T(8,128)(2,1)} %up.1) | copy-start | bytes 196612
  5.0 44.3 %copy-start.8 = (bf16[256,128]{1,0:T(8,128)(2,1)S(1)}, bf16[256,128]{1,0:T(8,128)(2,1)}, u32[]{:S(2)}) copy-start(bf16[256,128]{1,0:T(8,128)(2,1)} %down.1) | copy-start | bytes 196612
  32.1 17.1 %all-to-all-start.1 = ((bf16[32,32,128]{2,1,0:T(8,128)(2,1)}), bf16[32,32,128]{2,1,0:T(8,128)(2,1)S(1)}, u32[]{:S(2)}, u32[]{:S(2)}) async-start(bf16[32,32,128]{2,1,0:T(8,128)(2,1)} %route.1), calls=%async_computation.1 | async-start | bytes 524288 | tf_op jit(solution)/shard_map/all_to_all | solution.py:349
  49.3 1.0 copy-start.12
  59.5 5.4 %collective-permute-start = (bf16[2048,128]{1,0:T(8,128)(2,1)S(1)}, bf16[2048,128]{1,0:T(8,128)(2,1)}, u32[]{:S(2)}, u32[]{:S(2)}) collective-permute-start(bf16[2048,128]{1,0:T(8,128)(2,1)S(1)} %slice_bitcast_fusion), channel_id=1, source_target_pairs={{0,32},{32,0},{64,96},{96,64},{128,160},{160,128},{192,224},{224,1... | collective-permute-start | bytes 1572872 | tf_op jit(solution)/shard_map/ppermute | solution.py:379
  63.2 7.2 %copy-start.11 = (bf16[512,512]{1,0:T(8,128)(2,1)S(1)}, bf16[512,512]{1,0:T(8,128)(2,1)}, u32[]{:S(2)}) copy-start(bf16[512,512]{1,0:T(8,128)(2,1)} %constant.76.clone.pack) | copy-start | bytes 1572868
  66.2 10.4 %collective-permute-start.1 = (bf16[512,128]{1,0:T(8,128)(2,1)S(1)}, bf16[512,128]{1,0:T(8,128)(2,1)S(1)}, u32[]{:S(2)}, u32[]{:S(2)}) collective-permute-start(bf16[512,128]{1,0:T(8,128)(2,1)S(1)} %get-tuple-element.19), channel_id=1, source_target_pairs={{0,64},{32,96},{64,128},{96,160},{128,192},{160,224},{192,0},{224,... | collective-permute-start | bytes 393224 | tf_op jit(solution)/shard_map/ppermute | solution.py:385
  67.5 9.2 %collective-permute-start.3 = (bf16[512,128]{1,0:T(8,128)(2,1)S(1)}, bf16[512,128]{1,0:T(8,128)(2,1)S(1)}, u32[]{:S(2)}, u32[]{:S(2)}) collective-permute-start(bf16[512,128]{1,0:T(8,128)(2,1)S(1)} %get-tuple-element.20), channel_id=1, source_target_pairs={{0,192},{32,224},{64,0},{96,32},{128,64},{160,96},{192,128},{224,1... | collective-permute-start | bytes 393224 | tf_op jit(solution)/shard_map/ppermute | solution.py:385
  68.9 7.7 %collective-permute-start.2 = (bf16[512,128]{1,0:T(8,128)(2,1)S(1)}, bf16[512,128]{1,0:T(8,128)(2,1)S(1)}, u32[]{:S(2)}, u32[]{:S(2)}) collective-permute-start(bf16[512,128]{1,0:T(8,128)(2,1)S(1)} %get-tuple-element.21), channel_id=1, source_target_pairs={{0,128},{32,160},{64,192},{96,224},{128,0},{160,32},{192,64},{224,... | collective-permute-start | bytes 393224 | tf_op jit(solution)/shard_map/ppermute | solution.py:385
  77.5 15.0 %all-to-all-start.2 = ((bf16[32,48,128]{2,1,0:T(8,128)(2,1)}), bf16[32,48,128]{2,1,0:T(8,128)(2,1)S(1)}, u32[]{:S(2)}, u32[]{:S(2)}) async-start(bf16[32,48,128]{2,1,0:T(8,128)(2,1)} %pad_maximum_fusion.1), calls=%async_computation.2 | async-start | bytes 786432 | tf_op jit(solution)/shard_map/all_to_all | solution.py:401
  95.1 32.8 %copy-start = (bf16[512,512]{1,0:T(8,128)(2,1)S(1)}, bf16[512,512]{1,0:T(8,128)(2,1)}, u32[]{:S(2)}) copy-start(bf16[512,512]{1,0:T(8,128)(2,1)} %constant.77.clone.give) | copy-start | bytes 1572868
  95.1 17.9 %all-to-all-start.3 = ((bf16[32,48,128]{2,1,0:T(8,128)(2,1)}), bf16[32,48,128]{2,1,0:T(8,128)(2,1)S(1)}, u32[]{:S(2)}, u32[]{:S(2)}) async-start(bf16[32,48,128]{2,1,0:T(8,128)(2,1)} %merge.1), calls=%async_computation.3 | async-start | bytes 786432 | tf_op jit(solution)/shard_map/all_to_all | solution.py:405
  113.0 6.5 %collective-permute-start.6 = (bf16[512,128]{1,0:T(8,128)(2,1)S(1)}, bf16[512,128]{1,0:T(8,128)(2,1)S(1)}, u32[]{:S(2)}, u32[]{:S(2)}) collective-permute-start(bf16[512,128]{1,0:T(8,128)(2,1)S(1)} %bitcast.45), channel_id=1, source_target_pairs={{0,64},{32,96},{64,128},{96,160},{128,192},{160,224},{192,0},{224,... | collective-permute-start | bytes 393224 | tf_op jit(solution)/shard_map/ppermute | solution.py:409
  113.3 6.2 %collective-permute-start.5 = (bf16[512,128]{1,0:T(8,128)(2,1)S(1)}, bf16[512,128]{1,0:T(8,128)(2,1)S(1)}, u32[]{:S(2)}, u32[]{:S(2)}) collective-permute-start(bf16[512,128]{1,0:T(8,128)(2,1)S(1)} %bitcast.46), channel_id=1, source_target_pairs={{0,128},{32,160},{64,192},{96,224},{128,0},{160,32},{192,64},{224,... | collective-permute-start | bytes 393224 | tf_op jit(solution)/shard_map/ppermute | solution.py:409
  114.7 5.3 %collective-permute-start.4 = (bf16[512,128]{1,0:T(8,128)(2,1)S(1)}, bf16[512,128]{1,0:T(8,128)(2,1)S(1)}, u32[]{:S(2)}, u32[]{:S(2)}) collective-permute-start(bf16[512,128]{1,0:T(8,128)(2,1)S(1)} %bitcast.47), channel_id=1, source_target_pairs={{0,192},{32,224},{64,0},{96,32},{128,64},{160,96},{192,128},{224,1... | collective-permute-start | bytes 393224 | tf_op jit(solution)/shard_map/ppermute | solution.py:409
  121.1 8.3 %collective-permute-start.7 = (bf16[2048,128]{1,0:T(8,128)(2,1)S(1)}, bf16[2048,128]{1,0:T(8,128)(2,1)S(1)}, u32[]{:S(2)}, u32[]{:S(2)}) collective-permute-start(bf16[2048,128]{1,0:T(8,128)(2,1)S(1)} %bitcast_select_fusion), channel_id=1, source_target_pairs={{0,32},{32,0},{64,96},{96,64},{128,160},{160,128},{192,224},{224,1... | collective-permute-start | bytes 1572872 | tf_op jit(solution)/shard_map/ppermute | solution.py:420

commit v2 on v1

v2 whole, which is shorter than its diff:
```python
import functools

import jax
import jax.numpy as jnp
import numpy as np
from jax import lax
from jax.experimental import pallas as pl
from jax.experimental.pallas import tpu as pltpu
from jax.sharding import PartitionSpec as P

BF = jnp.bfloat16
F32 = jnp.float32

OFFSETS = [
    (a, b, c) for a in (-1, 0, 1) for b in (-1, 0, 1) for c in (-1, 0, 1) if (a, b, c) != (0, 0, 0)
]
FACES = [d for d in OFFSETS if sum(map(abs, d)) == 1]
EDGES = [d for d in OFFSETS if sum(map(abs, d)) == 2]
CORNERS = [d for d in OFFSETS if sum(map(abs, d)) == 3]
PIECE = {d: 64 * n for n, d in enumerate(FACES)}
PIECE.update({d: 384 + 8 * n for n, d in enumerate(EDGES)})
PIECE.update({d: 480 + n for n, d in enumerate(CORNERS)})


def piece_row(i, q):
    if q < 12:
        face = q // 2
        return 64 * face + 2 * i + q % 2, OFFSETS.index(FACES[face])
    if q < 15:
        flat = 32 * (q - 12) + i
        return 384 + flat, OFFSETS.index(EDGES[flat // 8])
    return 480 + i // 4, OFFSETS.index(CORNERS[i // 4])


def cut(step):
    return [7] if step < 0 else ([0] if step > 0 else list(range(8)))


def tables():
    voxel = np.full(512, -1)
    for (a, b, c), base in PIECE.items():
        cells = [x * 64 + y * 8 + z for x in cut(a) for y in cut(b) for z in cut(c)]
        voxel[base : base + len(cells)] = cells
    take = np.zeros((512, 512), np.float32)
    pack = np.zeros((512, 512), np.float32)
    unpack = np.zeros((512, 512), np.float32)
    give = np.zeros((512, 512), np.float32)
    ask = np.zeros((512, 128), np.float32)
    for i in range(32):
        for q in range(16):
            row, direction = piece_row(i, q)
            at = 16 * i + q
            take[at, voxel[row]] = 1
            pack[at, row] = 1
            ask[at, direction] = 1
            if q < 15 or i % 4 == 0:
                unpack[row, at] = 1
                give[voxel[row], at] = 1
    pool = np.zeros((2, 16, 512), np.float32)
    for v in range(512):
        a, b, c = v // 64, v // 8 % 8, v % 8
        at = (a // 4) * 4 + (b // 4) * 2 + c // 4
        pool[0, at, v] = pool[1, 8 + at, v] = 1
    return take, pack, unpack, give, ask, pool


TAKE, PACK, UNPACK, GIVE, ASK, POOL = tables()


def nn(x, y):
    return lax.dot_general(x, y, (((1,), (0,)), ((), ())), preferred_element_type=F32)


def nt(x, y):
    return lax.dot_general(x, y, (((1,), (1,)), ((), ())), preferred_element_type=F32)


def identity():
    rows = lax.broadcasted_iota(jnp.int32, (128, 128), 0)
    lanes = lax.broadcasted_iota(jnp.int32, (128, 128), 1)
    return (rows == lanes).astype(F32).astype(BF)


def ask_kernel(
    counts, feat, owner, slot, take, ask, msg, feat_v, owner_v, slot_v, take_v, ask_v, bricks, sems
):
    pairs = ((owner, owner_v), (slot, slot_v), (ask, ask_v), (feat, feat_v), (take, take_v))
    copies = [
        pltpu.make_async_copy(src, dst, sems.at[n]) for n, (src, dst) in enumerate(pairs)
    ]
    for copy in copies:
        copy.start()
    bricks[...] = jnp.zeros((128, 128), F32)
    copies[0].wait()
    copies[1].wait()
    named = jnp.where(owner_v[...] >= 0, owner_v[...] * 2 + slot_v[...], -1)
    bricks[0:2, 0:26] = named.astype(F32)
    copies[2].wait()
    rows = nt(ask_v[...], bricks[...].astype(BF)).astype(BF)
    msg[:, 32:48, :] = rows.reshape(32, 16, 128)
    copies[3].wait()
    copies[4].wait()
    for s in range(2):
        live = (counts[0] > s).astype(F32)
        held = nt(take_v[...], feat_v[s]) * live
        msg[:, 16 * s : 16 * s + 16, :] = held.astype(BF).reshape(32, 16, 128)


def same_part():
    rows = lax.broadcasted_iota(jnp.int32, (16, 128), 0)
    lanes = lax.broadcasted_iota(jnp.int32, (16, 128), 1) & 15
    return (rows == lanes).astype(F32).astype(BF)


def route_kernel(got, out, hot):
    same = jnp.broadcast_to(same_part()[None], (32, 16, 128))
    zero = jnp.zeros((32, 16, 128), BF)
    lanes = lax.broadcasted_iota(jnp.int32, (128, 128), 0)
    brick = lax.broadcasted_iota(jnp.int32, (16, 128), 1) >> 4
    table = got[:, 32:48, :].reshape(512, 128)
    data = got[:, 0:32, :].reshape(1024, 128)
    for s in range(2):
        spread = (lanes == s).astype(F32).astype(BF)
        asked = nn(table, spread).astype(BF).reshape(32, 16, 128)
        for n in range(8):
            here = (brick + 8 * n).astype(F32).astype(BF)
            hot[:, n * 128 : n * 128 + 128] = jnp.where(asked == here[None], same, zero).reshape(
                512, 128
            )
        picked = nn(hot[...], data).astype(BF)
        out[:, 16 * s : 16 * s + 16, :] = picked.reshape(32, 16, 128)


def prepare_kernel(counts, feat, gout, down, pool, mine, grad_coarse, grad_mid):
    pooled = jnp.zeros((16, 128), F32)
    for s in range(2):
        live = (counts[0] > s).astype(F32)
        mine[s] = (feat[s].astype(F32) * live).T
        pooled = pooled + nt(pool[s], gout[s]) * live
    grad_coarse[...] = pooled.astype(BF)
    grad_mid[...] = nt(grad_coarse[...], down[...])


def forward_kernel(
    counts, parent, child, core, feat, mine, grad_coarse, grad_mid, got, gout, weight, up, down,
    unpack, pool,
    out, grad, wsum,
    pc, s0, s1, s2, cols, grad_t, acts, slopes, pooled,
):
    eye = identity()
    pooled[...] = jnp.zeros((16, 128), F32)

    def brick(s, _):
        rows = got[:, pl.ds(pl.multiple_of(s * 16, 16), 16), :].reshape(512, 128)
        pc[...] = nn(unpack[...], rows)
        for a in range(8):
            s1[pl.ds(8 + ((a + 1) * 10 + 1) * 8, 64), :] = mine[s, a * 64 : a * 64 + 64, :]
            for d, b in (((0, -1, 0), 0), ((0, 1, 0), 9)):
                s1[pl.ds(8 + ((a + 1) * 10 + b) * 8, 8), :] = pc[pl.ds(PIECE[d] + 8 * a, 8), :]
        for a, x in ((-1, 0), (1, 9)):
            s1[pl.ds(8 + (x * 10 + 1) * 8, 64), :] = pc[pl.ds(PIECE[a, 0, 0], 64), :]
            for b, y in ((-1, 0), (1, 9)):
                s1[pl.ds(8 + (x * 10 + y) * 8, 8), :] = pc[pl.ds(PIECE[a, b, 0], 8), :]
        s0[...] = s1[pl.ds(7, 800), :]
        s2[...] = s1[pl.ds(9, 800), :]
        for c, ref, lane in ((-1, s0, 0), (1, s2, 7)):
            for a in range(8):
                ref[pl.ds(((a + 1) * 10 + 1) * 8 + lane, 8, stride=8), :] = pc[
                    pl.ds(PIECE[0, 0, c] + 8 * a, 8), :
                ]
            for a, x in ((-1, 0), (1, 9)):
                ref[pl.ds((x * 10 + 1) * 8 + lane, 8, stride=8), :] = pc[
                    pl.ds(PIECE[a, 0, c], 8), :
                ]
                ref[pl.ds((10 + x) * 8 + lane, 8, stride=80), :] = pc[pl.ds(PIECE[0, a, c], 8), :]
                for b, y in ((-1, 0), (1, 9)):
                    ref[pl.ds((x * 10 + y) * 8 + lane, 1), :] = pc[pl.ds(PIECE[a, b, c], 1), :]

        def plane(a, _):
            for b in range(3):
                for c, ref in enumerate((s0, s1, s2)):
                    start = pl.multiple_of((a * 10 + b) * 8 + (8 if c == 1 else 0), 8)
                    cols[s, pl.ds(pl.multiple_of(a * 64, 64), 64), pl.ds((3 * b + c) * 128, 128)] = ref[
                        pl.ds(start, 64), :
                    ].astype(BF)
            return 0

        lax.fori_loop(0, 10, plane, 0)
        pre = nn(cols[s, 0:512, :], weight[0])
        pre = pre + nn(cols[s, 64:576, :], weight[1])
        pre = pre + nn(cols[s, 128:640, :], weight[2])
        pre = pre.T
        gate = 1.0 / (1.0 + jnp.exp(-pre))
        active = pre * gate
        acts[s] = active
        slopes[s] = gate * (1.0 + pre * (1.0 - gate))
        high = active.astype(BF)
        low = (active - high.astype(F32)).astype(BF)
        pooled[...] += nt(pool[s], high) + nt(pool[s], low)
        return 0

    lax.fori_loop(0, 2, brick, 0)
    second = lax.broadcasted_iota(jnp.int32, (16, 1), 0) >= 8
    valid = [
        (
            (counts[0] > s) & (parent[s] >= 0) & (parent[s] * 64 + child[s] >= 0)
        ).astype(F32)
        for s in range(2)
    ]
    valid = jnp.where(second, valid[1], valid[0])
    coarse_in = (pooled[...] * (1.0 / 64.0) * valid).astype(BF)
    grad_out = (grad_coarse[...].astype(F32) * valid).astype(BF)
    coarse_pre = nn(coarse_in, up[...])
    gate = 1.0 / (1.0 + jnp.exp(-coarse_pre))
    coarse_mid = (coarse_pre * gate).astype(BF)
    grad_pre = grad_mid[...] * valid * (gate * (1.0 + coarse_pre * (1.0 - gate)))
    grad_pre = grad_pre.astype(BF)
    coarse_out = nn(coarse_mid, down[...]).astype(BF)
    grad_cin = nt(grad_pre, up[...]).astype(BF)
    lift = nt(eye, coarse_out).astype(BF)
    back = nt(eye, grad_cin).astype(BF)

    def blend(s, _):
        live = (counts[0] > s).astype(F32)
        out[s] = (feat[s].astype(F32) * live + acts[s] + nn(lift, pool[s])).astype(BF)
        grad_in = gout[s].astype(F32) * live + nn(back, pool[s]) * (1.0 / 64.0)
        grad_pre_conv = grad_in * slopes[s]
        grad_t[s] = grad_pre_conv.astype(BF)
        grad[s] = grad_pre_conv.T.astype(BF)
        return 0

    lax.fori_loop(0, 2, blend, 0)
    mine_core = core[0]

    def put(block, value):
        half, at = divmod(block, 16)
        wsum[half ^ mine_core, pl.ds(at * 128, 128), :] = value.astype(BF)

    grad_up = nn(nt(eye, coarse_in).astype(BF), grad_pre)
    for h in range(2):
        put(27 + h, grad_up[:, h * 128 : h * 128 + 128])
        middle = nt(eye, coarse_mid[:, h * 128 : h * 128 + 128]).astype(BF)
        put(29 + h, nn(middle, grad_out))
    put(31, jnp.zeros((128, 128), F32))
    for a in range(3):
        total = nn(grad_t[0], cols[0, a * 64 : a * 64 + 512, :])
        total = total + nn(grad_t[1], cols[1, a * 64 : a * 64 + 512, :])
        total = total.astype(BF)
        for n in range(9):
            put(9 * a + n, nt(eye, total[:, n * 128 : n * 128 + 128]))


def pair_kernel(line, wsum, other, own, one, two, three):
    for step, ref in enumerate((own, one, two, three)):
        at = pl.ds(pl.multiple_of(((line[0] + step) & 3) * 512, 512), 512)
        ref[...] = (wsum[0, at, :].astype(F32) + other[at, :].astype(F32)).astype(ref.dtype)


def backward_kernel(s, grad, weight, pack, own, msg, planes, acc, pc):
    planes[0:128, :] = jnp.zeros((128, 128), BF)
    planes[640:768, :] = jnp.zeros((128, 128), BF)
    planes[128:640, :] = grad[s]
    pc[488:512, :] = jnp.zeros((24, 128), F32)
    acc[...] = jnp.zeros_like(acc)
    low = (lax.broadcasted_iota(jnp.int32, (64, 1), 0) & 7) != 0
    high = (lax.broadcasted_iota(jnp.int32, (64, 1), 0) & 7) != 7

    def tap(n, _):
        c = lax.rem(n, 3)
        b = lax.div(n, 3)
        part = nt(planes[128:768, :], weight[n])
        part = part + nt(planes[64:704, :], weight[n + 9])
        part = part + nt(planes[0:640, :], weight[n + 18])
        for a in range(10):
            at = pl.ds(pl.multiple_of(8 + (a * 10 + b) * 8, 8), 64)
            acc[c, at, :] = acc[c, at, :] + part[a * 64 : a * 64 + 64]
        return 0

    lax.fori_loop(0, 9, tap, 0)

    def middle(row, size):
        at = 8 + row
        total = acc[1, pl.ds(at, size), :]
        total = total + jnp.where(high[:size], acc[0, pl.ds(at + 1, size), :], 0.0)
        return total + jnp.where(low[:size], acc[2, pl.ds(at - 1, size), :], 0.0)

    for a in range(8):
        own[pl.ds(a * 64, 64), :] = middle(((a + 1) * 10 + 1) * 8, 64)
        for d, b in (((0, -1, 0), 0), ((0, 1, 0), 9)):
            pc[pl.ds(PIECE[d] + 8 * a, 8), :] = middle(((a + 1) * 10 + b) * 8, 8)
    for a, x in ((-1, 0), (1, 9)):
        pc[pl.ds(PIECE[a, 0, 0], 64), :] = middle((x * 10 + 1) * 8, 64)
        for b, y in ((-1, 0), (1, 9)):
            pc[pl.ds(PIECE[a, b, 0], 8), :] = middle((x * 10 + y) * 8, 8)
    for c, ref, lane in ((-1, acc.at[0], 8), (1, acc.at[2], 15)):
        for a in range(8):
            pc[pl.ds(PIECE[0, 0, c] + 8 * a, 8), :] = ref[
                pl.ds(((a + 1) * 10 + 1) * 8 + lane, 8, stride=8), :
            ]
        for a, x in ((-1, 0), (1, 9)):
            pc[pl.ds(PIECE[a, 0, c], 8), :] = ref[pl.ds((x * 10 + 1) * 8 + lane, 8, stride=8), :]
            pc[pl.ds(PIECE[0, a, c], 8), :] = ref[pl.ds((10 + x) * 8 + lane, 8, stride=80), :]
            for b, y in ((-1, 0), (1, 9)):
                pc[pl.ds(PIECE[a, b, c], 1), :] = ref[pl.ds((x * 10 + y) * 8 + lane, 1), :]
    msg[...] = nn(pack[...], pc[...].astype(BF)).astype(BF).reshape(32, 16, 128)


def join_kernel(zero, one, own, away1, away2, away3, msg):
    msg[:, 0:16, :] = zero[...]
    msg[:, 16:32, :] = one[...]
    total = own[...] + away1[...].astype(F32) + away2[...].astype(F32) + away3[...].astype(F32)
    msg[:, 32:48, :] = total.astype(BF).reshape(32, 16, 128)


def merge_kernel(got, table, out, hot):
    same = same_part()
    zero = jnp.zeros((16, 128), BF)
    share = jnp.sum(got[:, 32:48, :].astype(F32), axis=0).astype(BF)
    out[:, 32:48, :] = jnp.broadcast_to(share[None], (32, 16, 128))
    for n in range(8):
        asked = table[:, n * 128 : n * 128 + 128]
        for brick in range(64):
            hot[brick * 16 : brick * 16 + 16, n * 128 : n * 128 + 128] = jnp.where(
                asked == jnp.full((16, 128), brick, BF), same, zero
            )
    total = nn(hot[...], got[:, 0:32, :].reshape(1024, 128))
    out[:, 0:32, :] = total.astype(BF).reshape(32, 32, 128)


def finish_kernel(counts, got, own0, own1, gout, give, out):
    for s, own in enumerate((own0, own1)):
        live = (counts[0] > s).astype(F32)
        rows = got[:, 16 * s : 16 * s + 16, :].reshape(512, 128)
        total = own[...] + nn(give[...], rows)
        out[s] = (total.T + gout[s].astype(F32) * live).astype(BF)


def assemble_kernel(core, line, *refs):
    parts, (conv, up, down) = refs[:8], refs[8:]
    for n, part in enumerate(parts):
        half = core[0] ^ (n // 4)
        first = half * 16 + ((line[0] + n % 4) & 3) * 4

        def block(at):
            return part[at * 128 : at * 128 + 128, :].astype(F32)

        @pl.when(first < 24)
        def _():
            for at in range(4):
                conv[first + at] = block(at)

        @pl.when(first == 24)
        def _():
            for at in range(3):
                conv[24 + at] = block(at)
            up[:, 0:128] = block(3)

        @pl.when(first == 28)
        def _():
            up[:, 128:256] = block(0)
            down[0:128, :] = block(1)
            down[128:256, :] = block(2)


VM = pl.BlockSpec(memory_space=pltpu.VMEM)
SM = pl.BlockSpec(memory_space=pltpu.SMEM)


def call(kernel, shapes, scalars, arrays, scratch=(), flops=1e6, space=VM, limit=20, name=None):
    moved = sum(x.size * x.dtype.itemsize for x in arrays)
    moved += sum(int(np.prod(s.shape)) * s.dtype.itemsize for s in shapes)
    return pl.pallas_call(
        kernel,
        out_shape=shapes,
        in_specs=[SM] * len(scalars) + [space] * len(arrays),
        out_specs=[VM] * len(shapes),
        scratch_shapes=list(scratch),
        compiler_params=pltpu.CompilerParams(vmem_limit_bytes=limit * 2**20),
        cost_estimate=pl.CostEstimate(
            flops=int(flops), bytes_accessed=int(moved), transcendentals=0
        ),
        name=name,
    )(*scalars, *arrays)


def shape(dims, dtype):
    return jax.ShapeDtypeStruct(dims, dtype)


def on_device(
    features,
    grad_out,
    conv_weight,
    coarse_up,
    coarse_down,
    counts,
    neighbour_owner,
    neighbour_slot,
    parent,
    child_slot,
):
    grp = lax.axis_index("grp").astype(jnp.int32)
    core = (grp & 1).reshape(1)
    line = (grp >> 1).reshape(1)
    pool = jnp.asarray(POOL, BF)
    swap = [(i, i ^ 1) for i in range(8)]
    (msg,) = call(
        ask_kernel,
        [shape((32, 48, 128), BF)],
        [counts],
        [features, neighbour_owner, neighbour_slot, jnp.asarray(TAKE, BF), jnp.asarray(ASK, BF)],
        [
            pltpu.VMEM((2, 128, 512), BF),
            pltpu.VMEM((2, 26), jnp.int32),
            pltpu.VMEM((2, 26), jnp.int32),
            pltpu.VMEM((512, 512), BF),
            pltpu.VMEM((512, 128), BF),
            pltpu.VMEM((128, 128), F32),
            pltpu.SemaphoreType.DMA((5,)),
        ],
        flops=2e8,
        space=pl.BlockSpec(memory_space=pltpu.HBM),
        name="ask",
    )
    first = lax.all_to_all(msg, "dev", split_axis=0, concat_axis=0, tiled=True)
    (answer,) = call(
        route_kernel,
        [shape((32, 32, 128), BF)],
        [],
        [first],
        [pltpu.VMEM((512, 1024), BF)],
        flops=3e8,
        name="route",
    )
    halo = lax.all_to_all(answer, "dev", split_axis=0, concat_axis=0, tiled=True)
    table = first[:, 32:48, 0:2].transpose(0, 2, 1).reshape(1, 1024)
    table = jnp.broadcast_to(table, (16, 1024))
    mine, grad_coarse, grad_mid = call(
        prepare_kernel,
        [shape((2, 512, 128), F32), shape((16, 128), BF), shape((16, 256), F32)],
        [counts],
        [features, grad_out, coarse_down, pool],
        flops=1e8,
        name="prepare",
    )
    output, grad_pre, wsum = call(
        forward_kernel,
        [shape((2, 128, 512), BF), shape((2, 512, 128), BF), shape((2, 2048, 128), BF)],
        [counts, parent, child_slot, core],
        [
            features,
            mine,
            grad_coarse,
            grad_mid,
            halo,
            grad_out,
            conv_weight.reshape(3, 1152, 128),
            coarse_up,
            coarse_down,
            jnp.asarray(UNPACK, BF),
            pool,
        ],
        [
            pltpu.VMEM((512, 128), F32),
            pltpu.VMEM((800, 128), F32),
            pltpu.VMEM((816, 128), F32),
            pltpu.VMEM((800, 128), F32),
            pltpu.VMEM((2, 640, 1152), BF),
            pltpu.VMEM((2, 128, 512), BF),
            pltpu.VMEM((2, 128, 512), F32),
            pltpu.VMEM((2, 128, 512), F32),
            pltpu.VMEM((16, 128), F32),
        ],
        flops=2e9,
        name="forward",
    )

    def backward(s, grad):
        return call(
            functools.partial(backward_kernel, s),
            [shape((512, 128), F32), shape((32, 16, 128), BF)],
            [],
            [grad, conv_weight, jnp.asarray(PACK, BF)],
            [
                pltpu.VMEM((768, 128), BF),
                pltpu.VMEM((3, 816, 128), F32),
                pltpu.VMEM((512, 128), F32),
            ],
            flops=2e9,
            name="backward",
        )

    other = lax.ppermute(wsum[1], "grp", swap)
    own0, terms0 = backward(0, grad_pre)
    own_sum, *away = call(
        pair_kernel,
        [shape((512, 128), F32)] + [shape((512, 128), BF)] * 3,
        [line],
        [wsum, other],
        name="pair",
    )
    grad_pre, own_sum = lax.optimization_barrier((grad_pre, own_sum))
    away = [
        lax.ppermute(x, "grp", [(i, (i + 2 * step) % 8) for i in range(8)])
        for step, x in zip((1, 2, 3), away)
    ]
    own1, terms1 = backward(1, grad_pre)
    (terms,) = call(
        join_kernel,
        [shape((32, 48, 128), BF)],
        [],
        [terms0, terms1, own_sum, *away],
        name="join",
    )
    terms = lax.all_to_all(terms, "dev", split_axis=0, concat_axis=0, tiled=True)
    (sums,) = call(
        merge_kernel,
        [shape((32, 48, 128), BF)],
        [],
        [terms, table],
        [pltpu.VMEM((1024, 1024), BF)],
        flops=3e8,
        name="merge",
    )
    back = lax.all_to_all(sums, "dev", split_axis=0, concat_axis=0, tiled=True)
    chunk = back[:, 32:48, :].reshape(512, 128)
    parts = [chunk] + [
        lax.ppermute(chunk, "grp", [(i, (i - 2 * step) % 8) for i in range(8)])
        for step in (1, 2, 3)
    ]
    parts = parts + [lax.ppermute(x, "grp", swap) for x in parts]
    (grad_features,) = call(
        finish_kernel,
        [shape((2, 128, 512), BF)],
        [counts],
        [back, own0, own1, grad_out, jnp.asarray(GIVE, BF)],
        flops=3e8,
        name="finish",
    )
    grad_conv, grad_up, grad_down = call(
        assemble_kernel,
        [shape((27, 128, 128), F32), shape((128, 256), F32), shape((256, 128), F32)],
        [core, line],
        parts,
        name="assemble",
    )
    return (output, grad_features, grad_conv, grad_up, grad_down)


def solution(mesh):
    return jax.shard_map(
        on_device,
        mesh=mesh,
        in_specs=(
            P(("grp", "dev"), None, None),
            P(("grp", "dev"), None, None),
            P(),
            P(),
            P(),
            P(("grp", "dev")),
            P(("grp", "dev"), None),
            P(("grp", "dev"), None),
            P(("grp", "dev")),
            P(("grp", "dev")),
        ),
        out_specs=(P(("grp", "dev"), None, None), P(("grp", "dev"), None, None), P(), P(), P()),
        check_vma=False,
    )
```

time: 133 us -> 132 us (level)
  blocking collectives: 23.5 us -> 41.9 us
  waiting for transfers between devices: 35.6 us -> 21.7 us
  other arithmetic: 5.19 us -> 0 us
  local copies, waits for them, and re-layouts: 6.48 us -> 11.1 us
  starting transfers between devices: 37.7 us -> 34 us
    all_to_all x0 -> x1, blocking collectives: none -> 18.3 us  [on_device(): back = lax.all_to_all(sums, 'dev', split_axis=0, concat_axis=0, tiled=True)]
    all_to_all x1 -> x0, waiting for transfers between devices: 10.2 us -> none  [on_device(): back = lax.all_to_all(sums, 'dev', split_axis=0, concat_axis=0, tiled=True)]
    all_to_all x1 -> x0, starting transfers between devices: 7.6 us -> none  [on_device(): back = lax.all_to_all(sums, 'dev', split_axis=0, concat_axis=0, tiled=True)]
    unnamed x30 -> x42, local copies, waits for them, and re-layouts: 4.05 us -> 9.85 us
    ppermute x5 -> x8, starting transfers between devices: 14.8 us -> 18.5 us  [the longest x4 9.97 us: on_device(): parts = parts + [lax.ppermute(x, 'grp', swap) for x in parts]]
    ppermute x3, waiting for transfers between devices: 3.49 us -> 0.01 us  [on_device(): lax.ppermute(chunk, 'grp', [(i, (i - 2 * step) % 8) for i in range(8)])]
    concatenate x3 -> x0, other arithmetic: 2.1 us -> none  [the longest x1 0.77 us: on_device(): jnp.concatenate([terms, chunk.astype(BF).reshape(32, 16, 128)], axis=1)]
    pallas_call x6 -> x11, Pallas kernels: 22.7 us -> 21.4 us  [call(): pl.pallas_call(kernel, out_shape=shapes, in_specs=[SM] * len(scalars) + [...]
  transfers between devices with their start and end apart: 11 -> 13, of which waited for: 7 -> 3; matrix products, arithmetic and copies ran while one was open for 0% -> 0% of each run, Pallas kernels for 6% -> 6%
where the time goes in v2:
time: 132 us
  blocking collectives  41.9 us (32%)
  starting transfers between devices  34 us (26%)
  waiting for transfers between devices  21.7 us (16%)
  Pallas kernels  21.4 us (16%)
  local copies, waits for them, and re-layouts  11.1 us (8%)
  between operations  1.52 us (1%)
    all_to_all x1, blocking collectives, on_device(): first = lax.all_to_all(msg, 'dev', split_axis=0, concat_axis=0, tiled=True)  23.6 us
    pallas_call x11, Pallas kernels, call(): pl.pallas_call(kernel, out_shape=shapes, in_specs=[SM] * len(scalars) + [...  21.4 us
    all_to_all x1, blocking collectives, on_device(): back = lax.all_to_all(sums, 'dev', split_axis=0, concat_axis=0, tiled=True)  18.3 us
    all_to_all x1, waiting for transfers between devices, on_device(): lax.all_to_all(terms, 'dev', split_axis=0, concat_axis=0, tiled=True)  10.9 us
    ppermute x4, starting transfers between devices, on_device(): parts = parts + [lax.ppermute(x, 'grp', swap) for x in parts]  9.97 us
    unnamed x42, local copies, waits for them, and re-layouts  9.85 us
    all_to_all x1, waiting for transfers between devices, on_device(): lax.all_to_all(answer, 'dev', split_axis=0, concat_axis=0, tiled=True)  8.5 us
    all_to_all x1, starting transfers between devices, on_device(): lax.all_to_all(answer, 'dev', split_axis=0, concat_axis=0, tiled=True)  7.47 us
  transfers between devices with their start and end apart: 13, of which 3 were waited for; matrix products, arithmetic and copies ran while one was open for 0% of the time, Pallas kernels for 6%

profile of v2, /device:TPU:1, one launch (start us, length us, event | category | flops | bytes accessed | tf_op | source)
XLA Modules:
  0.0 131.6 jit_solution(2254213358748267403)
XLA Ops:
  1.3 0.9 copy-done
  2.2 1.0 copy-done.4
  3.3 0.9 copy-done.5
  5.5 0.9 ask.2
  6.5 23.6 %all_to_all.20.got = bf16[32,48,128]{2,1,0:T(8,128)(2,1)S(1)} all-to-all(bf16[32,48,128]{2,1,0:T(8,128)(2,1)S(1)} %ask.2), channel_id=1, replica_groups=mesh['grp'=8,'dev'=32] {'dev'}, dimensions={0} | all-to-all | bytes 786432 | tf_op jit(solution)/shard_map/all_to_all | solution.py:425
  30.1 1.7 %route.1 = bf16[32,32,128]{2,1,0:T(8,128)(2,1)} custom-call(bf16[32,48,128]{2,1,0:T(8,128)(2,1)S(1)} %all_to_all.20.got), custom_call_target="tpu_custom_call" | custom-call | flops 300000000 | bytes 655360 | tf_op jit(solution)/shard_map/route/pallas_call | solution.py:372
  31.8 7.5 %all-to-all-start.1 = ((bf16[32,32,128]{2,1,0:T(8,128)(2,1)}), bf16[32,32,128]{2,1,0:T(8,128)(2,1)S(1)}, u32[]{:S(2)}, u32[]{:S(2)}) async-start(bf16[32,32,128]{2,1,0:T(8,128)(2,1)} %route.1), calls=%async_computation.1 | async-start | bytes 524288 | tf_op jit(solution)/shard_map/all_to_all | solution.py:435
  39.6 0.8 copy-done.11
  40.4 8.5 %all-to-all-done.1.got = bf16[32,32,128]{2,1,0:T(8,128)(2,1)S(1)} async-done(((bf16[32,32,128]{2,1,0:T(8,128)(2,1)}), bf16[32,32,128]{2,1,0:T(8,128)(2,1)S(1)}, u32[]{:S(2)}, u32[]{:S(2)}) %all-to-all-start.1) | async-done | bytes 262176 | tf_op jit(solution)/shard_map/all_to_all | solution.py:435
  49.0 1.0 copy-done.12
  50.0 1.0 copy-done.17
  51.0 7.9 %forward.1 = (bf16[2,128,512]{2,1,0:T(8,128)(2,1)}, bf16[2,512,128]{2,1,0:T(8,128)(2,1)S(1)}, bf16[2,2048,128]{2,1,0:T(8,128)(2,1)S(1)}) custom-call(s32[1]{0:T(128)S(6)} %copy.23.counts, s32[2]{0:T(128)S(1)} %copy-done.14, s32[2]{0:T(128)S(1)} %copy-done.15, s32[1]{0:T(128)} %bitcast.core, bf16[2,128,512]{2,1,0:T(8,128)(2,1)S(1)} %copy-done.1, ...), custom_call_target="tpu_custom_call" | custom-call | flops 2000000000 | bytes 4476928 | tf_op jit(solution)/shard_map/forward/pallas_call | solution.py:372
  59.6 0.8 slice_bitcast_fusion
  60.5 3.6 %collective-permute-start = (bf16[2048,128]{1,0:T(8,128)(2,1)}, bf16[2048,128]{1,0:T(8,128)(2,1)S(1)}, u32[]{:S(2)}, u32[]{:S(2)}) collective-permute-start(bf16[2048,128]{1,0:T(8,128)(2,1)} %slice_bitcast_fusion), channel_id=1, source_target_pairs={{0,32},{32,0},{64,96},{96,64},{128,160},{160,128},{192,224},{224,1... | collective-permute-start | bytes 1572872 | tf_op jit(solution)/shard_map/ppermute | solution.py:493
  64.1 1.0 copy-done.16
  65.1 0.9 copy-done.19
  66.1 3.1 %backward.2 = (f32[512,128]{1,0:T(8,128)S(1)}, bf16[32,16,128]{2,1,0:T(8,128)(2,1)S(1)}) custom-call(bf16[2,512,128]{2,1,0:T(8,128)(2,1)S(1)} %copy-done.19, bf16[27,128,128]{2,1,0:T(8,128)(2,1)S(1)} %copy-done.10, bf16[512,512]{1,0:T(8,128)(2,1)S(1)} %copy-done.16), custom_call_target="tpu_custom_call" | custom-call | flops 2000000000 | bytes 2064384 | tf_op jit(solution)/shard_map/backward/pallas_call | solution.py:372
  69.3 1.3 collective-permute-start.1
  70.6 2.5 %collective-permute-start.2 = (bf16[512,128]{1,0:T(8,128)(2,1)S(1)}, bf16[512,128]{1,0:T(8,128)(2,1)S(1)}, u32[]{:S(2)}, u32[]{:S(2)}) collective-permute-start(bf16[512,128]{1,0:T(8,128)(2,1)S(1)} %get-tuple-element.36), channel_id=1, source_target_pairs={{0,128},{32,160},{64,192},{96,224},{128,0},{160,32},{192,64},{224,... | collective-permute-start | bytes 393224 | tf_op jit(solution)/shard_map/ppermute | solution.py:504
  73.0 1.1 collective-permute-start.3
  74.2 3.1 %backward.3 = (f32[512,128]{1,0:T(8,128)S(1)}, bf16[32,16,128]{2,1,0:T(8,128)(2,1)S(1)}) custom-call(bf16[2,512,128]{2,1,0:T(8,128)(2,1)S(1)} %copy-done.20, bf16[27,128,128]{2,1,0:T(8,128)(2,1)S(1)} %copy-done.10, bf16[512,512]{1,0:T(8,128)(2,1)S(1)} %copy-done.16), custom_call_target="tpu_custom_call" | custom-call | flops 2000000000 | bytes 2064384 | tf_op jit(solution)/shard_map/backward/pallas_call | solution.py:372
  77.3 2.2 %collective-permute-done.2.away2 = bf16[512,128]{1,0:T(8,128)(2,1)S(1)} collective-permute-done((bf16[512,128]{1,0:T(8,128)(2,1)S(1)}, bf16[512,128]{1,0:T(8,128)(2,1)S(1)}, u32[]{:S(2)}, u32[]{:S(2)}) %collective-permute-start.2) | collective-permute-done | bytes 131104 | tf_op jit(solution)/shard_map/ppermute | solution.py:504
  79.5 0.8 join.1
  80.3 4.4 %all-to-all-start.2 = ((bf16[32,48,128]{2,1,0:T(8,128)(2,1)}), bf16[32,48,128]{2,1,0:T(8,128)(2,1)S(1)}, u32[]{:S(2)}, u32[]{:S(2)}) async-start(bf16[32,48,128]{2,1,0:T(8,128)(2,1)} %join.1), calls=%async_computation.2 | async-start | bytes 786432 | tf_op jit(solution)/shard_map/all_to_all | solution.py:515
  85.1 10.9 %all-to-all-done.2.got = bf16[32,48,128]{2,1,0:T(8,128)(2,1)S(1)} async-done(((bf16[32,48,128]{2,1,0:T(8,128)(2,1)}), bf16[32,48,128]{2,1,0:T(8,128)(2,1)S(1)}, u32[]{:S(2)}, u32[]{:S(2)}) %all-to-all-start.2) | async-done | bytes 393248 | tf_op jit(solution)/shard_map/all_to_all | solution.py:515
  96.8 18.3 %all_to_all.21.got = bf16[32,48,128]{2,1,0:T(8,128)(2,1)S(1)} all-to-all(bf16[32,48,128]{2,1,0:T(8,128)(2,1)S(1)} %merge.1), channel_id=1, replica_groups=mesh['grp'=8,'dev'=32] {'dev'}, dimensions={0} | all-to-all | bytes 786432 | tf_op jit(solution)/shard_map/all_to_all | solution.py:525
  115.4 3.2 %collective-permute-start.5 = (bf16[512,128]{1,0:T(8,128)(2,1)S(1)}, bf16[512,128]{1,0:T(8,128)(2,1)S(1)}, u32[]{:S(2)}, u32[]{:S(2)}) collective-permute-start(bf16[512,128]{1,0:T(8,128)(2,1)S(1)} %bitcast.9), channel_id=1, source_target_pairs={{0,128},{32,160},{64,192},{96,224},{128,0},{160,32},{192,64},{224,... | collective-permute-start | bytes 393224 | tf_op jit(solution)/shard_map/ppermute | solution.py:528
  118.8 5.7 %collective-permute-start.7 = (bf16[512,128]{1,0:T(8,128)(2,1)S(1)}, bf16[512,128]{1,0:T(8,128)(2,1)S(1)}, u32[]{:S(2)}, u32[]{:S(2)}) collective-permute-start(bf16[512,128]{1,0:T(8,128)(2,1)S(1)} %bitcast.11), channel_id=1, source_target_pairs={{0,32},{32,0},{64,96},{96,64},{128,160},{160,128},{192,224},{224,1... | collective-permute-start | bytes 393224 | tf_op jit(solution)/shard_map/ppermute | solution.py:531
  124.5 1.7 %collective-permute-start.10 = (bf16[512,128]{1,0:T(8,128)(2,1)S(1)}, bf16[512,128]{1,0:T(8,128)(2,1)S(1)}, u32[]{:S(2)}, u32[]{:S(2)}) collective-permute-start(bf16[512,128]{1,0:T(8,128)(2,1)S(1)} %collective-permute-done.6.refs_3_), channel_id=1, source_target_pairs={{0,32},{32,0},{64,96},{96,64},{128,160},{160,128},{192,224},{224,1... | collective-permute-start | bytes 393224 | tf_op jit(solution)/shard_map/ppermute | solution.py:531
  126.3 1.9 %collective-permute-start.9 = (bf16[512,128]{1,0:T(8,128)(2,1)S(1)}, bf16[512,128]{1,0:T(8,128)(2,1)S(1)}, u32[]{:S(2)}, u32[]{:S(2)}) collective-permute-start(bf16[512,128]{1,0:T(8,128)(2,1)S(1)} %collective-permute-done.5.refs_2_), channel_id=1, source_target_pairs={{0,32},{32,0},{64,96},{96,64},{128,160},{160,128},{192,224},{224,1... | collective-permute-start | bytes 393224 | tf_op jit(solution)/shard_map/ppermute | solution.py:531
  128.8 1.2 finish.1
  130.0 1.6 %assemble.1 = (f32[27,128,128]{2,1,0:T(8,128)}, f32[128,256]{1,0:T(8,128)}, f32[256,128]{1,0:T(8,128)}) custom-call(s32[1]{0:T(128)} %bitcast.core, s32[1]{0:T(128)} %bitcast.2.line, bf16[512,128]{1,0:T(8,128)(2,1)S(1)} %bitcast.12, bf16[512,128]{1,0:T(8,128)(2,1)S(1)} %collective-permute-done.4.refs_1_, ...), custom_call_target="tpu_custom_call" | custom-call | flops 1000000 | bytes 3080192 | tf_op jit(solution)/shard_map/assemble/pallas_call | solution.py:372
  (55 shorter events, 4.9 us)
Async XLA Ops:
  1.3 1.0 copy-start
  2.2 1.0 copy-start.4
  3.3 0.9 copy-start.5
  5.5 33.7 %copy-start.1 = (bf16[2,128,512]{2,1,0:T(8,128)(2,1)S(1)}, bf16[2,128,512]{2,1,0:T(8,128)(2,1)}, u32[]{:S(2)}) copy-start(bf16[2,128,512]{2,1,0:T(8,128)(2,1)} %feat.5) | copy-start | bytes 786436
  5.5 33.8 %copy-start.2 = (bf16[2,128,512]{2,1,0:T(8,128)(2,1)S(1)}, bf16[2,128,512]{2,1,0:T(8,128)(2,1)}, u32[]{:S(2)}) copy-start(bf16[2,128,512]{2,1,0:T(8,128)(2,1)} %gout.5) | copy-start | bytes 786436
  5.5 33.8 %copy-start.6 = (bf16[256,128]{1,0:T(8,128)(2,1)S(1)}, bf16[256,128]{1,0:T(8,128)(2,1)}, u32[]{:S(2)}) copy-start(bf16[256,128]{1,0:T(8,128)(2,1)} %down.3) | copy-start | bytes 196612
  5.5 33.8 %copy-start.7 = (bf16[2,16,512]{2,1,0:T(8,128)(2,1)S(1)}, bf16[2,16,512]{2,1,0:T(8,128)(2,1)}, u32[]{:S(2)}) copy-start(bf16[2,16,512]{2,1,0:T(8,128)(2,1)} %constant.20.clone.pool) | copy-start | bytes 98308
  6.5 42.5 %copy-start.10 = (bf16[27,128,128]{2,1,0:T(8,128)(2,1)S(1)}, bf16[27,128,128]{2,1,0:T(8,128)(2,1)}, u32[]{:S(2)}) copy-start(bf16[27,128,128]{2,1,0:T(8,128)(2,1)} %weight.3) | copy-start | bytes 2654212
  6.5 42.4 %copy-start.13 = (bf16[128,256]{1,0:T(8,128)(2,1)S(1)}, bf16[128,256]{1,0:T(8,128)(2,1)}, u32[]{:S(2)}) copy-start(bf16[128,256]{1,0:T(8,128)(2,1)} %up.1) | copy-start | bytes 196612
  6.5 42.4 %copy-start.14 = (s32[2]{0:T(128)S(1)}, s32[2]{0:T(128)}, u32[]{:S(2)}) copy-start(s32[2]{0:T(128)} %parent.1) | copy-start | bytes 28
  6.5 42.4 %copy-start.15 = (s32[2]{0:T(128)S(1)}, s32[2]{0:T(128)}, u32[]{:S(2)}) copy-start(s32[2]{0:T(128)} %child.1) | copy-start | bytes 28
  31.8 17.1 %all-to-all-start.1 = ((bf16[32,32,128]{2,1,0:T(8,128)(2,1)}), bf16[32,32,128]{2,1,0:T(8,128)(2,1)S(1)}, u32[]{:S(2)}, u32[]{:S(2)}) async-start(bf16[32,32,128]{2,1,0:T(8,128)(2,1)} %route.1), calls=%async_computation.1 | async-start | bytes 524288 | tf_op jit(solution)/shard_map/all_to_all | solution.py:435
  39.6 0.8 copy-start.11
  48.9 1.0 copy-start.12
  50.0 1.0 copy-start.17
  58.9 0.7 copy-start.18
  60.5 8.7 %collective-permute-start = (bf16[2048,128]{1,0:T(8,128)(2,1)}, bf16[2048,128]{1,0:T(8,128)(2,1)S(1)}, u32[]{:S(2)}, u32[]{:S(2)}) collective-permute-start(bf16[2048,128]{1,0:T(8,128)(2,1)} %slice_bitcast_fusion), channel_id=1, source_target_pairs={{0,32},{32,0},{64,96},{96,64},{128,160},{160,128},{192,224},{224,1... | collective-permute-start | bytes 1572872 | tf_op jit(solution)/shard_map/ppermute | solution.py:493
  64.1 1.0 copy-start.16
  65.1 0.9 copy-start.19
  66.1 8.1 %copy-start.20 = (bf16[2,512,128]{2,1,0:T(8,128)(2,1)S(1)}, bf16[2,512,128]{2,1,0:T(8,128)(2,1)}, u32[]{:S(2)}) copy-start(bf16[2,512,128]{2,1,0:T(8,128)(2,1)} %copy-done.18) | copy-start | bytes 786436
  69.3 8.0 %collective-permute-start.1 = (bf16[512,128]{1,0:T(8,128)(2,1)S(1)}, bf16[512,128]{1,0:T(8,128)(2,1)S(1)}, u32[]{:S(2)}, u32[]{:S(2)}) collective-permute-start(bf16[512,128]{1,0:T(8,128)(2,1)S(1)} %get-tuple-element.35), channel_id=1, source_target_pairs={{0,64},{32,96},{64,128},{96,160},{128,192},{160,224},{192,0},{224,... | collective-permute-start | bytes 393224 | tf_op jit(solution)/shard_map/ppermute | solution.py:504
  70.6 8.9 %collective-permute-start.2 = (bf16[512,128]{1,0:T(8,128)(2,1)S(1)}, bf16[512,128]{1,0:T(8,128)(2,1)S(1)}, u32[]{:S(2)}, u32[]{:S(2)}) collective-permute-start(bf16[512,128]{1,0:T(8,128)(2,1)S(1)} %get-tuple-element.36), channel_id=1, source_target_pairs={{0,128},{32,160},{64,192},{96,224},{128,0},{160,32},{192,64},{224,... | collective-permute-start | bytes 393224 | tf_op jit(solution)/shard_map/ppermute | solution.py:504
  73.0 6.5 %collective-permute-start.3 = (bf16[512,128]{1,0:T(8,128)(2,1)S(1)}, bf16[512,128]{1,0:T(8,128)(2,1)S(1)}, u32[]{:S(2)}, u32[]{:S(2)}) collective-permute-start(bf16[512,128]{1,0:T(8,128)(2,1)S(1)} %get-tuple-element.37), channel_id=1, source_target_pairs={{0,192},{32,224},{64,0},{96,32},{128,64},{160,96},{192,128},{224,1... | collective-permute-start | bytes 393224 | tf_op jit(solution)/shard_map/ppermute | solution.py:504
  80.3 48.5 %copy-start.3 = (bf16[512,512]{1,0:T(8,128)(2,1)S(1)}, bf16[512,512]{1,0:T(8,128)(2,1)}, u32[]{:S(2)}) copy-start(bf16[512,512]{1,0:T(8,128)(2,1)} %constant.25.clone.give) | copy-start | bytes 1572868
  80.3 15.7 %all-to-all-start.2 = ((bf16[32,48,128]{2,1,0:T(8,128)(2,1)}), bf16[32,48,128]{2,1,0:T(8,128)(2,1)S(1)}, u32[]{:S(2)}, u32[]{:S(2)}) async-start(bf16[32,48,128]{2,1,0:T(8,128)(2,1)} %join.1), calls=%async_computation.2 | async-start | bytes 786432 | tf_op jit(solution)/shard_map/all_to_all | solution.py:515
  115.1 9.4 %collective-permute-start.6 = (bf16[512,128]{1,0:T(8,128)(2,1)S(1)}, bf16[512,128]{1,0:T(8,128)(2,1)S(1)}, u32[]{:S(2)}, u32[]{:S(2)}) collective-permute-start(bf16[512,128]{1,0:T(8,128)(2,1)S(1)} %bitcast.8), channel_id=1, source_target_pairs={{0,64},{32,96},{64,128},{96,160},{128,192},{160,224},{192,0},{224,... | collective-permute-start | bytes 393224 | tf_op jit(solution)/shard_map/ppermute | solution.py:528
  115.4 10.9 %collective-permute-start.5 = (bf16[512,128]{1,0:T(8,128)(2,1)S(1)}, bf16[512,128]{1,0:T(8,128)(2,1)S(1)}, u32[]{:S(2)}, u32[]{:S(2)}) collective-permute-start(bf16[512,128]{1,0:T(8,128)(2,1)S(1)} %bitcast.9), channel_id=1, source_target_pairs={{0,128},{32,160},{64,192},{96,224},{128,0},{160,32},{192,64},{224,... | collective-permute-start | bytes 393224 | tf_op jit(solution)/shard_map/ppermute | solution.py:528
  118.6 9.6 %collective-permute-start.4 = (bf16[512,128]{1,0:T(8,128)(2,1)S(1)}, bf16[512,128]{1,0:T(8,128)(2,1)S(1)}, u32[]{:S(2)}, u32[]{:S(2)}) collective-permute-start(bf16[512,128]{1,0:T(8,128)(2,1)S(1)} %bitcast.10), channel_id=1, source_target_pairs={{0,192},{32,224},{64,0},{96,32},{128,64},{160,96},{192,128},{224,1... | collective-permute-start | bytes 393224 | tf_op jit(solution)/shard_map/ppermute | solution.py:528
  118.8 11.2 %collective-permute-start.7 = (bf16[512,128]{1,0:T(8,128)(2,1)S(1)}, bf16[512,128]{1,0:T(8,128)(2,1)S(1)}, u32[]{:S(2)}, u32[]{:S(2)}) collective-permute-start(bf16[512,128]{1,0:T(8,128)(2,1)S(1)} %bitcast.11), channel_id=1, source_target_pairs={{0,32},{32,0},{64,96},{96,64},{128,160},{160,128},{192,224},{224,1... | collective-permute-start | bytes 393224 | tf_op jit(solution)/shard_map/ppermute | solution.py:531
  124.5 5.5 %collective-permute-start.10 = (bf16[512,128]{1,0:T(8,128)(2,1)S(1)}, bf16[512,128]{1,0:T(8,128)(2,1)S(1)}, u32[]{:S(2)}, u32[]{:S(2)}) collective-permute-start(bf16[512,128]{1,0:T(8,128)(2,1)S(1)} %collective-permute-done.6.refs_3_), channel_id=1, source_target_pairs={{0,32},{32,0},{64,96},{96,64},{128,160},{160,128},{192,224},{224,1... | collective-permute-start | bytes 393224 | tf_op jit(solution)/shard_map/ppermute | solution.py:531
  126.3 3.8 %collective-permute-start.9 = (bf16[512,128]{1,0:T(8,128)(2,1)S(1)}, bf16[512,128]{1,0:T(8,128)(2,1)S(1)}, u32[]{:S(2)}, u32[]{:S(2)}) collective-permute-start(bf16[512,128]{1,0:T(8,128)(2,1)S(1)} %collective-permute-done.5.refs_2_), channel_id=1, source_target_pairs={{0,32},{32,0},{64,96},{96,64},{128,160},{160,128},{192,224},{224,1... | collective-permute-start | bytes 393224 | tf_op jit(solution)/shard_map/ppermute | solution.py:531
  128.2 1.9 %collective-permute-start.8 = (bf16[512,128]{1,0:T(8,128)(2,1)S(1)}, bf16[512,128]{1,0:T(8,128)(2,1)S(1)}, u32[]{:S(2)}, u32[]{:S(2)}) collective-permute-start(bf16[512,128]{1,0:T(8,128)(2,1)S(1)} %collective-permute-done.4.refs_1_), channel_id=1, source_target_pairs={{0,32},{32,0},{64,96},{96,64},{128,160},{160,128},{192,224},{224,1... | collective-permute-start | bytes 393224 | tf_op jit(solution)/shard_map/ppermute | solution.py:531
  (2 other events, 1.4 us)

commit v3 on v2

v3 whole, which is shorter than its diff:
```python
import functools

import jax
import jax.numpy as jnp
import numpy as np
from jax import lax
from jax.experimental import pallas as pl
from jax.experimental.pallas import tpu as pltpu
from jax.sharding import PartitionSpec as P

BF = jnp.bfloat16
F32 = jnp.float32

OFFSETS = [
    (a, b, c) for a in (-1, 0, 1) for b in (-1, 0, 1) for c in (-1, 0, 1) if (a, b, c) != (0, 0, 0)
]
FACES = [d for d in OFFSETS if sum(map(abs, d)) == 1]
EDGES = [d for d in OFFSETS if sum(map(abs, d)) == 2]
CORNERS = [d for d in OFFSETS if sum(map(abs, d)) == 3]
PIECE = {d: 64 * n for n, d in enumerate(FACES)}
PIECE.update({d: 384 + 8 * n for n, d in enumerate(EDGES)})
PIECE.update({d: 480 + n for n, d in enumerate(CORNERS)})


def voxel_runs(d):
    a, b, c = (7 if x < 0 else 0 for x in d)
    free = [x == 0 for x in d]
    if free == [True, True, False]:
        return [(0, c, 64, 8)]
    if free == [True, False, True]:
        return [(8 * x, x * 64 + b * 8, 8, 1) for x in range(8)]
    if free == [False, True, True]:
        return [(0, a * 64, 64, 1)]
    size = 8 if any(free) else 1
    stride = (64 if free[0] else 1) * (8 if free[1] else 1)
    return [(0, a * 64 + b * 8 + c, size, stride)]


def run(start, size, stride):
    return pl.ds(start, size) if stride == 1 else pl.ds(start, size, stride=stride)


SHARES = [((64 * f + p, 32, 2), (2 * f + p, 32, 16)) for f in range(6) for p in range(2)]
SHARES += [((384 + 32 * m, 32, 1), (12 + m, 32, 16)) for m in range(3)]
SHARES += [((480, 8, 1), (15 + 16 * n, 8, 64)) for n in range(4)]


def to_pieces(rows, pieces):
    for there, here in SHARES[:16]:
        pieces[run(*there), :] = rows[run(*here), :]


def to_shares(pieces, rows):
    for there, here in SHARES:
        rows[run(*here), :] = pieces[run(*there), :]


def nn(x, y):
    return lax.dot_general(x, y, (((1,), (0,)), ((), ())), preferred_element_type=F32)


def nt(x, y):
    return lax.dot_general(x, y, (((1,), (1,)), ((), ())), preferred_element_type=F32)


def identity():
    rows = lax.broadcasted_iota(jnp.int32, (128, 128), 0)
    lanes = lax.broadcasted_iota(jnp.int32, (128, 128), 1)
    return (rows == lanes).astype(F32).astype(BF)


def pool_rows(s):
    rows = lax.broadcasted_iota(jnp.int32, (16, 512), 0) - 8 * s
    lanes = lax.broadcasted_iota(jnp.int32, (16, 512), 1)
    block = ((lanes >> 8) & 1) * 4 + ((lanes >> 5) & 1) * 2 + ((lanes >> 2) & 1)
    return (rows == block).astype(F32).astype(BF)


def ask_kernel(
    counts, feat, owner, slot, msg, feat_v, owner_v, slot_v, bricks, voxels, pc, rows, sems
):
    pairs = ((owner, owner_v), (slot, slot_v), (feat, feat_v))
    copies = [
        pltpu.make_async_copy(src, dst, sems.at[n]) for n, (src, dst) in enumerate(pairs)
    ]
    for copy in copies:
        copy.start()
    bricks[...] = jnp.zeros((128, 128), F32)
    copies[0].wait()
    copies[1].wait()
    named = jnp.where(owner_v[...] >= 0, owner_v[...] * 2 + slot_v[...], -1)
    bricks[0:2, 0:26] = named.astype(F32)
    bricks[...] = bricks[...].T

    def ask(first, size, stride, direction):
        line = bricks[pl.ds(OFFSETS.index(direction), 1), :]
        rows[run(first, size, stride), :] = jnp.broadcast_to(line, (size, 128))

    for n, d in enumerate(FACES):
        ask(2 * n, 32, 16, d)
        ask(2 * n + 1, 32, 16, d)
    for n, d in enumerate(EDGES):
        ask(12 + n // 4 + 128 * (n % 4), 8, 16, d)
    for n, d in enumerate(CORNERS):
        ask(15 + 64 * n, 4, 16, d)
    msg[:, 32:48, :] = rows[...].astype(BF).reshape(32, 16, 128)
    copies[2].wait()
    for s in range(2):
        live = (counts[0] > s).astype(F32)
        voxels[...] = (feat_v[s].astype(F32) * live).T
        for d in OFFSETS:
            for at, first, size, stride in voxel_runs(d):
                pc[pl.ds(PIECE[d] + at, size), :] = voxels[run(first, size, stride), :]
        to_shares(pc, rows)
        msg[:, 16 * s : 16 * s + 16, :] = rows[...].astype(BF).reshape(32, 16, 128)


def same_part():
    rows = lax.broadcasted_iota(jnp.int32, (16, 128), 0)
    lanes = lax.broadcasted_iota(jnp.int32, (16, 128), 1) & 15
    return (rows == lanes).astype(F32).astype(BF)


def route_kernel(got, out, hot):
    same = jnp.broadcast_to(same_part()[None], (32, 16, 128))
    zero = jnp.zeros((32, 16, 128), BF)
    lanes = lax.broadcasted_iota(jnp.int32, (128, 128), 0)
    brick = lax.broadcasted_iota(jnp.int32, (16, 128), 1) >> 4
    table = got[:, 32:48, :].reshape(512, 128)
    data = got[:, 0:32, :].reshape(1024, 128)
    for s in range(2):
        spread = (lanes == s).astype(F32).astype(BF)
        asked = nn(table, spread).astype(BF).reshape(32, 16, 128)
        for n in range(8):
            here = (brick + 8 * n).astype(F32).astype(BF)
            hot[:, n * 128 : n * 128 + 128] = jnp.where(asked == here[None], same, zero).reshape(
                512, 128
            )
        picked = nn(hot[...], data).astype(BF)
        out[:, 16 * s : 16 * s + 16, :] = picked.reshape(32, 16, 128)


def forward_kernel(
    counts, parent, child, core, feat, got, gout, weight, up, down,
    out, grad, keep, send,
    rows, pc, mine, s0, s1, s2, cols, grad_t, acts, slopes, pooled, grad_pooled,
):
    eye = identity()
    pooled[...] = jnp.zeros((16, 128), F32)
    grad_pooled[...] = jnp.zeros((16, 128), F32)

    def brick(s, _):
        live = (counts[0] > s).astype(F32)
        pool = pool_rows(s)
        mine[...] = (feat[s].astype(F32) * live).T
        grad_pooled[...] += nt(pool, gout[s]) * live
        share = got[:, pl.ds(pl.multiple_of(s * 16, 16), 16), :]
        rows[...] = share.reshape(512, 128).astype(F32)
        to_pieces(rows, pc)
        for a in range(8):
            s1[pl.ds(8 + ((a + 1) * 10 + 1) * 8, 64), :] = mine[a * 64 : a * 64 + 64, :]
            for d, b in (((0, -1, 0), 0), ((0, 1, 0), 9)):
                s1[pl.ds(8 + ((a + 1) * 10 + b) * 8, 8), :] = pc[pl.ds(PIECE[d] + 8 * a, 8), :]
        for a, x in ((-1, 0), (1, 9)):
            s1[pl.ds(8 + (x * 10 + 1) * 8, 64), :] = pc[pl.ds(PIECE[a, 0, 0], 64), :]
            for b, y in ((-1, 0), (1, 9)):
                s1[pl.ds(8 + (x * 10 + y) * 8, 8), :] = pc[pl.ds(PIECE[a, b, 0], 8), :]
        s0[...] = s1[pl.ds(7, 800), :]
        s2[...] = s1[pl.ds(9, 800), :]
        for c, ref, lane in ((-1, s0, 0), (1, s2, 7)):
            for a in range(8):
                ref[pl.ds(((a + 1) * 10 + 1) * 8 + lane, 8, stride=8), :] = pc[
                    pl.ds(PIECE[0, 0, c] + 8 * a, 8), :
                ]
            for a, x in ((-1, 0), (1, 9)):
                ref[pl.ds((x * 10 + 1) * 8 + lane, 8, stride=8), :] = pc[
                    pl.ds(PIECE[a, 0, c], 8), :
                ]
                ref[pl.ds((10 + x) * 8 + lane, 8, stride=80), :] = pc[pl.ds(PIECE[0, a, c], 8), :]
                for b, y in ((-1, 0), (1, 9)):
                    ref[pl.ds((x * 10 + y) * 8 + lane, 1), :] = pc[pl.ds(PIECE[a, b, c], 1), :]

        def plane(a, _):
            for b in range(3):
                for c, ref in enumerate((s0, s1, s2)):
                    start = pl.multiple_of((a * 10 + b) * 8 + (8 if c == 1 else 0), 8)
                    cols[s, pl.ds(pl.multiple_of(a * 64, 64), 64), pl.ds((3 * b + c) * 128, 128)] = ref[
                        pl.ds(start, 64), :
                    ].astype(BF)
            return 0

        lax.fori_loop(0, 10, plane, 0)
        pre = nn(cols[s, 0:512, :], weight[0])
        pre = pre + nn(cols[s, 64:576, :], weight[1])
        pre = pre + nn(cols[s, 128:640, :], weight[2])
        pre = pre.T
        gate = 1.0 / (1.0 + jnp.exp(-pre))
        active = pre * gate
        acts[s] = active
        slopes[s] = gate * (1.0 + pre * (1.0 - gate))
        high = active.astype(BF)
        low = (active - high.astype(F32)).astype(BF)
        pooled[...] += nt(pool, high) + nt(pool, low)
        return 0

    lax.fori_loop(0, 2, brick, 0)
    second = lax.broadcasted_iota(jnp.int32, (16, 1), 0) >= 8
    valid = [
        (
            (counts[0] > s) & (parent[s] >= 0) & (parent[s] * 64 + child[s] >= 0)
        ).astype(F32)
        for s in range(2)
    ]
    valid = jnp.where(second, valid[1], valid[0])
    coarse_in = (pooled[...] * (1.0 / 64.0) * valid).astype(BF)
    grad_out = (grad_pooled[...] * valid).astype(BF)
    coarse_pre = nn(coarse_in, up[...])
    gate = 1.0 / (1.0 + jnp.exp(-coarse_pre))
    coarse_mid = (coarse_pre * gate).astype(BF)
    grad_pre = nt(grad_out, down[...]) * (gate * (1.0 + coarse_pre * (1.0 - gate)))
    grad_pre = grad_pre.astype(BF)
    coarse_out = nn(coarse_mid, down[...]).astype(BF)
    grad_cin = nt(grad_pre, up[...]).astype(BF)
    lift = nt(eye, coarse_out).astype(BF)
    back = nt(eye, grad_cin).astype(BF)

    def blend(s, _):
        live = (counts[0] > s).astype(F32)
        pool = pool_rows(s)
        out[s] = (feat[s].astype(F32) * live + acts[s] + nn(lift, pool)).astype(BF)
        grad_in = gout[s].astype(F32) * live + nn(back, pool) * (1.0 / 64.0)
        grad_pre_conv = grad_in * slopes[s]
        grad_t[s] = grad_pre_conv.astype(BF)
        grad[s] = grad_pre_conv.T.astype(BF)
        return 0

    lax.fori_loop(0, 2, blend, 0)

    def put(block, value):
        half, at = divmod(block, 16)
        value = value.astype(BF)

        @pl.when(core[0] == half)
        def _():
            keep[pl.ds(at * 128, 128), :] = value

        @pl.when(core[0] != half)
        def _():
            send[pl.ds(at * 128, 128), :] = value

    grad_up = nn(nt(eye, coarse_in).astype(BF), grad_pre)
    for h in range(2):
        put(27 + h, grad_up[:, h * 128 : h * 128 + 128])
        middle = nt(eye, coarse_mid[:, h * 128 : h * 128 + 128]).astype(BF)
        put(29 + h, nn(middle, grad_out))
    put(31, jnp.zeros((128, 128), F32))
    for a in range(3):
        total = nn(grad_t[0], cols[0, a * 64 : a * 64 + 512, :])
        total = total + nn(grad_t[1], cols[1, a * 64 : a * 64 + 512, :])
        total = total.astype(BF)
        for n in range(9):
            put(9 * a + n, nt(eye, total[:, n * 128 : n * 128 + 128]))


def pair_kernel(line, keep, other, own, one, two, three):
    for step, ref in enumerate((own, one, two, three)):
        at = pl.ds(pl.multiple_of(((line[0] + step) & 3) * 512, 512), 512)
        ref[...] = (keep[at, :].astype(F32) + other[at, :].astype(F32)).astype(ref.dtype)


def backward_kernel(grad, weight, own, msg, planes, acc, pc, rows):
    planes[0:128, :] = jnp.zeros((128, 128), BF)
    planes[640:768, :] = jnp.zeros((128, 128), BF)
    low = (lax.broadcasted_iota(jnp.int32, (64, 1), 0) & 7) != 0
    high = (lax.broadcasted_iota(jnp.int32, (64, 1), 0) & 7) != 7

    def brick(s, _):
        planes[128:640, :] = grad[s]
        acc[...] = jnp.zeros_like(acc)

        def tap(n, _):
            c = lax.rem(n, 3)
            b = lax.div(n, 3)
            part = nt(planes[128:768, :], weight[n])
            part = part + nt(planes[64:704, :], weight[n + 9])
            part = part + nt(planes[0:640, :], weight[n + 18])
            for a in range(10):
                at = pl.ds(pl.multiple_of(8 + (a * 10 + b) * 8, 8), 64)
                acc[c, at, :] = acc[c, at, :] + part[a * 64 : a * 64 + 64]
            return 0

        lax.fori_loop(0, 9, tap, 0)

        def middle(row, size):
            at = 8 + row
            total = acc[1, pl.ds(at, size), :]
            total = total + jnp.where(high[:size], acc[0, pl.ds(at + 1, size), :], 0.0)
            return total + jnp.where(low[:size], acc[2, pl.ds(at - 1, size), :], 0.0)

        for a in range(8):
            own[s, pl.ds(a * 64, 64), :] = middle(((a + 1) * 10 + 1) * 8, 64)
            for d, b in (((0, -1, 0), 0), ((0, 1, 0), 9)):
                pc[pl.ds(PIECE[d] + 8 * a, 8), :] = middle(((a + 1) * 10 + b) * 8, 8)
        for a, x in ((-1, 0), (1, 9)):
            pc[pl.ds(PIECE[a, 0, 0], 64), :] = middle((x * 10 + 1) * 8, 64)
            for b, y in ((-1, 0), (1, 9)):
                pc[pl.ds(PIECE[a, b, 0], 8), :] = middle((x * 10 + y) * 8, 8)
        for c, ref, lane in ((-1, acc.at[0], 8), (1, acc.at[2], 15)):
            for a in range(8):
                pc[pl.ds(PIECE[0, 0, c] + 8 * a, 8), :] = ref[
                    pl.ds(((a + 1) * 10 + 1) * 8 + lane, 8, stride=8), :
                ]
            for a, x in ((-1, 0), (1, 9)):
                pc[pl.ds(PIECE[a, 0, c], 8), :] = ref[pl.ds((x * 10 + 1) * 8 + lane, 8, stride=8), :]
                pc[pl.ds(PIECE[0, a, c], 8), :] = ref[pl.ds((10 + x) * 8 + lane, 8, stride=80), :]
                for b, y in ((-1, 0), (1, 9)):
                    pc[pl.ds(PIECE[a, b, c], 1), :] = ref[pl.ds((x * 10 + y) * 8 + lane, 1), :]
        to_shares(pc, rows)
        at = pl.ds(pl.multiple_of(s * 16, 16), 16)
        msg[:, at, :] = rows[...].astype(BF).reshape(32, 16, 128)
        return 0

    lax.fori_loop(0, 2, brick, 0)


def join_kernel(terms, own, away1, away2, away3, msg):
    msg[:, 0:32, :] = terms[...]
    total = own[...] + away1[...].astype(F32) + away2[...].astype(F32) + away3[...].astype(F32)
    msg[:, 32:48, :] = total.astype(BF).reshape(32, 16, 128)


def merge_kernel(got, table, out, hot):
    same = same_part()
    zero = jnp.zeros((16, 128), BF)
    share = jnp.sum(got[:, 32:48, :].astype(F32), axis=0).astype(BF)
    out[:, 32:48, :] = jnp.broadcast_to(share[None], (32, 16, 128))
    for n in range(8):
        asked = table[:, n * 128 : n * 128 + 128]
        for brick in range(64):
            hot[brick * 16 : brick * 16 + 16, n * 128 : n * 128 + 128] = jnp.where(
                asked == jnp.full((16, 128), brick, BF), same, zero
            )
    total = nn(hot[...], got[:, 0:32, :].reshape(1024, 128))
    out[:, 0:32, :] = total.astype(BF).reshape(32, 32, 128)


def finish_kernel(counts, got, own, gout, out, rows, pc, total):
    for s in range(2):
        live = (counts[0] > s).astype(F32)
        rows[...] = got[:, 16 * s : 16 * s + 16, :].reshape(512, 128).astype(F32)
        to_pieces(rows, pc)
        total[...] = own[s]
        for d in OFFSETS:
            for at, first, size, stride in voxel_runs(d):
                where = run(first, size, stride)
                total[where, :] = total[where, :] + pc[pl.ds(PIECE[d] + at, size), :]
        out[s] = (total[...].T + gout[s].astype(F32) * live).astype(BF)


def assemble_kernel(core, line, *refs):
    parts, (conv, up, down) = refs[:8], refs[8:]
    for n, part in enumerate(parts):
        half = core[0] ^ (n // 4)
        first = half * 16 + ((line[0] + n % 4) & 3) * 4

        def block(at):
            return part[at * 128 : at * 128 + 128, :].astype(F32)

        @pl.when(first < 24)
        def _():
            for at in range(4):
                conv[first + at] = block(at)

        @pl.when(first == 24)
        def _():
            for at in range(3):
                conv[24 + at] = block(at)
            up[:, 0:128] = block(3)

        @pl.when(first == 28)
        def _():
            up[:, 128:256] = block(0)
            down[0:128, :] = block(1)
            down[128:256, :] = block(2)


VM = pl.BlockSpec(memory_space=pltpu.VMEM)
SM = pl.BlockSpec(memory_space=pltpu.SMEM)


def call(kernel, shapes, scalars, arrays, scratch=(), flops=1e6, space=VM, limit=20, name=None):
    moved = sum(x.size * x.dtype.itemsize for x in arrays)
    moved += sum(int(np.prod(s.shape)) * s.dtype.itemsize for s in shapes)
    return pl.pallas_call(
        kernel,
        out_shape=shapes,
        in_specs=[SM] * len(scalars) + [space] * len(arrays),
        out_specs=[VM] * len(shapes),
        scratch_shapes=list(scratch),
        compiler_params=pltpu.CompilerParams(vmem_limit_bytes=limit * 2**20),
        cost_estimate=pl.CostEstimate(
            flops=int(flops), bytes_accessed=int(moved), transcendentals=0
        ),
        name=name,
    )(*scalars, *arrays)


def shape(dims, dtype):
    return jax.ShapeDtypeStruct(dims, dtype)


def on_device(
    features,
    grad_out,
    conv_weight,
    coarse_up,
    coarse_down,
    counts,
    neighbour_owner,
    neighbour_slot,
    parent,
    child_slot,
):
    grp = lax.axis_index("grp").astype(jnp.int32)
    core = (grp & 1).reshape(1)
    line = (grp >> 1).reshape(1)
    swap = [(i, i ^ 1) for i in range(8)]
    (msg,) = call(
        ask_kernel,
        [shape((32, 48, 128), BF)],
        [counts],
        [features, neighbour_owner, neighbour_slot],
        [
            pltpu.VMEM((2, 128, 512), BF),
            pltpu.VMEM((2, 26), jnp.int32),
            pltpu.VMEM((2, 26), jnp.int32),
            pltpu.VMEM((128, 128), F32),
            pltpu.VMEM((512, 128), F32),
            pltpu.VMEM((512, 128), F32),
            pltpu.VMEM((512, 128), F32),
            pltpu.SemaphoreType.DMA((3,)),
        ],
        flops=2e6,
        space=pl.BlockSpec(memory_space=pltpu.HBM),
        limit=60,
        name="ask",
    )
    first = lax.all_to_all(msg, "dev", split_axis=0, concat_axis=0, tiled=True)
    (answer,) = call(
        route_kernel,
        [shape((32, 32, 128), BF)],
        [],
        [first],
        [pltpu.VMEM((512, 1024), BF)],
        flops=3e8,
        name="route",
    )
    halo = lax.all_to_all(answer, "dev", split_axis=0, concat_axis=0, tiled=True)
    table = first[:, 32:48, 0:2].transpose(0, 2, 1).reshape(1, 1024)
    table = jnp.broadcast_to(table, (16, 1024))
    output, grad_pre, keep, send = call(
        forward_kernel,
        [
            shape((2, 128, 512), BF),
            shape((2, 512, 128), BF),
            shape((2048, 128), BF),
            shape((2048, 128), BF),
        ],
        [counts, parent, child_slot, core],
        [
            features,
            halo,
            grad_out,
            conv_weight.reshape(3, 1152, 128),
            coarse_up,
            coarse_down,
        ],
        [
            pltpu.VMEM((512, 128), F32),
            pltpu.VMEM((512, 128), F32),
            pltpu.VMEM((512, 128), F32),
            pltpu.VMEM((800, 128), F32),
            pltpu.VMEM((816, 128), F32),
            pltpu.VMEM((800, 128), F32),
            pltpu.VMEM((2, 640, 1152), BF),
            pltpu.VMEM((2, 128, 512), BF),
            pltpu.VMEM((2, 128, 512), F32),
            pltpu.VMEM((2, 128, 512), F32),
            pltpu.VMEM((16, 128), F32),
            pltpu.VMEM((16, 128), F32),
        ],
        flops=2e9,
        name="forward",
    )

    other = lax.ppermute(send, "grp", swap)
    own_sum, *away = call(
        pair_kernel,
        [shape((512, 128), F32)] + [shape((512, 128), BF)] * 3,
        [line],
        [keep, other],
        name="pair",
    )
    away = [
        lax.ppermute(x, "grp", [(i, (i + 2 * step) % 8) for i in range(8)])
        for step, x in zip((1, 2, 3), away)
    ]
    grad_pre, own_sum = lax.optimization_barrier((grad_pre, own_sum))
    own, terms = call(
        backward_kernel,
        [shape((2, 512, 128), F32), shape((32, 32, 128), BF)],
        [],
        [grad_pre, conv_weight],
        [
            pltpu.VMEM((768, 128), BF),
            pltpu.VMEM((3, 816, 128), F32),
            pltpu.VMEM((512, 128), F32),
            pltpu.VMEM((512, 128), F32),
        ],
        flops=4e9,
        name="backward",
    )
    (terms,) = call(
        join_kernel, [shape((32, 48, 128), BF)], [], [terms, own_sum, *away], name="join"
    )
    terms = lax.all_to_all(terms, "dev", split_axis=0, concat_axis=0, tiled=True)
    (sums,) = call(
        merge_kernel,
        [shape((32, 48, 128), BF)],
        [],
        [terms, table],
        [pltpu.VMEM((1024, 1024), BF)],
        flops=3e8,
        name="merge",
    )
    back = lax.all_to_all(sums, "dev", split_axis=0, concat_axis=0, tiled=True)
    chunk = back[:, 32:48, :].reshape(512, 128)
    parts = [chunk] + [
        lax.ppermute(chunk, "grp", [(i, (i - 2 * step) % 8) for i in range(8)])
        for step in (1, 2, 3)
    ]
    (grad_features,) = call(
        finish_kernel,
        [shape((2, 128, 512), BF)],
        [counts],
        [back, own, grad_out],
        [pltpu.VMEM((512, 128), F32)] * 3,
        flops=3e8,
        name="finish",
    )
    chunk = lax.ppermute(chunk, "grp", swap)
    parts, grad_features = lax.optimization_barrier((parts, grad_features))
    parts = parts + [chunk] + [lax.ppermute(x, "grp", swap) for x in parts[1:]]
    grad_conv, grad_up, grad_down = call(
        assemble_kernel,
        [shape((27, 128, 128), F32), shape((128, 256), F32), shape((256, 128), F32)],
        [core, line],
        parts,
        name="assemble",
    )
    return (output, grad_features, grad_conv, grad_up, grad_down)


def solution(mesh):
    return jax.shard_map(
        on_device,
        mesh=mesh,
        in_specs=(
            P(("grp", "dev"), None, None),
            P(("grp", "dev"), None, None),
            P(),
            P(),
            P(),
            P(("grp", "dev")),
            P(("grp", "dev"), None),
            P(("grp", "dev"), None),
            P(("grp", "dev")),
            P(("grp", "dev")),
        ),
        out_specs=(P(("grp", "dev"), None, None), P(("grp", "dev"), None, None), P(), P(), P()),
        check_vma=False,
    )
```

time: 132 us -> 126 us (0.955)
  local copies, waits for them, and re-layouts: 11.1 us -> 0.41 us
  Pallas kernels: 21.4 us -> 26.7 us
    unnamed x42 -> x14, local copies, waits for them, and re-layouts: 9.85 us -> 0.03 us
    pallas_call x11 -> x9, Pallas kernels: 21.4 us -> 26.7 us  [call(): pl.pallas_call(kernel, out_shape=shapes, in_specs=[SM] * len(scalars) + [...]
    ppermute x5, waiting for transfers between devices: 0.01 us -> 2.56 us  [the longest x1 1.54 us: on_device(): other = lax.ppermute(send, 'grp', swap)]
    ppermute x3, waiting for transfers between devices: 2.24 us -> 0.01 us  [on_device(): lax.ppermute(x, 'grp', [(i, (i + 2 * step) % 8) for i in range(8)])]
  transfers between devices with their start and end apart: 13 -> 13, of which waited for: 3 -> 6; matrix products, arithmetic and copies ran while one was open for 0% -> 0% of each run, Pallas kernels for 6% -> 6%
where the time goes in v3:
time: 126 us
  blocking collectives  41.2 us (33%)
  starting transfers between devices  33.2 us (26%)
  Pallas kernels  26.7 us (21%)
  waiting for transfers between devices  22.6 us (18%)
  between operations  1.58 us (1%)
    pallas_call x9, Pallas kernels, call(): pl.pallas_call(kernel, out_shape=shapes, in_specs=[SM] * len(scalars) + [...  26.7 us
    all_to_all x1, blocking collectives, on_device(): first = lax.all_to_all(msg, 'dev', split_axis=0, concat_axis=0, tiled=True)  23.7 us
    all_to_all x1, blocking collectives, on_device(): back = lax.all_to_all(sums, 'dev', split_axis=0, concat_axis=0, tiled=True)  17.5 us
    all_to_all x1, waiting for transfers between devices, on_device(): lax.all_to_all(terms, 'dev', split_axis=0, concat_axis=0, tiled=True)  10.4 us
    all_to_all x1, waiting for transfers between devices, on_device(): lax.all_to_all(answer, 'dev', split_axis=0, concat_axis=0, tiled=True)  9.65 us
    all_to_all x1, starting transfers between devices, on_device(): lax.all_to_all(answer, 'dev', split_axis=0, concat_axis=0, tiled=True)  7.47 us
    ppermute x1, starting transfers between devices, on_device(): chunk = lax.ppermute(chunk, 'grp', swap)  5.98 us
    ppermute x3, starting transfers between devices, on_device(): lax.ppermute(x, 'grp', [(i, (i + 2 * step) % 8) for i in range(8)])  4.9 us
  transfers between devices with their start and end apart: 13, of which 6 were waited for; matrix products, arithmetic and copies ran while one was open for 0% of the time, Pallas kernels for 6%

profile of v3, /device:TPU:1, one launch (start us, length us, event | category | flops | bytes accessed | tf_op | source)
XLA Modules:
  0.0 125.7 jit_solution(15122696938748678277)
XLA Ops:
  1.5 2.1 %ask.1 = bf16[32,48,128]{2,1,0:T(8,128)(2,1)} custom-call(s32[1]{0:T(128)S(6)} %copy.16.counts, bf16[2,128,512]{2,1,0:T(8,128)(2,1)} %feat.3, s32[2,26]{1,0:T(2,128)} %owner.1, s32[2,26]{1,0:T(2,128)} %slot.1), custom_call_target="tpu_custom_call" | custom-call | flops 2000000 | bytes 655776 | tf_op jit(solution)/shard_map/ask/pallas_call | solution.py:394
  3.6 23.7 %all_to_all.20.got = bf16[32,48,128]{2,1,0:T(8,128)(2,1)S(1)} all-to-all(bf16[32,48,128]{2,1,0:T(8,128)(2,1)} %ask.1), channel_id=1, replica_groups=mesh['grp'=8,'dev'=32] {'dev'}, dimensions={0} | all-to-all | bytes 786432 | tf_op jit(solution)/shard_map/all_to_all | solution.py:448
  27.3 1.7 %route.1 = bf16[32,32,128]{2,1,0:T(8,128)(2,1)} custom-call(bf16[32,48,128]{2,1,0:T(8,128)(2,1)S(1)} %all_to_all.20.got), custom_call_target="tpu_custom_call" | custom-call | flops 300000000 | bytes 655360 | tf_op jit(solution)/shard_map/route/pallas_call | solution.py:394
  29.0 7.5 %all-to-all-start.1 = ((bf16[32,32,128]{2,1,0:T(8,128)(2,1)}), bf16[32,32,128]{2,1,0:T(8,128)(2,1)S(1)}, u32[]{:S(2)}, u32[]{:S(2)}) async-start(bf16[32,32,128]{2,1,0:T(8,128)(2,1)} %route.1), calls=%async_computation.1 | async-start | bytes 524288 | tf_op jit(solution)/shard_map/all_to_all | solution.py:458
  36.4 9.6 %all-to-all-done.1.got = bf16[32,32,128]{2,1,0:T(8,128)(2,1)S(1)} async-done(((bf16[32,32,128]{2,1,0:T(8,128)(2,1)}), bf16[32,32,128]{2,1,0:T(8,128)(2,1)S(1)}, u32[]{:S(2)}, u32[]{:S(2)}) %all-to-all-start.1) | async-done | bytes 262176 | tf_op jit(solution)/shard_map/all_to_all | solution.py:458
  46.1 12.5 %forward.1 = (bf16[2,128,512]{2,1,0:T(8,128)(2,1)}, bf16[2,512,128]{2,1,0:T(8,128)(2,1)S(1)}, bf16[2048,128]{1,0:T(8,128)(2,1)S(1)}, bf16[2048,128]{1,0:T(8,128)(2,1)S(1)}) custom-call(s32[1]{0:T(128)S(6)} %copy.16.counts, s32[2]{0:T(128)S(1)} %copy-done.5, s32[2]{0:T(128)S(1)} %copy-done.6, s32[1]{0:T(128)} %bitcast.core, bf16[2,128,512]{2,1,0:T(8,128)(2,1)S(1)} %copy-done, ...), custom_call_target="tpu_custom_call" | custom-call | flops 2000000000 | bytes 3375104 | tf_op jit(solution)/shard_map/forward/pallas_call | solution.py:394
  58.7 3.6 %collective-permute-start = (bf16[2048,128]{1,0:T(8,128)(2,1)S(1)}, bf16[2048,128]{1,0:T(8,128)(2,1)S(1)}, u32[]{:S(2)}, u32[]{:S(2)}) collective-permute-start(bf16[2048,128]{1,0:T(8,128)(2,1)S(1)} %get-tuple-element.28), channel_id=1, source_target_pairs={{0,32},{32,0},{64,96},{96,64},{128,160},{160,128},{192,224},{224,1... | collective-permute-start | bytes 1572872 | tf_op jit(solution)/shard_map/ppermute | solution.py:496
  62.3 1.5 %collective-permute-done.other = bf16[2048,128]{1,0:T(8,128)(2,1)S(1)} collective-permute-done((bf16[2048,128]{1,0:T(8,128)(2,1)S(1)}, bf16[2048,128]{1,0:T(8,128)(2,1)S(1)}, u32[]{:S(2)}, u32[]{:S(2)}) %collective-permute-start) | collective-permute-done | bytes 524320 | tf_op jit(solution)/shard_map/ppermute | solution.py:496
  63.8 0.1 pair.1
  63.9 1.3 %collective-permute-start.1 = (bf16[512,128]{1,0:T(8,128)(2,1)S(1)}, bf16[512,128]{1,0:T(8,128)(2,1)S(1)}, u32[]{:S(2)}, u32[]{:S(2)}) collective-permute-start(bf16[512,128]{1,0:T(8,128)(2,1)S(1)} %get-tuple-element.33), channel_id=1, source_target_pairs={{0,64},{32,96},{64,128},{96,160},{128,192},{160,224},{192,0},{224,... | collective-permute-start | bytes 393224 | tf_op jit(solution)/shard_map/ppermute | solution.py:505
  65.2 2.5 %collective-permute-start.2 = (bf16[512,128]{1,0:T(8,128)(2,1)S(1)}, bf16[512,128]{1,0:T(8,128)(2,1)S(1)}, u32[]{:S(2)}, u32[]{:S(2)}) collective-permute-start(bf16[512,128]{1,0:T(8,128)(2,1)S(1)} %get-tuple-element.34), channel_id=1, source_target_pairs={{0,128},{32,160},{64,192},{96,224},{128,0},{160,32},{192,64},{224,... | collective-permute-start | bytes 393224 | tf_op jit(solution)/shard_map/ppermute | solution.py:505
  67.7 1.1 collective-permute-start.3
  68.8 5.9 %backward.1 = (f32[2,512,128]{2,1,0:T(8,128)S(1)}, bf16[32,32,128]{2,1,0:T(8,128)(2,1)S(1)}) custom-call(bf16[2,512,128]{2,1,0:T(8,128)(2,1)S(1)} %get-tuple-element.30.grad, bf16[27,128,128]{2,1,0:T(8,128)(2,1)S(1)} %copy-done.2), custom_call_target="tpu_custom_call" | custom-call | flops 4000000000 | bytes 1933312 | tf_op jit(solution)/shard_map/backward/pallas_call | solution.py:394
  74.7 0.8 join.1
  75.5 4.3 %all-to-all-start.2 = ((bf16[32,48,128]{2,1,0:T(8,128)(2,1)}), bf16[32,48,128]{2,1,0:T(8,128)(2,1)S(1)}, u32[]{:S(2)}, u32[]{:S(2)}) async-start(bf16[32,48,128]{2,1,0:T(8,128)(2,1)} %join.1), calls=%async_computation.2 | async-start | bytes 786432 | tf_op jit(solution)/shard_map/all_to_all | solution.py:526
  79.8 0.2 copy.15
  80.1 0.1 broadcast_in_dim.7
  80.2 10.4 %all-to-all-done.2.got = bf16[32,48,128]{2,1,0:T(8,128)(2,1)S(1)} async-done(((bf16[32,48,128]{2,1,0:T(8,128)(2,1)}), bf16[32,48,128]{2,1,0:T(8,128)(2,1)S(1)}, u32[]{:S(2)}, u32[]{:S(2)}) %all-to-all-start.2) | async-done | bytes 393248 | tf_op jit(solution)/shard_map/all_to_all | solution.py:526
  90.5 0.8 merge.1
  91.3 17.5 %all_to_all.21.got = bf16[32,48,128]{2,1,0:T(8,128)(2,1)S(1)} all-to-all(bf16[32,48,128]{2,1,0:T(8,128)(2,1)S(1)} %merge.1), channel_id=1, replica_groups=mesh['grp'=8,'dev'=32] {'dev'}, dimensions={0} | all-to-all | bytes 786432 | tf_op jit(solution)/shard_map/all_to_all | solution.py:536
  108.9 0.4 collective-permute-start.6
  109.2 2.5 %collective-permute-start.5 = (bf16[512,128]{1,0:T(8,128)(2,1)S(1)}, bf16[512,128]{1,0:T(8,128)(2,1)S(1)}, u32[]{:S(2)}, u32[]{:S(2)}) collective-permute-start(bf16[512,128]{1,0:T(8,128)(2,1)S(1)} %bitcast.7), channel_id=1, source_target_pairs={{0,128},{32,160},{64,192},{96,224},{128,0},{160,32},{192,64},{224,... | collective-permute-start | bytes 393224 | tf_op jit(solution)/shard_map/ppermute | solution.py:539
  111.7 0.2 collective-permute-start.4
  111.9 6.0 %collective-permute-start.7 = (bf16[512,128]{1,0:T(8,128)(2,1)S(1)}, bf16[512,128]{1,0:T(8,128)(2,1)S(1)}, u32[]{:S(2)}, u32[]{:S(2)}) collective-permute-start(bf16[512,128]{1,0:T(8,128)(2,1)S(1)} %bitcast.9), channel_id=1, source_target_pairs={{0,32},{32,0},{64,96},{96,64},{128,160},{160,128},{192,224},{224,1... | collective-permute-start | bytes 393224 | tf_op jit(solution)/shard_map/ppermute | solution.py:551
  117.9 1.3 %finish.1 = bf16[2,128,512]{2,1,0:T(8,128)(2,1)} custom-call(s32[1]{0:T(128)S(6)} %copy.16.counts, bf16[32,48,128]{2,1,0:T(8,128)(2,1)S(1)} %all_to_all.21.got, f32[2,512,128]{2,1,0:T(8,128)S(1)} %get-tuple-element.36.own, bf16[2,128,512]{2,1,0:T(8,128)(2,1)S(1)} %copy-done.1), custom_call_target="tpu_custom_call" | custom-call | flops 300000000 | bytes 1441792 | tf_op jit(solution)/shard_map/finish/pallas_call | solution.py:394
  119.2 3.5 %collective-permute-start.8 = (bf16[512,128]{1,0:T(8,128)(2,1)S(1)}, bf16[512,128]{1,0:T(8,128)(2,1)S(1)}, u32[]{:S(2)}, u32[]{:S(2)}) collective-permute-start(bf16[512,128]{1,0:T(8,128)(2,1)S(1)} %collective-permute-done.4.refs_1_), channel_id=1, source_target_pairs={{0,32},{32,0},{64,96},{96,64},{128,160},{160,128},{192,224},{224,1... | collective-permute-start | bytes 393224 | tf_op jit(solution)/shard_map/ppermute | solution.py:553
  122.6 0.0 collective-permute-start.9
  122.6 0.5 collective-permute-start.10
  123.2 0.5 collective-permute-done.8.refs_5_
  123.6 0.4 collective-permute-done.9.refs_6_
  124.0 0.2 collective-permute-done.10.refs_7_
  124.2 1.5 %assemble.1 = (f32[27,128,128]{2,1,0:T(8,128)}, f32[128,256]{1,0:T(8,128)}, f32[256,128]{1,0:T(8,128)}) custom-call(s32[1]{0:T(128)} %bitcast.core, s32[1]{0:T(128)} %bitcast.2.line, bf16[512,128]{1,0:T(8,128)(2,1)S(1)} %bitcast.10, bf16[512,128]{1,0:T(8,128)(2,1)S(1)} %collective-permute-done.4.refs_1_, ...), custom_call_target="tpu_custom_call" | custom-call | flops 1000000 | bytes 3080192 | tf_op jit(solution)/shard_map/assemble/pallas_call | solution.py:394
  (24 shorter events, 0.1 us)
Async XLA Ops:
  0.6 45.4 %copy-start = (bf16[2,128,512]{2,1,0:T(8,128)(2,1)S(1)}, bf16[2,128,512]{2,1,0:T(8,128)(2,1)}, u32[]{:S(2)}) copy-start(bf16[2,128,512]{2,1,0:T(8,128)(2,1)} %feat.3) | copy-start | bytes 786436
  0.6 45.4 %copy-start.1 = (bf16[2,128,512]{2,1,0:T(8,128)(2,1)S(1)}, bf16[2,128,512]{2,1,0:T(8,128)(2,1)}, u32[]{:S(2)}) copy-start(bf16[2,128,512]{2,1,0:T(8,128)(2,1)} %gout.3) | copy-start | bytes 786436
  0.7 45.4 %copy-start.2 = (bf16[27,128,128]{2,1,0:T(8,128)(2,1)S(1)}, bf16[27,128,128]{2,1,0:T(8,128)(2,1)}, u32[]{:S(2)}) copy-start(bf16[27,128,128]{2,1,0:T(8,128)(2,1)} %weight.1) | copy-start | bytes 2654212
  0.7 45.4 %copy-start.6 = (s32[2]{0:T(128)S(1)}, s32[2]{0:T(128)}, u32[]{:S(2)}) copy-start(s32[2]{0:T(128)} %child.1) | copy-start | bytes 28
  0.7 45.4 %copy-start.5 = (s32[2]{0:T(128)S(1)}, s32[2]{0:T(128)}, u32[]{:S(2)}) copy-start(s32[2]{0:T(128)} %parent.1) | copy-start | bytes 28
  0.7 45.4 %copy-start.4 = (bf16[256,128]{1,0:T(8,128)(2,1)S(1)}, bf16[256,128]{1,0:T(8,128)(2,1)}, u32[]{:S(2)}) copy-start(bf16[256,128]{1,0:T(8,128)(2,1)} %down.1) | copy-start | bytes 196612
  0.7 45.4 %copy-start.3 = (bf16[128,256]{1,0:T(8,128)(2,1)S(1)}, bf16[128,256]{1,0:T(8,128)(2,1)}, u32[]{:S(2)}) copy-start(bf16[128,256]{1,0:T(8,128)(2,1)} %up.1) | copy-start | bytes 196612
  29.0 17.1 %all-to-all-start.1 = ((bf16[32,32,128]{2,1,0:T(8,128)(2,1)}), bf16[32,32,128]{2,1,0:T(8,128)(2,1)S(1)}, u32[]{:S(2)}, u32[]{:S(2)}) async-start(bf16[32,32,128]{2,1,0:T(8,128)(2,1)} %route.1), calls=%async_computation.1 | async-start | bytes 524288 | tf_op jit(solution)/shard_map/all_to_all | solution.py:458
  58.7 5.1 %collective-permute-start = (bf16[2048,128]{1,0:T(8,128)(2,1)S(1)}, bf16[2048,128]{1,0:T(8,128)(2,1)S(1)}, u32[]{:S(2)}, u32[]{:S(2)}) collective-permute-start(bf16[2048,128]{1,0:T(8,128)(2,1)S(1)} %get-tuple-element.28), channel_id=1, source_target_pairs={{0,32},{32,0},{64,96},{96,64},{128,160},{160,128},{192,224},{224,1... | collective-permute-start | bytes 1572872 | tf_op jit(solution)/shard_map/ppermute | solution.py:496
  63.9 10.8 %collective-permute-start.1 = (bf16[512,128]{1,0:T(8,128)(2,1)S(1)}, bf16[512,128]{1,0:T(8,128)(2,1)S(1)}, u32[]{:S(2)}, u32[]{:S(2)}) collective-permute-start(bf16[512,128]{1,0:T(8,128)(2,1)S(1)} %get-tuple-element.33), channel_id=1, source_target_pairs={{0,64},{32,96},{64,128},{96,160},{128,192},{160,224},{192,0},{224,... | collective-permute-start | bytes 393224 | tf_op jit(solution)/shard_map/ppermute | solution.py:505
  65.2 9.5 %collective-permute-start.2 = (bf16[512,128]{1,0:T(8,128)(2,1)S(1)}, bf16[512,128]{1,0:T(8,128)(2,1)S(1)}, u32[]{:S(2)}, u32[]{:S(2)}) collective-permute-start(bf16[512,128]{1,0:T(8,128)(2,1)S(1)} %get-tuple-element.34), channel_id=1, source_target_pairs={{0,128},{32,160},{64,192},{96,224},{128,0},{160,32},{192,64},{224,... | collective-permute-start | bytes 393224 | tf_op jit(solution)/shard_map/ppermute | solution.py:505
  67.7 7.0 %collective-permute-start.3 = (bf16[512,128]{1,0:T(8,128)(2,1)S(1)}, bf16[512,128]{1,0:T(8,128)(2,1)S(1)}, u32[]{:S(2)}, u32[]{:S(2)}) collective-permute-start(bf16[512,128]{1,0:T(8,128)(2,1)S(1)} %get-tuple-element.35), channel_id=1, source_target_pairs={{0,192},{32,224},{64,0},{96,32},{128,64},{160,96},{192,128},{224,1... | collective-permute-start | bytes 393224 | tf_op jit(solution)/shard_map/ppermute | solution.py:505
  75.5 15.0 %all-to-all-start.2 = ((bf16[32,48,128]{2,1,0:T(8,128)(2,1)}), bf16[32,48,128]{2,1,0:T(8,128)(2,1)S(1)}, u32[]{:S(2)}, u32[]{:S(2)}) async-start(bf16[32,48,128]{2,1,0:T(8,128)(2,1)} %join.1), calls=%async_computation.2 | async-start | bytes 786432 | tf_op jit(solution)/shard_map/all_to_all | solution.py:526
  108.9 10.3 %collective-permute-start.6 = (bf16[512,128]{1,0:T(8,128)(2,1)S(1)}, bf16[512,128]{1,0:T(8,128)(2,1)S(1)}, u32[]{:S(2)}, u32[]{:S(2)}) collective-permute-start(bf16[512,128]{1,0:T(8,128)(2,1)S(1)} %bitcast.6), channel_id=1, source_target_pairs={{0,64},{32,96},{64,128},{96,160},{128,192},{160,224},{192,0},{224,... | collective-permute-start | bytes 393224 | tf_op jit(solution)/shard_map/ppermute | solution.py:539
  109.2 9.9 %collective-permute-start.5 = (bf16[512,128]{1,0:T(8,128)(2,1)S(1)}, bf16[512,128]{1,0:T(8,128)(2,1)S(1)}, u32[]{:S(2)}, u32[]{:S(2)}) collective-permute-start(bf16[512,128]{1,0:T(8,128)(2,1)S(1)} %bitcast.7), channel_id=1, source_target_pairs={{0,128},{32,160},{64,192},{96,224},{128,0},{160,32},{192,64},{224,... | collective-permute-start | bytes 393224 | tf_op jit(solution)/shard_map/ppermute | solution.py:539
  111.7 7.5 %collective-permute-start.4 = (bf16[512,128]{1,0:T(8,128)(2,1)S(1)}, bf16[512,128]{1,0:T(8,128)(2,1)S(1)}, u32[]{:S(2)}, u32[]{:S(2)}) collective-permute-start(bf16[512,128]{1,0:T(8,128)(2,1)S(1)} %bitcast.8), channel_id=1, source_target_pairs={{0,192},{32,224},{64,0},{96,32},{128,64},{160,96},{192,128},{224,1... | collective-permute-start | bytes 393224 | tf_op jit(solution)/shard_map/ppermute | solution.py:539
  111.9 11.2 %collective-permute-start.7 = (bf16[512,128]{1,0:T(8,128)(2,1)S(1)}, bf16[512,128]{1,0:T(8,128)(2,1)S(1)}, u32[]{:S(2)}, u32[]{:S(2)}) collective-permute-start(bf16[512,128]{1,0:T(8,128)(2,1)S(1)} %bitcast.9), channel_id=1, source_target_pairs={{0,32},{32,0},{64,96},{96,64},{128,160},{160,128},{192,224},{224,1... | collective-permute-start | bytes 393224 | tf_op jit(solution)/shard_map/ppermute | solution.py:551
  119.2 4.4 %collective-permute-start.8 = (bf16[512,128]{1,0:T(8,128)(2,1)S(1)}, bf16[512,128]{1,0:T(8,128)(2,1)S(1)}, u32[]{:S(2)}, u32[]{:S(2)}) collective-permute-start(bf16[512,128]{1,0:T(8,128)(2,1)S(1)} %collective-permute-done.4.refs_1_), channel_id=1, source_target_pairs={{0,32},{32,0},{64,96},{96,64},{128,160},{160,128},{192,224},{224,1... | collective-permute-start | bytes 393224 | tf_op jit(solution)/shard_map/ppermute | solution.py:553
  122.6 1.3 %collective-permute-start.9 = (bf16[512,128]{1,0:T(8,128)(2,1)S(1)}, bf16[512,128]{1,0:T(8,128)(2,1)S(1)}, u32[]{:S(2)}, u32[]{:S(2)}) collective-permute-start(bf16[512,128]{1,0:T(8,128)(2,1)S(1)} %collective-permute-done.5.refs_2_), channel_id=1, source_target_pairs={{0,32},{32,0},{64,96},{96,64},{128,160},{160,128},{192,224},{224,1... | collective-permute-start | bytes 393224 | tf_op jit(solution)/shard_map/ppermute | solution.py:553
  122.6 1.5 %collective-permute-start.10 = (bf16[512,128]{1,0:T(8,128)(2,1)S(1)}, bf16[512,128]{1,0:T(8,128)(2,1)S(1)}, u32[]{:S(2)}, u32[]{:S(2)}) collective-permute-start(bf16[512,128]{1,0:T(8,128)(2,1)S(1)} %collective-permute-done.6.refs_3_), channel_id=1, source_target_pairs={{0,32},{32,0},{64,96},{96,64},{128,160},{160,128},{192,224},{224,1... | collective-permute-start | bytes 393224 | tf_op jit(solution)/shard_map/ppermute | solution.py:553

commit v4 on v3

--- a/solution.py
+++ b/solution.py
@@ -127,35 +127,35 @@
     lanes = lax.broadcasted_iota(jnp.int32, (128, 128), 0)
     brick = lax.broadcasted_iota(jnp.int32, (16, 128), 1) >> 4
     table = got[:, 32:48, :].reshape(512, 128)
-    data = got[:, 0:32, :].reshape(1024, 128)
     for s in range(2):
         spread = (lanes == s).astype(F32).astype(BF)
         asked = nn(table, spread).astype(BF).reshape(32, 16, 128)
         for n in range(8):
             here = (brick + 8 * n).astype(F32).astype(BF)
-            hot[:, n * 128 : n * 128 + 128] = jnp.where(asked == here[None], same, zero).reshape(
-                512, 128
-            )
-        picked = nn(hot[...], data).astype(BF)
-        out[:, 16 * s : 16 * s + 16, :] = picked.reshape(32, 16, 128)
+            picked = jnp.where(asked == here[None], same, zero)
+            hot[s * 512 : s * 512 + 512, n * 128 : n * 128 + 128] = picked.reshape(512, 128)
+    answer = nn(hot[...], got[:, 0:32, :].reshape(1024, 128)).astype(BF)
+    for s in range(2):
+        out[:, 16 * s : 16 * s + 16, :] = answer[s * 512 : s * 512 + 512].reshape(32, 16, 128)
 
 
 def forward_kernel(
     counts, parent, child, core, feat, got, gout, weight, up, down,
-    out, grad, keep, send,
-    rows, pc, mine, s0, s1, s2, cols, grad_t, acts, slopes, pooled, grad_pooled,
+    out, grad, wsum, send,
+    rows_all, pc_all, mine_all, s0_all, s1_all, s2_all, cols, grad_t, pooled, grad_pooled,
+    out_v, sem,
 ):
     eye = identity()
-    pooled[...] = jnp.zeros((16, 128), F32)
-    grad_pooled[...] = jnp.zeros((16, 128), F32)
-
-    def brick(s, _):
+    acts, slopes = [], []
+    for s in range(2):
+        rows, pc, mine, s0, s1, s2 = (
+            x.at[s] for x in (rows_all, pc_all, mine_all, s0_all, s1_all, s2_all)
+        )
         live = (counts[0] > s).astype(F32)
         pool = pool_rows(s)
         mine[...] = (feat[s].astype(F32) * live).T
-        grad_pooled[...] += nt(pool, gout[s]) * live
-        share = got[:, pl.ds(pl.multiple_of(s * 16, 16), 16), :]
-        rows[...] = share.reshape(512, 128).astype(F32)
+        grad_pooled[s] = nt(pool, gout[s]) * live
+        rows[...] = got[:, 16 * s : 16 * s + 16, :].reshape(512, 128).astype(F32)
         to_pieces(rows, pc)
         for a in range(8):
             s1[pl.ds(8 + ((a + 1) * 10 + 1) * 8, 64), :] = mine[a * 64 : a * 64 + 64, :]
@@ -179,31 +179,24 @@
                 ref[pl.ds((10 + x) * 8 + lane, 8, stride=80), :] = pc[pl.ds(PIECE[0, a, c], 8), :]
                 for b, y in ((-1, 0), (1, 9)):
                     ref[pl.ds((x * 10 + y) * 8 + lane, 1), :] = pc[pl.ds(PIECE[a, b, c], 1), :]
-
-        def plane(a, _):
+        for a in range(10):
             for b in range(3):
                 for c, ref in enumerate((s0, s1, s2)):
-                    start = pl.multiple_of((a * 10 + b) * 8 + (8 if c == 1 else 0), 8)
-                    cols[s, pl.ds(pl.multiple_of(a * 64, 64), 64), pl.ds((3 * b + c) * 128, 128)] = ref[
+                    start = (a * 10 + b) * 8 + (8 if c == 1 else 0)
+                    at = 640 * s + 64 * a
+                    cols[at : at + 64, (3 * b + c) * 128 : (3 * b + c) * 128 + 128] = ref[
                         pl.ds(start, 64), :
                     ].astype(BF)
-            return 0
-
-        lax.fori_loop(0, 10, plane, 0)
-        pre = nn(cols[s, 0:512, :], weight[0])
-        pre = pre + nn(cols[s, 64:576, :], weight[1])
-        pre = pre + nn(cols[s, 128:640, :], weight[2])
+        taps = nn(cols[640 * s : 640 * s + 640, :], weight[...])
+        pre = taps[0:512, 0:128] + taps[64:576, 128:256] + taps[128:640, 256:384]
         pre = pre.T
         gate = 1.0 / (1.0 + jnp.exp(-pre))
         active = pre * gate
-        acts[s] = active
-        slopes[s] = gate * (1.0 + pre * (1.0 - gate))
+        acts.append(active)
+        slopes.append(gate * (1.0 + pre * (1.0 - gate)))
         high = active.astype(BF)
         low = (active - high.astype(F32)).astype(BF)
-        pooled[...] += nt(pool, high) + nt(pool, low)
-        return 0
-
-    lax.fori_loop(0, 2, brick, 0)
+        pooled[s] = nt(pool, high) + nt(pool, low)
     second = lax.broadcasted_iota(jnp.int32, (16, 1), 0) >= 8
     valid = [
         (
@@ -212,8 +205,8 @@
         for s in range(2)
     ]
     valid = jnp.where(second, valid[1], valid[0])
-    coarse_in = (pooled[...] * (1.0 / 64.0) * valid).astype(BF)
-    grad_out = (grad_pooled[...] * valid).astype(BF)
+    coarse_in = ((pooled[0] + pooled[1]) * (1.0 / 64.0) * valid).astype(BF)
+    grad_out = ((grad_pooled[0] + grad_pooled[1]) * valid).astype(BF)
     coarse_pre = nn(coarse_in, up[...])
     gate = 1.0 / (1.0 + jnp.exp(-coarse_pre))
     coarse_mid = (coarse_pre * gate).astype(BF)
@@ -223,30 +216,19 @@
     grad_cin = nt(grad_pre, up[...]).astype(BF)
     lift = nt(eye, coarse_out).astype(BF)
     back = nt(eye, grad_cin).astype(BF)
-
-    def blend(s, _):
+    for s in range(2):
         live = (counts[0] > s).astype(F32)
         pool = pool_rows(s)
-        out[s] = (feat[s].astype(F32) * live + acts[s] + nn(lift, pool)).astype(BF)
+        out_v[s] = (feat[s].astype(F32) * live + acts[s] + nn(lift, pool)).astype(BF)
         grad_in = gout[s].astype(F32) * live + nn(back, pool) * (1.0 / 64.0)
         grad_pre_conv = grad_in * slopes[s]
         grad_t[s] = grad_pre_conv.astype(BF)
         grad[s] = grad_pre_conv.T.astype(BF)
-        return 0
-
-    lax.fori_loop(0, 2, blend, 0)
+    copy = pltpu.make_async_copy(out_v, out, sem.at[0])
+    copy.start()
 
     def put(block, value):
-        half, at = divmod(block, 16)
-        value = value.astype(BF)
-
-        @pl.when(core[0] == half)
-        def _():
-            keep[pl.ds(at * 128, 128), :] = value
-
-        @pl.when(core[0] != half)
-        def _():
-            send[pl.ds(at * 128, 128), :] = value
+        wsum[pl.ds(block * 128, 128), :] = value.astype(BF)
 
     grad_up = nn(nt(eye, coarse_in).astype(BF), grad_pre)
     for h in range(2):
@@ -255,41 +237,42 @@
         put(29 + h, nn(middle, grad_out))
     put(31, jnp.zeros((128, 128), F32))
     for a in range(3):
-        total = nn(grad_t[0], cols[0, a * 64 : a * 64 + 512, :])
-        total = total + nn(grad_t[1], cols[1, a * 64 : a * 64 + 512, :])
+        total = nn(grad_t[0], cols[64 * a : 64 * a + 512, :])
+        total = total + nn(grad_t[1], cols[64 * a + 640 : 64 * a + 1152, :])
         total = total.astype(BF)
         for n in range(9):
             put(9 * a + n, nt(eye, total[:, n * 128 : n * 128 + 128]))
-
-
-def pair_kernel(line, keep, other, own, one, two, three):
+    send[...] = wsum[pl.ds(pl.multiple_of((1 - core[0]) * 2048, 2048), 2048), :]
+    copy.wait()
+
+
+def pair_kernel(core, line, wsum, other, own, one, two, three):
     for step, ref in enumerate((own, one, two, three)):
-        at = pl.ds(pl.multiple_of(((line[0] + step) & 3) * 512, 512), 512)
-        ref[...] = (keep[at, :].astype(F32) + other[at, :].astype(F32)).astype(ref.dtype)
-
-
-def backward_kernel(grad, weight, own, msg, planes, acc, pc, rows):
-    planes[0:128, :] = jnp.zeros((128, 128), BF)
-    planes[640:768, :] = jnp.zeros((128, 128), BF)
+        at = pl.multiple_of(((line[0] + step) & 3) * 512, 512)
+        kept = wsum[pl.ds(pl.multiple_of(core[0] * 2048 + at, 512), 512), :].astype(F32)
+        ref[...] = (kept + other[pl.ds(at, 512), :].astype(F32)).astype(ref.dtype)
+
+
+def backward_kernel(grad, weight, own, msg, lhs, acc_all, pc_all, rows_all):
+    zero = jnp.zeros((64, 128), BF)
+    for a in range(3):
+        for n in [*range(a), *range(8 + a, 10)]:
+            for s in range(2):
+                lhs[s, n * 64 : n * 64 + 64, a * 128 : a * 128 + 128] = zero
     low = (lax.broadcasted_iota(jnp.int32, (64, 1), 0) & 7) != 0
     high = (lax.broadcasted_iota(jnp.int32, (64, 1), 0) & 7) != 7
 
-    def brick(s, _):
-        planes[128:640, :] = grad[s]
+    for s in range(2):
+        acc, pc, rows = acc_all.at[s], pc_all.at[s], rows_all.at[s]
+        for a in range(3):
+            lhs[s, a * 64 : a * 64 + 512, a * 128 : a * 128 + 128] = grad[s]
         acc[...] = jnp.zeros_like(acc)
-
-        def tap(n, _):
-            c = lax.rem(n, 3)
-            b = lax.div(n, 3)
-            part = nt(planes[128:768, :], weight[n])
-            part = part + nt(planes[64:704, :], weight[n + 9])
-            part = part + nt(planes[0:640, :], weight[n + 18])
-            for a in range(10):
-                at = pl.ds(pl.multiple_of(8 + (a * 10 + b) * 8, 8), 64)
-                acc[c, at, :] = acc[c, at, :] + part[a * 64 : a * 64 + 64]
-            return 0
-
-        lax.fori_loop(0, 9, tap, 0)
+        for b in range(3):
+            part = nt(lhs[s], weight[b * 384 : b * 384 + 384, :])
+            for c in range(3):
+                for a in range(10):
+                    at = pl.ds(8 + (a * 10 + b) * 8, 64)
+                    acc[c, at, :] += part[a * 64 : a * 64 + 64, c * 128 : c * 128 + 128]
 
         def middle(row, size):
             at = 8 + row
@@ -316,11 +299,7 @@
                 for b, y in ((-1, 0), (1, 9)):
                     pc[pl.ds(PIECE[a, b, c], 1), :] = ref[pl.ds((x * 10 + y) * 8 + lane, 1), :]
         to_shares(pc, rows)
-        at = pl.ds(pl.multiple_of(s * 16, 16), 16)
-        msg[:, at, :] = rows[...].astype(BF).reshape(32, 16, 128)
-        return 0
-
-    lax.fori_loop(0, 2, brick, 0)
+        msg[:, 16 * s : 16 * s + 16, :] = rows[...].astype(BF).reshape(32, 16, 128)
 
 
 def join_kernel(terms, own, away1, away2, away3, msg):
@@ -388,14 +367,14 @@
 SM = pl.BlockSpec(memory_space=pltpu.SMEM)
 
 
-def call(kernel, shapes, scalars, arrays, scratch=(), flops=1e6, space=VM, limit=20, name=None):
+def call(kernel, shapes, scalars, arrays, scratch=(), flops=1e6, space=VM, limit=24, first=VM, name=None):
     moved = sum(x.size * x.dtype.itemsize for x in arrays)
     moved += sum(int(np.prod(s.shape)) * s.dtype.itemsize for s in shapes)
     return pl.pallas_call(
         kernel,
         out_shape=shapes,
         in_specs=[SM] * len(scalars) + [space] * len(arrays),
-        out_specs=[VM] * len(shapes),
+        out_specs=[first] + [VM] * (len(shapes) - 1),
         scratch_shapes=list(scratch),
         compiler_params=pltpu.CompilerParams(vmem_limit_bytes=limit * 2**20),
         cost_estimate=pl.CostEstimate(
@@ -451,19 +430,21 @@
         [shape((32, 32, 128), BF)],
         [],
         [first],
-        [pltpu.VMEM((512, 1024), BF)],
+        [pltpu.VMEM((1024, 1024), BF)],
         flops=3e8,
         name="route",
     )
     halo = lax.all_to_all(answer, "dev", split_axis=0, concat_axis=0, tiled=True)
     table = first[:, 32:48, 0:2].transpose(0, 2, 1).reshape(1, 1024)
     table = jnp.broadcast_to(table, (16, 1024))
-    output, grad_pre, keep, send = call(
+    taps = conv_weight.reshape(3, 1152, 128)
+    taps = jnp.concatenate([taps[0], taps[1], taps[2]], axis=1)
+    output, grad_pre, wsum, send = call(
         forward_kernel,
         [
             shape((2, 128, 512), BF),
             shape((2, 512, 128), BF),
-            shape((2048, 128), BF),
+            shape((4096, 128), BF),
             shape((2048, 128), BF),
         ],
         [counts, parent, child_slot, core],
@@ -471,24 +452,25 @@
             features,
             halo,
             grad_out,
-            conv_weight.reshape(3, 1152, 128),
+            taps,
             coarse_up,
             coarse_down,
         ],
         [
-            pltpu.VMEM((512, 128), F32),
-            pltpu.VMEM((512, 128), F32),
-            pltpu.VMEM((512, 128), F32),
-            pltpu.VMEM((800, 128), F32),
-            pltpu.VMEM((816, 128), F32),
-            pltpu.VMEM((800, 128), F32),
-            pltpu.VMEM((2, 640, 1152), BF),
+            pltpu.VMEM((2, 512, 128), F32),
+            pltpu.VMEM((2, 512, 128), F32),
+            pltpu.VMEM((2, 512, 128), F32),
+            pltpu.VMEM((2, 800, 128), F32),
+            pltpu.VMEM((2, 816, 128), F32),
+            pltpu.VMEM((2, 800, 128), F32),
+            pltpu.VMEM((1280, 1152), BF),
             pltpu.VMEM((2, 128, 512), BF),
-            pltpu.VMEM((2, 128, 512), F32),
-            pltpu.VMEM((2, 128, 512), F32),
-            pltpu.VMEM((16, 128), F32),
-            pltpu.VMEM((16, 128), F32),
+            pltpu.VMEM((2, 16, 128), F32),
+            pltpu.VMEM((2, 16, 128), F32),
+            pltpu.VMEM((2, 128, 512), BF),
+            pltpu.SemaphoreType.DMA((1,)),
         ],
+        first=pl.BlockSpec(memory_space=pltpu.HBM),
         flops=2e9,
         name="forward",
     )
@@ -497,8 +479,8 @@
     own_sum, *away = call(
         pair_kernel,
         [shape((512, 128), F32)] + [shape((512, 128), BF)] * 3,
-        [line],
-        [keep, other],
+        [core, line],
+        [wsum, other],
         name="pair",
     )
     away = [
@@ -510,18 +492,22 @@
         backward_kernel,
         [shape((2, 512, 128), F32), shape((32, 32, 128), BF)],
         [],
-        [grad_pre, conv_weight],
+        [grad_pre, taps],
         [
-            pltpu.VMEM((768, 128), BF),
-            pltpu.VMEM((3, 816, 128), F32),
-            pltpu.VMEM((512, 128), F32),
-            pltpu.VMEM((512, 128), F32),
+            pltpu.VMEM((2, 640, 384), BF),
+            pltpu.VMEM((2, 3, 816, 128), F32),
+            pltpu.VMEM((2, 512, 128), F32),
+            pltpu.VMEM((2, 512, 128), F32),
         ],
         flops=4e9,
         name="backward",
     )
     (terms,) = call(
-        join_kernel, [shape((32, 48, 128), BF)], [], [terms, own_sum, *away], name="join"
+        join_kernel,
+        [shape((32, 48, 128), BF)],
+        [],
+        [terms, own_sum, *away],
+        name="join",
     )
     terms = lax.all_to_all(terms, "dev", split_axis=0, concat_axis=0, tiled=True)
     (sums,) = call(

time: 126 us -> 120 us (0.952)
  blocking collectives: 41.2 us -> 17.5 us
  waiting for transfers between devices: 22.6 us -> 36.7 us
  starting transfers between devices: 33.2 us -> 46.1 us
  Pallas kernels: 26.7 us -> 17.2 us
    all_to_all x1 -> x0, blocking collectives: 23.7 us -> none  [on_device(): first = lax.all_to_all(msg, 'dev', split_axis=0, concat_axis=0, tiled=True)]
    all_to_all x0 -> x1, starting transfers between devices: none -> 12 us  [on_device(): first = lax.all_to_all(msg, 'dev', split_axis=0, concat_axis=0, tiled=True)]
    all_to_all x0 -> x1, waiting for transfers between devices: none -> 11.6 us  [on_device(): first = lax.all_to_all(msg, 'dev', split_axis=0, concat_axis=0, tiled=True)]
    pallas_call x9, Pallas kernels: 26.7 us -> 17.2 us  [call(): pl.pallas_call(kernel, out_shape=shapes, in_specs=[SM] * len(scalars) + [...]
    ppermute x3, waiting for transfers between devices: 0.01 us -> 2.6 us  [on_device(): lax.ppermute(x, 'grp', [(i, (i + 2 * step) % 8) for i in range(8)])]
  transfers between devices with their start and end apart: 13 -> 14, of which waited for: 6 -> 8; matrix products, arithmetic and copies ran while one was open for 0% -> 0% of each run, Pallas kernels for 6% -> 3%
where the time goes in v4:
time: 120 us
  starting transfers between devices  46.1 us (38%)
  waiting for transfers between devices  36.7 us (31%)
  blocking collectives  17.5 us (15%)
  Pallas kernels  17.2 us (14%)
  between operations  1.57 us (1%)
    all_to_all x1, blocking collectives, on_device(): back = lax.all_to_all(sums, 'dev', split_axis=0, concat_axis=0, tiled=True)  17.5 us
    pallas_call x9, Pallas kernels, call(): pl.pallas_call(kernel, out_shape=shapes, in_specs=[SM] * len(scalars) + [...  17.2 us
    all_to_all x1, starting transfers between devices, on_device(): first = lax.all_to_all(msg, 'dev', split_axis=0, concat_axis=0, tiled=True)  12 us
    all_to_all x1, waiting for transfers between devices, on_device(): first = lax.all_to_all(msg, 'dev', split_axis=0, concat_axis=0, tiled=True)  11.6 us
    all_to_all x1, waiting for transfers between devices, on_device(): lax.all_to_all(terms, 'dev', split_axis=0, concat_axis=0, tiled=True)  10.3 us
    all_to_all x1, waiting for transfers between devices, on_device(): lax.all_to_all(answer, 'dev', split_axis=0, concat_axis=0, tiled=True)  9.35 us
    all_to_all x1, starting transfers between devices, on_device(): lax.all_to_all(answer, 'dev', split_axis=0, concat_axis=0, tiled=True)  7.46 us
    ppermute x1, starting transfers between devices, on_device(): chunk = lax.ppermute(chunk, 'grp', swap)  6.09 us
  transfers between devices with their start and end apart: 14, of which 8 were waited for; matrix products, arithmetic and copies ran while one was open for 0% of the time, Pallas kernels for 3%

profile of v4, /device:TPU:1, one launch (start us, length us, event | category | flops | bytes accessed | tf_op | source)
XLA Modules:
  0.0 119.7 jit_solution(8663695494226960086)
XLA Ops:
  1.4 2.1 %ask.1 = bf16[32,48,128]{2,1,0:T(8,128)(2,1)} custom-call(s32[1]{0:T(128)S(6)} %copy.16.counts, bf16[2,128,512]{2,1,0:T(8,128)(2,1)} %feat.3, s32[2,26]{1,0:T(2,128)} %owner.1, s32[2,26]{1,0:T(2,128)} %slot.1), custom_call_target="tpu_custom_call" | custom-call | flops 2000000 | bytes 655776 | tf_op jit(solution)/shard_map/ask/pallas_call | solution.py:373
  3.5 12.0 %all-to-all-start = ((bf16[32,48,128]{2,1,0:T(8,128)(2,1)}), bf16[32,48,128]{2,1,0:T(8,128)(2,1)S(1)}, u32[]{:S(2)}, u32[]{:S(2)}) async-start(bf16[32,48,128]{2,1,0:T(8,128)(2,1)} %ask.1), calls=%async_computation | async-start | bytes 786432 | tf_op jit(solution)/shard_map/all_to_all | solution.py:427
  15.6 11.6 %all-to-all-done.got = bf16[32,48,128]{2,1,0:T(8,128)(2,1)S(1)} async-done(((bf16[32,48,128]{2,1,0:T(8,128)(2,1)}), bf16[32,48,128]{2,1,0:T(8,128)(2,1)S(1)}, u32[]{:S(2)}, u32[]{:S(2)}) %all-to-all-start) | async-done | bytes 393248 | tf_op jit(solution)/shard_map/all_to_all | solution.py:427
  27.2 1.6 %route.1 = bf16[32,32,128]{2,1,0:T(8,128)(2,1)} custom-call(bf16[32,48,128]{2,1,0:T(8,128)(2,1)S(1)} %all-to-all-done.got), custom_call_target="tpu_custom_call" | custom-call | flops 300000000 | bytes 655360 | tf_op jit(solution)/shard_map/route/pallas_call | solution.py:373
  28.8 7.5 %all-to-all-start.1 = ((bf16[32,32,128]{2,1,0:T(8,128)(2,1)}), bf16[32,32,128]{2,1,0:T(8,128)(2,1)S(1)}, u32[]{:S(2)}, u32[]{:S(2)}) async-start(bf16[32,32,128]{2,1,0:T(8,128)(2,1)} %route.1), calls=%async_computation.1 | async-start | bytes 524288 | tf_op jit(solution)/shard_map/all_to_all | solution.py:437
  36.4 0.1 pad_maximum_fusion.weight
  36.6 9.3 %all-to-all-done.1.got = bf16[32,32,128]{2,1,0:T(8,128)(2,1)S(1)} async-done(((bf16[32,32,128]{2,1,0:T(8,128)(2,1)}), bf16[32,32,128]{2,1,0:T(8,128)(2,1)S(1)}, u32[]{:S(2)}, u32[]{:S(2)}) %all-to-all-start.1) | async-done | bytes 262176 | tf_op jit(solution)/shard_map/all_to_all | solution.py:437
  46.0 6.6 %forward.1 = (bf16[2,128,512]{2,1,0:T(8,128)(2,1)}, bf16[2,512,128]{2,1,0:T(8,128)(2,1)S(1)}, bf16[4096,128]{1,0:T(8,128)(2,1)S(1)}, bf16[2048,128]{1,0:T(8,128)(2,1)}) custom-call(s32[1]{0:T(128)S(6)} %copy.16.counts, s32[2]{0:T(128)S(1)} %copy-done.4, s32[2]{0:T(128)S(1)} %copy-done.5, s32[1]{0:T(128)} %bitcast.core, bf16[2,128,512]{2,1,0:T(8,128)(2,1)S(1)} %copy-done, ...), custom_call_target="tpu_custom_call" | custom-call | flops 2000000000 | bytes 3899392 | tf_op jit(solution)/shard_map/forward/pallas_call | solution.py:373
  52.6 3.7 %collective-permute-start = (bf16[2048,128]{1,0:T(8,128)(2,1)}, bf16[2048,128]{1,0:T(8,128)(2,1)S(1)}, u32[]{:S(2)}, u32[]{:S(2)}) collective-permute-start(bf16[2048,128]{1,0:T(8,128)(2,1)} %get-tuple-element.28), channel_id=1, source_target_pairs={{0,32},{32,0},{64,96},{96,64},{128,160},{160,128},{192,224},{224,1... | collective-permute-start | bytes 1572872 | tf_op jit(solution)/shard_map/ppermute | solution.py:478
  56.3 1.7 %collective-permute-done.other = bf16[2048,128]{1,0:T(8,128)(2,1)S(1)} collective-permute-done((bf16[2048,128]{1,0:T(8,128)(2,1)}, bf16[2048,128]{1,0:T(8,128)(2,1)S(1)}, u32[]{:S(2)}, u32[]{:S(2)}) %collective-permute-start) | collective-permute-done | bytes 524320 | tf_op jit(solution)/shard_map/ppermute | solution.py:478
  58.1 0.1 pair.1
  58.2 1.3 %collective-permute-start.1 = (bf16[512,128]{1,0:T(8,128)(2,1)S(1)}, bf16[512,128]{1,0:T(8,128)(2,1)S(1)}, u32[]{:S(2)}, u32[]{:S(2)}) collective-permute-start(bf16[512,128]{1,0:T(8,128)(2,1)S(1)} %get-tuple-element.33), channel_id=1, source_target_pairs={{0,64},{32,96},{64,128},{96,160},{128,192},{160,224},{192,0},{224,... | collective-permute-start | bytes 393224 | tf_op jit(solution)/shard_map/ppermute | solution.py:487
  59.5 2.4 %collective-permute-start.2 = (bf16[512,128]{1,0:T(8,128)(2,1)S(1)}, bf16[512,128]{1,0:T(8,128)(2,1)S(1)}, u32[]{:S(2)}, u32[]{:S(2)}) collective-permute-start(bf16[512,128]{1,0:T(8,128)(2,1)S(1)} %get-tuple-element.34), channel_id=1, source_target_pairs={{0,128},{32,160},{64,192},{96,224},{128,0},{160,32},{192,64},{224,... | collective-permute-start | bytes 393224 | tf_op jit(solution)/shard_map/ppermute | solution.py:487
  61.9 1.2 collective-permute-start.3
  63.1 2.3 %backward.1 = (f32[2,512,128]{2,1,0:T(8,128)S(1)}, bf16[32,32,128]{2,1,0:T(8,128)(2,1)S(1)}) custom-call(bf16[2,512,128]{2,1,0:T(8,128)(2,1)S(1)} %get-tuple-element.30.grad, bf16[1152,384]{1,0:T(8,128)(2,1)S(1)} %pad_maximum_fusion.weight), custom_call_target="tpu_custom_call" | custom-call | flops 4000000000 | bytes 1933312 | tf_op jit(solution)/shard_map/backward/pallas_call | solution.py:373
  65.4 2.6 %collective-permute-done.2.away2 = bf16[512,128]{1,0:T(8,128)(2,1)S(1)} collective-permute-done((bf16[512,128]{1,0:T(8,128)(2,1)S(1)}, bf16[512,128]{1,0:T(8,128)(2,1)S(1)}, u32[]{:S(2)}, u32[]{:S(2)}) %collective-permute-start.2) | collective-permute-done | bytes 131104 | tf_op jit(solution)/shard_map/ppermute | solution.py:487
  68.0 0.8 join.1
  68.8 4.4 %all-to-all-start.2 = ((bf16[32,48,128]{2,1,0:T(8,128)(2,1)}), bf16[32,48,128]{2,1,0:T(8,128)(2,1)S(1)}, u32[]{:S(2)}, u32[]{:S(2)}) async-start(bf16[32,48,128]{2,1,0:T(8,128)(2,1)} %join.1), calls=%async_computation.2 | async-start | bytes 786432 | tf_op jit(solution)/shard_map/all_to_all | solution.py:512
  73.2 0.2 copy.15
  73.6 10.3 %all-to-all-done.2.got = bf16[32,48,128]{2,1,0:T(8,128)(2,1)S(1)} async-done(((bf16[32,48,128]{2,1,0:T(8,128)(2,1)}), bf16[32,48,128]{2,1,0:T(8,128)(2,1)S(1)}, u32[]{:S(2)}, u32[]{:S(2)}) %all-to-all-start.2) | async-done | bytes 393248 | tf_op jit(solution)/shard_map/all_to_all | solution.py:512
  84.0 0.8 merge.1
  84.8 17.5 %all_to_all.20.got = bf16[32,48,128]{2,1,0:T(8,128)(2,1)S(1)} all-to-all(bf16[32,48,128]{2,1,0:T(8,128)(2,1)S(1)} %merge.1), channel_id=1, replica_groups=mesh['grp'=8,'dev'=32] {'dev'}, dimensions={0} | all-to-all | bytes 786432 | tf_op jit(solution)/shard_map/all_to_all | solution.py:522
  102.3 1.1 collective-permute-start.6
  103.4 2.7 %collective-permute-start.5 = (bf16[512,128]{1,0:T(8,128)(2,1)S(1)}, bf16[512,128]{1,0:T(8,128)(2,1)S(1)}, u32[]{:S(2)}, u32[]{:S(2)}) collective-permute-start(bf16[512,128]{1,0:T(8,128)(2,1)S(1)} %bitcast.9), channel_id=1, source_target_pairs={{0,128},{32,160},{64,192},{96,224},{128,0},{160,32},{192,64},{224,... | collective-permute-start | bytes 393224 | tf_op jit(solution)/shard_map/ppermute | solution.py:525
  106.2 6.1 %collective-permute-start.7 = (bf16[512,128]{1,0:T(8,128)(2,1)S(1)}, bf16[512,128]{1,0:T(8,128)(2,1)S(1)}, u32[]{:S(2)}, u32[]{:S(2)}) collective-permute-start(bf16[512,128]{1,0:T(8,128)(2,1)S(1)} %bitcast.11), channel_id=1, source_target_pairs={{0,32},{32,0},{64,96},{96,64},{128,160},{160,128},{192,224},{224,1... | collective-permute-start | bytes 393224 | tf_op jit(solution)/shard_map/ppermute | solution.py:537
  112.3 1.3 %finish.1 = bf16[2,128,512]{2,1,0:T(8,128)(2,1)} custom-call(s32[1]{0:T(128)S(6)} %copy.16.counts, bf16[32,48,128]{2,1,0:T(8,128)(2,1)S(1)} %all_to_all.20.got, f32[2,512,128]{2,1,0:T(8,128)S(1)} %get-tuple-element.36.own, bf16[2,128,512]{2,1,0:T(8,128)(2,1)S(1)} %copy-done.1), custom_call_target="tpu_custom_call" | custom-call | flops 300000000 | bytes 1441792 | tf_op jit(solution)/shard_map/finish/pallas_call | solution.py:373
  113.6 3.0 %collective-permute-start.8 = (bf16[512,128]{1,0:T(8,128)(2,1)S(1)}, bf16[512,128]{1,0:T(8,128)(2,1)S(1)}, u32[]{:S(2)}, u32[]{:S(2)}) collective-permute-start(bf16[512,128]{1,0:T(8,128)(2,1)S(1)} %collective-permute-done.4.refs_1_), channel_id=1, source_target_pairs={{0,32},{32,0},{64,96},{96,64},{128,160},{160,128},{192,224},{224,1... | collective-permute-start | bytes 393224 | tf_op jit(solution)/shard_map/ppermute | solution.py:539
  116.6 0.5 collective-permute-start.10
  117.1 0.5 collective-permute-done.8.refs_5_
  117.6 0.4 collective-permute-done.9.refs_6_
  118.0 0.2 collective-permute-done.10.refs_7_
  118.1 1.5 %assemble.1 = (f32[27,128,128]{2,1,0:T(8,128)}, f32[128,256]{1,0:T(8,128)}, f32[256,128]{1,0:T(8,128)}) custom-call(s32[1]{0:T(128)} %bitcast.core, s32[1]{0:T(128)} %bitcast.4.line, bf16[512,128]{1,0:T(8,128)(2,1)S(1)} %bitcast.12, bf16[512,128]{1,0:T(8,128)(2,1)S(1)} %collective-permute-done.4.refs_1_, ...), custom_call_target="tpu_custom_call" | custom-call | flops 1000000 | bytes 3080192 | tf_op jit(solution)/shard_map/assemble/pallas_call | solution.py:373
  (27 shorter events, 0.3 us)
Async XLA Ops:
  0.6 35.6 %copy-start.6 = (bf16[27,128,128]{2,1,0:T(8,128)(2,1)S(1)}, bf16[27,128,128]{2,1,0:T(8,128)(2,1)}, u32[]{:S(2)}) copy-start(bf16[27,128,128]{2,1,0:T(8,128)(2,1)} %param.12) | copy-start | bytes 2654212
  3.5 23.7 %all-to-all-start = ((bf16[32,48,128]{2,1,0:T(8,128)(2,1)}), bf16[32,48,128]{2,1,0:T(8,128)(2,1)S(1)}, u32[]{:S(2)}, u32[]{:S(2)}) async-start(bf16[32,48,128]{2,1,0:T(8,128)(2,1)} %ask.1), calls=%async_computation | async-start | bytes 786432 | tf_op jit(solution)/shard_map/all_to_all | solution.py:427
  28.8 17.1 %all-to-all-start.1 = ((bf16[32,32,128]{2,1,0:T(8,128)(2,1)}), bf16[32,32,128]{2,1,0:T(8,128)(2,1)S(1)}, u32[]{:S(2)}, u32[]{:S(2)}) async-start(bf16[32,32,128]{2,1,0:T(8,128)(2,1)} %route.1), calls=%async_computation.1 | async-start | bytes 524288 | tf_op jit(solution)/shard_map/all_to_all | solution.py:437
  36.3 9.6 %copy-start = (bf16[2,128,512]{2,1,0:T(8,128)(2,1)S(1)}, bf16[2,128,512]{2,1,0:T(8,128)(2,1)}, u32[]{:S(2)}) copy-start(bf16[2,128,512]{2,1,0:T(8,128)(2,1)} %feat.3) | copy-start | bytes 786436
  36.3 9.6 %copy-start.1 = (bf16[2,128,512]{2,1,0:T(8,128)(2,1)S(1)}, bf16[2,128,512]{2,1,0:T(8,128)(2,1)}, u32[]{:S(2)}) copy-start(bf16[2,128,512]{2,1,0:T(8,128)(2,1)} %gout.3) | copy-start | bytes 786436
  36.3 9.6 %copy-start.2 = (bf16[128,256]{1,0:T(8,128)(2,1)S(1)}, bf16[128,256]{1,0:T(8,128)(2,1)}, u32[]{:S(2)}) copy-start(bf16[128,256]{1,0:T(8,128)(2,1)} %up.1) | copy-start | bytes 196612
  36.3 9.6 %copy-start.3 = (bf16[256,128]{1,0:T(8,128)(2,1)S(1)}, bf16[256,128]{1,0:T(8,128)(2,1)}, u32[]{:S(2)}) copy-start(bf16[256,128]{1,0:T(8,128)(2,1)} %down.1) | copy-start | bytes 196612
  36.3 9.6 %copy-start.4 = (s32[2]{0:T(128)S(1)}, s32[2]{0:T(128)}, u32[]{:S(2)}) copy-start(s32[2]{0:T(128)} %parent.1) | copy-start | bytes 28
  36.3 9.6 %copy-start.5 = (s32[2]{0:T(128)S(1)}, s32[2]{0:T(128)}, u32[]{:S(2)}) copy-start(s32[2]{0:T(128)} %child.1) | copy-start | bytes 28
  52.6 5.5 %collective-permute-start = (bf16[2048,128]{1,0:T(8,128)(2,1)}, bf16[2048,128]{1,0:T(8,128)(2,1)S(1)}, u32[]{:S(2)}, u32[]{:S(2)}) collective-permute-start(bf16[2048,128]{1,0:T(8,128)(2,1)} %get-tuple-element.28), channel_id=1, source_target_pairs={{0,32},{32,0},{64,96},{96,64},{128,160},{160,128},{192,224},{224,1... | collective-permute-start | bytes 1572872 | tf_op jit(solution)/shard_map/ppermute | solution.py:478
  58.2 7.2 %collective-permute-start.1 = (bf16[512,128]{1,0:T(8,128)(2,1)S(1)}, bf16[512,128]{1,0:T(8,128)(2,1)S(1)}, u32[]{:S(2)}, u32[]{:S(2)}) collective-permute-start(bf16[512,128]{1,0:T(8,128)(2,1)S(1)} %get-tuple-element.33), channel_id=1, source_target_pairs={{0,64},{32,96},{64,128},{96,160},{128,192},{160,224},{192,0},{224,... | collective-permute-start | bytes 393224 | tf_op jit(solution)/shard_map/ppermute | solution.py:487
  59.5 8.5 %collective-permute-start.2 = (bf16[512,128]{1,0:T(8,128)(2,1)S(1)}, bf16[512,128]{1,0:T(8,128)(2,1)S(1)}, u32[]{:S(2)}, u32[]{:S(2)}) collective-permute-start(bf16[512,128]{1,0:T(8,128)(2,1)S(1)} %get-tuple-element.34), channel_id=1, source_target_pairs={{0,128},{32,160},{64,192},{96,224},{128,0},{160,32},{192,64},{224,... | collective-permute-start | bytes 393224 | tf_op jit(solution)/shard_map/ppermute | solution.py:487
  61.9 6.1 %collective-permute-start.3 = (bf16[512,128]{1,0:T(8,128)(2,1)S(1)}, bf16[512,128]{1,0:T(8,128)(2,1)S(1)}, u32[]{:S(2)}, u32[]{:S(2)}) collective-permute-start(bf16[512,128]{1,0:T(8,128)(2,1)S(1)} %get-tuple-element.35), channel_id=1, source_target_pairs={{0,192},{32,224},{64,0},{96,32},{128,64},{160,96},{192,128},{224,1... | collective-permute-start | bytes 393224 | tf_op jit(solution)/shard_map/ppermute | solution.py:487
  68.8 15.2 %all-to-all-start.2 = ((bf16[32,48,128]{2,1,0:T(8,128)(2,1)}), bf16[32,48,128]{2,1,0:T(8,128)(2,1)S(1)}, u32[]{:S(2)}, u32[]{:S(2)}) async-start(bf16[32,48,128]{2,1,0:T(8,128)(2,1)} %join.1), calls=%async_computation.2 | async-start | bytes 786432 | tf_op jit(solution)/shard_map/all_to_all | solution.py:512
  102.3 11.3 %collective-permute-start.6 = (bf16[512,128]{1,0:T(8,128)(2,1)S(1)}, bf16[512,128]{1,0:T(8,128)(2,1)S(1)}, u32[]{:S(2)}, u32[]{:S(2)}) collective-permute-start(bf16[512,128]{1,0:T(8,128)(2,1)S(1)} %bitcast.8), channel_id=1, source_target_pairs={{0,64},{32,96},{64,128},{96,160},{128,192},{160,224},{192,0},{224,... | collective-permute-start | bytes 393224 | tf_op jit(solution)/shard_map/ppermute | solution.py:525
  103.4 10.2 %collective-permute-start.5 = (bf16[512,128]{1,0:T(8,128)(2,1)S(1)}, bf16[512,128]{1,0:T(8,128)(2,1)S(1)}, u32[]{:S(2)}, u32[]{:S(2)}) collective-permute-start(bf16[512,128]{1,0:T(8,128)(2,1)S(1)} %bitcast.9), channel_id=1, source_target_pairs={{0,128},{32,160},{64,192},{96,224},{128,0},{160,32},{192,64},{224,... | collective-permute-start | bytes 393224 | tf_op jit(solution)/shard_map/ppermute | solution.py:525
  106.2 7.4 %collective-permute-start.4 = (bf16[512,128]{1,0:T(8,128)(2,1)S(1)}, bf16[512,128]{1,0:T(8,128)(2,1)S(1)}, u32[]{:S(2)}, u32[]{:S(2)}) collective-permute-start(bf16[512,128]{1,0:T(8,128)(2,1)S(1)} %bitcast.10), channel_id=1, source_target_pairs={{0,192},{32,224},{64,0},{96,32},{128,64},{160,96},{192,128},{224,1... | collective-permute-start | bytes 393224 | tf_op jit(solution)/shard_map/ppermute | solution.py:525
  106.2 10.9 %collective-permute-start.7 = (bf16[512,128]{1,0:T(8,128)(2,1)S(1)}, bf16[512,128]{1,0:T(8,128)(2,1)S(1)}, u32[]{:S(2)}, u32[]{:S(2)}) collective-permute-start(bf16[512,128]{1,0:T(8,128)(2,1)S(1)} %bitcast.11), channel_id=1, source_target_pairs={{0,32},{32,0},{64,96},{96,64},{128,160},{160,128},{192,224},{224,1... | collective-permute-start | bytes 393224 | tf_op jit(solution)/shard_map/ppermute | solution.py:537
  113.6 4.0 %collective-permute-start.8 = (bf16[512,128]{1,0:T(8,128)(2,1)S(1)}, bf16[512,128]{1,0:T(8,128)(2,1)S(1)}, u32[]{:S(2)}, u32[]{:S(2)}) collective-permute-start(bf16[512,128]{1,0:T(8,128)(2,1)S(1)} %collective-permute-done.4.refs_1_), channel_id=1, source_target_pairs={{0,32},{32,0},{64,96},{96,64},{128,160},{160,128},{192,224},{224,1... | collective-permute-start | bytes 393224 | tf_op jit(solution)/shard_map/ppermute | solution.py:539
  116.6 1.3 %collective-permute-start.9 = (bf16[512,128]{1,0:T(8,128)(2,1)S(1)}, bf16[512,128]{1,0:T(8,128)(2,1)S(1)}, u32[]{:S(2)}, u32[]{:S(2)}) collective-permute-start(bf16[512,128]{1,0:T(8,128)(2,1)S(1)} %collective-permute-done.5.refs_2_), channel_id=1, source_target_pairs={{0,32},{32,0},{64,96},{96,64},{128,160},{160,128},{192,224},{224,1... | collective-permute-start | bytes 393224 | tf_op jit(solution)/shard_map/ppermute | solution.py:539
  116.6 1.5 %collective-permute-start.10 = (bf16[512,128]{1,0:T(8,128)(2,1)S(1)}, bf16[512,128]{1,0:T(8,128)(2,1)S(1)}, u32[]{:S(2)}, u32[]{:S(2)}) collective-permute-start(bf16[512,128]{1,0:T(8,128)(2,1)S(1)} %collective-permute-done.6.refs_3_), channel_id=1, source_target_pairs={{0,32},{32,0},{64,96},{96,64},{128,160},{160,128},{192,224},{224,1... | collective-permute-start | bytes 393224 | tf_op jit(solution)/shard_map/ppermute | solution.py:539

commit v5 on v4

--- a/solution.py
+++ b/solution.py
@@ -42,17 +42,44 @@
 
 SHARES = [((64 * f + p, 32, 2), (2 * f + p, 32, 16)) for f in range(6) for p in range(2)]
 SHARES += [((384 + 32 * m, 32, 1), (12 + m, 32, 16)) for m in range(3)]
-SHARES += [((480, 8, 1), (15 + 16 * n, 8, 64)) for n in range(4)]
+
+
+def share_directions(group):
+    edges = [EDGES[4 * m + group // 2] for m in range(3)]
+    return [OFFSETS.index(d) for d in [FACES[q // 2] for q in range(12)] + edges + [CORNERS[group]]]
+
+
+def choice_table():
+    table = np.zeros((128, 8, 128), np.float32)
+    for group in range(8):
+        for q, direction in enumerate(share_directions(group)):
+            table[direction, group, 32 + q] = 1
+    return table.reshape(128, 1024)
+
+
+def few_lanes(rows):
+    return lax.broadcasted_iota(jnp.int32, (rows, 128), 1) < 32
 
 
 def to_pieces(rows, pieces):
-    for there, here in SHARES[:16]:
+    for there, here in SHARES:
         pieces[run(*there), :] = rows[run(*here), :]
-
-
-def to_shares(pieces, rows):
+    total = jnp.zeros((8, 128), F32)
+    for n in range(4):
+        part = jnp.where(few_lanes(8), rows[pl.ds(15 + 16 * n, 8, stride=64), :], 0.0)
+        total = total + (pltpu.roll(part, 32 * n, 1) if n else part)
+    pieces[pl.ds(480, 8), :] = total
+
+
+def to_shares(pieces, rows, extra=None):
     for there, here in SHARES:
         rows[run(*here), :] = pieces[run(*there), :]
+    for n in range(4):
+        part = pieces[pl.ds(480, 8), :]
+        part = pltpu.roll(part, 128 - 32 * n, 1) if n else part
+        if extra is not None:
+            part = jnp.where(few_lanes(8), part, extra)
+        rows[pl.ds(15 + 16 * n, 8, stride=64), :] = part
 
 
 def nn(x, y):
@@ -77,42 +104,42 @@
 
 
 def ask_kernel(
-    counts, feat, owner, slot, msg, feat_v, owner_v, slot_v, bricks, voxels, pc, rows, sems
+    counts, feat, owner, slot, choice, msg,
+    feat_v, owner_v, slot_v, choice_v, bricks, tables, voxels, pc, rows, msg_v, sems,
 ):
-    pairs = ((owner, owner_v), (slot, slot_v), (feat, feat_v))
+    pairs = (
+        (owner, owner_v), (slot, slot_v), (choice, choice_v),
+        (feat.at[0], feat_v.at[0]), (feat.at[1], feat_v.at[1]),
+    )
     copies = [
         pltpu.make_async_copy(src, dst, sems.at[n]) for n, (src, dst) in enumerate(pairs)
     ]
     for copy in copies:
         copy.start()
-    bricks[...] = jnp.zeros((128, 128), F32)
-    copies[0].wait()
-    copies[1].wait()
+    bricks[...] = jnp.zeros((16, 128), F32)
+    for copy in copies[:3]:
+        copy.wait()
     named = jnp.where(owner_v[...] >= 0, owner_v[...] * 2 + slot_v[...], -1)
     bricks[0:2, 0:26] = named.astype(F32)
-    bricks[...] = bricks[...].T
-
-    def ask(first, size, stride, direction):
-        line = bricks[pl.ds(OFFSETS.index(direction), 1), :]
-        rows[run(first, size, stride), :] = jnp.broadcast_to(line, (size, 128))
-
-    for n, d in enumerate(FACES):
-        ask(2 * n, 32, 16, d)
-        ask(2 * n + 1, 32, 16, d)
-    for n, d in enumerate(EDGES):
-        ask(12 + n // 4 + 128 * (n % 4), 8, 16, d)
-    for n, d in enumerate(CORNERS):
-        ask(15 + 64 * n, 4, 16, d)
-    msg[:, 32:48, :] = rows[...].astype(BF).reshape(32, 16, 128)
-    copies[2].wait()
+    asked = nn(bricks[...].astype(BF), choice_v[...])
+    for group in range(8):
+        for s in range(2):
+            tables[s, group : group + 1, :] = asked[s : s + 1, group * 128 : group * 128 + 128]
+    sent = []
     for s in range(2):
+        copies[3 + s].wait()
         live = (counts[0] > s).astype(F32)
-        voxels[...] = (feat_v[s].astype(F32) * live).T
+        voxels[s] = (feat_v[s].astype(F32) * live).T
         for d in OFFSETS:
             for at, first, size, stride in voxel_runs(d):
-                pc[pl.ds(PIECE[d] + at, size), :] = voxels[run(first, size, stride), :]
-        to_shares(pc, rows)
-        msg[:, 16 * s : 16 * s + 16, :] = rows[...].astype(BF).reshape(32, 16, 128)
+                pc[s, pl.ds(PIECE[d] + at, size), :] = voxels.at[s][run(first, size, stride), :]
+        to_shares(pc.at[s], rows.at[s], tables[s])
+        at = pl.ds(16 * s, 16)
+        msg_v[:, at, :] = rows[s].astype(BF).reshape(32, 16, 128)
+        sent.append(pltpu.make_async_copy(msg_v.at[:, at, :], msg.at[:, at, :], sems.at[5 + s]))
+        sent[s].start()
+    for copy in sent:
+        copy.wait()
 
 
 def same_part():
@@ -121,32 +148,38 @@
     return (rows == lanes).astype(F32).astype(BF)
 
 
-def route_kernel(got, out, hot):
+def route_kernel(got, out, hot, out_v, sems):
     same = jnp.broadcast_to(same_part()[None], (32, 16, 128))
     zero = jnp.zeros((32, 16, 128), BF)
-    lanes = lax.broadcasted_iota(jnp.int32, (128, 128), 0)
-    brick = lax.broadcasted_iota(jnp.int32, (16, 128), 1) >> 4
-    table = got[:, 32:48, :].reshape(512, 128)
+    ones = jnp.ones((128, 128), BF)
+    part = lax.broadcasted_iota(jnp.int32, (16, 128), 0)
+    lanes = lax.broadcasted_iota(jnp.int32, (16, 128), 1)
+    place = (lanes == part + 32)[None]
+    sent = []
     for s in range(2):
-        spread = (lanes == s).astype(F32).astype(BF)
-        asked = nn(table, spread).astype(BF).reshape(32, 16, 128)
+        at = pl.ds(16 * s, 16)
+        table = got[:, at, :].astype(F32)[:, 15:16, :]
+        table = jnp.where(place, jnp.broadcast_to(table, (32, 16, 128)), 0.0)
+        asked = nn(table.astype(BF).reshape(512, 128), ones).astype(BF).reshape(32, 16, 128)
         for n in range(8):
-            here = (brick + 8 * n).astype(F32).astype(BF)
+            here = ((lanes >> 4) + 8 * n).astype(F32).astype(BF)
             picked = jnp.where(asked == here[None], same, zero)
-            hot[s * 512 : s * 512 + 512, n * 128 : n * 128 + 128] = picked.reshape(512, 128)
-    answer = nn(hot[...], got[:, 0:32, :].reshape(1024, 128)).astype(BF)
-    for s in range(2):
-        out[:, 16 * s : 16 * s + 16, :] = answer[s * 512 : s * 512 + 512].reshape(32, 16, 128)
+            hot[s, :, n * 128 : n * 128 + 128] = picked.reshape(512, 128)
+        answer = nn(hot[s], got[...].reshape(1024, 128)).astype(BF)
+        out_v[:, at, :] = answer.reshape(32, 16, 128)
+        sent.append(pltpu.make_async_copy(out_v.at[:, at, :], out.at[:, at, :], sems.at[s]))
+        sent[s].start()
+    for copy in sent:
+        copy.wait()
 
 
 def forward_kernel(
     counts, parent, child, core, feat, got, gout, weight, up, down,
-    out, grad, wsum, send,
-    rows_all, pc_all, mine_all, s0_all, s1_all, s2_all, cols, grad_t, pooled, grad_pooled,
-    out_v, sem,
+    grad_t, acts, lift, wsum, send,
+    rows_all, pc_all, mine_all, s0_all, s1_all, s2_all, cols, pooled, grad_pooled,
 ):
     eye = identity()
-    acts, slopes = [], []
+    slopes = []
     for s in range(2):
         rows, pc, mine, s0, s1, s2 = (
             x.at[s] for x in (rows_all, pc_all, mine_all, s0_all, s1_all, s2_all)
@@ -192,7 +225,7 @@
         pre = pre.T
         gate = 1.0 / (1.0 + jnp.exp(-pre))
         active = pre * gate
-        acts.append(active)
+        acts[s] = active
         slopes.append(gate * (1.0 + pre * (1.0 - gate)))
         high = active.astype(BF)
         low = (active - high.astype(F32)).astype(BF)
@@ -214,18 +247,12 @@
     grad_pre = grad_pre.astype(BF)
     coarse_out = nn(coarse_mid, down[...]).astype(BF)
     grad_cin = nt(grad_pre, up[...]).astype(BF)
-    lift = nt(eye, coarse_out).astype(BF)
+    lift[...] = nt(eye, coarse_out).astype(BF)
     back = nt(eye, grad_cin).astype(BF)
     for s in range(2):
         live = (counts[0] > s).astype(F32)
-        pool = pool_rows(s)
-        out_v[s] = (feat[s].astype(F32) * live + acts[s] + nn(lift, pool)).astype(BF)
-        grad_in = gout[s].astype(F32) * live + nn(back, pool) * (1.0 / 64.0)
-        grad_pre_conv = grad_in * slopes[s]
-        grad_t[s] = grad_pre_conv.astype(BF)
-        grad[s] = grad_pre_conv.T.astype(BF)
-    copy = pltpu.make_async_copy(out_v, out, sem.at[0])
-    copy.start()
+        grad_in = gout[s].astype(F32) * live + nn(back, pool_rows(s)) * (1.0 / 64.0)
+        grad_t[s] = (grad_in * slopes[s]).astype(BF)
 
     def put(block, value):
         wsum[pl.ds(block * 128, 128), :] = value.astype(BF)
@@ -243,7 +270,6 @@
         for n in range(9):
             put(9 * a + n, nt(eye, total[:, n * 128 : n * 128 + 128]))
     send[...] = wsum[pl.ds(pl.multiple_of((1 - core[0]) * 2048, 2048), 2048), :]
-    copy.wait()
 
 
 def pair_kernel(core, line, wsum, other, own, one, two, three):
@@ -253,7 +279,22 @@
         ref[...] = (kept + other[pl.ds(at, 512), :].astype(F32)).astype(ref.dtype)
 
 
-def backward_kernel(grad, weight, own, msg, lhs, acc_all, pc_all, rows_all):
+def backward_kernel(
+    counts, feat, grad_t, acts, lift, weight,
+    own, out, msg,
+    lhs, acc_all, pc_all, rows_all, out_v, msg_v, sems,
+):
+    sent = []
+
+    def send(src, dst):
+        sent.append(pltpu.make_async_copy(src, dst, sems.at[len(sent)]))
+        sent[-1].start()
+
+    for s in range(2):
+        live = (counts[0] > s).astype(F32)
+        value = feat[s].astype(F32) * live + acts[s] + nn(lift[...], pool_rows(s))
+        out_v[s] = value.astype(BF)
+    send(out_v, out)
     zero = jnp.zeros((64, 128), BF)
     for a in range(3):
         for n in [*range(a), *range(8 + a, 10)]:
@@ -264,8 +305,9 @@
 
     for s in range(2):
         acc, pc, rows = acc_all.at[s], pc_all.at[s], rows_all.at[s]
+        grad = grad_t[s].astype(F32).T.astype(BF)
         for a in range(3):
-            lhs[s, a * 64 : a * 64 + 512, a * 128 : a * 128 + 128] = grad[s]
+            lhs[s, a * 64 : a * 64 + 512, a * 128 : a * 128 + 128] = grad
         acc[...] = jnp.zeros_like(acc)
         for b in range(3):
             part = nt(lhs[s], weight[b * 384 : b * 384 + 384, :])
@@ -299,13 +341,19 @@
                 for b, y in ((-1, 0), (1, 9)):
                     pc[pl.ds(PIECE[a, b, c], 1), :] = ref[pl.ds((x * 10 + y) * 8 + lane, 1), :]
         to_shares(pc, rows)
-        msg[:, 16 * s : 16 * s + 16, :] = rows[...].astype(BF).reshape(32, 16, 128)
-
-
-def join_kernel(terms, own, away1, away2, away3, msg):
-    msg[:, 0:32, :] = terms[...]
+        at = pl.ds(16 * s, 16)
+        msg_v[:, at, :] = rows[...].astype(BF).reshape(32, 16, 128)
+        send(msg_v.at[:, at, :], msg.at[:, at, :])
+    for copy in sent:
+        copy.wait()
+
+
+def join_kernel(terms, own, away1, away2, away3, msg, share, sem):
     total = own[...] + away1[...].astype(F32) + away2[...].astype(F32) + away3[...].astype(F32)
-    msg[:, 32:48, :] = total.astype(BF).reshape(32, 16, 128)
+    share[...] = total.astype(BF).reshape(32, 16, 128)
+    copy = pltpu.make_async_copy(share, msg.at[:, pl.ds(32, 16), :], sem.at[0])
+    copy.start()
+    copy.wait()
 
 
 def merge_kernel(got, table, out, hot):
@@ -336,45 +384,72 @@
         out[s] = (total[...].T + gout[s].astype(F32) * live).astype(BF)
 
 
-def assemble_kernel(core, line, *refs):
-    parts, (conv, up, down) = refs[:8], refs[8:]
+def assemble_kernel(flip, core, line, *refs):
+    parts, (conv, up, down, held, sems) = refs[:4], refs[-5:]
+    half = core[0] ^ flip
+
+    def moves(n, first):
+        def copy(src, dst, k):
+            return pltpu.make_async_copy(src, dst, sems.at[n, k])
+
+        block = held.at[n]
+        return (
+            (first < 24, lambda: [copy(block, conv.at[pl.ds(first, 4)], 0)]),
+            (
+                first == 24,
+                lambda: [
+                    copy(block.at[0:3], conv.at[pl.ds(24, 3)], 0),
+                    copy(block.at[3], up.at[:, pl.ds(0, 128)], 1),
+                ],
+            ),
+            (
+                first == 28,
+                lambda: [
+                    copy(block.at[0], up.at[:, pl.ds(128, 128)], 0),
+                    copy(block.at[1], down.at[pl.ds(0, 128), :], 1),
+                    copy(block.at[2], down.at[pl.ds(128, 128), :], 2),
+                ],
+            ),
+        )
+
+    firsts = [half * 16 + ((line[0] + n) & 3) * 4 for n in range(4)]
     for n, part in enumerate(parts):
-        half = core[0] ^ (n // 4)
-        first = half * 16 + ((line[0] + n % 4) & 3) * 4
-
-        def block(at):
-            return part[at * 128 : at * 128 + 128, :].astype(F32)
-
-        @pl.when(first < 24)
-        def _():
-            for at in range(4):
-                conv[first + at] = block(at)
-
-        @pl.when(first == 24)
-        def _():
-            for at in range(3):
-                conv[24 + at] = block(at)
-            up[:, 0:128] = block(3)
-
-        @pl.when(first == 28)
-        def _():
-            up[:, 128:256] = block(0)
-            down[0:128, :] = block(1)
-            down[128:256, :] = block(2)
+        held[n] = part[...].astype(F32).reshape(4, 128, 128)
+        for when, copies in moves(n, firsts[n]):
+
+            @pl.when(when)
+            def _():
+                for copy in copies():
+                    copy.start()
+
+    for n in range(4):
+        for when, copies in moves(n, firsts[n]):
+
+            @pl.when(when)
+            def _():
+                for copy in copies():
+                    copy.wait()
 
 
 VM = pl.BlockSpec(memory_space=pltpu.VMEM)
 SM = pl.BlockSpec(memory_space=pltpu.SMEM)
 
 
-def call(kernel, shapes, scalars, arrays, scratch=(), flops=1e6, space=VM, limit=24, first=VM, name=None):
+HB = pl.BlockSpec(memory_space=pltpu.HBM)
+
+
+def call(
+    kernel, shapes, scalars, arrays, scratch=(), flops=1e6, limit=24, ins=None, outs=None,
+    alias=None, name=None,
+):
     moved = sum(x.size * x.dtype.itemsize for x in arrays)
     moved += sum(int(np.prod(s.shape)) * s.dtype.itemsize for s in shapes)
     return pl.pallas_call(
         kernel,
         out_shape=shapes,
-        in_specs=[SM] * len(scalars) + [space] * len(arrays),
-        out_specs=[first] + [VM] * (len(shapes) - 1),
+        in_specs=[SM] * len(scalars) + (ins or [VM] * len(arrays)),
+        out_specs=outs or [VM] * len(shapes),
+        input_output_aliases=alias or {},
         scratch_shapes=list(scratch),
         compiler_params=pltpu.CompilerParams(vmem_limit_bytes=limit * 2**20),
         cost_estimate=pl.CostEstimate(
@@ -406,22 +481,26 @@
     swap = [(i, i ^ 1) for i in range(8)]
     (msg,) = call(
         ask_kernel,
-        [shape((32, 48, 128), BF)],
+        [shape((32, 32, 128), BF)],
         [counts],
-        [features, neighbour_owner, neighbour_slot],
+        [features, neighbour_owner, neighbour_slot, jnp.asarray(choice_table(), BF)],
         [
             pltpu.VMEM((2, 128, 512), BF),
             pltpu.VMEM((2, 26), jnp.int32),
             pltpu.VMEM((2, 26), jnp.int32),
-            pltpu.VMEM((128, 128), F32),
-            pltpu.VMEM((512, 128), F32),
-            pltpu.VMEM((512, 128), F32),
-            pltpu.VMEM((512, 128), F32),
-            pltpu.SemaphoreType.DMA((3,)),
+            pltpu.VMEM((128, 1024), BF),
+            pltpu.VMEM((16, 128), F32),
+            pltpu.VMEM((2, 8, 128), F32),
+            pltpu.VMEM((2, 512, 128), F32),
+            pltpu.VMEM((2, 512, 128), F32),
+            pltpu.VMEM((2, 512, 128), F32),
+            pltpu.VMEM((32, 32, 128), BF),
+            pltpu.SemaphoreType.DMA((7,)),
         ],
         flops=2e6,
-        space=pl.BlockSpec(memory_space=pltpu.HBM),
         limit=60,
+        ins=[HB] * 3 + [pl.BlockSpec(memory_space=pl.ANY)],
+        outs=[HB],
         name="ask",
     )
     first = lax.all_to_all(msg, "dev", split_axis=0, concat_axis=0, tiled=True)
@@ -430,32 +509,31 @@
         [shape((32, 32, 128), BF)],
         [],
         [first],
-        [pltpu.VMEM((1024, 1024), BF)],
+        [
+            pltpu.VMEM((2, 512, 1024), BF),
+            pltpu.VMEM((32, 32, 128), BF),
+            pltpu.SemaphoreType.DMA((2,)),
+        ],
         flops=3e8,
+        outs=[HB],
         name="route",
     )
     halo = lax.all_to_all(answer, "dev", split_axis=0, concat_axis=0, tiled=True)
-    table = first[:, 32:48, 0:2].transpose(0, 2, 1).reshape(1, 1024)
+    table = first.reshape(32, 2, 16, 128)[:, :, 15, 32:48].reshape(1, 1024)
     table = jnp.broadcast_to(table, (16, 1024))
     taps = conv_weight.reshape(3, 1152, 128)
     taps = jnp.concatenate([taps[0], taps[1], taps[2]], axis=1)
-    output, grad_pre, wsum, send = call(
+    grad_pre, acts, lift, wsum, send = call(
         forward_kernel,
         [
             shape((2, 128, 512), BF),
-            shape((2, 512, 128), BF),
+            shape((2, 128, 512), F32),
+            shape((128, 16), BF),
             shape((4096, 128), BF),
             shape((2048, 128), BF),
         ],
         [counts, parent, child_slot, core],
-        [
-            features,
-            halo,
-            grad_out,
-            taps,
-            coarse_up,
-            coarse_down,
-        ],
+        [features, halo, grad_out, taps, coarse_up, coarse_down],
         [
             pltpu.VMEM((2, 512, 128), F32),
             pltpu.VMEM((2, 512, 128), F32),
@@ -464,17 +542,12 @@
             pltpu.VMEM((2, 816, 128), F32),
             pltpu.VMEM((2, 800, 128), F32),
             pltpu.VMEM((1280, 1152), BF),
-            pltpu.VMEM((2, 128, 512), BF),
             pltpu.VMEM((2, 16, 128), F32),
             pltpu.VMEM((2, 16, 128), F32),
-            pltpu.VMEM((2, 128, 512), BF),
-            pltpu.SemaphoreType.DMA((1,)),
         ],
-        first=pl.BlockSpec(memory_space=pltpu.HBM),
         flops=2e9,
         name="forward",
     )
-
     other = lax.ppermute(send, "grp", swap)
     own_sum, *away = call(
         pair_kernel,
@@ -484,22 +557,26 @@
         name="pair",
     )
     away = [
-        lax.ppermute(x, "grp", [(i, (i + 2 * step) % 8) for i in range(8)])
-        for step, x in zip((1, 2, 3), away)
+        lax.ppermute(away[step - 1], "grp", [(i, (i + 2 * step) % 8) for i in range(8)])
+        for step in (2, 1, 3)
     ]
     grad_pre, own_sum = lax.optimization_barrier((grad_pre, own_sum))
-    own, terms = call(
+    own, output, terms = call(
         backward_kernel,
-        [shape((2, 512, 128), F32), shape((32, 32, 128), BF)],
-        [],
-        [grad_pre, taps],
+        [shape((2, 512, 128), F32), shape((2, 128, 512), BF), shape((32, 48, 128), BF)],
+        [counts],
+        [features, grad_pre, acts, lift, taps],
         [
             pltpu.VMEM((2, 640, 384), BF),
             pltpu.VMEM((2, 3, 816, 128), F32),
             pltpu.VMEM((2, 512, 128), F32),
             pltpu.VMEM((2, 512, 128), F32),
+            pltpu.VMEM((2, 128, 512), BF),
+            pltpu.VMEM((32, 32, 128), BF),
+            pltpu.SemaphoreType.DMA((3,)),
         ],
         flops=4e9,
+        outs=[VM, HB, HB],
         name="backward",
     )
     (terms,) = call(
@@ -507,6 +584,10 @@
         [shape((32, 48, 128), BF)],
         [],
         [terms, own_sum, *away],
+        [pltpu.VMEM((32, 16, 128), BF), pltpu.SemaphoreType.DMA((1,))],
+        ins=[HB] + [VM] * 4,
+        outs=[HB],
+        alias={0: 0},
         name="join",
     )
     terms = lax.all_to_all(terms, "dev", split_axis=0, concat_axis=0, tiled=True)
@@ -521,10 +602,10 @@
     )
     back = lax.all_to_all(sums, "dev", split_axis=0, concat_axis=0, tiled=True)
     chunk = back[:, 32:48, :].reshape(512, 128)
-    parts = [chunk] + [
-        lax.ppermute(chunk, "grp", [(i, (i - 2 * step) % 8) for i in range(8)])
-        for step in (1, 2, 3)
-    ]
+    parts = {
+        step: lax.ppermute(chunk, "grp", [(i, (i - 2 * step) % 8) for i in range(8)])
+        for step in (2, 1, 3)
+    }
     (grad_features,) = call(
         finish_kernel,
         [shape((2, 128, 512), BF)],
@@ -534,16 +615,24 @@
         flops=3e8,
         name="finish",
     )
-    chunk = lax.ppermute(chunk, "grp", swap)
     parts, grad_features = lax.optimization_barrier((parts, grad_features))
-    parts = parts + [chunk] + [lax.ppermute(x, "grp", swap) for x in parts[1:]]
-    grad_conv, grad_up, grad_down = call(
-        assemble_kernel,
-        [shape((27, 128, 128), F32), shape((128, 256), F32), shape((256, 128), F32)],
-        [core, line],
-        parts,
-        name="assemble",
-    )
+    mine = [chunk, parts[1], parts[2], parts[3]]
+    others = [lax.ppermute(x, "grp", swap) for x in mine]
+
+    def assemble(flip, pieces, held):
+        return call(
+            functools.partial(assemble_kernel, flip),
+            [shape((27, 128, 128), F32), shape((128, 256), F32), shape((256, 128), F32)],
+            [core, line],
+            pieces + held,
+            [pltpu.VMEM((4, 4, 128, 128), F32), pltpu.SemaphoreType.DMA((4, 3))],
+            ins=[VM] * 4 + [HB] * len(held),
+            outs=[HB] * 3,
+            alias={6 + n: n for n in range(len(held))},
+            name="assemble",
+        )
+
+    grad_conv, grad_up, grad_down = assemble(1, others, list(assemble(0, mine, [])))
     return (output, grad_features, grad_conv, grad_up, grad_down)
 
 

time: 120 us -> 118 us (0.983)
  waiting for transfers between devices: 36.7 us -> 31.3 us
  local copies, waits for them, and re-layouts: 0.51 us -> 2.24 us
  Pallas kernels: 17.2 us -> 18.9 us
    ppermute x7, waiting for transfers between devices: 3.63 us -> 0.02 us  [the longest x4 0.01 us: on_device(): others = [lax.ppermute(x, 'grp', swap) for x in mine]]
    all_to_all x1, waiting for transfers between devices: 11.6 us -> 9.68 us  [on_device(): first = lax.all_to_all(msg, 'dev', split_axis=0, concat_axis=0, tiled=True)]
    unnamed x14 -> x18, local copies, waits for them, and re-layouts: 0.04 us -> 1.89 us
    ppermute x3, starting transfers between devices: 3.91 us -> 5.68 us  [on_device(): lax.ppermute(chunk, 'grp', [(i, (i - 2 * step) % 8) for i in range(8)])]
    pallas_call x9 -> x10, Pallas kernels: 17.2 us -> 18.9 us  [call(): pl.pallas_call(kernel, out_shape=shapes, in_specs=[SM] * len(scalars) + (...]
  transfers between devices with their start and end apart: 14 -> 14, of which waited for: 8 -> 4; matrix products, arithmetic and copies ran while one was open for 0% -> 0% of each run, Pallas kernels for 3% -> 5%
where the time goes in v5:
time: 118 us; the launch traced here: 117 us
  starting transfers between devices  45.5 us (39%)
  waiting for transfers between devices  31.3 us (27%)
  Pallas kernels  18.9 us (16%)
  blocking collectives  17.5 us (15%)
  local copies, waits for them, and re-layouts  2.24 us (2%)
  between operations  1.78 us (2%)
    pallas_call x10, Pallas kernels, call(): pl.pallas_call(kernel, out_shape=shapes, in_specs=[SM] * len(scalars) + (...  18.9 us
    all_to_all x1, blocking collectives, on_device(): back = lax.all_to_all(sums, 'dev', split_axis=0, concat_axis=0, tiled=True)  17.5 us
    all_to_all x1, starting transfers between devices, on_device(): first = lax.all_to_all(msg, 'dev', split_axis=0, concat_axis=0, tiled=True)  12 us
    all_to_all x1, waiting for transfers between devices, on_device(): lax.all_to_all(terms, 'dev', split_axis=0, concat_axis=0, tiled=True)  10.4 us
    all_to_all x1, waiting for transfers between devices, on_device(): first = lax.all_to_all(msg, 'dev', split_axis=0, concat_axis=0, tiled=True)  9.68 us
    all_to_all x1, waiting for transfers between devices, on_device(): lax.all_to_all(answer, 'dev', split_axis=0, concat_axis=0, tiled=True)  9.38 us
    ppermute x4, starting transfers between devices, on_device(): others = [lax.ppermute(x, 'grp', swap) for x in mine]  8.08 us
    all_to_all x1, starting transfers between devices, on_device(): lax.all_to_all(answer, 'dev', split_axis=0, concat_axis=0, tiled=True)  6.3 us
  transfers between devices with their start and end apart: 14, of which 4 were waited for; matrix products, arithmetic and copies ran while one was open for 0% of the time, Pallas kernels for 5%

profile of v5, /device:TPU:1, one launch (start us, length us, event | category | flops | bytes accessed | tf_op | source)
XLA Modules:
  0.0 117.3 jit_solution(13236286928669801395)
XLA Ops:
  1.4 2.4 %ask.1 = bf16[32,32,128]{2,1,0:T(8,128)(2,1)} custom-call(s32[1]{0:T(128)S(6)} %copy.26.counts, bf16[2,128,512]{2,1,0:T(8,128)(2,1)} %feat.5, s32[2,26]{1,0:T(2,128)} %owner.1, s32[2,26]{1,0:T(2,128)} %slot.1, bf16[128,1024]{1,0:T(8,128)(2,1)} %constant.10.clone.choice), custom_call_target="tpu_custom_call" | custom-call | flops 2000000 | bytes 786848 | tf_op jit(solution)/shard_map/ask/pallas_call | solution.py:447
  3.7 12.0 %all-to-all-start = ((bf16[32,32,128]{2,1,0:T(8,128)(2,1)}), bf16[32,32,128]{2,1,0:T(8,128)(2,1)S(1)}, u32[]{:S(2)}, u32[]{:S(2)}) async-start(bf16[32,32,128]{2,1,0:T(8,128)(2,1)} %ask.1), calls=%async_computation | async-start | bytes 524288 | tf_op jit(solution)/shard_map/all_to_all | solution.py:506
  15.8 9.7 %all-to-all-done.got = bf16[32,32,128]{2,1,0:T(8,128)(2,1)S(1)} async-done(((bf16[32,32,128]{2,1,0:T(8,128)(2,1)}), bf16[32,32,128]{2,1,0:T(8,128)(2,1)S(1)}, u32[]{:S(2)}, u32[]{:S(2)}) %all-to-all-start) | async-done | bytes 262176 | tf_op jit(solution)/shard_map/all_to_all | solution.py:506
  25.5 1.8 %route.1 = bf16[32,32,128]{2,1,0:T(8,128)(2,1)} custom-call(bf16[32,32,128]{2,1,0:T(8,128)(2,1)S(1)} %all-to-all-done.got), custom_call_target="tpu_custom_call" | custom-call | flops 300000000 | bytes 524288 | tf_op jit(solution)/shard_map/route/pallas_call | solution.py:447
  27.2 6.3 %all-to-all-start.1 = ((bf16[32,32,128]{2,1,0:T(8,128)(2,1)}), bf16[32,32,128]{2,1,0:T(8,128)(2,1)S(1)}, u32[]{:S(2)}, u32[]{:S(2)}) async-start(bf16[32,32,128]{2,1,0:T(8,128)(2,1)} %route.1), calls=%async_computation.1 | async-start | bytes 524288 | tf_op jit(solution)/shard_map/all_to_all | solution.py:521
  33.7 0.1 pad_maximum_fusion.weight
  33.8 9.4 %all-to-all-done.1.got = bf16[32,32,128]{2,1,0:T(8,128)(2,1)S(1)} async-done(((bf16[32,32,128]{2,1,0:T(8,128)(2,1)}), bf16[32,32,128]{2,1,0:T(8,128)(2,1)S(1)}, u32[]{:S(2)}, u32[]{:S(2)}) %all-to-all-start.1) | async-done | bytes 262176 | tf_op jit(solution)/shard_map/all_to_all | solution.py:521
  43.2 6.7 %forward.1 = (bf16[2,128,512]{2,1,0:T(8,128)(2,1)S(1)}, f32[2,128,512]{2,1,0:T(8,128)S(1)}, bf16[128,16]{1,0:T(8,128)(2,1)S(1)}, bf16[4096,128]{1,0:T(8,128)(2,1)S(1)}, bf16[2048,128]{1,0:T(8,128)(2,1)}) custom-call(s32[1]{0:T(128)S(6)} %copy.26.counts, s32[2]{0:T(128)S(1)} %copy-done.4, s32[2]{0:T(128)S(1)} %copy-done.5, s32[1]{0:T(128)} %bitcast.core, ...), custom_call_target="tpu_custom_call" | custom-call | flops 2000000000 | bytes 4165632 | tf_op jit(solution)/shard_map/forward/pallas_call | solution.py:447
  49.9 0.8 copy-done.6
  50.7 3.6 %collective-permute-start = (bf16[2048,128]{1,0:T(8,128)(2,1)}, bf16[2048,128]{1,0:T(8,128)(2,1)S(1)}, u32[]{:S(2)}, u32[]{:S(2)}) collective-permute-start(bf16[2048,128]{1,0:T(8,128)(2,1)} %get-tuple-element.31), channel_id=1, source_target_pairs={{0,32},{32,0},{64,96},{96,64},{128,160},{160,128},{192,224},{224,1... | collective-permute-start | bytes 1572872 | tf_op jit(solution)/shard_map/ppermute | solution.py:551
  54.3 1.7 %collective-permute-done.other = bf16[2048,128]{1,0:T(8,128)(2,1)S(1)} collective-permute-done((bf16[2048,128]{1,0:T(8,128)(2,1)}, bf16[2048,128]{1,0:T(8,128)(2,1)S(1)}, u32[]{:S(2)}, u32[]{:S(2)}) %collective-permute-start) | collective-permute-done | bytes 524320 | tf_op jit(solution)/shard_map/ppermute | solution.py:551
  56.0 0.1 pair.1
  56.2 2.8 %collective-permute-start.1 = (bf16[512,128]{1,0:T(8,128)(2,1)S(1)}, bf16[512,128]{1,0:T(8,128)(2,1)S(1)}, u32[]{:S(2)}, u32[]{:S(2)}) collective-permute-start(bf16[512,128]{1,0:T(8,128)(2,1)S(1)} %get-tuple-element.39), channel_id=1, source_target_pairs={{0,128},{32,160},{64,192},{96,224},{128,0},{160,32},{192,64},{224,... | collective-permute-start | bytes 393224 | tf_op jit(solution)/shard_map/ppermute | solution.py:560
  59.0 0.3 collective-permute-start.2
  59.3 2.4 %collective-permute-start.3 = (bf16[512,128]{1,0:T(8,128)(2,1)S(1)}, bf16[512,128]{1,0:T(8,128)(2,1)S(1)}, u32[]{:S(2)}, u32[]{:S(2)}) collective-permute-start(bf16[512,128]{1,0:T(8,128)(2,1)S(1)} %get-tuple-element.41), channel_id=1, source_target_pairs={{0,192},{32,224},{64,0},{96,32},{128,64},{160,96},{192,128},{224,1... | collective-permute-start | bytes 393224 | tf_op jit(solution)/shard_map/ppermute | solution.py:560
  61.7 1.0 copy-done.7
  62.7 3.1 %backward.1 = (f32[2,512,128]{2,1,0:T(8,128)S(1)}, bf16[2,128,512]{2,1,0:T(8,128)(2,1)}, bf16[32,48,128]{2,1,0:T(8,128)(2,1)}) custom-call(s32[1]{0:T(128)S(6)} %copy.26.counts, bf16[2,128,512]{2,1,0:T(8,128)(2,1)S(1)} %copy-done, bf16[2,128,512]{2,1,0:T(8,128)(2,1)S(1)} %get-tuple-element.33.grad_t, f32[2,128,512]{2,1,0:T(8,128)S(1)} %copy-done.7, ...), custom_call_target="tpu_custom_call" | custom-call | flops 4000000000 | bytes 3117056 | tf_op jit(solution)/shard_map/backward/pallas_call | solution.py:447
  65.8 0.7 join.1
  66.6 4.3 %all-to-all-start.2 = ((bf16[32,48,128]{2,1,0:T(8,128)(2,1)}), bf16[32,48,128]{2,1,0:T(8,128)(2,1)S(1)}, u32[]{:S(2)}, u32[]{:S(2)}) async-start(bf16[32,48,128]{2,1,0:T(8,128)(2,1)} %join.1), calls=%async_computation.2 | async-start | bytes 786432 | tf_op jit(solution)/shard_map/all_to_all | solution.py:593
  70.8 0.2 slice_reduce_fusion
  71.0 0.1 broadcast_in_dim.7
  71.1 10.4 %all-to-all-done.2.got = bf16[32,48,128]{2,1,0:T(8,128)(2,1)S(1)} async-done(((bf16[32,48,128]{2,1,0:T(8,128)(2,1)}), bf16[32,48,128]{2,1,0:T(8,128)(2,1)S(1)}, u32[]{:S(2)}, u32[]{:S(2)}) %all-to-all-start.2) | async-done | bytes 393248 | tf_op jit(solution)/shard_map/all_to_all | solution.py:593
  81.6 0.8 merge.1
  82.4 17.5 %all_to_all.20.got = bf16[32,48,128]{2,1,0:T(8,128)(2,1)S(1)} all-to-all(bf16[32,48,128]{2,1,0:T(8,128)(2,1)S(1)} %merge.1), channel_id=1, replica_groups=mesh['grp'=8,'dev'=32] {'dev'}, dimensions={0} | all-to-all | bytes 786432 | tf_op jit(solution)/shard_map/all_to_all | solution.py:603
  99.9 3.2 %collective-permute-start.6 = (bf16[512,128]{1,0:T(8,128)(2,1)S(1)}, bf16[512,128]{1,0:T(8,128)(2,1)S(1)}, u32[]{:S(2)}, u32[]{:S(2)}) collective-permute-start(bf16[512,128]{1,0:T(8,128)(2,1)S(1)} %bitcast.7), channel_id=1, source_target_pairs={{0,64},{32,96},{64,128},{96,160},{128,192},{160,224},{192,0},{224,... | collective-permute-start | bytes 393224 | tf_op jit(solution)/shard_map/ppermute | solution.py:606
  103.1 2.5 %collective-permute-start.4 = (bf16[512,128]{1,0:T(8,128)(2,1)S(1)}, bf16[512,128]{1,0:T(8,128)(2,1)S(1)}, u32[]{:S(2)}, u32[]{:S(2)}) collective-permute-start(bf16[512,128]{1,0:T(8,128)(2,1)S(1)} %bitcast.9), channel_id=1, source_target_pairs={{0,192},{32,224},{64,0},{96,32},{128,64},{160,96},{192,128},{224,1... | collective-permute-start | bytes 393224 | tf_op jit(solution)/shard_map/ppermute | solution.py:606
  105.6 5.2 %collective-permute-start.7 = (bf16[512,128]{1,0:T(8,128)(2,1)S(1)}, bf16[512,128]{1,0:T(8,128)(2,1)S(1)}, u32[]{:S(2)}, u32[]{:S(2)}) collective-permute-start(bf16[512,128]{1,0:T(8,128)(2,1)S(1)} %bitcast.10), channel_id=1, source_target_pairs={{0,32},{32,0},{64,96},{96,64},{128,160},{160,128},{192,224},{224,1... | collective-permute-start | bytes 393224 | tf_op jit(solution)/shard_map/ppermute | solution.py:620
  110.8 1.3 %finish.1 = bf16[2,128,512]{2,1,0:T(8,128)(2,1)} custom-call(s32[1]{0:T(128)S(6)} %copy.26.counts, bf16[32,48,128]{2,1,0:T(8,128)(2,1)S(1)} %all_to_all.20.got, f32[2,512,128]{2,1,0:T(8,128)S(1)} %get-tuple-element.42.own, bf16[2,128,512]{2,1,0:T(8,128)(2,1)S(1)} %copy-done.1), custom_call_target="tpu_custom_call" | custom-call | flops 300000000 | bytes 1441792 | tf_op jit(solution)/shard_map/finish/pallas_call | solution.py:447
  112.1 2.4 %collective-permute-start.8 = (bf16[512,128]{1,0:T(8,128)(2,1)S(1)}, bf16[512,128]{1,0:T(8,128)(2,1)S(1)}, u32[]{:S(2)}, u32[]{:S(2)}) collective-permute-start(bf16[512,128]{1,0:T(8,128)(2,1)S(1)} %collective-permute-done.4.refs_1_), channel_id=1, source_target_pairs={{0,32},{32,0},{64,96},{96,64},{128,160},{160,128},{192,224},{224,1... | collective-permute-start | bytes 393224 | tf_op jit(solution)/shard_map/ppermute | solution.py:620
  114.5 0.5 collective-permute-start.10
  115.0 1.1 assemble.2
  116.1 1.1 assemble.3
  (31 shorter events, 0.2 us)
Async XLA Ops:
  0.6 32.9 %copy-start.8 = (bf16[27,128,128]{2,1,0:T(8,128)(2,1)S(1)}, bf16[27,128,128]{2,1,0:T(8,128)(2,1)}, u32[]{:S(2)}) copy-start(bf16[27,128,128]{2,1,0:T(8,128)(2,1)} %param.13) | copy-start | bytes 2654212
  3.7 21.7 %all-to-all-start = ((bf16[32,32,128]{2,1,0:T(8,128)(2,1)}), bf16[32,32,128]{2,1,0:T(8,128)(2,1)S(1)}, u32[]{:S(2)}, u32[]{:S(2)}) async-start(bf16[32,32,128]{2,1,0:T(8,128)(2,1)} %ask.1), calls=%async_computation | async-start | bytes 524288 | tf_op jit(solution)/shard_map/all_to_all | solution.py:506
  27.2 16.0 %all-to-all-start.1 = ((bf16[32,32,128]{2,1,0:T(8,128)(2,1)}), bf16[32,32,128]{2,1,0:T(8,128)(2,1)S(1)}, u32[]{:S(2)}, u32[]{:S(2)}) async-start(bf16[32,32,128]{2,1,0:T(8,128)(2,1)} %route.1), calls=%async_computation.1 | async-start | bytes 524288 | tf_op jit(solution)/shard_map/all_to_all | solution.py:521
  33.5 9.7 %copy-start = (bf16[2,128,512]{2,1,0:T(8,128)(2,1)S(1)}, bf16[2,128,512]{2,1,0:T(8,128)(2,1)}, u32[]{:S(2)}) copy-start(bf16[2,128,512]{2,1,0:T(8,128)(2,1)} %feat.5) | copy-start | bytes 786436
  33.6 9.6 %copy-start.1 = (bf16[2,128,512]{2,1,0:T(8,128)(2,1)S(1)}, bf16[2,128,512]{2,1,0:T(8,128)(2,1)}, u32[]{:S(2)}) copy-start(bf16[2,128,512]{2,1,0:T(8,128)(2,1)} %gout.3) | copy-start | bytes 786436
  33.6 9.6 %copy-start.2 = (bf16[128,256]{1,0:T(8,128)(2,1)S(1)}, bf16[128,256]{1,0:T(8,128)(2,1)}, u32[]{:S(2)}) copy-start(bf16[128,256]{1,0:T(8,128)(2,1)} %up.1) | copy-start | bytes 196612
  33.6 9.6 %copy-start.3 = (bf16[256,128]{1,0:T(8,128)(2,1)S(1)}, bf16[256,128]{1,0:T(8,128)(2,1)}, u32[]{:S(2)}) copy-start(bf16[256,128]{1,0:T(8,128)(2,1)} %down.1) | copy-start | bytes 196612
  33.6 9.6 %copy-start.4 = (s32[2]{0:T(128)S(1)}, s32[2]{0:T(128)}, u32[]{:S(2)}) copy-start(s32[2]{0:T(128)} %parent.1) | copy-start | bytes 28
  33.6 9.6 %copy-start.5 = (s32[2]{0:T(128)S(1)}, s32[2]{0:T(128)}, u32[]{:S(2)}) copy-start(s32[2]{0:T(128)} %child.1) | copy-start | bytes 28
  49.9 0.8 copy-start.6
  50.7 5.3 %collective-permute-start = (bf16[2048,128]{1,0:T(8,128)(2,1)}, bf16[2048,128]{1,0:T(8,128)(2,1)S(1)}, u32[]{:S(2)}, u32[]{:S(2)}) collective-permute-start(bf16[2048,128]{1,0:T(8,128)(2,1)} %get-tuple-element.31), channel_id=1, source_target_pairs={{0,32},{32,0},{64,96},{96,64},{128,160},{160,128},{192,224},{224,1... | collective-permute-start | bytes 1572872 | tf_op jit(solution)/shard_map/ppermute | solution.py:551
  56.2 9.6 %collective-permute-start.1 = (bf16[512,128]{1,0:T(8,128)(2,1)S(1)}, bf16[512,128]{1,0:T(8,128)(2,1)S(1)}, u32[]{:S(2)}, u32[]{:S(2)}) collective-permute-start(bf16[512,128]{1,0:T(8,128)(2,1)S(1)} %get-tuple-element.39), channel_id=1, source_target_pairs={{0,128},{32,160},{64,192},{96,224},{128,0},{160,32},{192,64},{224,... | collective-permute-start | bytes 393224 | tf_op jit(solution)/shard_map/ppermute | solution.py:560
  59.0 6.8 %collective-permute-start.2 = (bf16[512,128]{1,0:T(8,128)(2,1)S(1)}, bf16[512,128]{1,0:T(8,128)(2,1)S(1)}, u32[]{:S(2)}, u32[]{:S(2)}) collective-permute-start(bf16[512,128]{1,0:T(8,128)(2,1)S(1)} %get-tuple-element.40), channel_id=1, source_target_pairs={{0,64},{32,96},{64,128},{96,160},{128,192},{160,224},{192,0},{224,... | collective-permute-start | bytes 393224 | tf_op jit(solution)/shard_map/ppermute | solution.py:560
  59.3 6.5 %collective-permute-start.3 = (bf16[512,128]{1,0:T(8,128)(2,1)S(1)}, bf16[512,128]{1,0:T(8,128)(2,1)S(1)}, u32[]{:S(2)}, u32[]{:S(2)}) collective-permute-start(bf16[512,128]{1,0:T(8,128)(2,1)S(1)} %get-tuple-element.41), channel_id=1, source_target_pairs={{0,192},{32,224},{64,0},{96,32},{128,64},{160,96},{192,128},{224,1... | collective-permute-start | bytes 393224 | tf_op jit(solution)/shard_map/ppermute | solution.py:560
  61.7 1.0 copy-start.7
  66.6 15.0 %all-to-all-start.2 = ((bf16[32,48,128]{2,1,0:T(8,128)(2,1)}), bf16[32,48,128]{2,1,0:T(8,128)(2,1)S(1)}, u32[]{:S(2)}, u32[]{:S(2)}) async-start(bf16[32,48,128]{2,1,0:T(8,128)(2,1)} %join.1), calls=%async_computation.2 | async-start | bytes 786432 | tf_op jit(solution)/shard_map/all_to_all | solution.py:593
  99.9 12.2 %collective-permute-start.6 = (bf16[512,128]{1,0:T(8,128)(2,1)S(1)}, bf16[512,128]{1,0:T(8,128)(2,1)S(1)}, u32[]{:S(2)}, u32[]{:S(2)}) collective-permute-start(bf16[512,128]{1,0:T(8,128)(2,1)S(1)} %bitcast.7), channel_id=1, source_target_pairs={{0,64},{32,96},{64,128},{96,160},{128,192},{160,224},{192,0},{224,... | collective-permute-start | bytes 393224 | tf_op jit(solution)/shard_map/ppermute | solution.py:606
  103.1 9.0 %collective-permute-start.5 = (bf16[512,128]{1,0:T(8,128)(2,1)S(1)}, bf16[512,128]{1,0:T(8,128)(2,1)S(1)}, u32[]{:S(2)}, u32[]{:S(2)}) collective-permute-start(bf16[512,128]{1,0:T(8,128)(2,1)S(1)} %bitcast.8), channel_id=1, source_target_pairs={{0,128},{32,160},{64,192},{96,224},{128,0},{160,32},{192,64},{224,... | collective-permute-start | bytes 393224 | tf_op jit(solution)/shard_map/ppermute | solution.py:606
  103.1 9.0 %collective-permute-start.4 = (bf16[512,128]{1,0:T(8,128)(2,1)S(1)}, bf16[512,128]{1,0:T(8,128)(2,1)S(1)}, u32[]{:S(2)}, u32[]{:S(2)}) collective-permute-start(bf16[512,128]{1,0:T(8,128)(2,1)S(1)} %bitcast.9), channel_id=1, source_target_pairs={{0,192},{32,224},{64,0},{96,32},{128,64},{160,96},{192,128},{224,1... | collective-permute-start | bytes 393224 | tf_op jit(solution)/shard_map/ppermute | solution.py:606
  105.6 10.5 %collective-permute-start.7 = (bf16[512,128]{1,0:T(8,128)(2,1)S(1)}, bf16[512,128]{1,0:T(8,128)(2,1)S(1)}, u32[]{:S(2)}, u32[]{:S(2)}) collective-permute-start(bf16[512,128]{1,0:T(8,128)(2,1)S(1)} %bitcast.10), channel_id=1, source_target_pairs={{0,32},{32,0},{64,96},{96,64},{128,160},{160,128},{192,224},{224,1... | collective-permute-start | bytes 393224 | tf_op jit(solution)/shard_map/ppermute | solution.py:620
  112.1 4.0 %collective-permute-start.8 = (bf16[512,128]{1,0:T(8,128)(2,1)S(1)}, bf16[512,128]{1,0:T(8,128)(2,1)S(1)}, u32[]{:S(2)}, u32[]{:S(2)}) collective-permute-start(bf16[512,128]{1,0:T(8,128)(2,1)S(1)} %collective-permute-done.4.refs_1_), channel_id=1, source_target_pairs={{0,32},{32,0},{64,96},{96,64},{128,160},{160,128},{192,224},{224,1... | collective-permute-start | bytes 393224 | tf_op jit(solution)/shard_map/ppermute | solution.py:620
  114.5 1.6 %collective-permute-start.9 = (bf16[512,128]{1,0:T(8,128)(2,1)S(1)}, bf16[512,128]{1,0:T(8,128)(2,1)S(1)}, u32[]{:S(2)}, u32[]{:S(2)}) collective-permute-start(bf16[512,128]{1,0:T(8,128)(2,1)S(1)} %collective-permute-done.5.refs_2_), channel_id=1, source_target_pairs={{0,32},{32,0},{64,96},{96,64},{128,160},{160,128},{192,224},{224,1... | collective-permute-start | bytes 393224 | tf_op jit(solution)/shard_map/ppermute | solution.py:620
  114.5 1.6 %collective-permute-start.10 = (bf16[512,128]{1,0:T(8,128)(2,1)S(1)}, bf16[512,128]{1,0:T(8,128)(2,1)S(1)}, u32[]{:S(2)}, u32[]{:S(2)}) collective-permute-start(bf16[512,128]{1,0:T(8,128)(2,1)S(1)} %collective-permute-done.6.refs_3_), channel_id=1, source_target_pairs={{0,32},{32,0},{64,96},{96,64},{128,160},{160,128},{192,224},{224,1... | collective-permute-start | bytes 393224 | tf_op jit(solution)/shard_map/ppermute | solution.py:620

commit v6 on v5

--- a/solution.py
+++ b/solution.py
@@ -104,11 +104,11 @@
 
 
 def ask_kernel(
-    counts, feat, owner, slot, choice, msg,
-    feat_v, owner_v, slot_v, choice_v, bricks, tables, voxels, pc, rows, msg_v, sems,
+    live_count, feat, owner, slot, choice, msg, flags,
+    counts, feat_v, owner_v, slot_v, choice_v, bricks, tables, voxels, pc, rows, msg_v, flags_v, sems,
 ):
     pairs = (
-        (owner, owner_v), (slot, slot_v), (choice, choice_v),
+        (owner, owner_v), (slot, slot_v), (choice, choice_v), (live_count, counts),
         (feat.at[0], feat_v.at[0]), (feat.at[1], feat_v.at[1]),
     )
     copies = [
@@ -117,7 +117,7 @@
     for copy in copies:
         copy.start()
     bricks[...] = jnp.zeros((16, 128), F32)
-    for copy in copies[:3]:
+    for copy in copies[:4]:
         copy.wait()
     named = jnp.where(owner_v[...] >= 0, owner_v[...] * 2 + slot_v[...], -1)
     bricks[0:2, 0:26] = named.astype(F32)
@@ -125,9 +125,12 @@
     for group in range(8):
         for s in range(2):
             tables[s, group : group + 1, :] = asked[s : s + 1, group * 128 : group * 128 + 128]
-    sent = []
-    for s in range(2):
-        copies[3 + s].wait()
+    slots = lax.broadcasted_iota(jnp.int32, (8, 128), 0)
+    flags_v[...] = (slots < counts[0]).astype(F32)
+    sent = [pltpu.make_async_copy(flags_v, flags, sems.at[8])]
+    sent[0].start()
+    for s in range(2):
+        copies[4 + s].wait()
         live = (counts[0] > s).astype(F32)
         voxels[s] = (feat_v[s].astype(F32) * live).T
         for d in OFFSETS:
@@ -136,8 +139,8 @@
         to_shares(pc.at[s], rows.at[s], tables[s])
         at = pl.ds(16 * s, 16)
         msg_v[:, at, :] = rows[s].astype(BF).reshape(32, 16, 128)
-        sent.append(pltpu.make_async_copy(msg_v.at[:, at, :], msg.at[:, at, :], sems.at[5 + s]))
-        sent[s].start()
+        sent.append(pltpu.make_async_copy(msg_v.at[:, at, :], msg.at[:, at, :], sems.at[6 + s]))
+        sent[-1].start()
     for copy in sent:
         copy.wait()
 
@@ -148,43 +151,40 @@
     return (rows == lanes).astype(F32).astype(BF)
 
 
-def route_kernel(got, out, hot, out_v, sems):
+def route_kernel(got, out, named, hot):
     same = jnp.broadcast_to(same_part()[None], (32, 16, 128))
     zero = jnp.zeros((32, 16, 128), BF)
     ones = jnp.ones((128, 128), BF)
     part = lax.broadcasted_iota(jnp.int32, (16, 128), 0)
     lanes = lax.broadcasted_iota(jnp.int32, (16, 128), 1)
     place = (lanes == part + 32)[None]
-    sent = []
-    for s in range(2):
-        at = pl.ds(16 * s, 16)
-        table = got[:, at, :].astype(F32)[:, 15:16, :]
+    for s in range(2):
+        table = got[:, 16 * s : 16 * s + 16, :].astype(F32)[:, 15:16, :]
         table = jnp.where(place, jnp.broadcast_to(table, (32, 16, 128)), 0.0)
-        asked = nn(table.astype(BF).reshape(512, 128), ones).astype(BF).reshape(32, 16, 128)
+        asked = nn(table.astype(BF).reshape(512, 128), ones)
+        named[s] = asked.T[0:16].astype(BF)
+        asked = asked.astype(BF).reshape(32, 16, 128)
         for n in range(8):
             here = ((lanes >> 4) + 8 * n).astype(F32).astype(BF)
             picked = jnp.where(asked == here[None], same, zero)
-            hot[s, :, n * 128 : n * 128 + 128] = picked.reshape(512, 128)
-        answer = nn(hot[s], got[...].reshape(1024, 128)).astype(BF)
-        out_v[:, at, :] = answer.reshape(32, 16, 128)
-        sent.append(pltpu.make_async_copy(out_v.at[:, at, :], out.at[:, at, :], sems.at[s]))
-        sent[s].start()
-    for copy in sent:
-        copy.wait()
+            hot[s * 512 : s * 512 + 512, n * 128 : n * 128 + 128] = picked.reshape(512, 128)
+    answer = nn(hot[...], got[...].reshape(1024, 128)).astype(BF)
+    for s in range(2):
+        out[:, 16 * s : 16 * s + 16, :] = answer[s * 512 : s * 512 + 512].reshape(32, 16, 128)
 
 
 def forward_kernel(
-    counts, parent, child, core, feat, got, gout, weight, up, down,
-    grad_t, acts, lift, wsum, send,
-    rows_all, pc_all, mine_all, s0_all, s1_all, s2_all, cols, pooled, grad_pooled,
+    parent, child, core, flags, feat, got, gout, weight, up, down,
+    out, grad_t, wsum, send,
+    rows_all, pc_all, mine_all, s0_all, s1_all, s2_all, cols, pooled, grad_pooled, out_v, sem,
 ):
     eye = identity()
-    slopes = []
+    acts, slopes = [], []
     for s in range(2):
         rows, pc, mine, s0, s1, s2 = (
             x.at[s] for x in (rows_all, pc_all, mine_all, s0_all, s1_all, s2_all)
         )
-        live = (counts[0] > s).astype(F32)
+        live = flags[s : s + 1, 0:1]
         pool = pool_rows(s)
         mine[...] = (feat[s].astype(F32) * live).T
         grad_pooled[s] = nt(pool, gout[s]) * live
@@ -220,21 +220,20 @@
                     cols[at : at + 64, (3 * b + c) * 128 : (3 * b + c) * 128 + 128] = ref[
                         pl.ds(start, 64), :
                     ].astype(BF)
-        taps = nn(cols[640 * s : 640 * s + 640, :], weight[...])
-        pre = taps[0:512, 0:128] + taps[64:576, 128:256] + taps[128:640, 256:384]
+        pre = nn(cols[640 * s : 640 * s + 512, :], weight[0])
+        pre = pre + nn(cols[640 * s + 64 : 640 * s + 576, :], weight[1])
+        pre = pre + nn(cols[640 * s + 128 : 640 * s + 640, :], weight[2])
         pre = pre.T
         gate = 1.0 / (1.0 + jnp.exp(-pre))
         active = pre * gate
-        acts[s] = active
+        acts.append(active)
         slopes.append(gate * (1.0 + pre * (1.0 - gate)))
         high = active.astype(BF)
         low = (active - high.astype(F32)).astype(BF)
         pooled[s] = nt(pool, high) + nt(pool, low)
     second = lax.broadcasted_iota(jnp.int32, (16, 1), 0) >= 8
     valid = [
-        (
-            (counts[0] > s) & (parent[s] >= 0) & (parent[s] * 64 + child[s] >= 0)
-        ).astype(F32)
+        ((parent[s] >= 0) & (parent[s] * 64 + child[s] >= 0)).astype(F32) * flags[s : s + 1, 0:1]
         for s in range(2)
     ]
     valid = jnp.where(second, valid[1], valid[0])
@@ -247,12 +246,16 @@
     grad_pre = grad_pre.astype(BF)
     coarse_out = nn(coarse_mid, down[...]).astype(BF)
     grad_cin = nt(grad_pre, up[...]).astype(BF)
-    lift[...] = nt(eye, coarse_out).astype(BF)
+    lift = nt(eye, coarse_out).astype(BF)
     back = nt(eye, grad_cin).astype(BF)
     for s in range(2):
-        live = (counts[0] > s).astype(F32)
-        grad_in = gout[s].astype(F32) * live + nn(back, pool_rows(s)) * (1.0 / 64.0)
+        live = flags[s : s + 1, 0:1]
+        pool = pool_rows(s)
+        grad_in = gout[s].astype(F32) * live + nn(back, pool) * (1.0 / 64.0)
         grad_t[s] = (grad_in * slopes[s]).astype(BF)
+        out_v[s] = (feat[s].astype(F32) * live + acts[s] + nn(lift, pool)).astype(BF)
+    copy = pltpu.make_async_copy(out_v, out, sem.at[0])
+    copy.start()
 
     def put(block, value):
         wsum[pl.ds(block * 128, 128), :] = value.astype(BF)
@@ -270,6 +273,7 @@
         for n in range(9):
             put(9 * a + n, nt(eye, total[:, n * 128 : n * 128 + 128]))
     send[...] = wsum[pl.ds(pl.multiple_of((1 - core[0]) * 2048, 2048), 2048), :]
+    copy.wait()
 
 
 def pair_kernel(core, line, wsum, other, own, one, two, three):
@@ -279,24 +283,10 @@
         ref[...] = (kept + other[pl.ds(at, 512), :].astype(F32)).astype(ref.dtype)
 
 
-def backward_kernel(
-    counts, feat, grad_t, acts, lift, weight,
-    own, out, msg,
-    lhs, acc_all, pc_all, rows_all, out_v, msg_v, sems,
-):
-    sent = []
-
-    def send(src, dst):
-        sent.append(pltpu.make_async_copy(src, dst, sems.at[len(sent)]))
-        sent[-1].start()
-
-    for s in range(2):
-        live = (counts[0] > s).astype(F32)
-        value = feat[s].astype(F32) * live + acts[s] + nn(lift[...], pool_rows(s))
-        out_v[s] = value.astype(BF)
-    send(out_v, out)
+def backward_kernel(grad_t, weight, own, msg, lhs, rhs, acc_all, pc_all, rows_all):
     zero = jnp.zeros((64, 128), BF)
     for a in range(3):
+        rhs[:, a * 128 : a * 128 + 128] = weight[a]
         for n in [*range(a), *range(8 + a, 10)]:
             for s in range(2):
                 lhs[s, n * 64 : n * 64 + 64, a * 128 : a * 128 + 128] = zero
@@ -310,7 +300,7 @@
             lhs[s, a * 64 : a * 64 + 512, a * 128 : a * 128 + 128] = grad
         acc[...] = jnp.zeros_like(acc)
         for b in range(3):
-            part = nt(lhs[s], weight[b * 384 : b * 384 + 384, :])
+            part = nt(lhs[s], rhs[b * 384 : b * 384 + 384, :])
             for c in range(3):
                 for a in range(10):
                     at = pl.ds(8 + (a * 10 + b) * 8, 64)
@@ -341,39 +331,35 @@
                 for b, y in ((-1, 0), (1, 9)):
                     pc[pl.ds(PIECE[a, b, c], 1), :] = ref[pl.ds((x * 10 + y) * 8 + lane, 1), :]
         to_shares(pc, rows)
-        at = pl.ds(16 * s, 16)
-        msg_v[:, at, :] = rows[...].astype(BF).reshape(32, 16, 128)
-        send(msg_v.at[:, at, :], msg.at[:, at, :])
-    for copy in sent:
-        copy.wait()
-
-
-def join_kernel(terms, own, away1, away2, away3, msg, share, sem):
+        msg[:, 16 * s : 16 * s + 16, :] = rows[...].astype(BF).reshape(32, 16, 128)
+
+
+def join_kernel(terms, own, away1, away2, away3, msg):
+    msg[:, 0:32, :] = terms[...]
     total = own[...] + away1[...].astype(F32) + away2[...].astype(F32) + away3[...].astype(F32)
-    share[...] = total.astype(BF).reshape(32, 16, 128)
-    copy = pltpu.make_async_copy(share, msg.at[:, pl.ds(32, 16), :], sem.at[0])
-    copy.start()
-    copy.wait()
-
-
-def merge_kernel(got, table, out, hot):
+    msg[:, 32:48, :] = total.astype(BF).reshape(32, 16, 128)
+
+
+def merge_kernel(got, named, out, hot):
     same = same_part()
     zero = jnp.zeros((16, 128), BF)
     share = jnp.sum(got[:, 32:48, :].astype(F32), axis=0).astype(BF)
     out[:, 32:48, :] = jnp.broadcast_to(share[None], (32, 16, 128))
-    for n in range(8):
-        asked = table[:, n * 128 : n * 128 + 128]
-        for brick in range(64):
-            hot[brick * 16 : brick * 16 + 16, n * 128 : n * 128 + 128] = jnp.where(
-                asked == jnp.full((16, 128), brick, BF), same, zero
-            )
-    total = nn(hot[...], got[:, 0:32, :].reshape(1024, 128))
+    total = jnp.zeros((1024, 128), F32)
+    for s in range(2):
+        for n in range(4):
+            asked = named[s, :, n * 128 : n * 128 + 128]
+            for brick in range(64):
+                hot[s, brick * 16 : brick * 16 + 16, n * 128 : n * 128 + 128] = jnp.where(
+                    asked == jnp.full((16, 128), brick, BF), same, zero
+                )
+        total = total + nn(hot[s], got[:, 16 * s : 16 * s + 16, :].reshape(512, 128))
     out[:, 0:32, :] = total.astype(BF).reshape(32, 32, 128)
 
 
-def finish_kernel(counts, got, own, gout, out, rows, pc, total):
-    for s in range(2):
-        live = (counts[0] > s).astype(F32)
+def finish_kernel(flags, got, own, gout, out, rows, pc, total):
+    for s in range(2):
+        live = flags[s : s + 1, 0:1]
         rows[...] = got[:, 16 * s : 16 * s + 16, :].reshape(512, 128).astype(F32)
         to_pieces(rows, pc)
         total[...] = own[s]
@@ -479,12 +465,13 @@
     core = (grp & 1).reshape(1)
     line = (grp >> 1).reshape(1)
     swap = [(i, i ^ 1) for i in range(8)]
-    (msg,) = call(
+    msg, flags = call(
         ask_kernel,
-        [shape((32, 32, 128), BF)],
-        [counts],
-        [features, neighbour_owner, neighbour_slot, jnp.asarray(choice_table(), BF)],
+        [shape((32, 32, 128), BF), shape((8, 128), F32)],
+        [],
+        [counts, features, neighbour_owner, neighbour_slot, jnp.asarray(choice_table(), BF)],
         [
+            pltpu.SMEM((1,), jnp.int32),
             pltpu.VMEM((2, 128, 512), BF),
             pltpu.VMEM((2, 26), jnp.int32),
             pltpu.VMEM((2, 26), jnp.int32),
@@ -495,45 +482,37 @@
             pltpu.VMEM((2, 512, 128), F32),
             pltpu.VMEM((2, 512, 128), F32),
             pltpu.VMEM((32, 32, 128), BF),
-            pltpu.SemaphoreType.DMA((7,)),
+            pltpu.VMEM((8, 128), F32),
+            pltpu.SemaphoreType.DMA((9,)),
         ],
         flops=2e6,
         limit=60,
-        ins=[HB] * 3 + [pl.BlockSpec(memory_space=pl.ANY)],
-        outs=[HB],
+        ins=[HB] * 4 + [pl.BlockSpec(memory_space=pl.ANY)],
+        outs=[HB] * 2,
         name="ask",
     )
     first = lax.all_to_all(msg, "dev", split_axis=0, concat_axis=0, tiled=True)
-    (answer,) = call(
+    answer, table = call(
         route_kernel,
-        [shape((32, 32, 128), BF)],
+        [shape((32, 32, 128), BF), shape((2, 16, 512), BF)],
         [],
         [first],
-        [
-            pltpu.VMEM((2, 512, 1024), BF),
-            pltpu.VMEM((32, 32, 128), BF),
-            pltpu.SemaphoreType.DMA((2,)),
-        ],
+        [pltpu.VMEM((1024, 1024), BF)],
         flops=3e8,
-        outs=[HB],
         name="route",
     )
     halo = lax.all_to_all(answer, "dev", split_axis=0, concat_axis=0, tiled=True)
-    table = first.reshape(32, 2, 16, 128)[:, :, 15, 32:48].reshape(1, 1024)
-    table = jnp.broadcast_to(table, (16, 1024))
-    taps = conv_weight.reshape(3, 1152, 128)
-    taps = jnp.concatenate([taps[0], taps[1], taps[2]], axis=1)
-    grad_pre, acts, lift, wsum, send = call(
+    weight = conv_weight.reshape(3, 1152, 128)
+    output, grad_pre, wsum, send = call(
         forward_kernel,
         [
             shape((2, 128, 512), BF),
-            shape((2, 128, 512), F32),
-            shape((128, 16), BF),
+            shape((2, 128, 512), BF),
             shape((4096, 128), BF),
             shape((2048, 128), BF),
         ],
-        [counts, parent, child_slot, core],
-        [features, halo, grad_out, taps, coarse_up, coarse_down],
+        [parent, child_slot, core],
+        [flags, features, halo, grad_out, weight, coarse_up, coarse_down],
         [
             pltpu.VMEM((2, 512, 128), F32),
             pltpu.VMEM((2, 512, 128), F32),
@@ -544,8 +523,11 @@
             pltpu.VMEM((1280, 1152), BF),
             pltpu.VMEM((2, 16, 128), F32),
             pltpu.VMEM((2, 16, 128), F32),
+            pltpu.VMEM((2, 128, 512), BF),
+            pltpu.SemaphoreType.DMA((1,)),
         ],
         flops=2e9,
+        outs=[HB, VM, VM, VM],
         name="forward",
     )
     other = lax.ppermute(send, "grp", swap)
@@ -561,34 +543,23 @@
         for step in (2, 1, 3)
     ]
     grad_pre, own_sum = lax.optimization_barrier((grad_pre, own_sum))
-    own, output, terms = call(
+    own, terms = call(
         backward_kernel,
-        [shape((2, 512, 128), F32), shape((2, 128, 512), BF), shape((32, 48, 128), BF)],
-        [counts],
-        [features, grad_pre, acts, lift, taps],
+        [shape((2, 512, 128), F32), shape((32, 32, 128), BF)],
+        [],
+        [grad_pre, weight],
         [
             pltpu.VMEM((2, 640, 384), BF),
+            pltpu.VMEM((1152, 384), BF),
             pltpu.VMEM((2, 3, 816, 128), F32),
             pltpu.VMEM((2, 512, 128), F32),
             pltpu.VMEM((2, 512, 128), F32),
-            pltpu.VMEM((2, 128, 512), BF),
-            pltpu.VMEM((32, 32, 128), BF),
-            pltpu.SemaphoreType.DMA((3,)),
         ],
         flops=4e9,
-        outs=[VM, HB, HB],
         name="backward",
     )
     (terms,) = call(
-        join_kernel,
-        [shape((32, 48, 128), BF)],
-        [],
-        [terms, own_sum, *away],
-        [pltpu.VMEM((32, 16, 128), BF), pltpu.SemaphoreType.DMA((1,))],
-        ins=[HB] + [VM] * 4,
-        outs=[HB],
-        alias={0: 0},
-        name="join",
+        join_kernel, [shape((32, 48, 128), BF)], [], [terms, own_sum, *away], name="join"
     )
     terms = lax.all_to_all(terms, "dev", split_axis=0, concat_axis=0, tiled=True)
     (sums,) = call(
@@ -596,7 +567,7 @@
         [shape((32, 48, 128), BF)],
         [],
         [terms, table],
-        [pltpu.VMEM((1024, 1024), BF)],
+        [pltpu.VMEM((2, 1024, 512), BF)],
         flops=3e8,
         name="merge",
     )
@@ -609,8 +580,8 @@
     (grad_features,) = call(
         finish_kernel,
         [shape((2, 128, 512), BF)],
-        [counts],
-        [back, own, grad_out],
+        [],
+        [flags, back, own, grad_out],
         [pltpu.VMEM((512, 128), F32)] * 3,
         flops=3e8,
         name="finish",

time: 118 us -> 117 us (level)
  blocking collectives: 17.5 us -> 54.8 us
  waiting for transfers between devices: 31.3 us -> 11.9 us
  starting transfers between devices: 45.5 us -> 28.4 us
  Pallas kernels: 18.9 us -> 17.6 us
    all_to_all x0 -> x2, blocking collectives: none -> 36.7 us  [the longest x1 21.7 us: on_device(): first = lax.all_to_all(msg, 'dev', split_axis=0, concat_axis=0, tiled=True)]
    all_to_all x2 -> x0, waiting for transfers between devices: 20.1 us -> none  [the longest x1 10.4 us: on_device(): lax.all_to_all(terms, 'dev', split_axis=0, concat_axis=0, tiled=True)]
    all_to_all x2 -> x0, starting transfers between devices: 16.3 us -> none  [the longest x1 12 us: on_device(): first = lax.all_to_all(msg, 'dev', split_axis=0, concat_axis=0, tiled=True)]
    pallas_call x10, Pallas kernels: 18.9 us -> 17.6 us  [call(): pl.pallas_call(kernel, out_shape=shapes, in_specs=[SM] * len(scalars) + (...]
  transfers between devices with their start and end apart: 14 -> 12, of which waited for: 4 -> 3; matrix products, arithmetic and copies ran while one was open for 0% -> 0% of each run, Pallas kernels for 5% -> 4%
where the time goes in v6:
time: 117 us; the launch traced here: 116 us
  blocking collectives  54.8 us (47%)
  starting transfers between devices  28.4 us (24%)
  Pallas kernels  17.6 us (15%)
  waiting for transfers between devices  11.9 us (10%)
  between operations  1.78 us (2%)
  local copies, waits for them, and re-layouts  1.69 us (1%)
    all_to_all x1, blocking collectives, on_device(): first = lax.all_to_all(msg, 'dev', split_axis=0, concat_axis=0, tiled=True)  21.7 us
    all_to_all x1, blocking collectives, on_device(): back = lax.all_to_all(sums, 'dev', split_axis=0, concat_axis=0, tiled=True)  18.2 us
    pallas_call x10, Pallas kernels, call(): pl.pallas_call(kernel, out_shape=shapes, in_specs=[SM] * len(scalars) + (...  17.6 us
    all_to_all x1, blocking collectives, on_device(): lax.all_to_all(terms, 'dev', split_axis=0, concat_axis=0, tiled=True)  14.9 us
    all_to_all x1, waiting for transfers between devices, on_device(): lax.all_to_all(answer, 'dev', split_axis=0, concat_axis=0, tiled=True)  9.65 us
    ppermute x4, starting transfers between devices, on_device(): others = [lax.ppermute(x, 'grp', swap) for x in mine]  8.08 us
    all_to_all x1, starting transfers between devices, on_device(): lax.all_to_all(answer, 'dev', split_axis=0, concat_axis=0, tiled=True)  6.29 us
    ppermute x3, starting transfers between devices, on_device(): lax.ppermute(away[step - 1], 'grp', [(i, (i + 2 * step) % 8) for i in ran...  5.51 us
  transfers between devices with their start and end apart: 12, of which 3 were waited for; matrix products, arithmetic and copies ran while one was open for 0% of the time, Pallas kernels for 4%

profile of v6, /device:TPU:1, one launch (start us, length us, event | category | flops | bytes accessed | tf_op | source)
XLA Modules:
  0.0 116.2 jit_solution(12442214529608310132)
XLA Ops:
  1.5 2.4 %ask.1 = (bf16[32,32,128]{2,1,0:T(8,128)(2,1)}, f32[8,128]{1,0:T(8,128)}) custom-call(s32[1]{0:T(128)S(6)} %copy.22.live_count, bf16[2,128,512]{2,1,0:T(8,128)(2,1)} %feat.3, s32[2,26]{1,0:T(2,128)} %owner.1, s32[2,26]{1,0:T(2,128)} %slot.1, bf16[128,1024]{1,0:T(8,128)(2,1)} %constant.10.clone.choice), custom_call_target="tpu_custom_call" | custom-call | flops 2000000 | bytes 790948 | tf_op jit(solution)/shard_map/ask/pallas_call | solution.py:433
  3.8 0.0 copy-start.2
  3.9 21.7 %all_to_all.20.got = bf16[32,32,128]{2,1,0:T(8,128)(2,1)S(1)} all-to-all(bf16[32,32,128]{2,1,0:T(8,128)(2,1)} %get-tuple-element.32), channel_id=1, replica_groups=mesh['grp'=8,'dev'=32] {'dev'}, dimensions={0} | all-to-all | bytes 524288 | tf_op jit(solution)/shard_map/all_to_all | solution.py:494
  25.6 1.5 %route.1 = (bf16[32,32,128]{2,1,0:T(8,128)(2,1)}, bf16[2,16,512]{2,1,0:T(8,128)(2,1)S(1)}) custom-call(bf16[32,32,128]{2,1,0:T(8,128)(2,1)S(1)} %all_to_all.20.got), custom_call_target="tpu_custom_call" | custom-call | flops 300000000 | bytes 557056 | tf_op jit(solution)/shard_map/route/pallas_call | solution.py:433
  27.1 6.3 %all-to-all-start.1 = ((bf16[32,32,128]{2,1,0:T(8,128)(2,1)}), bf16[32,32,128]{2,1,0:T(8,128)(2,1)S(1)}, u32[]{:S(2)}, u32[]{:S(2)}) async-start(bf16[32,32,128]{2,1,0:T(8,128)(2,1)} %get-tuple-element.33), calls=%async_computation.1 | async-start | bytes 524288 | tf_op jit(solution)/shard_map/all_to_all | solution.py:504
  33.4 9.7 %all-to-all-done.1.got = bf16[32,32,128]{2,1,0:T(8,128)(2,1)S(1)} async-done(((bf16[32,32,128]{2,1,0:T(8,128)(2,1)}), bf16[32,32,128]{2,1,0:T(8,128)(2,1)S(1)}, u32[]{:S(2)}, u32[]{:S(2)}) %all-to-all-start.1) | async-done | bytes 262176 | tf_op jit(solution)/shard_map/all_to_all | solution.py:504
  43.2 6.8 %forward.1 = (bf16[2,128,512]{2,1,0:T(8,128)(2,1)}, bf16[2,128,512]{2,1,0:T(8,128)(2,1)S(1)}, bf16[4096,128]{1,0:T(8,128)(2,1)S(1)}, bf16[2048,128]{1,0:T(8,128)(2,1)S(1)}) custom-call(s32[2]{0:T(128)S(1)} %copy-done.6, s32[2]{0:T(128)S(1)} %copy-done.7, s32[1]{0:T(128)} %bitcast.core, f32[8,128]{1,0:T(8,128)S(1)} %copy-done.2, ...), custom_call_target="tpu_custom_call" | custom-call | flops 2000000000 | bytes 3903488 | tf_op jit(solution)/shard_map/forward/pallas_call | solution.py:433
  50.0 0.0 copy-start.8
  50.0 0.7 copy-done.8
  50.7 3.6 %collective-permute-start = (bf16[2048,128]{1,0:T(8,128)(2,1)S(1)}, bf16[2048,128]{1,0:T(8,128)(2,1)S(1)}, u32[]{:S(2)}, u32[]{:S(2)}) collective-permute-start(bf16[2048,128]{1,0:T(8,128)(2,1)S(1)} %get-tuple-element.37), channel_id=1, source_target_pairs={{0,32},{32,0},{64,96},{96,64},{128,160},{160,128},{192,224},{224,1... | collective-permute-start | bytes 1572872 | tf_op jit(solution)/shard_map/ppermute | solution.py:533
  54.3 1.5 %collective-permute-done.other = bf16[2048,128]{1,0:T(8,128)(2,1)S(1)} collective-permute-done((bf16[2048,128]{1,0:T(8,128)(2,1)S(1)}, bf16[2048,128]{1,0:T(8,128)(2,1)S(1)}, u32[]{:S(2)}, u32[]{:S(2)}) %collective-permute-start) | collective-permute-done | bytes 524320 | tf_op jit(solution)/shard_map/ppermute | solution.py:533
  55.8 0.1 pair.1
  55.9 2.8 %collective-permute-start.1 = (bf16[512,128]{1,0:T(8,128)(2,1)S(1)}, bf16[512,128]{1,0:T(8,128)(2,1)S(1)}, u32[]{:S(2)}, u32[]{:S(2)}) collective-permute-start(bf16[512,128]{1,0:T(8,128)(2,1)S(1)} %get-tuple-element.42), channel_id=1, source_target_pairs={{0,128},{32,160},{64,192},{96,224},{128,0},{160,32},{192,64},{224,... | collective-permute-start | bytes 393224 | tf_op jit(solution)/shard_map/ppermute | solution.py:542
  58.8 0.3 collective-permute-start.2
  59.1 2.4 %collective-permute-start.3 = (bf16[512,128]{1,0:T(8,128)(2,1)S(1)}, bf16[512,128]{1,0:T(8,128)(2,1)S(1)}, u32[]{:S(2)}, u32[]{:S(2)}) collective-permute-start(bf16[512,128]{1,0:T(8,128)(2,1)S(1)} %get-tuple-element.44), channel_id=1, source_target_pairs={{0,192},{32,224},{64,0},{96,32},{128,64},{160,96},{192,128},{224,1... | collective-permute-start | bytes 393224 | tf_op jit(solution)/shard_map/ppermute | solution.py:542
  61.5 0.9 copy-done.9
  62.4 2.4 %backward.1 = (f32[2,512,128]{2,1,0:T(8,128)S(1)}, bf16[32,32,128]{2,1,0:T(8,128)(2,1)S(1)}) custom-call(bf16[2,128,512]{2,1,0:T(8,128)(2,1)S(1)} %copy-done.9, bf16[3,1152,128]{2,1,0:T(8,128)(2,1)S(1)} %bitcast.10), custom_call_target="tpu_custom_call" | custom-call | flops 4000000000 | bytes 1933312 | tf_op jit(solution)/shard_map/backward/pallas_call | solution.py:433
  64.8 0.0 collective-permute-done.1.away1
  64.9 0.7 collective-permute-done.2.away2
  65.5 0.1 join.1
  65.6 14.9 %all_to_all.21.got = bf16[32,48,128]{2,1,0:T(8,128)(2,1)S(1)} all-to-all(bf16[32,48,128]{2,1,0:T(8,128)(2,1)S(1)} %join.1), channel_id=1, replica_groups=mesh['grp'=8,'dev'=32] {'dev'}, dimensions={0} | all-to-all | bytes 786432 | tf_op jit(solution)/shard_map/all_to_all | solution.py:564
  80.5 0.8 merge.1
  81.3 18.2 %all_to_all.22.got = bf16[32,48,128]{2,1,0:T(8,128)(2,1)S(1)} all-to-all(bf16[32,48,128]{2,1,0:T(8,128)(2,1)S(1)} %merge.1), channel_id=1, replica_groups=mesh['grp'=8,'dev'=32] {'dev'}, dimensions={0} | all-to-all | bytes 786432 | tf_op jit(solution)/shard_map/all_to_all | solution.py:574
  99.5 2.4 %collective-permute-start.6 = (bf16[512,128]{1,0:T(8,128)(2,1)S(1)}, bf16[512,128]{1,0:T(8,128)(2,1)S(1)}, u32[]{:S(2)}, u32[]{:S(2)}) collective-permute-start(bf16[512,128]{1,0:T(8,128)(2,1)S(1)} %bitcast.4), channel_id=1, source_target_pairs={{0,64},{32,96},{64,128},{96,160},{128,192},{160,224},{192,0},{224,... | collective-permute-start | bytes 393224 | tf_op jit(solution)/shard_map/ppermute | solution.py:577
  102.0 2.5 %collective-permute-start.4 = (bf16[512,128]{1,0:T(8,128)(2,1)S(1)}, bf16[512,128]{1,0:T(8,128)(2,1)S(1)}, u32[]{:S(2)}, u32[]{:S(2)}) collective-permute-start(bf16[512,128]{1,0:T(8,128)(2,1)S(1)} %bitcast.6), channel_id=1, source_target_pairs={{0,192},{32,224},{64,0},{96,32},{128,64},{160,96},{192,128},{224,1... | collective-permute-start | bytes 393224 | tf_op jit(solution)/shard_map/ppermute | solution.py:577
  104.5 5.2 %collective-permute-start.7 = (bf16[512,128]{1,0:T(8,128)(2,1)S(1)}, bf16[512,128]{1,0:T(8,128)(2,1)S(1)}, u32[]{:S(2)}, u32[]{:S(2)}) collective-permute-start(bf16[512,128]{1,0:T(8,128)(2,1)S(1)} %bitcast.7), channel_id=1, source_target_pairs={{0,32},{32,0},{64,96},{96,64},{128,160},{160,128},{192,224},{224,1... | collective-permute-start | bytes 393224 | tf_op jit(solution)/shard_map/ppermute | solution.py:591
  109.7 1.3 %finish.1 = bf16[2,128,512]{2,1,0:T(8,128)(2,1)} custom-call(f32[8,128]{1,0:T(8,128)S(1)} %copy-done.2, bf16[32,48,128]{2,1,0:T(8,128)(2,1)S(1)} %all_to_all.22.got, f32[2,512,128]{2,1,0:T(8,128)S(1)} %get-tuple-element.46.own, bf16[2,128,512]{2,1,0:T(8,128)(2,1)S(1)} %copy-done.1), custom_call_target="tpu_custom_call" | custom-call | flops 300000000 | bytes 1445888 | tf_op jit(solution)/shard_map/finish/pallas_call | solution.py:433
  111.0 2.4 %collective-permute-start.8 = (bf16[512,128]{1,0:T(8,128)(2,1)S(1)}, bf16[512,128]{1,0:T(8,128)(2,1)S(1)}, u32[]{:S(2)}, u32[]{:S(2)}) collective-permute-start(bf16[512,128]{1,0:T(8,128)(2,1)S(1)} %collective-permute-done.4.refs_1_), channel_id=1, source_target_pairs={{0,32},{32,0},{64,96},{96,64},{128,160},{160,128},{192,224},{224,1... | collective-permute-start | bytes 393224 | tf_op jit(solution)/shard_map/ppermute | solution.py:591
  113.4 0.0 collective-permute-start.9
  113.4 0.5 collective-permute-start.10
  113.9 1.1 assemble.2
  115.0 1.1 assemble.3
  (26 shorter events, 0.1 us)
Async XLA Ops:
  0.6 42.5 %copy-start = (bf16[2,128,512]{2,1,0:T(8,128)(2,1)S(1)}, bf16[2,128,512]{2,1,0:T(8,128)(2,1)}, u32[]{:S(2)}) copy-start(bf16[2,128,512]{2,1,0:T(8,128)(2,1)} %feat.3) | copy-start | bytes 786436
  0.6 42.5 %copy-start.1 = (bf16[2,128,512]{2,1,0:T(8,128)(2,1)S(1)}, bf16[2,128,512]{2,1,0:T(8,128)(2,1)}, u32[]{:S(2)}) copy-start(bf16[2,128,512]{2,1,0:T(8,128)(2,1)} %gout.3) | copy-start | bytes 786436
  0.7 42.4 %copy-start.7 = (s32[2]{0:T(128)S(1)}, s32[2]{0:T(128)}, u32[]{:S(2)}) copy-start(s32[2]{0:T(128)} %child.1) | copy-start | bytes 28
  0.7 42.4 %copy-start.6 = (s32[2]{0:T(128)S(1)}, s32[2]{0:T(128)}, u32[]{:S(2)}) copy-start(s32[2]{0:T(128)} %parent.1) | copy-start | bytes 28
  0.7 42.4 %copy-start.5 = (bf16[256,128]{1,0:T(8,128)(2,1)S(1)}, bf16[256,128]{1,0:T(8,128)(2,1)}, u32[]{:S(2)}) copy-start(bf16[256,128]{1,0:T(8,128)(2,1)} %down.1) | copy-start | bytes 196612
  0.7 42.4 %copy-start.4 = (bf16[128,256]{1,0:T(8,128)(2,1)S(1)}, bf16[128,256]{1,0:T(8,128)(2,1)}, u32[]{:S(2)}) copy-start(bf16[128,256]{1,0:T(8,128)(2,1)} %up.1) | copy-start | bytes 196612
  0.7 42.4 %copy-start.3 = (bf16[27,128,128]{2,1,0:T(8,128)(2,1)S(1)}, bf16[27,128,128]{2,1,0:T(8,128)(2,1)}, u32[]{:S(2)}) copy-start(bf16[27,128,128]{2,1,0:T(8,128)(2,1)} %param.13) | copy-start | bytes 2654212
  3.8 39.3 %copy-start.2 = (f32[8,128]{1,0:T(8,128)S(1)}, f32[8,128]{1,0:T(8,128)}, u32[]{:S(2)}) copy-start(f32[8,128]{1,0:T(8,128)} %get-tuple-element.31.flags) | copy-start | bytes 12292
  27.1 16.0 %all-to-all-start.1 = ((bf16[32,32,128]{2,1,0:T(8,128)(2,1)}), bf16[32,32,128]{2,1,0:T(8,128)(2,1)S(1)}, u32[]{:S(2)}, u32[]{:S(2)}) async-start(bf16[32,32,128]{2,1,0:T(8,128)(2,1)} %get-tuple-element.33), calls=%async_computation.1 | async-start | bytes 524288 | tf_op jit(solution)/shard_map/all_to_all | solution.py:504
  50.0 0.7 copy-start.8
  50.7 5.1 %collective-permute-start = (bf16[2048,128]{1,0:T(8,128)(2,1)S(1)}, bf16[2048,128]{1,0:T(8,128)(2,1)S(1)}, u32[]{:S(2)}, u32[]{:S(2)}) collective-permute-start(bf16[2048,128]{1,0:T(8,128)(2,1)S(1)} %get-tuple-element.37), channel_id=1, source_target_pairs={{0,32},{32,0},{64,96},{96,64},{128,160},{160,128},{192,224},{224,1... | collective-permute-start | bytes 1572872 | tf_op jit(solution)/shard_map/ppermute | solution.py:533
  55.9 8.9 %collective-permute-start.1 = (bf16[512,128]{1,0:T(8,128)(2,1)S(1)}, bf16[512,128]{1,0:T(8,128)(2,1)S(1)}, u32[]{:S(2)}, u32[]{:S(2)}) collective-permute-start(bf16[512,128]{1,0:T(8,128)(2,1)S(1)} %get-tuple-element.42), channel_id=1, source_target_pairs={{0,128},{32,160},{64,192},{96,224},{128,0},{160,32},{192,64},{224,... | collective-permute-start | bytes 393224 | tf_op jit(solution)/shard_map/ppermute | solution.py:542
  58.8 6.7 %collective-permute-start.2 = (bf16[512,128]{1,0:T(8,128)(2,1)S(1)}, bf16[512,128]{1,0:T(8,128)(2,1)S(1)}, u32[]{:S(2)}, u32[]{:S(2)}) collective-permute-start(bf16[512,128]{1,0:T(8,128)(2,1)S(1)} %get-tuple-element.43), channel_id=1, source_target_pairs={{0,64},{32,96},{64,128},{96,160},{128,192},{160,224},{192,0},{224,... | collective-permute-start | bytes 393224 | tf_op jit(solution)/shard_map/ppermute | solution.py:542
  59.1 6.4 %collective-permute-start.3 = (bf16[512,128]{1,0:T(8,128)(2,1)S(1)}, bf16[512,128]{1,0:T(8,128)(2,1)S(1)}, u32[]{:S(2)}, u32[]{:S(2)}) collective-permute-start(bf16[512,128]{1,0:T(8,128)(2,1)S(1)} %get-tuple-element.44), channel_id=1, source_target_pairs={{0,192},{32,224},{64,0},{96,32},{128,64},{160,96},{192,128},{224,1... | collective-permute-start | bytes 393224 | tf_op jit(solution)/shard_map/ppermute | solution.py:542
  61.5 0.9 copy-start.9
  99.5 11.5 %collective-permute-start.6 = (bf16[512,128]{1,0:T(8,128)(2,1)S(1)}, bf16[512,128]{1,0:T(8,128)(2,1)S(1)}, u32[]{:S(2)}, u32[]{:S(2)}) collective-permute-start(bf16[512,128]{1,0:T(8,128)(2,1)S(1)} %bitcast.4), channel_id=1, source_target_pairs={{0,64},{32,96},{64,128},{96,160},{128,192},{160,224},{192,0},{224,... | collective-permute-start | bytes 393224 | tf_op jit(solution)/shard_map/ppermute | solution.py:577
  102.0 9.0 %collective-permute-start.5 = (bf16[512,128]{1,0:T(8,128)(2,1)S(1)}, bf16[512,128]{1,0:T(8,128)(2,1)S(1)}, u32[]{:S(2)}, u32[]{:S(2)}) collective-permute-start(bf16[512,128]{1,0:T(8,128)(2,1)S(1)} %bitcast.5), channel_id=1, source_target_pairs={{0,128},{32,160},{64,192},{96,224},{128,0},{160,32},{192,64},{224,... | collective-permute-start | bytes 393224 | tf_op jit(solution)/shard_map/ppermute | solution.py:577
  102.0 9.0 %collective-permute-start.4 = (bf16[512,128]{1,0:T(8,128)(2,1)S(1)}, bf16[512,128]{1,0:T(8,128)(2,1)S(1)}, u32[]{:S(2)}, u32[]{:S(2)}) collective-permute-start(bf16[512,128]{1,0:T(8,128)(2,1)S(1)} %bitcast.6), channel_id=1, source_target_pairs={{0,192},{32,224},{64,0},{96,32},{128,64},{160,96},{192,128},{224,1... | collective-permute-start | bytes 393224 | tf_op jit(solution)/shard_map/ppermute | solution.py:577
  104.5 10.5 %collective-permute-start.7 = (bf16[512,128]{1,0:T(8,128)(2,1)S(1)}, bf16[512,128]{1,0:T(8,128)(2,1)S(1)}, u32[]{:S(2)}, u32[]{:S(2)}) collective-permute-start(bf16[512,128]{1,0:T(8,128)(2,1)S(1)} %bitcast.7), channel_id=1, source_target_pairs={{0,32},{32,0},{64,96},{96,64},{128,160},{160,128},{192,224},{224,1... | collective-permute-start | bytes 393224 | tf_op jit(solution)/shard_map/ppermute | solution.py:591
  111.0 4.0 %collective-permute-start.8 = (bf16[512,128]{1,0:T(8,128)(2,1)S(1)}, bf16[512,128]{1,0:T(8,128)(2,1)S(1)}, u32[]{:S(2)}, u32[]{:S(2)}) collective-permute-start(bf16[512,128]{1,0:T(8,128)(2,1)S(1)} %collective-permute-done.4.refs_1_), channel_id=1, source_target_pairs={{0,32},{32,0},{64,96},{96,64},{128,160},{160,128},{192,224},{224,1... | collective-permute-start | bytes 393224 | tf_op jit(solution)/shard_map/ppermute | solution.py:591
  113.4 1.6 %collective-permute-start.9 = (bf16[512,128]{1,0:T(8,128)(2,1)S(1)}, bf16[512,128]{1,0:T(8,128)(2,1)S(1)}, u32[]{:S(2)}, u32[]{:S(2)}) collective-permute-start(bf16[512,128]{1,0:T(8,128)(2,1)S(1)} %collective-permute-done.5.refs_2_), channel_id=1, source_target_pairs={{0,32},{32,0},{64,96},{96,64},{128,160},{160,128},{192,224},{224,1... | collective-permute-start | bytes 393224 | tf_op jit(solution)/shard_map/ppermute | solution.py:591
  113.4 1.6 %collective-permute-start.10 = (bf16[512,128]{1,0:T(8,128)(2,1)S(1)}, bf16[512,128]{1,0:T(8,128)(2,1)S(1)}, u32[]{:S(2)}, u32[]{:S(2)}) collective-permute-start(bf16[512,128]{1,0:T(8,128)(2,1)S(1)} %collective-permute-done.6.refs_3_), channel_id=1, source_target_pairs={{0,32},{32,0},{64,96},{96,64},{128,160},{160,128},{192,224},{224,1... | collective-permute-start | bytes 393224 | tf_op jit(solution)/shard_map/ppermute | solution.py:591

commit v7 on v6

--- a/solution.py
+++ b/solution.py
@@ -103,12 +103,26 @@
     return (rows == block).astype(F32).astype(BF)
 
 
+def pool_voxels(values, sums, first):
+    for a in range(2):
+        planes = values[a * 256 : a * 256 + 64]
+        for n in range(1, 4):
+            planes = planes + values[a * 256 + n * 64 : a * 256 + n * 64 + 64]
+        for b in range(2):
+            line = planes[b * 32 : b * 32 + 8]
+            for n in range(1, 4):
+                line = line + planes[b * 32 + n * 8 : b * 32 + n * 8 + 8]
+            for c in range(2):
+                at = first + 4 * a + 2 * b + c
+                sums[at : at + 1, :] = jnp.sum(line[4 * c : 4 * c + 4], axis=0, keepdims=True)
+
+
 def ask_kernel(
-    live_count, feat, owner, slot, choice, msg, flags,
-    counts, feat_v, owner_v, slot_v, choice_v, bricks, tables, voxels, pc, rows, msg_v, flags_v, sems,
+    feat, owner, slot, choice, msg,
+    feat_v, owner_v, slot_v, choice_v, bricks, tables, voxels, pc, rows, msg_v, sems,
 ):
     pairs = (
-        (owner, owner_v), (slot, slot_v), (choice, choice_v), (live_count, counts),
+        (owner, owner_v), (slot, slot_v), (choice, choice_v),
         (feat.at[0], feat_v.at[0]), (feat.at[1], feat_v.at[1]),
     )
     copies = [
@@ -117,7 +131,7 @@
     for copy in copies:
         copy.start()
     bricks[...] = jnp.zeros((16, 128), F32)
-    for copy in copies[:4]:
+    for copy in copies[:3]:
         copy.wait()
     named = jnp.where(owner_v[...] >= 0, owner_v[...] * 2 + slot_v[...], -1)
     bricks[0:2, 0:26] = named.astype(F32)
@@ -125,21 +139,17 @@
     for group in range(8):
         for s in range(2):
             tables[s, group : group + 1, :] = asked[s : s + 1, group * 128 : group * 128 + 128]
-    slots = lax.broadcasted_iota(jnp.int32, (8, 128), 0)
-    flags_v[...] = (slots < counts[0]).astype(F32)
-    sent = [pltpu.make_async_copy(flags_v, flags, sems.at[8])]
-    sent[0].start()
-    for s in range(2):
-        copies[4 + s].wait()
-        live = (counts[0] > s).astype(F32)
-        voxels[s] = (feat_v[s].astype(F32) * live).T
+    sent = []
+    for s in range(2):
+        copies[3 + s].wait()
+        voxels[s] = feat_v[s].astype(F32).T
         for d in OFFSETS:
             for at, first, size, stride in voxel_runs(d):
                 pc[s, pl.ds(PIECE[d] + at, size), :] = voxels.at[s][run(first, size, stride), :]
         to_shares(pc.at[s], rows.at[s], tables[s])
         at = pl.ds(16 * s, 16)
         msg_v[:, at, :] = rows[s].astype(BF).reshape(32, 16, 128)
-        sent.append(pltpu.make_async_copy(msg_v.at[:, at, :], msg.at[:, at, :], sems.at[6 + s]))
+        sent.append(pltpu.make_async_copy(msg_v.at[:, at, :], msg.at[:, at, :], sems.at[5 + s]))
         sent[-1].start()
     for copy in sent:
         copy.wait()
@@ -175,8 +185,8 @@
 
 def forward_kernel(
     parent, child, core, flags, feat, got, gout, weight, up, down,
-    out, grad_t, wsum, send,
-    rows_all, pc_all, mine_all, s0_all, s1_all, s2_all, cols, pooled, grad_pooled, out_v, sem,
+    out, grad_out_t, wsum, send,
+    rows_all, pc_all, mine_all, s0_all, s1_all, s2_all, cols, pooled, grad_pooled, out_v, grad_t, sems,
 ):
     eye = identity()
     acts, slopes = [], []
@@ -220,24 +230,20 @@
                     cols[at : at + 64, (3 * b + c) * 128 : (3 * b + c) * 128 + 128] = ref[
                         pl.ds(start, 64), :
                     ].astype(BF)
-        pre = nn(cols[640 * s : 640 * s + 512, :], weight[0])
-        pre = pre + nn(cols[640 * s + 64 : 640 * s + 576, :], weight[1])
-        pre = pre + nn(cols[640 * s + 128 : 640 * s + 640, :], weight[2])
+        taps = nn(cols[640 * s : 640 * s + 640, :], weight[...])
+        pre = taps[0:512, 0:128] + taps[64:576, 128:256] + taps[128:640, 256:384]
+        pool_voxels(pre * (1.0 / (1.0 + jnp.exp(-pre))), pooled, 8 * s)
         pre = pre.T
         gate = 1.0 / (1.0 + jnp.exp(-pre))
-        active = pre * gate
-        acts.append(active)
+        acts.append(pre * gate)
         slopes.append(gate * (1.0 + pre * (1.0 - gate)))
-        high = active.astype(BF)
-        low = (active - high.astype(F32)).astype(BF)
-        pooled[s] = nt(pool, high) + nt(pool, low)
     second = lax.broadcasted_iota(jnp.int32, (16, 1), 0) >= 8
     valid = [
         ((parent[s] >= 0) & (parent[s] * 64 + child[s] >= 0)).astype(F32) * flags[s : s + 1, 0:1]
         for s in range(2)
     ]
     valid = jnp.where(second, valid[1], valid[0])
-    coarse_in = ((pooled[0] + pooled[1]) * (1.0 / 64.0) * valid).astype(BF)
+    coarse_in = (pooled[...] * (1.0 / 64.0) * valid).astype(BF)
     grad_out = ((grad_pooled[0] + grad_pooled[1]) * valid).astype(BF)
     coarse_pre = nn(coarse_in, up[...])
     gate = 1.0 / (1.0 + jnp.exp(-coarse_pre))
@@ -254,8 +260,12 @@
         grad_in = gout[s].astype(F32) * live + nn(back, pool) * (1.0 / 64.0)
         grad_t[s] = (grad_in * slopes[s]).astype(BF)
         out_v[s] = (feat[s].astype(F32) * live + acts[s] + nn(lift, pool)).astype(BF)
-    copy = pltpu.make_async_copy(out_v, out, sem.at[0])
-    copy.start()
+    copies = [
+        pltpu.make_async_copy(grad_t, grad_out_t, sems.at[0]),
+        pltpu.make_async_copy(out_v, out, sems.at[1]),
+    ]
+    for copy in copies:
+        copy.start()
 
     def put(block, value):
         wsum[pl.ds(block * 128, 128), :] = value.astype(BF)
@@ -269,11 +279,11 @@
     for a in range(3):
         total = nn(grad_t[0], cols[64 * a : 64 * a + 512, :])
         total = total + nn(grad_t[1], cols[64 * a + 640 : 64 * a + 1152, :])
-        total = total.astype(BF)
         for n in range(9):
-            put(9 * a + n, nt(eye, total[:, n * 128 : n * 128 + 128]))
+            put(9 * a + n, total[:, n * 128 : n * 128 + 128].T)
     send[...] = wsum[pl.ds(pl.multiple_of((1 - core[0]) * 2048, 2048), 2048), :]
-    copy.wait()
+    for copy in copies:
+        copy.wait()
 
 
 def pair_kernel(core, line, wsum, other, own, one, two, three):
@@ -283,24 +293,26 @@
         ref[...] = (kept + other[pl.ds(at, 512), :].astype(F32)).astype(ref.dtype)
 
 
-def backward_kernel(grad_t, weight, own, msg, lhs, rhs, acc_all, pc_all, rows_all):
+def backward_kernel(grad, weight, own, msg, lhs, acc_all, pc_all, rows_all, grad_t, sem):
+    copy = pltpu.make_async_copy(grad, grad_t, sem.at[0])
+    copy.start()
     zero = jnp.zeros((64, 128), BF)
     for a in range(3):
-        rhs[:, a * 128 : a * 128 + 128] = weight[a]
         for n in [*range(a), *range(8 + a, 10)]:
             for s in range(2):
                 lhs[s, n * 64 : n * 64 + 64, a * 128 : a * 128 + 128] = zero
+    copy.wait()
     low = (lax.broadcasted_iota(jnp.int32, (64, 1), 0) & 7) != 0
     high = (lax.broadcasted_iota(jnp.int32, (64, 1), 0) & 7) != 7
 
     for s in range(2):
         acc, pc, rows = acc_all.at[s], pc_all.at[s], rows_all.at[s]
-        grad = grad_t[s].astype(F32).T.astype(BF)
+        values = grad_t[s].astype(F32).T.astype(BF)
         for a in range(3):
-            lhs[s, a * 64 : a * 64 + 512, a * 128 : a * 128 + 128] = grad
+            lhs[s, a * 64 : a * 64 + 512, a * 128 : a * 128 + 128] = values
         acc[...] = jnp.zeros_like(acc)
         for b in range(3):
-            part = nt(lhs[s], rhs[b * 384 : b * 384 + 384, :])
+            part = nt(lhs[s], weight[b * 384 : b * 384 + 384, :])
             for c in range(3):
                 for a in range(10):
                     at = pl.ds(8 + (a * 10 + b) * 8, 64)
@@ -465,13 +477,14 @@
     core = (grp & 1).reshape(1)
     line = (grp >> 1).reshape(1)
     swap = [(i, i ^ 1) for i in range(8)]
-    msg, flags = call(
+    slots = lax.broadcasted_iota(jnp.int32, (8, 128), 0)
+    flags = (slots < counts[0]).astype(F32)
+    (msg,) = call(
         ask_kernel,
-        [shape((32, 32, 128), BF), shape((8, 128), F32)],
+        [shape((32, 32, 128), BF)],
         [],
-        [counts, features, neighbour_owner, neighbour_slot, jnp.asarray(choice_table(), BF)],
+        [features, neighbour_owner, neighbour_slot, jnp.asarray(choice_table(), BF)],
         [
-            pltpu.SMEM((1,), jnp.int32),
             pltpu.VMEM((2, 128, 512), BF),
             pltpu.VMEM((2, 26), jnp.int32),
             pltpu.VMEM((2, 26), jnp.int32),
@@ -482,13 +495,12 @@
             pltpu.VMEM((2, 512, 128), F32),
             pltpu.VMEM((2, 512, 128), F32),
             pltpu.VMEM((32, 32, 128), BF),
-            pltpu.VMEM((8, 128), F32),
-            pltpu.SemaphoreType.DMA((9,)),
+            pltpu.SemaphoreType.DMA((7,)),
         ],
         flops=2e6,
         limit=60,
-        ins=[HB] * 4 + [pl.BlockSpec(memory_space=pl.ANY)],
-        outs=[HB] * 2,
+        ins=[HB] * 3 + [pl.BlockSpec(memory_space=pl.ANY)],
+        outs=[HB],
         name="ask",
     )
     first = lax.all_to_all(msg, "dev", split_axis=0, concat_axis=0, tiled=True)
@@ -503,6 +515,7 @@
     )
     halo = lax.all_to_all(answer, "dev", split_axis=0, concat_axis=0, tiled=True)
     weight = conv_weight.reshape(3, 1152, 128)
+    weight = jnp.concatenate([weight[0], weight[1], weight[2]], axis=1)
     output, grad_pre, wsum, send = call(
         forward_kernel,
         [
@@ -521,13 +534,14 @@
             pltpu.VMEM((2, 816, 128), F32),
             pltpu.VMEM((2, 800, 128), F32),
             pltpu.VMEM((1280, 1152), BF),
-            pltpu.VMEM((2, 16, 128), F32),
+            pltpu.VMEM((16, 128), F32),
             pltpu.VMEM((2, 16, 128), F32),
             pltpu.VMEM((2, 128, 512), BF),
-            pltpu.SemaphoreType.DMA((1,)),
+            pltpu.VMEM((2, 128, 512), BF),
+            pltpu.SemaphoreType.DMA((2,)),
         ],
         flops=2e9,
-        outs=[HB, VM, VM, VM],
+        outs=[HB, HB, VM, VM],
         name="forward",
     )
     other = lax.ppermute(send, "grp", swap)
@@ -550,12 +564,14 @@
         [grad_pre, weight],
         [
             pltpu.VMEM((2, 640, 384), BF),
-            pltpu.VMEM((1152, 384), BF),
             pltpu.VMEM((2, 3, 816, 128), F32),
             pltpu.VMEM((2, 512, 128), F32),
             pltpu.VMEM((2, 512, 128), F32),
+            pltpu.VMEM((2, 128, 512), BF),
+            pltpu.SemaphoreType.DMA((1,)),
         ],
         flops=4e9,
+        ins=[HB, VM],
         name="backward",
     )
     (terms,) = call(

time: 117 us -> 114 us (0.974)
  blocking collectives: 54.8 us -> 33.1 us
  starting transfers between devices: 28.4 us -> 40.5 us
  waiting for transfers between devices: 11.9 us -> 20.6 us
  Pallas kernels: 17.6 us -> 16.2 us
    all_to_all x1 -> x0, blocking collectives: 21.7 us -> none  [on_device(): first = lax.all_to_all(msg, 'dev', split_axis=0, concat_axis=0, tiled=True)]
    all_to_all x0 -> x1, starting transfers between devices: none -> 12 us  [on_device(): first = lax.all_to_all(msg, 'dev', split_axis=0, concat_axis=0, tiled=True)]
    all_to_all x0 -> x1, waiting for transfers between devices: none -> 9.02 us  [on_device(): first = lax.all_to_all(msg, 'dev', split_axis=0, concat_axis=0, tiled=True)]
    pallas_call x10, Pallas kernels: 17.6 us -> 16.2 us  [call(): pl.pallas_call(kernel, out_shape=shapes, in_specs=[SM] * len(scalars) + (...]
  transfers between devices with their start and end apart: 12 -> 13, of which waited for: 3 -> 4; matrix products, arithmetic and copies ran while one was open for 0% -> 0% of each run, Pallas kernels for 4% -> 4%
where the time goes in v7:
time: 114 us
  starting transfers between devices  40.5 us (36%)
  blocking collectives  33.1 us (29%)
  waiting for transfers between devices  20.6 us (18%)
  Pallas kernels  16.2 us (14%)
  local copies, waits for them, and re-layouts  1.83 us (2%)
  between operations  1.68 us (1%)
    all_to_all x1, blocking collectives, on_device(): back = lax.all_to_all(sums, 'dev', split_axis=0, concat_axis=0, tiled=True)  18.2 us
    pallas_call x10, Pallas kernels, call(): pl.pallas_call(kernel, out_shape=shapes, in_specs=[SM] * len(scalars) + (...  16.2 us
    all_to_all x1, blocking collectives, on_device(): lax.all_to_all(terms, 'dev', split_axis=0, concat_axis=0, tiled=True)  14.9 us
    all_to_all x1, starting transfers between devices, on_device(): first = lax.all_to_all(msg, 'dev', split_axis=0, concat_axis=0, tiled=True)  12 us
    all_to_all x1, waiting for transfers between devices, on_device(): lax.all_to_all(answer, 'dev', split_axis=0, concat_axis=0, tiled=True)  9.38 us
    all_to_all x1, waiting for transfers between devices, on_device(): first = lax.all_to_all(msg, 'dev', split_axis=0, concat_axis=0, tiled=True)  9.02 us
    ppermute x4, starting transfers between devices, on_device(): others = [lax.ppermute(x, 'grp', swap) for x in mine]  8.05 us
    all_to_all x1, starting transfers between devices, on_device(): lax.all_to_all(answer, 'dev', split_axis=0, concat_axis=0, tiled=True)  6.29 us
  transfers between devices with their start and end apart: 13, of which 4 were waited for; matrix products, arithmetic and copies ran while one was open for 0% of the time, Pallas kernels for 4%

profile of v7, /device:TPU:1, one launch (start us, length us, event | category | flops | bytes accessed | tf_op | source)
XLA Modules:
  0.0 114.1 jit_solution(13100121070379861648)
XLA Ops:
  0.6 2.5 %ask.1 = bf16[32,32,128]{2,1,0:T(8,128)(2,1)} custom-call(bf16[2,128,512]{2,1,0:T(8,128)(2,1)} %feat.3, s32[2,26]{1,0:T(2,128)} %owner.1, s32[2,26]{1,0:T(2,128)} %slot.1, bf16[128,1024]{1,0:T(8,128)(2,1)} %constant.10.clone.choice), custom_call_target="tpu_custom_call" | custom-call | flops 2000000 | bytes 786848 | tf_op jit(solution)/shard_map/ask/pallas_call | solution.py:445
  3.2 12.0 %all-to-all-start = ((bf16[32,32,128]{2,1,0:T(8,128)(2,1)}), bf16[32,32,128]{2,1,0:T(8,128)(2,1)S(1)}, u32[]{:S(2)}, u32[]{:S(2)}) async-start(bf16[32,32,128]{2,1,0:T(8,128)(2,1)} %ask.1), calls=%async_computation | async-start | bytes 524288 | tf_op jit(solution)/shard_map/all_to_all | solution.py:506
  15.9 9.0 %all-to-all-done.got = bf16[32,32,128]{2,1,0:T(8,128)(2,1)S(1)} async-done(((bf16[32,32,128]{2,1,0:T(8,128)(2,1)}), bf16[32,32,128]{2,1,0:T(8,128)(2,1)S(1)}, u32[]{:S(2)}, u32[]{:S(2)}) %all-to-all-start) | async-done | bytes 262176 | tf_op jit(solution)/shard_map/all_to_all | solution.py:506
  24.9 1.5 %route.1 = (bf16[32,32,128]{2,1,0:T(8,128)(2,1)}, bf16[2,16,512]{2,1,0:T(8,128)(2,1)S(1)}) custom-call(bf16[32,32,128]{2,1,0:T(8,128)(2,1)S(1)} %all-to-all-done.got), custom_call_target="tpu_custom_call" | custom-call | flops 300000000 | bytes 557056 | tf_op jit(solution)/shard_map/route/pallas_call | solution.py:445
  26.5 6.3 %all-to-all-start.1 = ((bf16[32,32,128]{2,1,0:T(8,128)(2,1)}), bf16[32,32,128]{2,1,0:T(8,128)(2,1)S(1)}, u32[]{:S(2)}, u32[]{:S(2)}) async-start(bf16[32,32,128]{2,1,0:T(8,128)(2,1)} %get-tuple-element.29), calls=%async_computation.1 | async-start | bytes 524288 | tf_op jit(solution)/shard_map/all_to_all | solution.py:516
  32.8 0.1 fusion
  32.9 0.1 pad_maximum_fusion.weight
  33.0 9.4 %all-to-all-done.1.got = bf16[32,32,128]{2,1,0:T(8,128)(2,1)S(1)} async-done(((bf16[32,32,128]{2,1,0:T(8,128)(2,1)}), bf16[32,32,128]{2,1,0:T(8,128)(2,1)S(1)}, u32[]{:S(2)}, u32[]{:S(2)}) %all-to-all-start.1) | async-done | bytes 262176 | tf_op jit(solution)/shard_map/all_to_all | solution.py:516
  42.4 0.1 iota.7.flags
  42.5 5.3 %forward.1 = (bf16[2,128,512]{2,1,0:T(8,128)(2,1)}, bf16[2,128,512]{2,1,0:T(8,128)(2,1)S(1)}, bf16[4096,128]{1,0:T(8,128)(2,1)S(1)}, bf16[2048,128]{1,0:T(8,128)(2,1)S(1)}) custom-call(s32[2]{0:T(128)S(1)} %copy-done.4, s32[2]{0:T(128)S(1)} %copy-done.5, s32[1]{0:T(128)} %bitcast.core, f32[8,128]{1,0:T(8,128)S(1)} %iota.7.flags, ...), custom_call_target="tpu_custom_call" | custom-call | flops 2000000000 | bytes 3903488 | tf_op jit(solution)/shard_map/forward/pallas_call | solution.py:445
  47.8 0.7 copy-done.6
  48.5 3.6 %collective-permute-start = (bf16[2048,128]{1,0:T(8,128)(2,1)S(1)}, bf16[2048,128]{1,0:T(8,128)(2,1)S(1)}, u32[]{:S(2)}, u32[]{:S(2)}) collective-permute-start(bf16[2048,128]{1,0:T(8,128)(2,1)S(1)} %get-tuple-element.33), channel_id=1, source_target_pairs={{0,32},{32,0},{64,96},{96,64},{128,160},{160,128},{192,224},{224,1... | collective-permute-start | bytes 1572872 | tf_op jit(solution)/shard_map/ppermute | solution.py:547
  52.1 1.5 %collective-permute-done.other = bf16[2048,128]{1,0:T(8,128)(2,1)S(1)} collective-permute-done((bf16[2048,128]{1,0:T(8,128)(2,1)S(1)}, bf16[2048,128]{1,0:T(8,128)(2,1)S(1)}, u32[]{:S(2)}, u32[]{:S(2)}) %collective-permute-start) | collective-permute-done | bytes 524320 | tf_op jit(solution)/shard_map/ppermute | solution.py:547
  53.6 0.1 pair.1
  53.8 2.8 %collective-permute-start.1 = (bf16[512,128]{1,0:T(8,128)(2,1)S(1)}, bf16[512,128]{1,0:T(8,128)(2,1)S(1)}, u32[]{:S(2)}, u32[]{:S(2)}) collective-permute-start(bf16[512,128]{1,0:T(8,128)(2,1)S(1)} %get-tuple-element.38), channel_id=1, source_target_pairs={{0,128},{32,160},{64,192},{96,224},{128,0},{160,32},{192,64},{224,... | collective-permute-start | bytes 393224 | tf_op jit(solution)/shard_map/ppermute | solution.py:556
  56.6 0.3 collective-permute-start.2
  56.9 2.4 %collective-permute-start.3 = (bf16[512,128]{1,0:T(8,128)(2,1)S(1)}, bf16[512,128]{1,0:T(8,128)(2,1)S(1)}, u32[]{:S(2)}, u32[]{:S(2)}) collective-permute-start(bf16[512,128]{1,0:T(8,128)(2,1)S(1)} %get-tuple-element.40), channel_id=1, source_target_pairs={{0,192},{32,224},{64,0},{96,32},{128,64},{160,96},{192,128},{224,1... | collective-permute-start | bytes 393224 | tf_op jit(solution)/shard_map/ppermute | solution.py:556
  59.3 0.9 copy-done.7
  60.2 2.4 %backward.1 = (f32[2,512,128]{2,1,0:T(8,128)S(1)}, bf16[32,32,128]{2,1,0:T(8,128)(2,1)S(1)}) custom-call(bf16[2,128,512]{2,1,0:T(8,128)(2,1)S(1)} %copy-done.7, bf16[1152,384]{1,0:T(8,128)(2,1)S(1)} %pad_maximum_fusion.weight), custom_call_target="tpu_custom_call" | custom-call | flops 4000000000 | bytes 1933312 | tf_op jit(solution)/shard_map/backward/pallas_call | solution.py:445
  62.7 0.7 collective-permute-done.2.away2
  63.3 0.1 join.1
  63.4 14.9 %all_to_all.20.got = bf16[32,48,128]{2,1,0:T(8,128)(2,1)S(1)} all-to-all(bf16[32,48,128]{2,1,0:T(8,128)(2,1)S(1)} %join.1), channel_id=1, replica_groups=mesh['grp'=8,'dev'=32] {'dev'}, dimensions={0} | all-to-all | bytes 786432 | tf_op jit(solution)/shard_map/all_to_all | solution.py:580
  78.3 0.8 merge.1
  79.1 18.2 %all_to_all.21.got = bf16[32,48,128]{2,1,0:T(8,128)(2,1)S(1)} all-to-all(bf16[32,48,128]{2,1,0:T(8,128)(2,1)S(1)} %merge.1), channel_id=1, replica_groups=mesh['grp'=8,'dev'=32] {'dev'}, dimensions={0} | all-to-all | bytes 786432 | tf_op jit(solution)/shard_map/all_to_all | solution.py:590
  97.3 2.5 %collective-permute-start.6 = (bf16[512,128]{1,0:T(8,128)(2,1)S(1)}, bf16[512,128]{1,0:T(8,128)(2,1)S(1)}, u32[]{:S(2)}, u32[]{:S(2)}) collective-permute-start(bf16[512,128]{1,0:T(8,128)(2,1)S(1)} %bitcast.8), channel_id=1, source_target_pairs={{0,64},{32,96},{64,128},{96,160},{128,192},{160,224},{192,0},{224,... | collective-permute-start | bytes 393224 | tf_op jit(solution)/shard_map/ppermute | solution.py:593
  99.8 2.5 %collective-permute-start.4 = (bf16[512,128]{1,0:T(8,128)(2,1)S(1)}, bf16[512,128]{1,0:T(8,128)(2,1)S(1)}, u32[]{:S(2)}, u32[]{:S(2)}) collective-permute-start(bf16[512,128]{1,0:T(8,128)(2,1)S(1)} %bitcast.10), channel_id=1, source_target_pairs={{0,192},{32,224},{64,0},{96,32},{128,64},{160,96},{192,128},{224,1... | collective-permute-start | bytes 393224 | tf_op jit(solution)/shard_map/ppermute | solution.py:593
  102.3 5.2 %collective-permute-start.7 = (bf16[512,128]{1,0:T(8,128)(2,1)S(1)}, bf16[512,128]{1,0:T(8,128)(2,1)S(1)}, u32[]{:S(2)}, u32[]{:S(2)}) collective-permute-start(bf16[512,128]{1,0:T(8,128)(2,1)S(1)} %bitcast.11), channel_id=1, source_target_pairs={{0,32},{32,0},{64,96},{96,64},{128,160},{160,128},{192,224},{224,1... | collective-permute-start | bytes 393224 | tf_op jit(solution)/shard_map/ppermute | solution.py:607
  107.5 1.3 %finish.1 = bf16[2,128,512]{2,1,0:T(8,128)(2,1)} custom-call(f32[8,128]{1,0:T(8,128)S(1)} %iota.7.flags, bf16[32,48,128]{2,1,0:T(8,128)(2,1)S(1)} %all_to_all.21.got, f32[2,512,128]{2,1,0:T(8,128)S(1)} %get-tuple-element.42.own, bf16[2,128,512]{2,1,0:T(8,128)(2,1)S(1)} %copy-done.1), custom_call_target="tpu_custom_call" | custom-call | flops 300000000 | bytes 1445888 | tf_op jit(solution)/shard_map/finish/pallas_call | solution.py:445
  108.8 2.4 %collective-permute-start.8 = (bf16[512,128]{1,0:T(8,128)(2,1)S(1)}, bf16[512,128]{1,0:T(8,128)(2,1)S(1)}, u32[]{:S(2)}, u32[]{:S(2)}) collective-permute-start(bf16[512,128]{1,0:T(8,128)(2,1)S(1)} %collective-permute-done.4.refs_1_), channel_id=1, source_target_pairs={{0,32},{32,0},{64,96},{96,64},{128,160},{160,128},{192,224},{224,1... | collective-permute-start | bytes 393224 | tf_op jit(solution)/shard_map/ppermute | solution.py:607
  111.2 0.5 collective-permute-start.10
  111.7 1.1 assemble.2
  112.8 1.1 assemble.3
  (29 shorter events, 0.1 us)
Async XLA Ops:
  0.6 32.1 %copy-start.8 = (bf16[27,128,128]{2,1,0:T(8,128)(2,1)S(1)}, bf16[27,128,128]{2,1,0:T(8,128)(2,1)}, u32[]{:S(2)}) copy-start(bf16[27,128,128]{2,1,0:T(8,128)(2,1)} %param.13) | copy-start | bytes 2654212
  3.2 21.7 %all-to-all-start = ((bf16[32,32,128]{2,1,0:T(8,128)(2,1)}), bf16[32,32,128]{2,1,0:T(8,128)(2,1)S(1)}, u32[]{:S(2)}, u32[]{:S(2)}) async-start(bf16[32,32,128]{2,1,0:T(8,128)(2,1)} %ask.1), calls=%async_computation | async-start | bytes 524288 | tf_op jit(solution)/shard_map/all_to_all | solution.py:506
  26.5 16.0 %all-to-all-start.1 = ((bf16[32,32,128]{2,1,0:T(8,128)(2,1)}), bf16[32,32,128]{2,1,0:T(8,128)(2,1)S(1)}, u32[]{:S(2)}, u32[]{:S(2)}) async-start(bf16[32,32,128]{2,1,0:T(8,128)(2,1)} %get-tuple-element.29), calls=%async_computation.1 | async-start | bytes 524288 | tf_op jit(solution)/shard_map/all_to_all | solution.py:516
  32.8 9.7 %copy-start = (bf16[2,128,512]{2,1,0:T(8,128)(2,1)S(1)}, bf16[2,128,512]{2,1,0:T(8,128)(2,1)}, u32[]{:S(2)}) copy-start(bf16[2,128,512]{2,1,0:T(8,128)(2,1)} %feat.3) | copy-start | bytes 786436
  32.8 9.7 %copy-start.1 = (bf16[2,128,512]{2,1,0:T(8,128)(2,1)S(1)}, bf16[2,128,512]{2,1,0:T(8,128)(2,1)}, u32[]{:S(2)}) copy-start(bf16[2,128,512]{2,1,0:T(8,128)(2,1)} %gout.3) | copy-start | bytes 786436
  32.8 9.7 %copy-start.2 = (bf16[128,256]{1,0:T(8,128)(2,1)S(1)}, bf16[128,256]{1,0:T(8,128)(2,1)}, u32[]{:S(2)}) copy-start(bf16[128,256]{1,0:T(8,128)(2,1)} %up.1) | copy-start | bytes 196612
  32.8 9.7 %copy-start.3 = (bf16[256,128]{1,0:T(8,128)(2,1)S(1)}, bf16[256,128]{1,0:T(8,128)(2,1)}, u32[]{:S(2)}) copy-start(bf16[256,128]{1,0:T(8,128)(2,1)} %down.1) | copy-start | bytes 196612
  32.8 9.7 %copy-start.4 = (s32[2]{0:T(128)S(1)}, s32[2]{0:T(128)}, u32[]{:S(2)}) copy-start(s32[2]{0:T(128)} %parent.1) | copy-start | bytes 28
  32.8 9.7 %copy-start.5 = (s32[2]{0:T(128)S(1)}, s32[2]{0:T(128)}, u32[]{:S(2)}) copy-start(s32[2]{0:T(128)} %child.1) | copy-start | bytes 28
  47.8 0.7 copy-start.6
  48.5 5.1 %collective-permute-start = (bf16[2048,128]{1,0:T(8,128)(2,1)S(1)}, bf16[2048,128]{1,0:T(8,128)(2,1)S(1)}, u32[]{:S(2)}, u32[]{:S(2)}) collective-permute-start(bf16[2048,128]{1,0:T(8,128)(2,1)S(1)} %get-tuple-element.33), channel_id=1, source_target_pairs={{0,32},{32,0},{64,96},{96,64},{128,160},{160,128},{192,224},{224,1... | collective-permute-start | bytes 1572872 | tf_op jit(solution)/shard_map/ppermute | solution.py:547
  53.8 8.9 %collective-permute-start.1 = (bf16[512,128]{1,0:T(8,128)(2,1)S(1)}, bf16[512,128]{1,0:T(8,128)(2,1)S(1)}, u32[]{:S(2)}, u32[]{:S(2)}) collective-permute-start(bf16[512,128]{1,0:T(8,128)(2,1)S(1)} %get-tuple-element.38), channel_id=1, source_target_pairs={{0,128},{32,160},{64,192},{96,224},{128,0},{160,32},{192,64},{224,... | collective-permute-start | bytes 393224 | tf_op jit(solution)/shard_map/ppermute | solution.py:556
  56.6 6.7 %collective-permute-start.2 = (bf16[512,128]{1,0:T(8,128)(2,1)S(1)}, bf16[512,128]{1,0:T(8,128)(2,1)S(1)}, u32[]{:S(2)}, u32[]{:S(2)}) collective-permute-start(bf16[512,128]{1,0:T(8,128)(2,1)S(1)} %get-tuple-element.39), channel_id=1, source_target_pairs={{0,64},{32,96},{64,128},{96,160},{128,192},{160,224},{192,0},{224,... | collective-permute-start | bytes 393224 | tf_op jit(solution)/shard_map/ppermute | solution.py:556
  56.9 6.4 %collective-permute-start.3 = (bf16[512,128]{1,0:T(8,128)(2,1)S(1)}, bf16[512,128]{1,0:T(8,128)(2,1)S(1)}, u32[]{:S(2)}, u32[]{:S(2)}) collective-permute-start(bf16[512,128]{1,0:T(8,128)(2,1)S(1)} %get-tuple-element.40), channel_id=1, source_target_pairs={{0,192},{32,224},{64,0},{96,32},{128,64},{160,96},{192,128},{224,1... | collective-permute-start | bytes 393224 | tf_op jit(solution)/shard_map/ppermute | solution.py:556
  59.3 0.9 copy-start.7
  97.3 11.5 %collective-permute-start.6 = (bf16[512,128]{1,0:T(8,128)(2,1)S(1)}, bf16[512,128]{1,0:T(8,128)(2,1)S(1)}, u32[]{:S(2)}, u32[]{:S(2)}) collective-permute-start(bf16[512,128]{1,0:T(8,128)(2,1)S(1)} %bitcast.8), channel_id=1, source_target_pairs={{0,64},{32,96},{64,128},{96,160},{128,192},{160,224},{192,0},{224,... | collective-permute-start | bytes 393224 | tf_op jit(solution)/shard_map/ppermute | solution.py:593
  99.8 9.0 %collective-permute-start.5 = (bf16[512,128]{1,0:T(8,128)(2,1)S(1)}, bf16[512,128]{1,0:T(8,128)(2,1)S(1)}, u32[]{:S(2)}, u32[]{:S(2)}) collective-permute-start(bf16[512,128]{1,0:T(8,128)(2,1)S(1)} %bitcast.9), channel_id=1, source_target_pairs={{0,128},{32,160},{64,192},{96,224},{128,0},{160,32},{192,64},{224,... | collective-permute-start | bytes 393224 | tf_op jit(solution)/shard_map/ppermute | solution.py:593
  99.8 9.0 %collective-permute-start.4 = (bf16[512,128]{1,0:T(8,128)(2,1)S(1)}, bf16[512,128]{1,0:T(8,128)(2,1)S(1)}, u32[]{:S(2)}, u32[]{:S(2)}) collective-permute-start(bf16[512,128]{1,0:T(8,128)(2,1)S(1)} %bitcast.10), channel_id=1, source_target_pairs={{0,192},{32,224},{64,0},{96,32},{128,64},{160,96},{192,128},{224,1... | collective-permute-start | bytes 393224 | tf_op jit(solution)/shard_map/ppermute | solution.py:593
  102.3 10.5 %collective-permute-start.7 = (bf16[512,128]{1,0:T(8,128)(2,1)S(1)}, bf16[512,128]{1,0:T(8,128)(2,1)S(1)}, u32[]{:S(2)}, u32[]{:S(2)}) collective-permute-start(bf16[512,128]{1,0:T(8,128)(2,1)S(1)} %bitcast.11), channel_id=1, source_target_pairs={{0,32},{32,0},{64,96},{96,64},{128,160},{160,128},{192,224},{224,1... | collective-permute-start | bytes 393224 | tf_op jit(solution)/shard_map/ppermute | solution.py:607
  108.8 3.9 %collective-permute-start.8 = (bf16[512,128]{1,0:T(8,128)(2,1)S(1)}, bf16[512,128]{1,0:T(8,128)(2,1)S(1)}, u32[]{:S(2)}, u32[]{:S(2)}) collective-permute-start(bf16[512,128]{1,0:T(8,128)(2,1)S(1)} %collective-permute-done.4.refs_1_), channel_id=1, source_target_pairs={{0,32},{32,0},{64,96},{96,64},{128,160},{160,128},{192,224},{224,1... | collective-permute-start | bytes 393224 | tf_op jit(solution)/shard_map/ppermute | solution.py:607
  111.2 1.6 %collective-permute-start.9 = (bf16[512,128]{1,0:T(8,128)(2,1)S(1)}, bf16[512,128]{1,0:T(8,128)(2,1)S(1)}, u32[]{:S(2)}, u32[]{:S(2)}) collective-permute-start(bf16[512,128]{1,0:T(8,128)(2,1)S(1)} %collective-permute-done.5.refs_2_), channel_id=1, source_target_pairs={{0,32},{32,0},{64,96},{96,64},{128,160},{160,128},{192,224},{224,1... | collective-permute-start | bytes 393224 | tf_op jit(solution)/shard_map/ppermute | solution.py:607
  111.2 1.6 %collective-permute-start.10 = (bf16[512,128]{1,0:T(8,128)(2,1)S(1)}, bf16[512,128]{1,0:T(8,128)(2,1)S(1)}, u32[]{:S(2)}, u32[]{:S(2)}) collective-permute-start(bf16[512,128]{1,0:T(8,128)(2,1)S(1)} %collective-permute-done.6.refs_3_), channel_id=1, source_target_pairs={{0,32},{32,0},{64,96},{96,64},{128,160},{160,128},{192,224},{224,1... | collective-permute-start | bytes 393224 | tf_op jit(solution)/shard_map/ppermute | solution.py:607

commit v8 on v7

--- a/solution.py
+++ b/solution.py
@@ -184,11 +184,12 @@
 
 
 def forward_kernel(
-    parent, child, core, flags, feat, got, gout, weight, up, down,
-    out, grad_out_t, wsum, send,
-    rows_all, pc_all, mine_all, s0_all, s1_all, s2_all, cols, pooled, grad_pooled, out_v, grad_t, sems,
+    parent, child, core, flags, feat, got, gout, weight,
+    out, grad_t, wsum, send,
+    rows_all, pc_all, mine_all, s0_all, s1_all, s2_all, cols, pooled, grad_pooled, out_v, sem,
 ):
     eye = identity()
+    up, down = weight[1152:1280, 0:256], weight[1152:1408, 256:384]
     acts, slopes = [], []
     for s in range(2):
         rows, pc, mine, s0, s1, s2 = (
@@ -230,7 +231,7 @@
                     cols[at : at + 64, (3 * b + c) * 128 : (3 * b + c) * 128 + 128] = ref[
                         pl.ds(start, 64), :
                     ].astype(BF)
-        taps = nn(cols[640 * s : 640 * s + 640, :], weight[...])
+        taps = nn(cols[640 * s : 640 * s + 640, :], weight[0:1152, :])
         pre = taps[0:512, 0:128] + taps[64:576, 128:256] + taps[128:640, 256:384]
         pool_voxels(pre * (1.0 / (1.0 + jnp.exp(-pre))), pooled, 8 * s)
         pre = pre.T
@@ -245,13 +246,13 @@
     valid = jnp.where(second, valid[1], valid[0])
     coarse_in = (pooled[...] * (1.0 / 64.0) * valid).astype(BF)
     grad_out = ((grad_pooled[0] + grad_pooled[1]) * valid).astype(BF)
-    coarse_pre = nn(coarse_in, up[...])
+    coarse_pre = nn(coarse_in, up)
     gate = 1.0 / (1.0 + jnp.exp(-coarse_pre))
     coarse_mid = (coarse_pre * gate).astype(BF)
-    grad_pre = nt(grad_out, down[...]) * (gate * (1.0 + coarse_pre * (1.0 - gate)))
+    grad_pre = nt(grad_out, down) * (gate * (1.0 + coarse_pre * (1.0 - gate)))
     grad_pre = grad_pre.astype(BF)
-    coarse_out = nn(coarse_mid, down[...]).astype(BF)
-    grad_cin = nt(grad_pre, up[...]).astype(BF)
+    coarse_out = nn(coarse_mid, down).astype(BF)
+    grad_cin = nt(grad_pre, up).astype(BF)
     lift = nt(eye, coarse_out).astype(BF)
     back = nt(eye, grad_cin).astype(BF)
     for s in range(2):
@@ -260,12 +261,8 @@
         grad_in = gout[s].astype(F32) * live + nn(back, pool) * (1.0 / 64.0)
         grad_t[s] = (grad_in * slopes[s]).astype(BF)
         out_v[s] = (feat[s].astype(F32) * live + acts[s] + nn(lift, pool)).astype(BF)
-    copies = [
-        pltpu.make_async_copy(grad_t, grad_out_t, sems.at[0]),
-        pltpu.make_async_copy(out_v, out, sems.at[1]),
-    ]
-    for copy in copies:
-        copy.start()
+    copy = pltpu.make_async_copy(out_v, out, sem.at[0])
+    copy.start()
 
     def put(block, value):
         wsum[pl.ds(block * 128, 128), :] = value.astype(BF)
@@ -282,26 +279,23 @@
         for n in range(9):
             put(9 * a + n, total[:, n * 128 : n * 128 + 128].T)
     send[...] = wsum[pl.ds(pl.multiple_of((1 - core[0]) * 2048, 2048), 2048), :]
-    for copy in copies:
-        copy.wait()
-
-
-def pair_kernel(core, line, wsum, other, own, one, two, three):
+    copy.wait()
+
+
+def pair_kernel(core, line, wsum, other, grad, own, one, two, three, held):
+    held[...] = grad[...]
     for step, ref in enumerate((own, one, two, three)):
         at = pl.multiple_of(((line[0] + step) & 3) * 512, 512)
         kept = wsum[pl.ds(pl.multiple_of(core[0] * 2048 + at, 512), 512), :].astype(F32)
         ref[...] = (kept + other[pl.ds(at, 512), :].astype(F32)).astype(ref.dtype)
 
 
-def backward_kernel(grad, weight, own, msg, lhs, acc_all, pc_all, rows_all, grad_t, sem):
-    copy = pltpu.make_async_copy(grad, grad_t, sem.at[0])
-    copy.start()
+def backward_kernel(grad_t, weight, own, msg, lhs, acc_all, pc_all, rows_all):
     zero = jnp.zeros((64, 128), BF)
     for a in range(3):
         for n in [*range(a), *range(8 + a, 10)]:
             for s in range(2):
                 lhs[s, n * 64 : n * 64 + 64, a * 128 : a * 128 + 128] = zero
-    copy.wait()
     low = (lax.broadcasted_iota(jnp.int32, (64, 1), 0) & 7) != 0
     high = (lax.broadcasted_iota(jnp.int32, (64, 1), 0) & 7) != 7
 
@@ -516,6 +510,8 @@
     halo = lax.all_to_all(answer, "dev", split_axis=0, concat_axis=0, tiled=True)
     weight = conv_weight.reshape(3, 1152, 128)
     weight = jnp.concatenate([weight[0], weight[1], weight[2]], axis=1)
+    coarse = jnp.concatenate([jnp.pad(coarse_up, ((0, 128), (0, 0))), coarse_down], axis=1)
+    weight = jnp.concatenate([weight, coarse], axis=0)
     output, grad_pre, wsum, send = call(
         forward_kernel,
         [
@@ -525,7 +521,7 @@
             shape((2048, 128), BF),
         ],
         [parent, child_slot, core],
-        [flags, features, halo, grad_out, weight, coarse_up, coarse_down],
+        [flags, features, halo, grad_out, weight],
         [
             pltpu.VMEM((2, 512, 128), F32),
             pltpu.VMEM((2, 512, 128), F32),
@@ -537,26 +533,24 @@
             pltpu.VMEM((16, 128), F32),
             pltpu.VMEM((2, 16, 128), F32),
             pltpu.VMEM((2, 128, 512), BF),
-            pltpu.VMEM((2, 128, 512), BF),
-            pltpu.SemaphoreType.DMA((2,)),
+            pltpu.SemaphoreType.DMA((1,)),
         ],
         flops=2e9,
-        outs=[HB, HB, VM, VM],
+        outs=[HB, VM, VM, VM],
         name="forward",
     )
     other = lax.ppermute(send, "grp", swap)
-    own_sum, *away = call(
+    own_sum, *away, grad_pre = call(
         pair_kernel,
-        [shape((512, 128), F32)] + [shape((512, 128), BF)] * 3,
+        [shape((512, 128), F32)] + [shape((512, 128), BF)] * 3 + [shape((2, 128, 512), BF)],
         [core, line],
-        [wsum, other],
+        [wsum, other, grad_pre],
         name="pair",
     )
     away = [
         lax.ppermute(away[step - 1], "grp", [(i, (i + 2 * step) % 8) for i in range(8)])
         for step in (2, 1, 3)
     ]
-    grad_pre, own_sum = lax.optimization_barrier((grad_pre, own_sum))
     own, terms = call(
         backward_kernel,
         [shape((2, 512, 128), F32), shape((32, 32, 128), BF)],
@@ -567,11 +561,8 @@
             pltpu.VMEM((2, 3, 816, 128), F32),
             pltpu.VMEM((2, 512, 128), F32),
             pltpu.VMEM((2, 512, 128), F32),
-            pltpu.VMEM((2, 128, 512), BF),
-            pltpu.SemaphoreType.DMA((1,)),
         ],
         flops=4e9,
-        ins=[HB, VM],
         name="backward",
     )
     (terms,) = call(

time: 114 us -> 115 us (level)
  local copies, waits for them, and re-layouts: 1.83 us -> 0.18 us
  waiting for transfers between devices: 20.6 us -> 21.8 us
    unnamed x18 -> x14, local copies, waits for them, and re-layouts: 1.69 us -> 0.04 us
where the time goes in v8:
time: 115 us; the launch traced here: 114 us
  starting transfers between devices  40.5 us (35%)
  blocking collectives  33.1 us (29%)
  waiting for transfers between devices  21.8 us (19%)
  Pallas kernels  16.8 us (15%)
  between operations  1.71 us (1%)
    all_to_all x1, blocking collectives, on_device(): back = lax.all_to_all(sums, 'dev', split_axis=0, concat_axis=0, tiled=True)  18.2 us
    pallas_call x10, Pallas kernels, call(): pl.pallas_call(kernel, out_shape=shapes, in_specs=[SM] * len(scalars) + (...  16.8 us
    all_to_all x1, blocking collectives, on_device(): lax.all_to_all(terms, 'dev', split_axis=0, concat_axis=0, tiled=True)  14.9 us
    all_to_all x1, starting transfers between devices, on_device(): first = lax.all_to_all(msg, 'dev', split_axis=0, concat_axis=0, tiled=True)  12 us
    all_to_all x1, waiting for transfers between devices, on_device(): lax.all_to_all(answer, 'dev', split_axis=0, concat_axis=0, tiled=True)  9.36 us
    all_to_all x1, waiting for transfers between devices, on_device(): first = lax.all_to_all(msg, 'dev', split_axis=0, concat_axis=0, tiled=True)  8.96 us
    ppermute x4, starting transfers between devices, on_device(): others = [lax.ppermute(x, 'grp', swap) for x in mine]  8.06 us
    all_to_all x1, starting transfers between devices, on_device(): lax.all_to_all(answer, 'dev', split_axis=0, concat_axis=0, tiled=True)  6.29 us
  transfers between devices with their start and end apart: 13, of which 4 were waited for; matrix products, arithmetic and copies ran while one was open for 0% of the time, Pallas kernels for 4%

profile of v8, /device:TPU:1, one launch (start us, length us, event | category | flops | bytes accessed | tf_op | source)
XLA Modules:
  0.0 114.3 jit_solution(12704453999741531102)
XLA Ops:
  0.6 2.5 %ask.1 = bf16[32,32,128]{2,1,0:T(8,128)(2,1)} custom-call(bf16[2,128,512]{2,1,0:T(8,128)(2,1)} %feat.3, s32[2,26]{1,0:T(2,128)} %owner.1, s32[2,26]{1,0:T(2,128)} %slot.1, bf16[128,1024]{1,0:T(8,128)(2,1)} %constant.13.clone.choice), custom_call_target="tpu_custom_call" | custom-call | flops 2000000 | bytes 786848 | tf_op jit(solution)/shard_map/ask/pallas_call | solution.py:439
  3.2 12.0 %all-to-all-start = ((bf16[32,32,128]{2,1,0:T(8,128)(2,1)}), bf16[32,32,128]{2,1,0:T(8,128)(2,1)S(1)}, u32[]{:S(2)}, u32[]{:S(2)}) async-start(bf16[32,32,128]{2,1,0:T(8,128)(2,1)} %ask.1), calls=%async_computation | async-start | bytes 524288 | tf_op jit(solution)/shard_map/all_to_all | solution.py:500
  15.9 9.0 %all-to-all-done.got = bf16[32,32,128]{2,1,0:T(8,128)(2,1)S(1)} async-done(((bf16[32,32,128]{2,1,0:T(8,128)(2,1)}), bf16[32,32,128]{2,1,0:T(8,128)(2,1)S(1)}, u32[]{:S(2)}, u32[]{:S(2)}) %all-to-all-start) | async-done | bytes 262176 | tf_op jit(solution)/shard_map/all_to_all | solution.py:500
  24.9 1.5 %route.1 = (bf16[32,32,128]{2,1,0:T(8,128)(2,1)}, bf16[2,16,512]{2,1,0:T(8,128)(2,1)S(1)}) custom-call(bf16[32,32,128]{2,1,0:T(8,128)(2,1)S(1)} %all-to-all-done.got), custom_call_target="tpu_custom_call" | custom-call | flops 300000000 | bytes 557056 | tf_op jit(solution)/shard_map/route/pallas_call | solution.py:439
  26.5 6.3 %all-to-all-start.1 = ((bf16[32,32,128]{2,1,0:T(8,128)(2,1)}), bf16[32,32,128]{2,1,0:T(8,128)(2,1)S(1)}, u32[]{:S(2)}, u32[]{:S(2)}) async-start(bf16[32,32,128]{2,1,0:T(8,128)(2,1)} %get-tuple-element.28), calls=%async_computation.1 | async-start | bytes 524288 | tf_op jit(solution)/shard_map/all_to_all | solution.py:510
  32.8 0.0 copy-start.1
  32.8 0.0 copy-start.2
  32.8 0.1 fusion.5
  32.9 0.1 fusion.4.weight
  33.0 9.4 %all-to-all-done.1.got = bf16[32,32,128]{2,1,0:T(8,128)(2,1)S(1)} async-done(((bf16[32,32,128]{2,1,0:T(8,128)(2,1)}), bf16[32,32,128]{2,1,0:T(8,128)(2,1)S(1)}, u32[]{:S(2)}, u32[]{:S(2)}) %all-to-all-start.1) | async-done | bytes 262176 | tf_op jit(solution)/shard_map/all_to_all | solution.py:510
  42.4 0.1 iota.7.flags
  42.5 6.0 %forward.1 = (bf16[2,128,512]{2,1,0:T(8,128)(2,1)}, bf16[2,128,512]{2,1,0:T(8,128)(2,1)S(1)}, bf16[4096,128]{1,0:T(8,128)(2,1)S(1)}, bf16[2048,128]{1,0:T(8,128)(2,1)}) custom-call(s32[2]{0:T(128)S(1)} %copy-done.2, s32[2]{0:T(128)S(1)} %copy-done.3, s32[1]{0:T(128)} %bitcast.core, f32[8,128]{1,0:T(8,128)S(1)} %iota.7.flags, ...), custom_call_target="tpu_custom_call" | custom-call | flops 2000000000 | bytes 3969024 | tf_op jit(solution)/shard_map/forward/pallas_call | solution.py:439
  48.5 3.7 %collective-permute-start = (bf16[2048,128]{1,0:T(8,128)(2,1)}, bf16[2048,128]{1,0:T(8,128)(2,1)S(1)}, u32[]{:S(2)}, u32[]{:S(2)}) collective-permute-start(bf16[2048,128]{1,0:T(8,128)(2,1)} %get-tuple-element.31), channel_id=1, source_target_pairs={{0,32},{32,0},{64,96},{96,64},{128,160},{160,128},{192,224},{224,1... | collective-permute-start | bytes 1572872 | tf_op jit(solution)/shard_map/ppermute | solution.py:542
  52.1 1.7 %collective-permute-done.other = bf16[2048,128]{1,0:T(8,128)(2,1)S(1)} collective-permute-done((bf16[2048,128]{1,0:T(8,128)(2,1)}, bf16[2048,128]{1,0:T(8,128)(2,1)S(1)}, u32[]{:S(2)}, u32[]{:S(2)}) %collective-permute-start) | collective-permute-done | bytes 524320 | tf_op jit(solution)/shard_map/ppermute | solution.py:542
  53.9 0.1 pair.1
  54.0 2.8 %collective-permute-start.1 = (bf16[512,128]{1,0:T(8,128)(2,1)S(1)}, bf16[512,128]{1,0:T(8,128)(2,1)S(1)}, u32[]{:S(2)}, u32[]{:S(2)}) collective-permute-start(bf16[512,128]{1,0:T(8,128)(2,1)S(1)} %get-tuple-element.36), channel_id=1, source_target_pairs={{0,128},{32,160},{64,192},{96,224},{128,0},{160,32},{192,64},{224,... | collective-permute-start | bytes 393224 | tf_op jit(solution)/shard_map/ppermute | solution.py:551
  56.9 0.3 collective-permute-start.2
  57.2 2.4 %collective-permute-start.3 = (bf16[512,128]{1,0:T(8,128)(2,1)S(1)}, bf16[512,128]{1,0:T(8,128)(2,1)S(1)}, u32[]{:S(2)}, u32[]{:S(2)}) collective-permute-start(bf16[512,128]{1,0:T(8,128)(2,1)S(1)} %get-tuple-element.38), channel_id=1, source_target_pairs={{0,192},{32,224},{64,0},{96,32},{128,64},{160,96},{192,128},{224,1... | collective-permute-start | bytes 393224 | tf_op jit(solution)/shard_map/ppermute | solution.py:551
  59.5 2.4 %backward.1 = (f32[2,512,128]{2,1,0:T(8,128)S(1)}, bf16[32,32,128]{2,1,0:T(8,128)(2,1)S(1)}) custom-call(bf16[2,128,512]{2,1,0:T(8,128)(2,1)S(1)} %get-tuple-element.33.grad_t, bf16[1408,384]{1,0:T(8,128)(2,1)S(1)} %fusion.4.weight), custom_call_target="tpu_custom_call" | custom-call | flops 4000000000 | bytes 2129920 | tf_op jit(solution)/shard_map/backward/pallas_call | solution.py:439
  61.9 1.7 %collective-permute-done.2.away2 = bf16[512,128]{1,0:T(8,128)(2,1)S(1)} collective-permute-done((bf16[512,128]{1,0:T(8,128)(2,1)S(1)}, bf16[512,128]{1,0:T(8,128)(2,1)S(1)}, u32[]{:S(2)}, u32[]{:S(2)}) %collective-permute-start.2) | collective-permute-done | bytes 131104 | tf_op jit(solution)/shard_map/ppermute | solution.py:551
  63.6 0.1 join.1
  63.7 14.9 %all_to_all.20.got = bf16[32,48,128]{2,1,0:T(8,128)(2,1)S(1)} all-to-all(bf16[32,48,128]{2,1,0:T(8,128)(2,1)S(1)} %join.1), channel_id=1, replica_groups=mesh['grp'=8,'dev'=32] {'dev'}, dimensions={0} | all-to-all | bytes 786432 | tf_op jit(solution)/shard_map/all_to_all | solution.py:571
  78.6 0.8 merge.1
  79.4 18.2 %all_to_all.21.got = bf16[32,48,128]{2,1,0:T(8,128)(2,1)S(1)} all-to-all(bf16[32,48,128]{2,1,0:T(8,128)(2,1)S(1)} %merge.1), channel_id=1, replica_groups=mesh['grp'=8,'dev'=32] {'dev'}, dimensions={0} | all-to-all | bytes 786432 | tf_op jit(solution)/shard_map/all_to_all | solution.py:581
  97.6 2.5 %collective-permute-start.6 = (bf16[512,128]{1,0:T(8,128)(2,1)S(1)}, bf16[512,128]{1,0:T(8,128)(2,1)S(1)}, u32[]{:S(2)}, u32[]{:S(2)}) collective-permute-start(bf16[512,128]{1,0:T(8,128)(2,1)S(1)} %bitcast.8), channel_id=1, source_target_pairs={{0,64},{32,96},{64,128},{96,160},{128,192},{160,224},{192,0},{224,... | collective-permute-start | bytes 393224 | tf_op jit(solution)/shard_map/ppermute | solution.py:584
  100.1 2.5 %collective-permute-start.4 = (bf16[512,128]{1,0:T(8,128)(2,1)S(1)}, bf16[512,128]{1,0:T(8,128)(2,1)S(1)}, u32[]{:S(2)}, u32[]{:S(2)}) collective-permute-start(bf16[512,128]{1,0:T(8,128)(2,1)S(1)} %bitcast.10), channel_id=1, source_target_pairs={{0,192},{32,224},{64,0},{96,32},{128,64},{160,96},{192,128},{224,1... | collective-permute-start | bytes 393224 | tf_op jit(solution)/shard_map/ppermute | solution.py:584
  102.5 5.2 %collective-permute-start.7 = (bf16[512,128]{1,0:T(8,128)(2,1)S(1)}, bf16[512,128]{1,0:T(8,128)(2,1)S(1)}, u32[]{:S(2)}, u32[]{:S(2)}) collective-permute-start(bf16[512,128]{1,0:T(8,128)(2,1)S(1)} %bitcast.11), channel_id=1, source_target_pairs={{0,32},{32,0},{64,96},{96,64},{128,160},{160,128},{192,224},{224,1... | collective-permute-start | bytes 393224 | tf_op jit(solution)/shard_map/ppermute | solution.py:598
  107.7 1.3 %finish.1 = bf16[2,128,512]{2,1,0:T(8,128)(2,1)} custom-call(f32[8,128]{1,0:T(8,128)S(1)} %iota.7.flags, bf16[32,48,128]{2,1,0:T(8,128)(2,1)S(1)} %all_to_all.21.got, f32[2,512,128]{2,1,0:T(8,128)S(1)} %get-tuple-element.40.own, bf16[2,128,512]{2,1,0:T(8,128)(2,1)S(1)} %copy-done.1), custom_call_target="tpu_custom_call" | custom-call | flops 300000000 | bytes 1445888 | tf_op jit(solution)/shard_map/finish/pallas_call | solution.py:439
  109.1 2.4 %collective-permute-start.8 = (bf16[512,128]{1,0:T(8,128)(2,1)S(1)}, bf16[512,128]{1,0:T(8,128)(2,1)S(1)}, u32[]{:S(2)}, u32[]{:S(2)}) collective-permute-start(bf16[512,128]{1,0:T(8,128)(2,1)S(1)} %collective-permute-done.4.refs_1_), channel_id=1, source_target_pairs={{0,32},{32,0},{64,96},{96,64},{128,160},{160,128},{192,224},{224,1... | collective-permute-start | bytes 393224 | tf_op jit(solution)/shard_map/ppermute | solution.py:598
  111.5 0.5 collective-permute-start.10
  112.0 1.1 assemble.2
  113.1 1.1 assemble.3
  (25 shorter events, 0.1 us)
Async XLA Ops:
  0.6 32.1 %copy-start.4 = (bf16[27,128,128]{2,1,0:T(8,128)(2,1)S(1)}, bf16[27,128,128]{2,1,0:T(8,128)(2,1)}, u32[]{:S(2)}) copy-start(bf16[27,128,128]{2,1,0:T(8,128)(2,1)} %param.13) | copy-start | bytes 2654212
  3.2 21.7 %all-to-all-start = ((bf16[32,32,128]{2,1,0:T(8,128)(2,1)}), bf16[32,32,128]{2,1,0:T(8,128)(2,1)S(1)}, u32[]{:S(2)}, u32[]{:S(2)}) async-start(bf16[32,32,128]{2,1,0:T(8,128)(2,1)} %ask.1), calls=%async_computation | async-start | bytes 524288 | tf_op jit(solution)/shard_map/all_to_all | solution.py:500
  15.2 17.7 %copy-start.5 = (bf16[128,256]{1,0:T(8,128)(2,1)S(1)}, bf16[128,256]{1,0:T(8,128)(2,1)}, u32[]{:S(2)}) copy-start(bf16[128,256]{1,0:T(8,128)(2,1)} %param.14) | copy-start | bytes 196612
  15.2 17.7 %copy-start.6 = (bf16[256,128]{1,0:T(8,128)(2,1)S(1)}, bf16[256,128]{1,0:T(8,128)(2,1)}, u32[]{:S(2)}) copy-start(bf16[256,128]{1,0:T(8,128)(2,1)} %param.15) | copy-start | bytes 196612
  26.5 16.0 %all-to-all-start.1 = ((bf16[32,32,128]{2,1,0:T(8,128)(2,1)}), bf16[32,32,128]{2,1,0:T(8,128)(2,1)S(1)}, u32[]{:S(2)}, u32[]{:S(2)}) async-start(bf16[32,32,128]{2,1,0:T(8,128)(2,1)} %get-tuple-element.28), calls=%async_computation.1 | async-start | bytes 524288 | tf_op jit(solution)/shard_map/all_to_all | solution.py:510
  32.8 9.7 %copy-start = (bf16[2,128,512]{2,1,0:T(8,128)(2,1)S(1)}, bf16[2,128,512]{2,1,0:T(8,128)(2,1)}, u32[]{:S(2)}) copy-start(bf16[2,128,512]{2,1,0:T(8,128)(2,1)} %feat.3) | copy-start | bytes 786436
  32.8 9.7 %copy-start.1 = (bf16[2,128,512]{2,1,0:T(8,128)(2,1)S(1)}, bf16[2,128,512]{2,1,0:T(8,128)(2,1)}, u32[]{:S(2)}) copy-start(bf16[2,128,512]{2,1,0:T(8,128)(2,1)} %gout.3) | copy-start | bytes 786436
  32.8 9.7 %copy-start.2 = (s32[2]{0:T(128)S(1)}, s32[2]{0:T(128)}, u32[]{:S(2)}) copy-start(s32[2]{0:T(128)} %parent.1) | copy-start | bytes 28
  32.8 9.7 %copy-start.3 = (s32[2]{0:T(128)S(1)}, s32[2]{0:T(128)}, u32[]{:S(2)}) copy-start(s32[2]{0:T(128)} %child.1) | copy-start | bytes 28
  48.5 5.4 %collective-permute-start = (bf16[2048,128]{1,0:T(8,128)(2,1)}, bf16[2048,128]{1,0:T(8,128)(2,1)S(1)}, u32[]{:S(2)}, u32[]{:S(2)}) collective-permute-start(bf16[2048,128]{1,0:T(8,128)(2,1)} %get-tuple-element.31), channel_id=1, source_target_pairs={{0,32},{32,0},{64,96},{96,64},{128,160},{160,128},{192,224},{224,1... | collective-permute-start | bytes 1572872 | tf_op jit(solution)/shard_map/ppermute | solution.py:542
  54.0 7.9 %collective-permute-start.1 = (bf16[512,128]{1,0:T(8,128)(2,1)S(1)}, bf16[512,128]{1,0:T(8,128)(2,1)S(1)}, u32[]{:S(2)}, u32[]{:S(2)}) collective-permute-start(bf16[512,128]{1,0:T(8,128)(2,1)S(1)} %get-tuple-element.36), channel_id=1, source_target_pairs={{0,128},{32,160},{64,192},{96,224},{128,0},{160,32},{192,64},{224,... | collective-permute-start | bytes 393224 | tf_op jit(solution)/shard_map/ppermute | solution.py:551
  56.9 6.7 %collective-permute-start.2 = (bf16[512,128]{1,0:T(8,128)(2,1)S(1)}, bf16[512,128]{1,0:T(8,128)(2,1)S(1)}, u32[]{:S(2)}, u32[]{:S(2)}) collective-permute-start(bf16[512,128]{1,0:T(8,128)(2,1)S(1)} %get-tuple-element.37), channel_id=1, source_target_pairs={{0,64},{32,96},{64,128},{96,160},{128,192},{160,224},{192,0},{224,... | collective-permute-start | bytes 393224 | tf_op jit(solution)/shard_map/ppermute | solution.py:551
  57.2 6.4 %collective-permute-start.3 = (bf16[512,128]{1,0:T(8,128)(2,1)S(1)}, bf16[512,128]{1,0:T(8,128)(2,1)S(1)}, u32[]{:S(2)}, u32[]{:S(2)}) collective-permute-start(bf16[512,128]{1,0:T(8,128)(2,1)S(1)} %get-tuple-element.38), channel_id=1, source_target_pairs={{0,192},{32,224},{64,0},{96,32},{128,64},{160,96},{192,128},{224,1... | collective-permute-start | bytes 393224 | tf_op jit(solution)/shard_map/ppermute | solution.py:551
  97.6 11.5 %collective-permute-start.6 = (bf16[512,128]{1,0:T(8,128)(2,1)S(1)}, bf16[512,128]{1,0:T(8,128)(2,1)S(1)}, u32[]{:S(2)}, u32[]{:S(2)}) collective-permute-start(bf16[512,128]{1,0:T(8,128)(2,1)S(1)} %bitcast.8), channel_id=1, source_target_pairs={{0,64},{32,96},{64,128},{96,160},{128,192},{160,224},{192,0},{224,... | collective-permute-start | bytes 393224 | tf_op jit(solution)/shard_map/ppermute | solution.py:584
  100.1 9.0 %collective-permute-start.5 = (bf16[512,128]{1,0:T(8,128)(2,1)S(1)}, bf16[512,128]{1,0:T(8,128)(2,1)S(1)}, u32[]{:S(2)}, u32[]{:S(2)}) collective-permute-start(bf16[512,128]{1,0:T(8,128)(2,1)S(1)} %bitcast.9), channel_id=1, source_target_pairs={{0,128},{32,160},{64,192},{96,224},{128,0},{160,32},{192,64},{224,... | collective-permute-start | bytes 393224 | tf_op jit(solution)/shard_map/ppermute | solution.py:584
  100.1 9.0 %collective-permute-start.4 = (bf16[512,128]{1,0:T(8,128)(2,1)S(1)}, bf16[512,128]{1,0:T(8,128)(2,1)S(1)}, u32[]{:S(2)}, u32[]{:S(2)}) collective-permute-start(bf16[512,128]{1,0:T(8,128)(2,1)S(1)} %bitcast.10), channel_id=1, source_target_pairs={{0,192},{32,224},{64,0},{96,32},{128,64},{160,96},{192,128},{224,1... | collective-permute-start | bytes 393224 | tf_op jit(solution)/shard_map/ppermute | solution.py:584
  102.5 10.5 %collective-permute-start.7 = (bf16[512,128]{1,0:T(8,128)(2,1)S(1)}, bf16[512,128]{1,0:T(8,128)(2,1)S(1)}, u32[]{:S(2)}, u32[]{:S(2)}) collective-permute-start(bf16[512,128]{1,0:T(8,128)(2,1)S(1)} %bitcast.11), channel_id=1, source_target_pairs={{0,32},{32,0},{64,96},{96,64},{128,160},{160,128},{192,224},{224,1... | collective-permute-start | bytes 393224 | tf_op jit(solution)/shard_map/ppermute | solution.py:598
  109.1 3.9 %collective-permute-start.8 = (bf16[512,128]{1,0:T(8,128)(2,1)S(1)}, bf16[512,128]{1,0:T(8,128)(2,1)S(1)}, u32[]{:S(2)}, u32[]{:S(2)}) collective-permute-start(bf16[512,128]{1,0:T(8,128)(2,1)S(1)} %collective-permute-done.4.refs_1_), channel_id=1, source_target_pairs={{0,32},{32,0},{64,96},{96,64},{128,160},{160,128},{192,224},{224,1... | collective-permute-start | bytes 393224 | tf_op jit(solution)/shard_map/ppermute | solution.py:598
  111.5 1.6 %collective-permute-start.9 = (bf16[512,128]{1,0:T(8,128)(2,1)S(1)}, bf16[512,128]{1,0:T(8,128)(2,1)S(1)}, u32[]{:S(2)}, u32[]{:S(2)}) collective-permute-start(bf16[512,128]{1,0:T(8,128)(2,1)S(1)} %collective-permute-done.5.refs_2_), channel_id=1, source_target_pairs={{0,32},{32,0},{64,96},{96,64},{128,160},{160,128},{192,224},{224,1... | collective-permute-start | bytes 393224 | tf_op jit(solution)/shard_map/ppermute | solution.py:598
  111.5 1.6 %collective-permute-start.10 = (bf16[512,128]{1,0:T(8,128)(2,1)S(1)}, bf16[512,128]{1,0:T(8,128)(2,1)S(1)}, u32[]{:S(2)}, u32[]{:S(2)}) collective-permute-start(bf16[512,128]{1,0:T(8,128)(2,1)S(1)} %collective-permute-done.6.refs_3_), channel_id=1, source_target_pairs={{0,32},{32,0},{64,96},{96,64},{128,160},{160,128},{192,224},{224,1... | collective-permute-start | bytes 393224 | tf_op jit(solution)/shard_map/ppermute | solution.py:598

commit v9 on v8

--- a/solution.py
+++ b/solution.py
@@ -185,8 +185,8 @@
 
 def forward_kernel(
     parent, child, core, flags, feat, got, gout, weight,
-    out, grad_t, wsum, send,
-    rows_all, pc_all, mine_all, s0_all, s1_all, s2_all, cols, pooled, grad_pooled, out_v, sem,
+    out, grad_t, keep, send,
+    rows_all, pc_all, mine_all, s0_all, s1_all, s2_all, cols, pooled, grad_pooled, out_v, wsum, sem,
 ):
     eye = identity()
     up, down = weight[1152:1280, 0:256], weight[1152:1408, 256:384]
@@ -279,6 +279,7 @@
         for n in range(9):
             put(9 * a + n, total[:, n * 128 : n * 128 + 128].T)
     send[...] = wsum[pl.ds(pl.multiple_of((1 - core[0]) * 2048, 2048), 2048), :]
+    keep[...] = wsum[pl.ds(pl.multiple_of(core[0] * 2048, 2048), 2048), :]
     copy.wait()
 
 
@@ -286,7 +287,7 @@
     held[...] = grad[...]
     for step, ref in enumerate((own, one, two, three)):
         at = pl.multiple_of(((line[0] + step) & 3) * 512, 512)
-        kept = wsum[pl.ds(pl.multiple_of(core[0] * 2048 + at, 512), 512), :].astype(F32)
+        kept = wsum[pl.ds(at, 512), :].astype(F32)
         ref[...] = (kept + other[pl.ds(at, 512), :].astype(F32)).astype(ref.dtype)
 
 
@@ -517,7 +518,7 @@
         [
             shape((2, 128, 512), BF),
             shape((2, 128, 512), BF),
-            shape((4096, 128), BF),
+            shape((2048, 128), BF),
             shape((2048, 128), BF),
         ],
         [parent, child_slot, core],
@@ -533,6 +534,7 @@
             pltpu.VMEM((16, 128), F32),
             pltpu.VMEM((2, 16, 128), F32),
             pltpu.VMEM((2, 128, 512), BF),
+            pltpu.VMEM((4096, 128), BF),
             pltpu.SemaphoreType.DMA((1,)),
         ],
         flops=2e9,
@@ -549,7 +551,7 @@
     )
     away = [
         lax.ppermute(away[step - 1], "grp", [(i, (i + 2 * step) % 8) for i in range(8)])
-        for step in (2, 1, 3)
+        for step in (1, 3, 2)
     ]
     own, terms = call(
         backward_kernel,
@@ -582,7 +584,7 @@
     chunk = back[:, 32:48, :].reshape(512, 128)
     parts = {
         step: lax.ppermute(chunk, "grp", [(i, (i - 2 * step) % 8) for i in range(8)])
-        for step in (2, 1, 3)
+        for step in (1, 3, 2)
     }
     (grad_features,) = call(
         finish_kernel,

time: 115 us -> 114 us (level)
  starting transfers between devices: 40.5 us -> 39.3 us
  waiting for transfers between devices: 21.8 us -> 23 us
    ppermute x3, starting transfers between devices: 4.95 us -> 2.78 us  [on_device(): lax.ppermute(chunk, 'grp', [(i, (i - 2 * step) % 8) for i in range(8)])]
    ppermute x4, starting transfers between devices: 8.06 us -> 10.2 us  [on_device(): others = [lax.ppermute(x, 'grp', swap) for x in mine]]
    ppermute x3, waiting for transfers between devices: 1.69 us -> 3.13 us  [on_device(): lax.ppermute(away[step - 1], 'grp', [(i, (i + 2 * step) % 8) for i in ran...]
    ppermute x3, starting transfers between devices: 5.51 us -> 4.29 us  [on_device(): lax.ppermute(away[step - 1], 'grp', [(i, (i + 2 * step) % 8) for i in ran...]
where the time goes in v9:
time: 114 us; the launch traced here: 113 us
  starting transfers between devices  39.3 us (34%)
  blocking collectives  32.3 us (28%)
  waiting for transfers between devices  23 us (20%)
  Pallas kernels  16.5 us (14%)
  between operations  1.71 us (2%)
    all_to_all x1, blocking collectives, on_device(): back = lax.all_to_all(sums, 'dev', split_axis=0, concat_axis=0, tiled=True)  17.5 us
    pallas_call x10, Pallas kernels, call(): pl.pallas_call(kernel, out_shape=shapes, in_specs=[SM] * len(scalars) + (...  16.5 us
    all_to_all x1, blocking collectives, on_device(): lax.all_to_all(terms, 'dev', split_axis=0, concat_axis=0, tiled=True)  14.8 us
    all_to_all x1, starting transfers between devices, on_device(): first = lax.all_to_all(msg, 'dev', split_axis=0, concat_axis=0, tiled=True)  12 us
    ppermute x4, starting transfers between devices, on_device(): others = [lax.ppermute(x, 'grp', swap) for x in mine]  10.2 us
    all_to_all x1, waiting for transfers between devices, on_device(): lax.all_to_all(answer, 'dev', split_axis=0, concat_axis=0, tiled=True)  9.36 us
    all_to_all x1, waiting for transfers between devices, on_device(): first = lax.all_to_all(msg, 'dev', split_axis=0, concat_axis=0, tiled=True)  8.96 us
    all_to_all x1, starting transfers between devices, on_device(): lax.all_to_all(answer, 'dev', split_axis=0, concat_axis=0, tiled=True)  6.29 us
  transfers between devices with their start and end apart: 13, of which 4 were waited for; matrix products, arithmetic and copies ran while one was open for 0% of the time, Pallas kernels for 4%

profile of v9, /device:TPU:1, one launch (start us, length us, event | category | flops | bytes accessed | tf_op | source)
XLA Modules:
  0.0 113.2 jit_solution(2323409811652809286)
XLA Ops:
  0.6 2.5 %ask.1 = bf16[32,32,128]{2,1,0:T(8,128)(2,1)} custom-call(bf16[2,128,512]{2,1,0:T(8,128)(2,1)} %feat.3, s32[2,26]{1,0:T(2,128)} %owner.1, s32[2,26]{1,0:T(2,128)} %slot.1, bf16[128,1024]{1,0:T(8,128)(2,1)} %constant.13.clone.choice), custom_call_target="tpu_custom_call" | custom-call | flops 2000000 | bytes 786848 | tf_op jit(solution)/shard_map/ask/pallas_call | solution.py:440
  3.2 12.0 %all-to-all-start = ((bf16[32,32,128]{2,1,0:T(8,128)(2,1)}), bf16[32,32,128]{2,1,0:T(8,128)(2,1)S(1)}, u32[]{:S(2)}, u32[]{:S(2)}) async-start(bf16[32,32,128]{2,1,0:T(8,128)(2,1)} %ask.1), calls=%async_computation | async-start | bytes 524288 | tf_op jit(solution)/shard_map/all_to_all | solution.py:501
  15.2 0.0 copy-start.5
  15.9 9.0 %all-to-all-done.got = bf16[32,32,128]{2,1,0:T(8,128)(2,1)S(1)} async-done(((bf16[32,32,128]{2,1,0:T(8,128)(2,1)}), bf16[32,32,128]{2,1,0:T(8,128)(2,1)S(1)}, u32[]{:S(2)}, u32[]{:S(2)}) %all-to-all-start) | async-done | bytes 262176 | tf_op jit(solution)/shard_map/all_to_all | solution.py:501
  24.9 1.5 %route.1 = (bf16[32,32,128]{2,1,0:T(8,128)(2,1)}, bf16[2,16,512]{2,1,0:T(8,128)(2,1)S(1)}) custom-call(bf16[32,32,128]{2,1,0:T(8,128)(2,1)S(1)} %all-to-all-done.got), custom_call_target="tpu_custom_call" | custom-call | flops 300000000 | bytes 557056 | tf_op jit(solution)/shard_map/route/pallas_call | solution.py:440
  26.5 6.3 %all-to-all-start.1 = ((bf16[32,32,128]{2,1,0:T(8,128)(2,1)}), bf16[32,32,128]{2,1,0:T(8,128)(2,1)S(1)}, u32[]{:S(2)}, u32[]{:S(2)}) async-start(bf16[32,32,128]{2,1,0:T(8,128)(2,1)} %get-tuple-element.28), calls=%async_computation.1 | async-start | bytes 524288 | tf_op jit(solution)/shard_map/all_to_all | solution.py:511
  32.8 0.1 fusion.5
  32.9 0.1 fusion.4.weight
  33.0 9.4 %all-to-all-done.1.got = bf16[32,32,128]{2,1,0:T(8,128)(2,1)S(1)} async-done(((bf16[32,32,128]{2,1,0:T(8,128)(2,1)}), bf16[32,32,128]{2,1,0:T(8,128)(2,1)S(1)}, u32[]{:S(2)}, u32[]{:S(2)}) %all-to-all-start.1) | async-done | bytes 262176 | tf_op jit(solution)/shard_map/all_to_all | solution.py:511
  42.4 0.1 iota.7.flags
  42.5 5.6 %forward.1 = (bf16[2,128,512]{2,1,0:T(8,128)(2,1)}, bf16[2,128,512]{2,1,0:T(8,128)(2,1)S(1)}, bf16[2048,128]{1,0:T(8,128)(2,1)S(1)}, bf16[2048,128]{1,0:T(8,128)(2,1)S(1)}) custom-call(s32[2]{0:T(128)S(1)} %copy-done.2, s32[2]{0:T(128)S(1)} %copy-done.3, s32[1]{0:T(128)} %bitcast.core, f32[8,128]{1,0:T(8,128)S(1)} %iota.7.flags, ...), custom_call_target="tpu_custom_call" | custom-call | flops 2000000000 | bytes 3444736 | tf_op jit(solution)/shard_map/forward/pallas_call | solution.py:440
  48.1 3.7 %collective-permute-start = (bf16[2048,128]{1,0:T(8,128)(2,1)S(1)}, bf16[2048,128]{1,0:T(8,128)(2,1)S(1)}, u32[]{:S(2)}, u32[]{:S(2)}) collective-permute-start(bf16[2048,128]{1,0:T(8,128)(2,1)S(1)} %get-tuple-element.31), channel_id=1, source_target_pairs={{0,32},{32,0},{64,96},{96,64},{128,160},{160,128},{192,224},{224,1... | collective-permute-start | bytes 1572872 | tf_op jit(solution)/shard_map/ppermute | solution.py:544
  51.8 1.5 %collective-permute-done.other = bf16[2048,128]{1,0:T(8,128)(2,1)S(1)} collective-permute-done((bf16[2048,128]{1,0:T(8,128)(2,1)S(1)}, bf16[2048,128]{1,0:T(8,128)(2,1)S(1)}, u32[]{:S(2)}, u32[]{:S(2)}) %collective-permute-start) | collective-permute-done | bytes 524320 | tf_op jit(solution)/shard_map/ppermute | solution.py:544
  53.4 0.1 pair.1
  53.5 1.3 %collective-permute-start.1 = (bf16[512,128]{1,0:T(8,128)(2,1)S(1)}, bf16[512,128]{1,0:T(8,128)(2,1)S(1)}, u32[]{:S(2)}, u32[]{:S(2)}) collective-permute-start(bf16[512,128]{1,0:T(8,128)(2,1)S(1)} %get-tuple-element.36), channel_id=1, source_target_pairs={{0,64},{32,96},{64,128},{96,160},{128,192},{160,224},{192,0},{224,... | collective-permute-start | bytes 393224 | tf_op jit(solution)/shard_map/ppermute | solution.py:553
  54.8 1.5 %collective-permute-start.2 = (bf16[512,128]{1,0:T(8,128)(2,1)S(1)}, bf16[512,128]{1,0:T(8,128)(2,1)S(1)}, u32[]{:S(2)}, u32[]{:S(2)}) collective-permute-start(bf16[512,128]{1,0:T(8,128)(2,1)S(1)} %get-tuple-element.37), channel_id=1, source_target_pairs={{0,192},{32,224},{64,0},{96,32},{128,64},{160,96},{192,128},{224,1... | collective-permute-start | bytes 393224 | tf_op jit(solution)/shard_map/ppermute | solution.py:553
  56.3 1.5 %collective-permute-start.3 = (bf16[512,128]{1,0:T(8,128)(2,1)S(1)}, bf16[512,128]{1,0:T(8,128)(2,1)S(1)}, u32[]{:S(2)}, u32[]{:S(2)}) collective-permute-start(bf16[512,128]{1,0:T(8,128)(2,1)S(1)} %get-tuple-element.38), channel_id=1, source_target_pairs={{0,128},{32,160},{64,192},{96,224},{128,0},{160,32},{192,64},{224,... | collective-permute-start | bytes 393224 | tf_op jit(solution)/shard_map/ppermute | solution.py:553
  57.8 2.4 %backward.1 = (f32[2,512,128]{2,1,0:T(8,128)S(1)}, bf16[32,32,128]{2,1,0:T(8,128)(2,1)S(1)}) custom-call(bf16[2,128,512]{2,1,0:T(8,128)(2,1)S(1)} %get-tuple-element.33.grad_t, bf16[1408,384]{1,0:T(8,128)(2,1)S(1)} %fusion.4.weight), custom_call_target="tpu_custom_call" | custom-call | flops 4000000000 | bytes 2129920 | tf_op jit(solution)/shard_map/backward/pallas_call | solution.py:440
  60.2 3.1 %collective-permute-done.3.away3 = bf16[512,128]{1,0:T(8,128)(2,1)S(1)} collective-permute-done((bf16[512,128]{1,0:T(8,128)(2,1)S(1)}, bf16[512,128]{1,0:T(8,128)(2,1)S(1)}, u32[]{:S(2)}, u32[]{:S(2)}) %collective-permute-start.3) | collective-permute-done | bytes 131104 | tf_op jit(solution)/shard_map/ppermute | solution.py:553
  63.3 0.1 join.1
  63.4 14.8 %all_to_all.20.got = bf16[32,48,128]{2,1,0:T(8,128)(2,1)S(1)} all-to-all(bf16[32,48,128]{2,1,0:T(8,128)(2,1)S(1)} %join.1), channel_id=1, replica_groups=mesh['grp'=8,'dev'=32] {'dev'}, dimensions={0} | all-to-all | bytes 786432 | tf_op jit(solution)/shard_map/all_to_all | solution.py:573
  78.2 0.8 merge.1
  79.0 17.5 %all_to_all.21.got = bf16[32,48,128]{2,1,0:T(8,128)(2,1)S(1)} all-to-all(bf16[32,48,128]{2,1,0:T(8,128)(2,1)S(1)} %merge.1), channel_id=1, replica_groups=mesh['grp'=8,'dev'=32] {'dev'}, dimensions={0} | all-to-all | bytes 786432 | tf_op jit(solution)/shard_map/all_to_all | solution.py:583
  96.5 0.3 collective-permute-start.6
  96.8 1.8 %collective-permute-start.5 = (bf16[512,128]{1,0:T(8,128)(2,1)S(1)}, bf16[512,128]{1,0:T(8,128)(2,1)S(1)}, u32[]{:S(2)}, u32[]{:S(2)}) collective-permute-start(bf16[512,128]{1,0:T(8,128)(2,1)S(1)} %bitcast.9), channel_id=1, source_target_pairs={{0,128},{32,160},{64,192},{96,224},{128,0},{160,32},{192,64},{224,... | collective-permute-start | bytes 393224 | tf_op jit(solution)/shard_map/ppermute | solution.py:586
  98.6 0.7 collective-permute-start.4
  99.3 5.8 %collective-permute-start.7 = (bf16[512,128]{1,0:T(8,128)(2,1)S(1)}, bf16[512,128]{1,0:T(8,128)(2,1)S(1)}, u32[]{:S(2)}, u32[]{:S(2)}) collective-permute-start(bf16[512,128]{1,0:T(8,128)(2,1)S(1)} %bitcast.11), channel_id=1, source_target_pairs={{0,32},{32,0},{64,96},{96,64},{128,160},{160,128},{192,224},{224,1... | collective-permute-start | bytes 393224 | tf_op jit(solution)/shard_map/ppermute | solution.py:600
  105.1 1.3 %finish.1 = bf16[2,128,512]{2,1,0:T(8,128)(2,1)} custom-call(f32[8,128]{1,0:T(8,128)S(1)} %iota.7.flags, bf16[32,48,128]{2,1,0:T(8,128)(2,1)S(1)} %all_to_all.21.got, f32[2,512,128]{2,1,0:T(8,128)S(1)} %get-tuple-element.40.own, bf16[2,128,512]{2,1,0:T(8,128)(2,1)S(1)} %copy-done.1), custom_call_target="tpu_custom_call" | custom-call | flops 300000000 | bytes 1445888 | tf_op jit(solution)/shard_map/finish/pallas_call | solution.py:440
  106.5 3.9 %collective-permute-start.8 = (bf16[512,128]{1,0:T(8,128)(2,1)S(1)}, bf16[512,128]{1,0:T(8,128)(2,1)S(1)}, u32[]{:S(2)}, u32[]{:S(2)}) collective-permute-start(bf16[512,128]{1,0:T(8,128)(2,1)S(1)} %collective-permute-done.4.refs_1_), channel_id=1, source_target_pairs={{0,32},{32,0},{64,96},{96,64},{128,160},{160,128},{192,224},{224,1... | collective-permute-start | bytes 393224 | tf_op jit(solution)/shard_map/ppermute | solution.py:600
  110.3 0.5 collective-permute-start.10
  110.8 1.1 assemble.2
  111.9 1.1 assemble.3
  (25 shorter events, 0.1 us)
Async XLA Ops:
  0.6 32.1 %copy-start.4 = (bf16[27,128,128]{2,1,0:T(8,128)(2,1)S(1)}, bf16[27,128,128]{2,1,0:T(8,128)(2,1)}, u32[]{:S(2)}) copy-start(bf16[27,128,128]{2,1,0:T(8,128)(2,1)} %param.13) | copy-start | bytes 2654212
  3.2 21.7 %all-to-all-start = ((bf16[32,32,128]{2,1,0:T(8,128)(2,1)}), bf16[32,32,128]{2,1,0:T(8,128)(2,1)S(1)}, u32[]{:S(2)}, u32[]{:S(2)}) async-start(bf16[32,32,128]{2,1,0:T(8,128)(2,1)} %ask.1), calls=%async_computation | async-start | bytes 524288 | tf_op jit(solution)/shard_map/all_to_all | solution.py:501
  15.2 17.7 %copy-start.5 = (bf16[128,256]{1,0:T(8,128)(2,1)S(1)}, bf16[128,256]{1,0:T(8,128)(2,1)}, u32[]{:S(2)}) copy-start(bf16[128,256]{1,0:T(8,128)(2,1)} %param.14) | copy-start | bytes 196612
  15.2 17.7 %copy-start.6 = (bf16[256,128]{1,0:T(8,128)(2,1)S(1)}, bf16[256,128]{1,0:T(8,128)(2,1)}, u32[]{:S(2)}) copy-start(bf16[256,128]{1,0:T(8,128)(2,1)} %param.15) | copy-start | bytes 196612
  26.5 16.0 %all-to-all-start.1 = ((bf16[32,32,128]{2,1,0:T(8,128)(2,1)}), bf16[32,32,128]{2,1,0:T(8,128)(2,1)S(1)}, u32[]{:S(2)}, u32[]{:S(2)}) async-start(bf16[32,32,128]{2,1,0:T(8,128)(2,1)} %get-tuple-element.28), calls=%async_computation.1 | async-start | bytes 524288 | tf_op jit(solution)/shard_map/all_to_all | solution.py:511
  32.8 9.7 %copy-start = (bf16[2,128,512]{2,1,0:T(8,128)(2,1)S(1)}, bf16[2,128,512]{2,1,0:T(8,128)(2,1)}, u32[]{:S(2)}) copy-start(bf16[2,128,512]{2,1,0:T(8,128)(2,1)} %feat.3) | copy-start | bytes 786436
  32.8 9.7 %copy-start.1 = (bf16[2,128,512]{2,1,0:T(8,128)(2,1)S(1)}, bf16[2,128,512]{2,1,0:T(8,128)(2,1)}, u32[]{:S(2)}) copy-start(bf16[2,128,512]{2,1,0:T(8,128)(2,1)} %gout.3) | copy-start | bytes 786436
  32.8 9.7 %copy-start.2 = (s32[2]{0:T(128)S(1)}, s32[2]{0:T(128)}, u32[]{:S(2)}) copy-start(s32[2]{0:T(128)} %parent.1) | copy-start | bytes 28
  32.8 9.7 %copy-start.3 = (s32[2]{0:T(128)S(1)}, s32[2]{0:T(128)}, u32[]{:S(2)}) copy-start(s32[2]{0:T(128)} %child.1) | copy-start | bytes 28
  48.1 5.2 %collective-permute-start = (bf16[2048,128]{1,0:T(8,128)(2,1)S(1)}, bf16[2048,128]{1,0:T(8,128)(2,1)S(1)}, u32[]{:S(2)}, u32[]{:S(2)}) collective-permute-start(bf16[2048,128]{1,0:T(8,128)(2,1)S(1)} %get-tuple-element.31), channel_id=1, source_target_pairs={{0,32},{32,0},{64,96},{96,64},{128,160},{160,128},{192,224},{224,1... | collective-permute-start | bytes 1572872 | tf_op jit(solution)/shard_map/ppermute | solution.py:544
  53.5 6.7 %collective-permute-start.1 = (bf16[512,128]{1,0:T(8,128)(2,1)S(1)}, bf16[512,128]{1,0:T(8,128)(2,1)S(1)}, u32[]{:S(2)}, u32[]{:S(2)}) collective-permute-start(bf16[512,128]{1,0:T(8,128)(2,1)S(1)} %get-tuple-element.36), channel_id=1, source_target_pairs={{0,64},{32,96},{64,128},{96,160},{128,192},{160,224},{192,0},{224,... | collective-permute-start | bytes 393224 | tf_op jit(solution)/shard_map/ppermute | solution.py:553
  54.8 5.4 %collective-permute-start.2 = (bf16[512,128]{1,0:T(8,128)(2,1)S(1)}, bf16[512,128]{1,0:T(8,128)(2,1)S(1)}, u32[]{:S(2)}, u32[]{:S(2)}) collective-permute-start(bf16[512,128]{1,0:T(8,128)(2,1)S(1)} %get-tuple-element.37), channel_id=1, source_target_pairs={{0,192},{32,224},{64,0},{96,32},{128,64},{160,96},{192,128},{224,1... | collective-permute-start | bytes 393224 | tf_op jit(solution)/shard_map/ppermute | solution.py:553
  56.3 7.0 %collective-permute-start.3 = (bf16[512,128]{1,0:T(8,128)(2,1)S(1)}, bf16[512,128]{1,0:T(8,128)(2,1)S(1)}, u32[]{:S(2)}, u32[]{:S(2)}) collective-permute-start(bf16[512,128]{1,0:T(8,128)(2,1)S(1)} %get-tuple-element.38), channel_id=1, source_target_pairs={{0,128},{32,160},{64,192},{96,224},{128,0},{160,32},{192,64},{224,... | collective-permute-start | bytes 393224 | tf_op jit(solution)/shard_map/ppermute | solution.py:553
  96.5 9.9 %collective-permute-start.6 = (bf16[512,128]{1,0:T(8,128)(2,1)S(1)}, bf16[512,128]{1,0:T(8,128)(2,1)S(1)}, u32[]{:S(2)}, u32[]{:S(2)}) collective-permute-start(bf16[512,128]{1,0:T(8,128)(2,1)S(1)} %bitcast.8), channel_id=1, source_target_pairs={{0,64},{32,96},{64,128},{96,160},{128,192},{160,224},{192,0},{224,... | collective-permute-start | bytes 393224 | tf_op jit(solution)/shard_map/ppermute | solution.py:586
  96.8 9.7 %collective-permute-start.5 = (bf16[512,128]{1,0:T(8,128)(2,1)S(1)}, bf16[512,128]{1,0:T(8,128)(2,1)S(1)}, u32[]{:S(2)}, u32[]{:S(2)}) collective-permute-start(bf16[512,128]{1,0:T(8,128)(2,1)S(1)} %bitcast.9), channel_id=1, source_target_pairs={{0,128},{32,160},{64,192},{96,224},{128,0},{160,32},{192,64},{224,... | collective-permute-start | bytes 393224 | tf_op jit(solution)/shard_map/ppermute | solution.py:586
  98.6 7.9 %collective-permute-start.4 = (bf16[512,128]{1,0:T(8,128)(2,1)S(1)}, bf16[512,128]{1,0:T(8,128)(2,1)S(1)}, u32[]{:S(2)}, u32[]{:S(2)}) collective-permute-start(bf16[512,128]{1,0:T(8,128)(2,1)S(1)} %bitcast.10), channel_id=1, source_target_pairs={{0,192},{32,224},{64,0},{96,32},{128,64},{160,96},{192,128},{224,1... | collective-permute-start | bytes 393224 | tf_op jit(solution)/shard_map/ppermute | solution.py:586
  99.3 12.6 %collective-permute-start.7 = (bf16[512,128]{1,0:T(8,128)(2,1)S(1)}, bf16[512,128]{1,0:T(8,128)(2,1)S(1)}, u32[]{:S(2)}, u32[]{:S(2)}) collective-permute-start(bf16[512,128]{1,0:T(8,128)(2,1)S(1)} %bitcast.11), channel_id=1, source_target_pairs={{0,32},{32,0},{64,96},{96,64},{128,160},{160,128},{192,224},{224,1... | collective-permute-start | bytes 393224 | tf_op jit(solution)/shard_map/ppermute | solution.py:600
  106.5 5.5 %collective-permute-start.8 = (bf16[512,128]{1,0:T(8,128)(2,1)S(1)}, bf16[512,128]{1,0:T(8,128)(2,1)S(1)}, u32[]{:S(2)}, u32[]{:S(2)}) collective-permute-start(bf16[512,128]{1,0:T(8,128)(2,1)S(1)} %collective-permute-done.4.refs_1_), channel_id=1, source_target_pairs={{0,32},{32,0},{64,96},{96,64},{128,160},{160,128},{192,224},{224,1... | collective-permute-start | bytes 393224 | tf_op jit(solution)/shard_map/ppermute | solution.py:600
  110.3 1.6 %collective-permute-start.9 = (bf16[512,128]{1,0:T(8,128)(2,1)S(1)}, bf16[512,128]{1,0:T(8,128)(2,1)S(1)}, u32[]{:S(2)}, u32[]{:S(2)}) collective-permute-start(bf16[512,128]{1,0:T(8,128)(2,1)S(1)} %collective-permute-done.5.refs_2_), channel_id=1, source_target_pairs={{0,32},{32,0},{64,96},{96,64},{128,160},{160,128},{192,224},{224,1... | collective-permute-start | bytes 393224 | tf_op jit(solution)/shard_map/ppermute | solution.py:600
  110.3 1.6 %collective-permute-start.10 = (bf16[512,128]{1,0:T(8,128)(2,1)S(1)}, bf16[512,128]{1,0:T(8,128)(2,1)S(1)}, u32[]{:S(2)}, u32[]{:S(2)}) collective-permute-start(bf16[512,128]{1,0:T(8,128)(2,1)S(1)} %collective-permute-done.6.refs_3_), channel_id=1, source_target_pairs={{0,32},{32,0},{64,96},{96,64},{128,160},{160,128},{192,224},{224,1... | collective-permute-start | bytes 393224 | tf_op jit(solution)/shard_map/ppermute | solution.py:600

commit v10 on v9

--- a/solution.py
+++ b/solution.py
@@ -156,31 +156,41 @@
 
 
 def same_part():
-    rows = lax.broadcasted_iota(jnp.int32, (16, 128), 0)
-    lanes = lax.broadcasted_iota(jnp.int32, (16, 128), 1) & 15
+    rows = lax.broadcasted_iota(jnp.int32, (16, 128), 0) & 7
+    lanes = lax.broadcasted_iota(jnp.int32, (16, 128), 1) & 7
     return (rows == lanes).astype(F32).astype(BF)
 
 
+def split_parts(got, s):
+    rows = got[:, 16 * s : 16 * s + 16, :].astype(F32)
+    return rows[:, 0:8, :], rows[:, 8:16, :]
+
+
 def route_kernel(got, out, named, hot):
-    same = jnp.broadcast_to(same_part()[None], (32, 16, 128))
-    zero = jnp.zeros((32, 16, 128), BF)
+    same = jnp.broadcast_to(same_part()[None], (16, 16, 128))
+    zero = jnp.zeros((16, 16, 128), BF)
     ones = jnp.ones((128, 128), BF)
-    part = lax.broadcasted_iota(jnp.int32, (16, 128), 0)
-    lanes = lax.broadcasted_iota(jnp.int32, (16, 128), 1)
-    place = (lanes == part + 32)[None]
-    for s in range(2):
-        table = got[:, 16 * s : 16 * s + 16, :].astype(F32)[:, 15:16, :]
-        table = jnp.where(place, jnp.broadcast_to(table, (32, 16, 128)), 0.0)
-        asked = nn(table.astype(BF).reshape(512, 128), ones)
-        named[s] = asked.T[0:16].astype(BF)
-        asked = asked.astype(BF).reshape(32, 16, 128)
-        for n in range(8):
-            here = ((lanes >> 4) + 8 * n).astype(F32).astype(BF)
-            picked = jnp.where(asked == here[None], same, zero)
-            hot[s * 512 : s * 512 + 512, n * 128 : n * 128 + 128] = picked.reshape(512, 128)
-    answer = nn(hot[...], got[...].reshape(1024, 128)).astype(BF)
-    for s in range(2):
-        out[:, 16 * s : 16 * s + 16, :] = answer[s * 512 : s * 512 + 512].reshape(32, 16, 128)
+    part = lax.broadcasted_iota(jnp.int32, (8, 128), 0)
+    lanes = lax.broadcasted_iota(jnp.int32, (8, 128), 1)
+    brick = lax.broadcasted_iota(jnp.int32, (16, 128), 1) >> 3
+    split = [split_parts(got, s) for s in range(2)]
+    answers = []
+    for h in range(2):
+        for s in range(2):
+            table = jnp.broadcast_to(split[s][1][:, 7:8, :], (32, 8, 128))
+            table = jnp.where((lanes == part + 32 + 8 * h)[None], table, 0.0)
+            asked = nn(table.reshape(256, 128).astype(BF), ones)
+            named[h, :, s * 256 : s * 256 + 256] = asked.T[0:16].astype(BF)
+            asked = asked.astype(BF).reshape(16, 16, 128)
+            for n in range(4):
+                here = (brick + 16 * n).astype(F32).astype(BF)
+                picked = jnp.where(asked == here[None], same, zero).reshape(256, 128)
+                hot[h, s * 256 : s * 256 + 256, n * 128 : n * 128 + 128] = picked
+        held = jnp.stack([split[0][h], split[1][h]], axis=1).reshape(512, 128).astype(BF)
+        answers.append(nn(hot[h], held))
+    for s in range(2):
+        rows = [x[s * 256 : s * 256 + 256].reshape(32, 8, 128) for x in answers]
+        out[:, 16 * s : 16 * s + 16, :] = jnp.concatenate(rows, axis=1).astype(BF)
 
 
 def forward_kernel(
@@ -231,8 +241,13 @@
                     cols[at : at + 64, (3 * b + c) * 128 : (3 * b + c) * 128 + 128] = ref[
                         pl.ds(start, 64), :
                     ].astype(BF)
+    pres = []
+    for s in range(2):
         taps = nn(cols[640 * s : 640 * s + 640, :], weight[0:1152, :])
         pre = taps[0:512, 0:128] + taps[64:576, 128:256] + taps[128:640, 256:384]
+        pres.append(pre)
+    for s in range(2):
+        pre = pres[s]
         pool_voxels(pre * (1.0 / (1.0 + jnp.exp(-pre))), pooled, 8 * s)
         pre = pre.T
         gate = 1.0 / (1.0 + jnp.exp(-pre))
@@ -352,16 +367,21 @@
     zero = jnp.zeros((16, 128), BF)
     share = jnp.sum(got[:, 32:48, :].astype(F32), axis=0).astype(BF)
     out[:, 32:48, :] = jnp.broadcast_to(share[None], (32, 16, 128))
-    total = jnp.zeros((1024, 128), F32)
-    for s in range(2):
+    second = lax.broadcasted_iota(jnp.int32, (16, 128), 0) >> 3
+    split = [split_parts(got, s) for s in range(2)]
+    totals = []
+    for h in range(2):
         for n in range(4):
-            asked = named[s, :, n * 128 : n * 128 + 128]
-            for brick in range(64):
-                hot[s, brick * 16 : brick * 16 + 16, n * 128 : n * 128 + 128] = jnp.where(
-                    asked == jnp.full((16, 128), brick, BF), same, zero
+            asked = named[h, :, n * 128 : n * 128 + 128]
+            for pair in range(32):
+                here = (second + 2 * pair).astype(F32).astype(BF)
+                hot[h, pair * 16 : pair * 16 + 16, n * 128 : n * 128 + 128] = jnp.where(
+                    asked == here, same, zero
                 )
-        total = total + nn(hot[s], got[:, 16 * s : 16 * s + 16, :].reshape(512, 128))
-    out[:, 0:32, :] = total.astype(BF).reshape(32, 32, 128)
+        held = [x[h].reshape(256, 128) for x in split]
+        totals.append(nn(hot[h], jnp.concatenate(held, axis=0).astype(BF)).reshape(64, 8, 128))
+    total = jnp.concatenate(totals, axis=1).astype(BF)
+    out[:, 0:32, :] = total.reshape(32, 32, 128)
 
 
 def finish_kernel(flags, got, own, gout, out, rows, pc, total):
@@ -504,7 +524,7 @@
         [shape((32, 32, 128), BF), shape((2, 16, 512), BF)],
         [],
         [first],
-        [pltpu.VMEM((1024, 1024), BF)],
+        [pltpu.VMEM((2, 512, 512), BF)],
         flops=3e8,
         name="route",
     )
@@ -576,7 +596,7 @@
         [shape((32, 48, 128), BF)],
         [],
         [terms, table],
-        [pltpu.VMEM((2, 1024, 512), BF)],
+        [pltpu.VMEM((2, 512, 512), BF)],
         flops=3e8,
         name="merge",
     )
@@ -595,7 +615,8 @@
         flops=3e8,
         name="finish",
     )
-    parts, grad_features = lax.optimization_barrier((parts, grad_features))
+    for step in (1, 3, 2):
+        parts[step], grad_features = lax.optimization_barrier((parts[step], grad_features))
     mine = [chunk, parts[1], parts[2], parts[3]]
     others = [lax.ppermute(x, "grp", swap) for x in mine]
 

time: 114 us -> 113 us (level)
  transfers between devices with their start and end apart: 13 -> 13, of which waited for: 4 -> 5; matrix products, arithmetic and copies ran while one was open for 0% -> 0% of each run, Pallas kernels for 4% -> 4%
where the time goes in v10:
time: 113 us
  starting transfers between devices  38.9 us (34%)
  blocking collectives  32.3 us (29%)
  waiting for transfers between devices  23.3 us (21%)
  Pallas kernels  16 us (14%)
  between operations  1.7 us (2%)
    all_to_all x1, blocking collectives, on_device(): back = lax.all_to_all(sums, 'dev', split_axis=0, concat_axis=0, tiled=True)  17.5 us
    pallas_call x10, Pallas kernels, call(): pl.pallas_call(kernel, out_shape=shapes, in_specs=[SM] * len(scalars) + (...  16 us
    all_to_all x1, blocking collectives, on_device(): lax.all_to_all(terms, 'dev', split_axis=0, concat_axis=0, tiled=True)  14.8 us
    all_to_all x1, starting transfers between devices, on_device(): first = lax.all_to_all(msg, 'dev', split_axis=0, concat_axis=0, tiled=True)  12 us
    ppermute x4, starting transfers between devices, on_device(): others = [lax.ppermute(x, 'grp', swap) for x in mine]  10.5 us
    all_to_all x1, waiting for transfers between devices, on_device(): lax.all_to_all(answer, 'dev', split_axis=0, concat_axis=0, tiled=True)  9.36 us
    all_to_all x1, waiting for transfers between devices, on_device(): first = lax.all_to_all(msg, 'dev', split_axis=0, concat_axis=0, tiled=True)  8.96 us
    all_to_all x1, starting transfers between devices, on_device(): lax.all_to_all(answer, 'dev', split_axis=0, concat_axis=0, tiled=True)  6.29 us
  transfers between devices with their start and end apart: 13, of which 5 were waited for; matrix products, arithmetic and copies ran while one was open for 0% of the time, Pallas kernels for 4%

profile of v10, /device:TPU:1, one launch (start us, length us, event | category | flops | bytes accessed | tf_op | source)
XLA Modules:
  0.0 112.6 jit_solution(2097485535100668077)
XLA Ops:
  0.6 2.5 %ask.1 = bf16[32,32,128]{2,1,0:T(8,128)(2,1)} custom-call(bf16[2,128,512]{2,1,0:T(8,128)(2,1)} %feat.3, s32[2,26]{1,0:T(2,128)} %owner.1, s32[2,26]{1,0:T(2,128)} %slot.1, bf16[128,1024]{1,0:T(8,128)(2,1)} %constant.13.clone.choice), custom_call_target="tpu_custom_call" | custom-call | flops 2000000 | bytes 786848 | tf_op jit(solution)/shard_map/ask/pallas_call | solution.py:460
  3.2 12.0 %all-to-all-start = ((bf16[32,32,128]{2,1,0:T(8,128)(2,1)}), bf16[32,32,128]{2,1,0:T(8,128)(2,1)S(1)}, u32[]{:S(2)}, u32[]{:S(2)}) async-start(bf16[32,32,128]{2,1,0:T(8,128)(2,1)} %ask.1), calls=%async_computation | async-start | bytes 524288 | tf_op jit(solution)/shard_map/all_to_all | solution.py:521
  15.9 9.0 %all-to-all-done.got = bf16[32,32,128]{2,1,0:T(8,128)(2,1)S(1)} async-done(((bf16[32,32,128]{2,1,0:T(8,128)(2,1)}), bf16[32,32,128]{2,1,0:T(8,128)(2,1)S(1)}, u32[]{:S(2)}, u32[]{:S(2)}) %all-to-all-start) | async-done | bytes 262176 | tf_op jit(solution)/shard_map/all_to_all | solution.py:521
  24.9 1.3 %route.1 = (bf16[32,32,128]{2,1,0:T(8,128)(2,1)}, bf16[2,16,512]{2,1,0:T(8,128)(2,1)S(1)}) custom-call(bf16[32,32,128]{2,1,0:T(8,128)(2,1)S(1)} %all-to-all-done.got), custom_call_target="tpu_custom_call" | custom-call | flops 300000000 | bytes 557056 | tf_op jit(solution)/shard_map/route/pallas_call | solution.py:460
  26.2 6.3 %all-to-all-start.1 = ((bf16[32,32,128]{2,1,0:T(8,128)(2,1)}), bf16[32,32,128]{2,1,0:T(8,128)(2,1)S(1)}, u32[]{:S(2)}, u32[]{:S(2)}) async-start(bf16[32,32,128]{2,1,0:T(8,128)(2,1)} %get-tuple-element.30), calls=%async_computation.1 | async-start | bytes 524288 | tf_op jit(solution)/shard_map/all_to_all | solution.py:531
  32.6 0.1 fusion.5
  32.7 0.1 fusion.4.weight
  32.8 9.4 %all-to-all-done.1.got = bf16[32,32,128]{2,1,0:T(8,128)(2,1)S(1)} async-done(((bf16[32,32,128]{2,1,0:T(8,128)(2,1)}), bf16[32,32,128]{2,1,0:T(8,128)(2,1)S(1)}, u32[]{:S(2)}, u32[]{:S(2)}) %all-to-all-start.1) | async-done | bytes 262176 | tf_op jit(solution)/shard_map/all_to_all | solution.py:531
  42.2 0.1 iota.7.flags
  42.3 5.6 %forward.1 = (bf16[2,128,512]{2,1,0:T(8,128)(2,1)}, bf16[2,128,512]{2,1,0:T(8,128)(2,1)S(1)}, bf16[2048,128]{1,0:T(8,128)(2,1)S(1)}, bf16[2048,128]{1,0:T(8,128)(2,1)S(1)}) custom-call(s32[2]{0:T(128)S(1)} %copy-done.2, s32[2]{0:T(128)S(1)} %copy-done.3, s32[1]{0:T(128)} %bitcast.core, f32[8,128]{1,0:T(8,128)S(1)} %iota.7.flags, ...), custom_call_target="tpu_custom_call" | custom-call | flops 2000000000 | bytes 3444736 | tf_op jit(solution)/shard_map/forward/pallas_call | solution.py:460
  47.9 3.7 %collective-permute-start = (bf16[2048,128]{1,0:T(8,128)(2,1)S(1)}, bf16[2048,128]{1,0:T(8,128)(2,1)S(1)}, u32[]{:S(2)}, u32[]{:S(2)}) collective-permute-start(bf16[2048,128]{1,0:T(8,128)(2,1)S(1)} %get-tuple-element.33), channel_id=1, source_target_pairs={{0,32},{32,0},{64,96},{96,64},{128,160},{160,128},{192,224},{224,1... | collective-permute-start | bytes 1572872 | tf_op jit(solution)/shard_map/ppermute | solution.py:564
  51.6 1.5 %collective-permute-done.other = bf16[2048,128]{1,0:T(8,128)(2,1)S(1)} collective-permute-done((bf16[2048,128]{1,0:T(8,128)(2,1)S(1)}, bf16[2048,128]{1,0:T(8,128)(2,1)S(1)}, u32[]{:S(2)}, u32[]{:S(2)}) %collective-permute-start) | collective-permute-done | bytes 524320 | tf_op jit(solution)/shard_map/ppermute | solution.py:564
  53.1 0.1 pair.1
  53.3 1.3 %collective-permute-start.1 = (bf16[512,128]{1,0:T(8,128)(2,1)S(1)}, bf16[512,128]{1,0:T(8,128)(2,1)S(1)}, u32[]{:S(2)}, u32[]{:S(2)}) collective-permute-start(bf16[512,128]{1,0:T(8,128)(2,1)S(1)} %get-tuple-element.38), channel_id=1, source_target_pairs={{0,64},{32,96},{64,128},{96,160},{128,192},{160,224},{192,0},{224,... | collective-permute-start | bytes 393224 | tf_op jit(solution)/shard_map/ppermute | solution.py:573
  54.6 1.5 %collective-permute-start.2 = (bf16[512,128]{1,0:T(8,128)(2,1)S(1)}, bf16[512,128]{1,0:T(8,128)(2,1)S(1)}, u32[]{:S(2)}, u32[]{:S(2)}) collective-permute-start(bf16[512,128]{1,0:T(8,128)(2,1)S(1)} %get-tuple-element.39), channel_id=1, source_target_pairs={{0,192},{32,224},{64,0},{96,32},{128,64},{160,96},{192,128},{224,1... | collective-permute-start | bytes 393224 | tf_op jit(solution)/shard_map/ppermute | solution.py:573
  56.0 1.5 %collective-permute-start.3 = (bf16[512,128]{1,0:T(8,128)(2,1)S(1)}, bf16[512,128]{1,0:T(8,128)(2,1)S(1)}, u32[]{:S(2)}, u32[]{:S(2)}) collective-permute-start(bf16[512,128]{1,0:T(8,128)(2,1)S(1)} %get-tuple-element.40), channel_id=1, source_target_pairs={{0,128},{32,160},{64,192},{96,224},{128,0},{160,32},{192,64},{224,... | collective-permute-start | bytes 393224 | tf_op jit(solution)/shard_map/ppermute | solution.py:573
  57.6 2.4 %backward.1 = (f32[2,512,128]{2,1,0:T(8,128)S(1)}, bf16[32,32,128]{2,1,0:T(8,128)(2,1)S(1)}) custom-call(bf16[2,128,512]{2,1,0:T(8,128)(2,1)S(1)} %get-tuple-element.35.grad_t, bf16[1408,384]{1,0:T(8,128)(2,1)S(1)} %fusion.4.weight), custom_call_target="tpu_custom_call" | custom-call | flops 4000000000 | bytes 2129920 | tf_op jit(solution)/shard_map/backward/pallas_call | solution.py:460
  60.0 3.1 %collective-permute-done.3.away3 = bf16[512,128]{1,0:T(8,128)(2,1)S(1)} collective-permute-done((bf16[512,128]{1,0:T(8,128)(2,1)S(1)}, bf16[512,128]{1,0:T(8,128)(2,1)S(1)}, u32[]{:S(2)}, u32[]{:S(2)}) %collective-permute-start.3) | collective-permute-done | bytes 131104 | tf_op jit(solution)/shard_map/ppermute | solution.py:573
  63.1 0.1 join.1
  63.2 14.8 %all_to_all.20.got = bf16[32,48,128]{2,1,0:T(8,128)(2,1)S(1)} all-to-all(bf16[32,48,128]{2,1,0:T(8,128)(2,1)S(1)} %join.1), channel_id=1, replica_groups=mesh['grp'=8,'dev'=32] {'dev'}, dimensions={0} | all-to-all | bytes 786432 | tf_op jit(solution)/shard_map/all_to_all | solution.py:593
  78.0 0.5 merge.1
  78.4 17.5 %all_to_all.21.got = bf16[32,48,128]{2,1,0:T(8,128)(2,1)S(1)} all-to-all(bf16[32,48,128]{2,1,0:T(8,128)(2,1)S(1)} %merge.1), channel_id=1, replica_groups=mesh['grp'=8,'dev'=32] {'dev'}, dimensions={0} | all-to-all | bytes 786432 | tf_op jit(solution)/shard_map/all_to_all | solution.py:603
  96.0 0.9 collective-permute-start.6
  96.8 0.7 collective-permute-start.5
  97.5 0.6 collective-permute-start.4
  98.1 5.8 %collective-permute-start.7 = (bf16[512,128]{1,0:T(8,128)(2,1)S(1)}, bf16[512,128]{1,0:T(8,128)(2,1)S(1)}, u32[]{:S(2)}, u32[]{:S(2)}) collective-permute-start(bf16[512,128]{1,0:T(8,128)(2,1)S(1)} %bitcast.11), channel_id=1, source_target_pairs={{0,32},{32,0},{64,96},{96,64},{128,160},{160,128},{192,224},{224,1... | collective-permute-start | bytes 393224 | tf_op jit(solution)/shard_map/ppermute | solution.py:621
  103.9 1.3 %finish.1 = bf16[2,128,512]{2,1,0:T(8,128)(2,1)} custom-call(f32[8,128]{1,0:T(8,128)S(1)} %iota.7.flags, bf16[32,48,128]{2,1,0:T(8,128)(2,1)S(1)} %all_to_all.21.got, f32[2,512,128]{2,1,0:T(8,128)S(1)} %get-tuple-element.42.own, bf16[2,128,512]{2,1,0:T(8,128)(2,1)S(1)} %copy-done.1), custom_call_target="tpu_custom_call" | custom-call | flops 300000000 | bytes 1445888 | tf_op jit(solution)/shard_map/finish/pallas_call | solution.py:460
  105.3 1.0 collective-permute-start.8
  106.3 3.7 %collective-permute-start.10 = (bf16[512,128]{1,0:T(8,128)(2,1)S(1)}, bf16[512,128]{1,0:T(8,128)(2,1)S(1)}, u32[]{:S(2)}, u32[]{:S(2)}) collective-permute-start(bf16[512,128]{1,0:T(8,128)(2,1)S(1)} %collective-permute-done.5.refs_3_), channel_id=1, source_target_pairs={{0,32},{32,0},{64,96},{96,64},{128,160},{160,128},{192,224},{224,1... | collective-permute-start | bytes 393224 | tf_op jit(solution)/shard_map/ppermute | solution.py:621
  110.0 1.1 assemble.2
  111.1 0.3 collective-permute-done.9.refs_2_
  111.3 1.1 assemble.3
  (25 shorter events, 0.1 us)
Async XLA Ops:
  0.6 31.9 %copy-start.4 = (bf16[27,128,128]{2,1,0:T(8,128)(2,1)S(1)}, bf16[27,128,128]{2,1,0:T(8,128)(2,1)}, u32[]{:S(2)}) copy-start(bf16[27,128,128]{2,1,0:T(8,128)(2,1)} %param.13) | copy-start | bytes 2654212
  3.2 21.7 %all-to-all-start = ((bf16[32,32,128]{2,1,0:T(8,128)(2,1)}), bf16[32,32,128]{2,1,0:T(8,128)(2,1)S(1)}, u32[]{:S(2)}, u32[]{:S(2)}) async-start(bf16[32,32,128]{2,1,0:T(8,128)(2,1)} %ask.1), calls=%async_computation | async-start | bytes 524288 | tf_op jit(solution)/shard_map/all_to_all | solution.py:521
  15.2 17.4 %copy-start.5 = (bf16[128,256]{1,0:T(8,128)(2,1)S(1)}, bf16[128,256]{1,0:T(8,128)(2,1)}, u32[]{:S(2)}) copy-start(bf16[128,256]{1,0:T(8,128)(2,1)} %param.14) | copy-start | bytes 196612
  15.2 17.4 %copy-start.6 = (bf16[256,128]{1,0:T(8,128)(2,1)S(1)}, bf16[256,128]{1,0:T(8,128)(2,1)}, u32[]{:S(2)}) copy-start(bf16[256,128]{1,0:T(8,128)(2,1)} %param.15) | copy-start | bytes 196612
  26.2 16.0 %all-to-all-start.1 = ((bf16[32,32,128]{2,1,0:T(8,128)(2,1)}), bf16[32,32,128]{2,1,0:T(8,128)(2,1)S(1)}, u32[]{:S(2)}, u32[]{:S(2)}) async-start(bf16[32,32,128]{2,1,0:T(8,128)(2,1)} %get-tuple-element.30), calls=%async_computation.1 | async-start | bytes 524288 | tf_op jit(solution)/shard_map/all_to_all | solution.py:531
  32.5 9.7 %copy-start = (bf16[2,128,512]{2,1,0:T(8,128)(2,1)S(1)}, bf16[2,128,512]{2,1,0:T(8,128)(2,1)}, u32[]{:S(2)}) copy-start(bf16[2,128,512]{2,1,0:T(8,128)(2,1)} %feat.3) | copy-start | bytes 786436
  32.6 9.7 %copy-start.1 = (bf16[2,128,512]{2,1,0:T(8,128)(2,1)S(1)}, bf16[2,128,512]{2,1,0:T(8,128)(2,1)}, u32[]{:S(2)}) copy-start(bf16[2,128,512]{2,1,0:T(8,128)(2,1)} %gout.3) | copy-start | bytes 786436
  32.6 9.7 %copy-start.2 = (s32[2]{0:T(128)S(1)}, s32[2]{0:T(128)}, u32[]{:S(2)}) copy-start(s32[2]{0:T(128)} %parent.1) | copy-start | bytes 28
  32.6 9.7 %copy-start.3 = (s32[2]{0:T(128)S(1)}, s32[2]{0:T(128)}, u32[]{:S(2)}) copy-start(s32[2]{0:T(128)} %child.1) | copy-start | bytes 28
  47.9 5.2 %collective-permute-start = (bf16[2048,128]{1,0:T(8,128)(2,1)S(1)}, bf16[2048,128]{1,0:T(8,128)(2,1)S(1)}, u32[]{:S(2)}, u32[]{:S(2)}) collective-permute-start(bf16[2048,128]{1,0:T(8,128)(2,1)S(1)} %get-tuple-element.33), channel_id=1, source_target_pairs={{0,32},{32,0},{64,96},{96,64},{128,160},{160,128},{192,224},{224,1... | collective-permute-start | bytes 1572872 | tf_op jit(solution)/shard_map/ppermute | solution.py:564
  53.3 6.7 %collective-permute-start.1 = (bf16[512,128]{1,0:T(8,128)(2,1)S(1)}, bf16[512,128]{1,0:T(8,128)(2,1)S(1)}, u32[]{:S(2)}, u32[]{:S(2)}) collective-permute-start(bf16[512,128]{1,0:T(8,128)(2,1)S(1)} %get-tuple-element.38), channel_id=1, source_target_pairs={{0,64},{32,96},{64,128},{96,160},{128,192},{160,224},{192,0},{224,... | collective-permute-start | bytes 393224 | tf_op jit(solution)/shard_map/ppermute | solution.py:573
  54.6 5.4 %collective-permute-start.2 = (bf16[512,128]{1,0:T(8,128)(2,1)S(1)}, bf16[512,128]{1,0:T(8,128)(2,1)S(1)}, u32[]{:S(2)}, u32[]{:S(2)}) collective-permute-start(bf16[512,128]{1,0:T(8,128)(2,1)S(1)} %get-tuple-element.39), channel_id=1, source_target_pairs={{0,192},{32,224},{64,0},{96,32},{128,64},{160,96},{192,128},{224,1... | collective-permute-start | bytes 393224 | tf_op jit(solution)/shard_map/ppermute | solution.py:573
  56.0 7.0 %collective-permute-start.3 = (bf16[512,128]{1,0:T(8,128)(2,1)S(1)}, bf16[512,128]{1,0:T(8,128)(2,1)S(1)}, u32[]{:S(2)}, u32[]{:S(2)}) collective-permute-start(bf16[512,128]{1,0:T(8,128)(2,1)S(1)} %get-tuple-element.40), channel_id=1, source_target_pairs={{0,128},{32,160},{64,192},{96,224},{128,0},{160,32},{192,64},{224,... | collective-permute-start | bytes 393224 | tf_op jit(solution)/shard_map/ppermute | solution.py:573
  96.0 9.3 %collective-permute-start.6 = (bf16[512,128]{1,0:T(8,128)(2,1)S(1)}, bf16[512,128]{1,0:T(8,128)(2,1)S(1)}, u32[]{:S(2)}, u32[]{:S(2)}) collective-permute-start(bf16[512,128]{1,0:T(8,128)(2,1)S(1)} %bitcast.8), channel_id=1, source_target_pairs={{0,192},{32,224},{64,0},{96,32},{128,64},{160,96},{192,128},{224,1... | collective-permute-start | bytes 393224 | tf_op jit(solution)/shard_map/ppermute | solution.py:606
  96.8 9.4 %collective-permute-start.5 = (bf16[512,128]{1,0:T(8,128)(2,1)S(1)}, bf16[512,128]{1,0:T(8,128)(2,1)S(1)}, u32[]{:S(2)}, u32[]{:S(2)}) collective-permute-start(bf16[512,128]{1,0:T(8,128)(2,1)S(1)} %bitcast.9), channel_id=1, source_target_pairs={{0,64},{32,96},{64,128},{96,160},{128,192},{160,224},{192,0},{224,... | collective-permute-start | bytes 393224 | tf_op jit(solution)/shard_map/ppermute | solution.py:606
  97.5 12.4 %collective-permute-start.4 = (bf16[512,128]{1,0:T(8,128)(2,1)S(1)}, bf16[512,128]{1,0:T(8,128)(2,1)S(1)}, u32[]{:S(2)}, u32[]{:S(2)}) collective-permute-start(bf16[512,128]{1,0:T(8,128)(2,1)S(1)} %bitcast.10), channel_id=1, source_target_pairs={{0,128},{32,160},{64,192},{96,224},{128,0},{160,32},{192,64},{224,... | collective-permute-start | bytes 393224 | tf_op jit(solution)/shard_map/ppermute | solution.py:606
  98.1 12.9 %collective-permute-start.7 = (bf16[512,128]{1,0:T(8,128)(2,1)S(1)}, bf16[512,128]{1,0:T(8,128)(2,1)S(1)}, u32[]{:S(2)}, u32[]{:S(2)}) collective-permute-start(bf16[512,128]{1,0:T(8,128)(2,1)S(1)} %bitcast.11), channel_id=1, source_target_pairs={{0,32},{32,0},{64,96},{96,64},{128,160},{160,128},{192,224},{224,1... | collective-permute-start | bytes 393224 | tf_op jit(solution)/shard_map/ppermute | solution.py:621
  105.3 5.8 %collective-permute-start.8 = (bf16[512,128]{1,0:T(8,128)(2,1)S(1)}, bf16[512,128]{1,0:T(8,128)(2,1)S(1)}, u32[]{:S(2)}, u32[]{:S(2)}) collective-permute-start(bf16[512,128]{1,0:T(8,128)(2,1)S(1)} %collective-permute-done.6.refs_1_), channel_id=1, source_target_pairs={{0,32},{32,0},{64,96},{96,64},{128,160},{160,128},{192,224},{224,1... | collective-permute-start | bytes 393224 | tf_op jit(solution)/shard_map/ppermute | solution.py:621
  106.3 4.8 %collective-permute-start.10 = (bf16[512,128]{1,0:T(8,128)(2,1)S(1)}, bf16[512,128]{1,0:T(8,128)(2,1)S(1)}, u32[]{:S(2)}, u32[]{:S(2)}) collective-permute-start(bf16[512,128]{1,0:T(8,128)(2,1)S(1)} %collective-permute-done.5.refs_3_), channel_id=1, source_target_pairs={{0,32},{32,0},{64,96},{96,64},{128,160},{160,128},{192,224},{224,1... | collective-permute-start | bytes 393224 | tf_op jit(solution)/shard_map/ppermute | solution.py:621
  110.0 1.3 %collective-permute-start.9 = (bf16[512,128]{1,0:T(8,128)(2,1)S(1)}, bf16[512,128]{1,0:T(8,128)(2,1)S(1)}, u32[]{:S(2)}, u32[]{:S(2)}) collective-permute-start(bf16[512,128]{1,0:T(8,128)(2,1)S(1)} %collective-permute-done.4.refs_2_), channel_id=1, source_target_pairs={{0,32},{32,0},{64,96},{96,64},{128,160},{160,128},{192,224},{224,1... | collective-permute-start | bytes 393224 | tf_op jit(solution)/shard_map/ppermute | solution.py:621

commit v11 on v10

--- a/solution.py
+++ b/solution.py
@@ -196,23 +196,21 @@
 def forward_kernel(
     parent, child, core, flags, feat, got, gout, weight,
     out, grad_t, keep, send,
-    rows_all, pc_all, mine_all, s0_all, s1_all, s2_all, cols, pooled, grad_pooled, out_v, wsum, sem,
+    rows_all, pc_all, s0_all, s1_all, s2_all, cols, pooled, grad_pooled, out_v, wsum, sem,
 ):
     eye = identity()
     up, down = weight[1152:1280, 0:256], weight[1152:1408, 256:384]
     acts, slopes = [], []
     for s in range(2):
-        rows, pc, mine, s0, s1, s2 = (
-            x.at[s] for x in (rows_all, pc_all, mine_all, s0_all, s1_all, s2_all)
-        )
+        rows, pc, s0, s1, s2 = (x.at[s] for x in (rows_all, pc_all, s0_all, s1_all, s2_all))
         live = flags[s : s + 1, 0:1]
         pool = pool_rows(s)
-        mine[...] = (feat[s].astype(F32) * live).T
+        mine = (feat[s].astype(F32) * live).T
         grad_pooled[s] = nt(pool, gout[s]) * live
         rows[...] = got[:, 16 * s : 16 * s + 16, :].reshape(512, 128).astype(F32)
         to_pieces(rows, pc)
         for a in range(8):
-            s1[pl.ds(8 + ((a + 1) * 10 + 1) * 8, 64), :] = mine[a * 64 : a * 64 + 64, :]
+            s1[pl.ds(8 + ((a + 1) * 10 + 1) * 8, 64), :] = mine[a * 64 : a * 64 + 64]
             for d, b in (((0, -1, 0), 0), ((0, 1, 0), 9)):
                 s1[pl.ds(8 + ((a + 1) * 10 + b) * 8, 8), :] = pc[pl.ds(PIECE[d] + 8 * a, 8), :]
         for a, x in ((-1, 0), (1, 9)):
@@ -546,7 +544,6 @@
         [
             pltpu.VMEM((2, 512, 128), F32),
             pltpu.VMEM((2, 512, 128), F32),
-            pltpu.VMEM((2, 512, 128), F32),
             pltpu.VMEM((2, 800, 128), F32),
             pltpu.VMEM((2, 816, 128), F32),
             pltpu.VMEM((2, 800, 128), F32),

time: 113 us -> 113 us (level)
  no operation moved by 1% of the time
where the time goes in v11:
time: 113 us
  starting transfers between devices  38.9 us (34%)
  blocking collectives  32.3 us (29%)
  waiting for transfers between devices  23.3 us (21%)
  Pallas kernels  16 us (14%)
  between operations  1.7 us (2%)
    all_to_all x1, blocking collectives, on_device(): back = lax.all_to_all(sums, 'dev', split_axis=0, concat_axis=0, tiled=True)  17.5 us
    pallas_call x10, Pallas kernels, call(): pl.pallas_call(kernel, out_shape=shapes, in_specs=[SM] * len(scalars) + (...  16 us
    all_to_all x1, blocking collectives, on_device(): lax.all_to_all(terms, 'dev', split_axis=0, concat_axis=0, tiled=True)  14.8 us
    all_to_all x1, starting transfers between devices, on_device(): first = lax.all_to_all(msg, 'dev', split_axis=0, concat_axis=0, tiled=True)  12 us
    ppermute x4, starting transfers between devices, on_device(): others = [lax.ppermute(x, 'grp', swap) for x in mine]  10.5 us
    all_to_all x1, waiting for transfers between devices, on_device(): lax.all_to_all(answer, 'dev', split_axis=0, concat_axis=0, tiled=True)  9.36 us
    all_to_all x1, waiting for transfers between devices, on_device(): first = lax.all_to_all(msg, 'dev', split_axis=0, concat_axis=0, tiled=True)  8.96 us
    all_to_all x1, starting transfers between devices, on_device(): lax.all_to_all(answer, 'dev', split_axis=0, concat_axis=0, tiled=True)  6.29 us
  transfers between devices with their start and end apart: 13, of which 5 were waited for; matrix products, arithmetic and copies ran while one was open for 0% of the time, Pallas kernels for 4%

profile of v11, /device:TPU:1, one launch (start us, length us, event | category | flops | bytes accessed | tf_op | source)
XLA Modules:
  0.0 112.6 jit_solution(2097485535100668077)
XLA Ops:
  0.6 2.5 %ask.1 = bf16[32,32,128]{2,1,0:T(8,128)(2,1)} custom-call(bf16[2,128,512]{2,1,0:T(8,128)(2,1)} %feat.3, s32[2,26]{1,0:T(2,128)} %owner.1, s32[2,26]{1,0:T(2,128)} %slot.1, bf16[128,1024]{1,0:T(8,128)(2,1)} %constant.13.clone.choice), custom_call_target="tpu_custom_call" | custom-call | flops 2000000 | bytes 786848 | tf_op jit(solution)/shard_map/ask/pallas_call | solution.py:458
  3.2 12.0 %all-to-all-start = ((bf16[32,32,128]{2,1,0:T(8,128)(2,1)}), bf16[32,32,128]{2,1,0:T(8,128)(2,1)S(1)}, u32[]{:S(2)}, u32[]{:S(2)}) async-start(bf16[32,32,128]{2,1,0:T(8,128)(2,1)} %ask.1), calls=%async_computation | async-start | bytes 524288 | tf_op jit(solution)/shard_map/all_to_all | solution.py:519
  15.9 9.0 %all-to-all-done.got = bf16[32,32,128]{2,1,0:T(8,128)(2,1)S(1)} async-done(((bf16[32,32,128]{2,1,0:T(8,128)(2,1)}), bf16[32,32,128]{2,1,0:T(8,128)(2,1)S(1)}, u32[]{:S(2)}, u32[]{:S(2)}) %all-to-all-start) | async-done | bytes 262176 | tf_op jit(solution)/shard_map/all_to_all | solution.py:519
  24.9 1.3 %route.1 = (bf16[32,32,128]{2,1,0:T(8,128)(2,1)}, bf16[2,16,512]{2,1,0:T(8,128)(2,1)S(1)}) custom-call(bf16[32,32,128]{2,1,0:T(8,128)(2,1)S(1)} %all-to-all-done.got), custom_call_target="tpu_custom_call" | custom-call | flops 300000000 | bytes 557056 | tf_op jit(solution)/shard_map/route/pallas_call | solution.py:458
  26.2 6.3 %all-to-all-start.1 = ((bf16[32,32,128]{2,1,0:T(8,128)(2,1)}), bf16[32,32,128]{2,1,0:T(8,128)(2,1)S(1)}, u32[]{:S(2)}, u32[]{:S(2)}) async-start(bf16[32,32,128]{2,1,0:T(8,128)(2,1)} %get-tuple-element.30), calls=%async_computation.1 | async-start | bytes 524288 | tf_op jit(solution)/shard_map/all_to_all | solution.py:529
  32.6 0.1 fusion.5
  32.7 0.1 fusion.4.weight
  32.8 9.4 %all-to-all-done.1.got = bf16[32,32,128]{2,1,0:T(8,128)(2,1)S(1)} async-done(((bf16[32,32,128]{2,1,0:T(8,128)(2,1)}), bf16[32,32,128]{2,1,0:T(8,128)(2,1)S(1)}, u32[]{:S(2)}, u32[]{:S(2)}) %all-to-all-start.1) | async-done | bytes 262176 | tf_op jit(solution)/shard_map/all_to_all | solution.py:529
  42.2 0.1 iota.7.flags
  42.3 5.6 %forward.1 = (bf16[2,128,512]{2,1,0:T(8,128)(2,1)}, bf16[2,128,512]{2,1,0:T(8,128)(2,1)S(1)}, bf16[2048,128]{1,0:T(8,128)(2,1)S(1)}, bf16[2048,128]{1,0:T(8,128)(2,1)S(1)}) custom-call(s32[2]{0:T(128)S(1)} %copy-done.2, s32[2]{0:T(128)S(1)} %copy-done.3, s32[1]{0:T(128)} %bitcast.core, f32[8,128]{1,0:T(8,128)S(1)} %iota.7.flags, ...), custom_call_target="tpu_custom_call" | custom-call | flops 2000000000 | bytes 3444736 | tf_op jit(solution)/shard_map/forward/pallas_call | solution.py:458
  47.9 3.7 %collective-permute-start = (bf16[2048,128]{1,0:T(8,128)(2,1)S(1)}, bf16[2048,128]{1,0:T(8,128)(2,1)S(1)}, u32[]{:S(2)}, u32[]{:S(2)}) collective-permute-start(bf16[2048,128]{1,0:T(8,128)(2,1)S(1)} %get-tuple-element.33), channel_id=1, source_target_pairs={{0,32},{32,0},{64,96},{96,64},{128,160},{160,128},{192,224},{224,1... | collective-permute-start | bytes 1572872 | tf_op jit(solution)/shard_map/ppermute | solution.py:561
  51.6 1.5 %collective-permute-done.other = bf16[2048,128]{1,0:T(8,128)(2,1)S(1)} collective-permute-done((bf16[2048,128]{1,0:T(8,128)(2,1)S(1)}, bf16[2048,128]{1,0:T(8,128)(2,1)S(1)}, u32[]{:S(2)}, u32[]{:S(2)}) %collective-permute-start) | collective-permute-done | bytes 524320 | tf_op jit(solution)/shard_map/ppermute | solution.py:561
  53.1 0.1 pair.1
  53.3 1.3 %collective-permute-start.1 = (bf16[512,128]{1,0:T(8,128)(2,1)S(1)}, bf16[512,128]{1,0:T(8,128)(2,1)S(1)}, u32[]{:S(2)}, u32[]{:S(2)}) collective-permute-start(bf16[512,128]{1,0:T(8,128)(2,1)S(1)} %get-tuple-element.38), channel_id=1, source_target_pairs={{0,64},{32,96},{64,128},{96,160},{128,192},{160,224},{192,0},{224,... | collective-permute-start | bytes 393224 | tf_op jit(solution)/shard_map/ppermute | solution.py:570
  54.6 1.5 %collective-permute-start.2 = (bf16[512,128]{1,0:T(8,128)(2,1)S(1)}, bf16[512,128]{1,0:T(8,128)(2,1)S(1)}, u32[]{:S(2)}, u32[]{:S(2)}) collective-permute-start(bf16[512,128]{1,0:T(8,128)(2,1)S(1)} %get-tuple-element.39), channel_id=1, source_target_pairs={{0,192},{32,224},{64,0},{96,32},{128,64},{160,96},{192,128},{224,1... | collective-permute-start | bytes 393224 | tf_op jit(solution)/shard_map/ppermute | solution.py:570
  56.0 1.5 %collective-permute-start.3 = (bf16[512,128]{1,0:T(8,128)(2,1)S(1)}, bf16[512,128]{1,0:T(8,128)(2,1)S(1)}, u32[]{:S(2)}, u32[]{:S(2)}) collective-permute-start(bf16[512,128]{1,0:T(8,128)(2,1)S(1)} %get-tuple-element.40), channel_id=1, source_target_pairs={{0,128},{32,160},{64,192},{96,224},{128,0},{160,32},{192,64},{224,... | collective-permute-start | bytes 393224 | tf_op jit(solution)/shard_map/ppermute | solution.py:570
  57.6 2.4 %backward.1 = (f32[2,512,128]{2,1,0:T(8,128)S(1)}, bf16[32,32,128]{2,1,0:T(8,128)(2,1)S(1)}) custom-call(bf16[2,128,512]{2,1,0:T(8,128)(2,1)S(1)} %get-tuple-element.35.grad_t, bf16[1408,384]{1,0:T(8,128)(2,1)S(1)} %fusion.4.weight), custom_call_target="tpu_custom_call" | custom-call | flops 4000000000 | bytes 2129920 | tf_op jit(solution)/shard_map/backward/pallas_call | solution.py:458
  60.0 3.1 %collective-permute-done.3.away3 = bf16[512,128]{1,0:T(8,128)(2,1)S(1)} collective-permute-done((bf16[512,128]{1,0:T(8,128)(2,1)S(1)}, bf16[512,128]{1,0:T(8,128)(2,1)S(1)}, u32[]{:S(2)}, u32[]{:S(2)}) %collective-permute-start.3) | collective-permute-done | bytes 131104 | tf_op jit(solution)/shard_map/ppermute | solution.py:570
  63.1 0.1 join.1
  63.2 14.8 %all_to_all.20.got = bf16[32,48,128]{2,1,0:T(8,128)(2,1)S(1)} all-to-all(bf16[32,48,128]{2,1,0:T(8,128)(2,1)S(1)} %join.1), channel_id=1, replica_groups=mesh['grp'=8,'dev'=32] {'dev'}, dimensions={0} | all-to-all | bytes 786432 | tf_op jit(solution)/shard_map/all_to_all | solution.py:590
  78.0 0.5 merge.1
  78.4 17.5 %all_to_all.21.got = bf16[32,48,128]{2,1,0:T(8,128)(2,1)S(1)} all-to-all(bf16[32,48,128]{2,1,0:T(8,128)(2,1)S(1)} %merge.1), channel_id=1, replica_groups=mesh['grp'=8,'dev'=32] {'dev'}, dimensions={0} | all-to-all | bytes 786432 | tf_op jit(solution)/shard_map/all_to_all | solution.py:600
  96.0 0.9 collective-permute-start.6
  96.8 0.7 collective-permute-start.5
  97.5 0.6 collective-permute-start.4
  98.1 5.8 %collective-permute-start.7 = (bf16[512,128]{1,0:T(8,128)(2,1)S(1)}, bf16[512,128]{1,0:T(8,128)(2,1)S(1)}, u32[]{:S(2)}, u32[]{:S(2)}) collective-permute-start(bf16[512,128]{1,0:T(8,128)(2,1)S(1)} %bitcast.11), channel_id=1, source_target_pairs={{0,32},{32,0},{64,96},{96,64},{128,160},{160,128},{192,224},{224,1... | collective-permute-start | bytes 393224 | tf_op jit(solution)/shard_map/ppermute | solution.py:618
  103.9 1.3 %finish.1 = bf16[2,128,512]{2,1,0:T(8,128)(2,1)} custom-call(f32[8,128]{1,0:T(8,128)S(1)} %iota.7.flags, bf16[32,48,128]{2,1,0:T(8,128)(2,1)S(1)} %all_to_all.21.got, f32[2,512,128]{2,1,0:T(8,128)S(1)} %get-tuple-element.42.own, bf16[2,128,512]{2,1,0:T(8,128)(2,1)S(1)} %copy-done.1), custom_call_target="tpu_custom_call" | custom-call | flops 300000000 | bytes 1445888 | tf_op jit(solution)/shard_map/finish/pallas_call | solution.py:458
  105.3 1.0 collective-permute-start.8
  106.3 3.7 %collective-permute-start.10 = (bf16[512,128]{1,0:T(8,128)(2,1)S(1)}, bf16[512,128]{1,0:T(8,128)(2,1)S(1)}, u32[]{:S(2)}, u32[]{:S(2)}) collective-permute-start(bf16[512,128]{1,0:T(8,128)(2,1)S(1)} %collective-permute-done.5.refs_3_), channel_id=1, source_target_pairs={{0,32},{32,0},{64,96},{96,64},{128,160},{160,128},{192,224},{224,1... | collective-permute-start | bytes 393224 | tf_op jit(solution)/shard_map/ppermute | solution.py:618
  110.0 1.1 assemble.2
  111.1 0.3 collective-permute-done.9.refs_2_
  111.3 1.1 assemble.3
  (25 shorter events, 0.1 us)
Async XLA Ops:
  0.6 31.9 %copy-start.4 = (bf16[27,128,128]{2,1,0:T(8,128)(2,1)S(1)}, bf16[27,128,128]{2,1,0:T(8,128)(2,1)}, u32[]{:S(2)}) copy-start(bf16[27,128,128]{2,1,0:T(8,128)(2,1)} %param.13) | copy-start | bytes 2654212
  3.2 21.7 %all-to-all-start = ((bf16[32,32,128]{2,1,0:T(8,128)(2,1)}), bf16[32,32,128]{2,1,0:T(8,128)(2,1)S(1)}, u32[]{:S(2)}, u32[]{:S(2)}) async-start(bf16[32,32,128]{2,1,0:T(8,128)(2,1)} %ask.1), calls=%async_computation | async-start | bytes 524288 | tf_op jit(solution)/shard_map/all_to_all | solution.py:519
  15.2 17.4 %copy-start.5 = (bf16[128,256]{1,0:T(8,128)(2,1)S(1)}, bf16[128,256]{1,0:T(8,128)(2,1)}, u32[]{:S(2)}) copy-start(bf16[128,256]{1,0:T(8,128)(2,1)} %param.14) | copy-start | bytes 196612
  15.2 17.4 %copy-start.6 = (bf16[256,128]{1,0:T(8,128)(2,1)S(1)}, bf16[256,128]{1,0:T(8,128)(2,1)}, u32[]{:S(2)}) copy-start(bf16[256,128]{1,0:T(8,128)(2,1)} %param.15) | copy-start | bytes 196612
  26.2 16.0 %all-to-all-start.1 = ((bf16[32,32,128]{2,1,0:T(8,128)(2,1)}), bf16[32,32,128]{2,1,0:T(8,128)(2,1)S(1)}, u32[]{:S(2)}, u32[]{:S(2)}) async-start(bf16[32,32,128]{2,1,0:T(8,128)(2,1)} %get-tuple-element.30), calls=%async_computation.1 | async-start | bytes 524288 | tf_op jit(solution)/shard_map/all_to_all | solution.py:529
  32.5 9.7 %copy-start = (bf16[2,128,512]{2,1,0:T(8,128)(2,1)S(1)}, bf16[2,128,512]{2,1,0:T(8,128)(2,1)}, u32[]{:S(2)}) copy-start(bf16[2,128,512]{2,1,0:T(8,128)(2,1)} %feat.3) | copy-start | bytes 786436
  32.6 9.7 %copy-start.1 = (bf16[2,128,512]{2,1,0:T(8,128)(2,1)S(1)}, bf16[2,128,512]{2,1,0:T(8,128)(2,1)}, u32[]{:S(2)}) copy-start(bf16[2,128,512]{2,1,0:T(8,128)(2,1)} %gout.3) | copy-start | bytes 786436
  32.6 9.7 %copy-start.2 = (s32[2]{0:T(128)S(1)}, s32[2]{0:T(128)}, u32[]{:S(2)}) copy-start(s32[2]{0:T(128)} %parent.1) | copy-start | bytes 28
  32.6 9.7 %copy-start.3 = (s32[2]{0:T(128)S(1)}, s32[2]{0:T(128)}, u32[]{:S(2)}) copy-start(s32[2]{0:T(128)} %child.1) | copy-start | bytes 28
  47.9 5.2 %collective-permute-start = (bf16[2048,128]{1,0:T(8,128)(2,1)S(1)}, bf16[2048,128]{1,0:T(8,128)(2,1)S(1)}, u32[]{:S(2)}, u32[]{:S(2)}) collective-permute-start(bf16[2048,128]{1,0:T(8,128)(2,1)S(1)} %get-tuple-element.33), channel_id=1, source_target_pairs={{0,32},{32,0},{64,96},{96,64},{128,160},{160,128},{192,224},{224,1... | collective-permute-start | bytes 1572872 | tf_op jit(solution)/shard_map/ppermute | solution.py:561
  53.3 6.7 %collective-permute-start.1 = (bf16[512,128]{1,0:T(8,128)(2,1)S(1)}, bf16[512,128]{1,0:T(8,128)(2,1)S(1)}, u32[]{:S(2)}, u32[]{:S(2)}) collective-permute-start(bf16[512,128]{1,0:T(8,128)(2,1)S(1)} %get-tuple-element.38), channel_id=1, source_target_pairs={{0,64},{32,96},{64,128},{96,160},{128,192},{160,224},{192,0},{224,... | collective-permute-start | bytes 393224 | tf_op jit(solution)/shard_map/ppermute | solution.py:570
  54.6 5.4 %collective-permute-start.2 = (bf16[512,128]{1,0:T(8,128)(2,1)S(1)}, bf16[512,128]{1,0:T(8,128)(2,1)S(1)}, u32[]{:S(2)}, u32[]{:S(2)}) collective-permute-start(bf16[512,128]{1,0:T(8,128)(2,1)S(1)} %get-tuple-element.39), channel_id=1, source_target_pairs={{0,192},{32,224},{64,0},{96,32},{128,64},{160,96},{192,128},{224,1... | collective-permute-start | bytes 393224 | tf_op jit(solution)/shard_map/ppermute | solution.py:570
  56.0 7.0 %collective-permute-start.3 = (bf16[512,128]{1,0:T(8,128)(2,1)S(1)}, bf16[512,128]{1,0:T(8,128)(2,1)S(1)}, u32[]{:S(2)}, u32[]{:S(2)}) collective-permute-start(bf16[512,128]{1,0:T(8,128)(2,1)S(1)} %get-tuple-element.40), channel_id=1, source_target_pairs={{0,128},{32,160},{64,192},{96,224},{128,0},{160,32},{192,64},{224,... | collective-permute-start | bytes 393224 | tf_op jit(solution)/shard_map/ppermute | solution.py:570
  96.0 9.3 %collective-permute-start.6 = (bf16[512,128]{1,0:T(8,128)(2,1)S(1)}, bf16[512,128]{1,0:T(8,128)(2,1)S(1)}, u32[]{:S(2)}, u32[]{:S(2)}) collective-permute-start(bf16[512,128]{1,0:T(8,128)(2,1)S(1)} %bitcast.8), channel_id=1, source_target_pairs={{0,192},{32,224},{64,0},{96,32},{128,64},{160,96},{192,128},{224,1... | collective-permute-start | bytes 393224 | tf_op jit(solution)/shard_map/ppermute | solution.py:603
  96.8 9.4 %collective-permute-start.5 = (bf16[512,128]{1,0:T(8,128)(2,1)S(1)}, bf16[512,128]{1,0:T(8,128)(2,1)S(1)}, u32[]{:S(2)}, u32[]{:S(2)}) collective-permute-start(bf16[512,128]{1,0:T(8,128)(2,1)S(1)} %bitcast.9), channel_id=1, source_target_pairs={{0,64},{32,96},{64,128},{96,160},{128,192},{160,224},{192,0},{224,... | collective-permute-start | bytes 393224 | tf_op jit(solution)/shard_map/ppermute | solution.py:603
  97.5 12.4 %collective-permute-start.4 = (bf16[512,128]{1,0:T(8,128)(2,1)S(1)}, bf16[512,128]{1,0:T(8,128)(2,1)S(1)}, u32[]{:S(2)}, u32[]{:S(2)}) collective-permute-start(bf16[512,128]{1,0:T(8,128)(2,1)S(1)} %bitcast.10), channel_id=1, source_target_pairs={{0,128},{32,160},{64,192},{96,224},{128,0},{160,32},{192,64},{224,... | collective-permute-start | bytes 393224 | tf_op jit(solution)/shard_map/ppermute | solution.py:603
  98.1 12.9 %collective-permute-start.7 = (bf16[512,128]{1,0:T(8,128)(2,1)S(1)}, bf16[512,128]{1,0:T(8,128)(2,1)S(1)}, u32[]{:S(2)}, u32[]{:S(2)}) collective-permute-start(bf16[512,128]{1,0:T(8,128)(2,1)S(1)} %bitcast.11), channel_id=1, source_target_pairs={{0,32},{32,0},{64,96},{96,64},{128,160},{160,128},{192,224},{224,1... | collective-permute-start | bytes 393224 | tf_op jit(solution)/shard_map/ppermute | solution.py:618
  105.3 5.8 %collective-permute-start.8 = (bf16[512,128]{1,0:T(8,128)(2,1)S(1)}, bf16[512,128]{1,0:T(8,128)(2,1)S(1)}, u32[]{:S(2)}, u32[]{:S(2)}) collective-permute-start(bf16[512,128]{1,0:T(8,128)(2,1)S(1)} %collective-permute-done.6.refs_1_), channel_id=1, source_target_pairs={{0,32},{32,0},{64,96},{96,64},{128,160},{160,128},{192,224},{224,1... | collective-permute-start | bytes 393224 | tf_op jit(solution)/shard_map/ppermute | solution.py:618
  106.3 4.8 %collective-permute-start.10 = (bf16[512,128]{1,0:T(8,128)(2,1)S(1)}, bf16[512,128]{1,0:T(8,128)(2,1)S(1)}, u32[]{:S(2)}, u32[]{:S(2)}) collective-permute-start(bf16[512,128]{1,0:T(8,128)(2,1)S(1)} %collective-permute-done.5.refs_3_), channel_id=1, source_target_pairs={{0,32},{32,0},{64,96},{96,64},{128,160},{160,128},{192,224},{224,1... | collective-permute-start | bytes 393224 | tf_op jit(solution)/shard_map/ppermute | solution.py:618
  110.0 1.3 %collective-permute-start.9 = (bf16[512,128]{1,0:T(8,128)(2,1)S(1)}, bf16[512,128]{1,0:T(8,128)(2,1)S(1)}, u32[]{:S(2)}, u32[]{:S(2)}) collective-permute-start(bf16[512,128]{1,0:T(8,128)(2,1)S(1)} %collective-permute-done.4.refs_2_), channel_id=1, source_target_pairs={{0,32},{32,0},{64,96},{96,64},{128,160},{160,128},{192,224},{224,1... | collective-permute-start | bytes 393224 | tf_op jit(solution)/shard_map/ppermute | solution.py:618

commit v12 on v11

--- a/solution.py
+++ b/solution.py
@@ -128,8 +128,8 @@
     copies = [
         pltpu.make_async_copy(src, dst, sems.at[n]) for n, (src, dst) in enumerate(pairs)
     ]
-    for copy in copies:
-        copy.start()
+    for n in (3, 0, 1, 2, 4):
+        copies[n].start()
     bricks[...] = jnp.zeros((16, 128), F32)
     for copy in copies[:3]:
         copy.wait()

time: 113 us -> 113 us (level)
  no operation moved by 1% of the time
where the time goes in v12:
time: 113 us
  starting transfers between devices  38.9 us (34%)
  blocking collectives  32.3 us (29%)
  waiting for transfers between devices  23.3 us (21%)
  Pallas kernels  16 us (14%)
  between operations  1.7 us (2%)
    all_to_all x1, blocking collectives, on_device(): back = lax.all_to_all(sums, 'dev', split_axis=0, concat_axis=0, tiled=True)  17.5 us
    pallas_call x10, Pallas kernels, call(): pl.pallas_call(kernel, out_shape=shapes, in_specs=[SM] * len(scalars) + (...  16 us
    all_to_all x1, blocking collectives, on_device(): lax.all_to_all(terms, 'dev', split_axis=0, concat_axis=0, tiled=True)  14.8 us
    all_to_all x1, starting transfers between devices, on_device(): first = lax.all_to_all(msg, 'dev', split_axis=0, concat_axis=0, tiled=True)  12 us
    ppermute x4, starting transfers between devices, on_device(): others = [lax.ppermute(x, 'grp', swap) for x in mine]  10.5 us
    all_to_all x1, waiting for transfers between devices, on_device(): lax.all_to_all(answer, 'dev', split_axis=0, concat_axis=0, tiled=True)  9.36 us
    all_to_all x1, waiting for transfers between devices, on_device(): first = lax.all_to_all(msg, 'dev', split_axis=0, concat_axis=0, tiled=True)  8.96 us
    all_to_all x1, starting transfers between devices, on_device(): lax.all_to_all(answer, 'dev', split_axis=0, concat_axis=0, tiled=True)  6.29 us
  transfers between devices with their start and end apart: 13, of which 5 were waited for; matrix products, arithmetic and copies ran while one was open for 0% of the time, Pallas kernels for 4%

profile of v12, /device:TPU:1, one launch (start us, length us, event | category | flops | bytes accessed | tf_op | source)
XLA Modules:
  0.0 112.6 jit_solution(12989187110157013331)
XLA Ops:
  0.6 2.6 %ask.1 = bf16[32,32,128]{2,1,0:T(8,128)(2,1)} custom-call(bf16[2,128,512]{2,1,0:T(8,128)(2,1)} %feat.3, s32[2,26]{1,0:T(2,128)} %owner.1, s32[2,26]{1,0:T(2,128)} %slot.1, bf16[128,1024]{1,0:T(8,128)(2,1)} %constant.13.clone.choice), custom_call_target="tpu_custom_call" | custom-call | flops 2000000 | bytes 786848 | tf_op jit(solution)/shard_map/ask/pallas_call | solution.py:458
  3.2 12.0 %all-to-all-start = ((bf16[32,32,128]{2,1,0:T(8,128)(2,1)}), bf16[32,32,128]{2,1,0:T(8,128)(2,1)S(1)}, u32[]{:S(2)}, u32[]{:S(2)}) async-start(bf16[32,32,128]{2,1,0:T(8,128)(2,1)} %ask.1), calls=%async_computation | async-start | bytes 524288 | tf_op jit(solution)/shard_map/all_to_all | solution.py:519
  16.0 9.0 %all-to-all-done.got = bf16[32,32,128]{2,1,0:T(8,128)(2,1)S(1)} async-done(((bf16[32,32,128]{2,1,0:T(8,128)(2,1)}), bf16[32,32,128]{2,1,0:T(8,128)(2,1)S(1)}, u32[]{:S(2)}, u32[]{:S(2)}) %all-to-all-start) | async-done | bytes 262176 | tf_op jit(solution)/shard_map/all_to_all | solution.py:519
  25.0 1.3 %route.1 = (bf16[32,32,128]{2,1,0:T(8,128)(2,1)}, bf16[2,16,512]{2,1,0:T(8,128)(2,1)S(1)}) custom-call(bf16[32,32,128]{2,1,0:T(8,128)(2,1)S(1)} %all-to-all-done.got), custom_call_target="tpu_custom_call" | custom-call | flops 300000000 | bytes 557056 | tf_op jit(solution)/shard_map/route/pallas_call | solution.py:458
  26.3 6.3 %all-to-all-start.1 = ((bf16[32,32,128]{2,1,0:T(8,128)(2,1)}), bf16[32,32,128]{2,1,0:T(8,128)(2,1)S(1)}, u32[]{:S(2)}, u32[]{:S(2)}) async-start(bf16[32,32,128]{2,1,0:T(8,128)(2,1)} %get-tuple-element.30), calls=%async_computation.1 | async-start | bytes 524288 | tf_op jit(solution)/shard_map/all_to_all | solution.py:529
  32.7 0.1 fusion.5
  32.7 0.1 fusion.4.weight
  32.9 9.4 %all-to-all-done.1.got = bf16[32,32,128]{2,1,0:T(8,128)(2,1)S(1)} async-done(((bf16[32,32,128]{2,1,0:T(8,128)(2,1)}), bf16[32,32,128]{2,1,0:T(8,128)(2,1)S(1)}, u32[]{:S(2)}, u32[]{:S(2)}) %all-to-all-start.1) | async-done | bytes 262176 | tf_op jit(solution)/shard_map/all_to_all | solution.py:529
  42.3 0.1 iota.7.flags
  42.3 5.6 %forward.1 = (bf16[2,128,512]{2,1,0:T(8,128)(2,1)}, bf16[2,128,512]{2,1,0:T(8,128)(2,1)S(1)}, bf16[2048,128]{1,0:T(8,128)(2,1)S(1)}, bf16[2048,128]{1,0:T(8,128)(2,1)S(1)}) custom-call(s32[2]{0:T(128)S(1)} %copy-done.2, s32[2]{0:T(128)S(1)} %copy-done.3, s32[1]{0:T(128)} %bitcast.core, f32[8,128]{1,0:T(8,128)S(1)} %iota.7.flags, ...), custom_call_target="tpu_custom_call" | custom-call | flops 2000000000 | bytes 3444736 | tf_op jit(solution)/shard_map/forward/pallas_call | solution.py:458
  48.0 3.7 %collective-permute-start = (bf16[2048,128]{1,0:T(8,128)(2,1)S(1)}, bf16[2048,128]{1,0:T(8,128)(2,1)S(1)}, u32[]{:S(2)}, u32[]{:S(2)}) collective-permute-start(bf16[2048,128]{1,0:T(8,128)(2,1)S(1)} %get-tuple-element.33), channel_id=1, source_target_pairs={{0,32},{32,0},{64,96},{96,64},{128,160},{160,128},{192,224},{224,1... | collective-permute-start | bytes 1572872 | tf_op jit(solution)/shard_map/ppermute | solution.py:561
  51.7 1.5 %collective-permute-done.other = bf16[2048,128]{1,0:T(8,128)(2,1)S(1)} collective-permute-done((bf16[2048,128]{1,0:T(8,128)(2,1)S(1)}, bf16[2048,128]{1,0:T(8,128)(2,1)S(1)}, u32[]{:S(2)}, u32[]{:S(2)}) %collective-permute-start) | collective-permute-done | bytes 524320 | tf_op jit(solution)/shard_map/ppermute | solution.py:561
  53.2 0.1 pair.1
  53.4 1.3 %collective-permute-start.1 = (bf16[512,128]{1,0:T(8,128)(2,1)S(1)}, bf16[512,128]{1,0:T(8,128)(2,1)S(1)}, u32[]{:S(2)}, u32[]{:S(2)}) collective-permute-start(bf16[512,128]{1,0:T(8,128)(2,1)S(1)} %get-tuple-element.38), channel_id=1, source_target_pairs={{0,64},{32,96},{64,128},{96,160},{128,192},{160,224},{192,0},{224,... | collective-permute-start | bytes 393224 | tf_op jit(solution)/shard_map/ppermute | solution.py:570
  54.6 1.5 %collective-permute-start.2 = (bf16[512,128]{1,0:T(8,128)(2,1)S(1)}, bf16[512,128]{1,0:T(8,128)(2,1)S(1)}, u32[]{:S(2)}, u32[]{:S(2)}) collective-permute-start(bf16[512,128]{1,0:T(8,128)(2,1)S(1)} %get-tuple-element.39), channel_id=1, source_target_pairs={{0,192},{32,224},{64,0},{96,32},{128,64},{160,96},{192,128},{224,1... | collective-permute-start | bytes 393224 | tf_op jit(solution)/shard_map/ppermute | solution.py:570
  56.1 1.5 %collective-permute-start.3 = (bf16[512,128]{1,0:T(8,128)(2,1)S(1)}, bf16[512,128]{1,0:T(8,128)(2,1)S(1)}, u32[]{:S(2)}, u32[]{:S(2)}) collective-permute-start(bf16[512,128]{1,0:T(8,128)(2,1)S(1)} %get-tuple-element.40), channel_id=1, source_target_pairs={{0,128},{32,160},{64,192},{96,224},{128,0},{160,32},{192,64},{224,... | collective-permute-start | bytes 393224 | tf_op jit(solution)/shard_map/ppermute | solution.py:570
  57.6 2.4 %backward.1 = (f32[2,512,128]{2,1,0:T(8,128)S(1)}, bf16[32,32,128]{2,1,0:T(8,128)(2,1)S(1)}) custom-call(bf16[2,128,512]{2,1,0:T(8,128)(2,1)S(1)} %get-tuple-element.35.grad_t, bf16[1408,384]{1,0:T(8,128)(2,1)S(1)} %fusion.4.weight), custom_call_target="tpu_custom_call" | custom-call | flops 4000000000 | bytes 2129920 | tf_op jit(solution)/shard_map/backward/pallas_call | solution.py:458
  60.0 3.1 %collective-permute-done.3.away3 = bf16[512,128]{1,0:T(8,128)(2,1)S(1)} collective-permute-done((bf16[512,128]{1,0:T(8,128)(2,1)S(1)}, bf16[512,128]{1,0:T(8,128)(2,1)S(1)}, u32[]{:S(2)}, u32[]{:S(2)}) %collective-permute-start.3) | collective-permute-done | bytes 131104 | tf_op jit(solution)/shard_map/ppermute | solution.py:570
  63.2 0.1 join.1
  63.2 14.8 %all_to_all.20.got = bf16[32,48,128]{2,1,0:T(8,128)(2,1)S(1)} all-to-all(bf16[32,48,128]{2,1,0:T(8,128)(2,1)S(1)} %join.1), channel_id=1, replica_groups=mesh['grp'=8,'dev'=32] {'dev'}, dimensions={0} | all-to-all | bytes 786432 | tf_op jit(solution)/shard_map/all_to_all | solution.py:590
  78.0 0.5 merge.1
  78.5 17.5 %all_to_all.21.got = bf16[32,48,128]{2,1,0:T(8,128)(2,1)S(1)} all-to-all(bf16[32,48,128]{2,1,0:T(8,128)(2,1)S(1)} %merge.1), channel_id=1, replica_groups=mesh['grp'=8,'dev'=32] {'dev'}, dimensions={0} | all-to-all | bytes 786432 | tf_op jit(solution)/shard_map/all_to_all | solution.py:600
  96.0 0.9 collective-permute-start.6
  96.9 0.7 collective-permute-start.5
  97.6 0.6 collective-permute-start.4
  98.2 5.8 %collective-permute-start.7 = (bf16[512,128]{1,0:T(8,128)(2,1)S(1)}, bf16[512,128]{1,0:T(8,128)(2,1)S(1)}, u32[]{:S(2)}, u32[]{:S(2)}) collective-permute-start(bf16[512,128]{1,0:T(8,128)(2,1)S(1)} %bitcast.11), channel_id=1, source_target_pairs={{0,32},{32,0},{64,96},{96,64},{128,160},{160,128},{192,224},{224,1... | collective-permute-start | bytes 393224 | tf_op jit(solution)/shard_map/ppermute | solution.py:618
  104.0 1.3 %finish.1 = bf16[2,128,512]{2,1,0:T(8,128)(2,1)} custom-call(f32[8,128]{1,0:T(8,128)S(1)} %iota.7.flags, bf16[32,48,128]{2,1,0:T(8,128)(2,1)S(1)} %all_to_all.21.got, f32[2,512,128]{2,1,0:T(8,128)S(1)} %get-tuple-element.42.own, bf16[2,128,512]{2,1,0:T(8,128)(2,1)S(1)} %copy-done.1), custom_call_target="tpu_custom_call" | custom-call | flops 300000000 | bytes 1445888 | tf_op jit(solution)/shard_map/finish/pallas_call | solution.py:458
  105.3 1.0 collective-permute-start.8
  106.3 3.7 %collective-permute-start.10 = (bf16[512,128]{1,0:T(8,128)(2,1)S(1)}, bf16[512,128]{1,0:T(8,128)(2,1)S(1)}, u32[]{:S(2)}, u32[]{:S(2)}) collective-permute-start(bf16[512,128]{1,0:T(8,128)(2,1)S(1)} %collective-permute-done.5.refs_3_), channel_id=1, source_target_pairs={{0,32},{32,0},{64,96},{96,64},{128,160},{160,128},{192,224},{224,1... | collective-permute-start | bytes 393224 | tf_op jit(solution)/shard_map/ppermute | solution.py:618
  110.0 1.1 assemble.2
  111.1 0.3 collective-permute-done.9.refs_2_
  111.4 1.1 assemble.3
  (25 shorter events, 0.1 us)
Async XLA Ops:
  0.6 32.0 %copy-start.4 = (bf16[27,128,128]{2,1,0:T(8,128)(2,1)S(1)}, bf16[27,128,128]{2,1,0:T(8,128)(2,1)}, u32[]{:S(2)}) copy-start(bf16[27,128,128]{2,1,0:T(8,128)(2,1)} %param.13) | copy-start | bytes 2654212
  3.2 21.7 %all-to-all-start = ((bf16[32,32,128]{2,1,0:T(8,128)(2,1)}), bf16[32,32,128]{2,1,0:T(8,128)(2,1)S(1)}, u32[]{:S(2)}, u32[]{:S(2)}) async-start(bf16[32,32,128]{2,1,0:T(8,128)(2,1)} %ask.1), calls=%async_computation | async-start | bytes 524288 | tf_op jit(solution)/shard_map/all_to_all | solution.py:519
  15.3 17.4 %copy-start.5 = (bf16[128,256]{1,0:T(8,128)(2,1)S(1)}, bf16[128,256]{1,0:T(8,128)(2,1)}, u32[]{:S(2)}) copy-start(bf16[128,256]{1,0:T(8,128)(2,1)} %param.14) | copy-start | bytes 196612
  15.3 17.4 %copy-start.6 = (bf16[256,128]{1,0:T(8,128)(2,1)S(1)}, bf16[256,128]{1,0:T(8,128)(2,1)}, u32[]{:S(2)}) copy-start(bf16[256,128]{1,0:T(8,128)(2,1)} %param.15) | copy-start | bytes 196612
  26.3 16.0 %all-to-all-start.1 = ((bf16[32,32,128]{2,1,0:T(8,128)(2,1)}), bf16[32,32,128]{2,1,0:T(8,128)(2,1)S(1)}, u32[]{:S(2)}, u32[]{:S(2)}) async-start(bf16[32,32,128]{2,1,0:T(8,128)(2,1)} %get-tuple-element.30), calls=%async_computation.1 | async-start | bytes 524288 | tf_op jit(solution)/shard_map/all_to_all | solution.py:529
  32.6 9.7 %copy-start = (bf16[2,128,512]{2,1,0:T(8,128)(2,1)S(1)}, bf16[2,128,512]{2,1,0:T(8,128)(2,1)}, u32[]{:S(2)}) copy-start(bf16[2,128,512]{2,1,0:T(8,128)(2,1)} %feat.3) | copy-start | bytes 786436
  32.6 9.7 %copy-start.1 = (bf16[2,128,512]{2,1,0:T(8,128)(2,1)S(1)}, bf16[2,128,512]{2,1,0:T(8,128)(2,1)}, u32[]{:S(2)}) copy-start(bf16[2,128,512]{2,1,0:T(8,128)(2,1)} %gout.3) | copy-start | bytes 786436
  32.6 9.7 %copy-start.2 = (s32[2]{0:T(128)S(1)}, s32[2]{0:T(128)}, u32[]{:S(2)}) copy-start(s32[2]{0:T(128)} %parent.1) | copy-start | bytes 28
  32.6 9.7 %copy-start.3 = (s32[2]{0:T(128)S(1)}, s32[2]{0:T(128)}, u32[]{:S(2)}) copy-start(s32[2]{0:T(128)} %child.1) | copy-start | bytes 28
  48.0 5.2 %collective-permute-start = (bf16[2048,128]{1,0:T(8,128)(2,1)S(1)}, bf16[2048,128]{1,0:T(8,128)(2,1)S(1)}, u32[]{:S(2)}, u32[]{:S(2)}) collective-permute-start(bf16[2048,128]{1,0:T(8,128)(2,1)S(1)} %get-tuple-element.33), channel_id=1, source_target_pairs={{0,32},{32,0},{64,96},{96,64},{128,160},{160,128},{192,224},{224,1... | collective-permute-start | bytes 1572872 | tf_op jit(solution)/shard_map/ppermute | solution.py:561
  53.4 6.6 %collective-permute-start.1 = (bf16[512,128]{1,0:T(8,128)(2,1)S(1)}, bf16[512,128]{1,0:T(8,128)(2,1)S(1)}, u32[]{:S(2)}, u32[]{:S(2)}) collective-permute-start(bf16[512,128]{1,0:T(8,128)(2,1)S(1)} %get-tuple-element.38), channel_id=1, source_target_pairs={{0,64},{32,96},{64,128},{96,160},{128,192},{160,224},{192,0},{224,... | collective-permute-start | bytes 393224 | tf_op jit(solution)/shard_map/ppermute | solution.py:570
  54.6 5.4 %collective-permute-start.2 = (bf16[512,128]{1,0:T(8,128)(2,1)S(1)}, bf16[512,128]{1,0:T(8,128)(2,1)S(1)}, u32[]{:S(2)}, u32[]{:S(2)}) collective-permute-start(bf16[512,128]{1,0:T(8,128)(2,1)S(1)} %get-tuple-element.39), channel_id=1, source_target_pairs={{0,192},{32,224},{64,0},{96,32},{128,64},{160,96},{192,128},{224,1... | collective-permute-start | bytes 393224 | tf_op jit(solution)/shard_map/ppermute | solution.py:570
  56.1 7.0 %collective-permute-start.3 = (bf16[512,128]{1,0:T(8,128)(2,1)S(1)}, bf16[512,128]{1,0:T(8,128)(2,1)S(1)}, u32[]{:S(2)}, u32[]{:S(2)}) collective-permute-start(bf16[512,128]{1,0:T(8,128)(2,1)S(1)} %get-tuple-element.40), channel_id=1, source_target_pairs={{0,128},{32,160},{64,192},{96,224},{128,0},{160,32},{192,64},{224,... | collective-permute-start | bytes 393224 | tf_op jit(solution)/shard_map/ppermute | solution.py:570
  96.0 9.3 %collective-permute-start.6 = (bf16[512,128]{1,0:T(8,128)(2,1)S(1)}, bf16[512,128]{1,0:T(8,128)(2,1)S(1)}, u32[]{:S(2)}, u32[]{:S(2)}) collective-permute-start(bf16[512,128]{1,0:T(8,128)(2,1)S(1)} %bitcast.8), channel_id=1, source_target_pairs={{0,192},{32,224},{64,0},{96,32},{128,64},{160,96},{192,128},{224,1... | collective-permute-start | bytes 393224 | tf_op jit(solution)/shard_map/ppermute | solution.py:603
  96.9 9.4 %collective-permute-start.5 = (bf16[512,128]{1,0:T(8,128)(2,1)S(1)}, bf16[512,128]{1,0:T(8,128)(2,1)S(1)}, u32[]{:S(2)}, u32[]{:S(2)}) collective-permute-start(bf16[512,128]{1,0:T(8,128)(2,1)S(1)} %bitcast.9), channel_id=1, source_target_pairs={{0,64},{32,96},{64,128},{96,160},{128,192},{160,224},{192,0},{224,... | collective-permute-start | bytes 393224 | tf_op jit(solution)/shard_map/ppermute | solution.py:603
  97.6 12.4 %collective-permute-start.4 = (bf16[512,128]{1,0:T(8,128)(2,1)S(1)}, bf16[512,128]{1,0:T(8,128)(2,1)S(1)}, u32[]{:S(2)}, u32[]{:S(2)}) collective-permute-start(bf16[512,128]{1,0:T(8,128)(2,1)S(1)} %bitcast.10), channel_id=1, source_target_pairs={{0,128},{32,160},{64,192},{96,224},{128,0},{160,32},{192,64},{224,... | collective-permute-start | bytes 393224 | tf_op jit(solution)/shard_map/ppermute | solution.py:603
  98.2 12.9 %collective-permute-start.7 = (bf16[512,128]{1,0:T(8,128)(2,1)S(1)}, bf16[512,128]{1,0:T(8,128)(2,1)S(1)}, u32[]{:S(2)}, u32[]{:S(2)}) collective-permute-start(bf16[512,128]{1,0:T(8,128)(2,1)S(1)} %bitcast.11), channel_id=1, source_target_pairs={{0,32},{32,0},{64,96},{96,64},{128,160},{160,128},{192,224},{224,1... | collective-permute-start | bytes 393224 | tf_op jit(solution)/shard_map/ppermute | solution.py:618
  105.3 5.8 %collective-permute-start.8 = (bf16[512,128]{1,0:T(8,128)(2,1)S(1)}, bf16[512,128]{1,0:T(8,128)(2,1)S(1)}, u32[]{:S(2)}, u32[]{:S(2)}) collective-permute-start(bf16[512,128]{1,0:T(8,128)(2,1)S(1)} %collective-permute-done.6.refs_1_), channel_id=1, source_target_pairs={{0,32},{32,0},{64,96},{96,64},{128,160},{160,128},{192,224},{224,1... | collective-permute-start | bytes 393224 | tf_op jit(solution)/shard_map/ppermute | solution.py:618
  106.3 4.8 %collective-permute-start.10 = (bf16[512,128]{1,0:T(8,128)(2,1)S(1)}, bf16[512,128]{1,0:T(8,128)(2,1)S(1)}, u32[]{:S(2)}, u32[]{:S(2)}) collective-permute-start(bf16[512,128]{1,0:T(8,128)(2,1)S(1)} %collective-permute-done.5.refs_3_), channel_id=1, source_target_pairs={{0,32},{32,0},{64,96},{96,64},{128,160},{160,128},{192,224},{224,1... | collective-permute-start | bytes 393224 | tf_op jit(solution)/shard_map/ppermute | solution.py:618
  110.0 1.3 %collective-permute-start.9 = (bf16[512,128]{1,0:T(8,128)(2,1)S(1)}, bf16[512,128]{1,0:T(8,128)(2,1)S(1)}, u32[]{:S(2)}, u32[]{:S(2)}) collective-permute-start(bf16[512,128]{1,0:T(8,128)(2,1)S(1)} %collective-permute-done.4.refs_2_), channel_id=1, source_target_pairs={{0,32},{32,0},{64,96},{96,64},{128,160},{160,128},{192,224},{224,1... | collective-permute-start | bytes 393224 | tf_op jit(solution)/shard_map/ppermute | solution.py:618
